TPU v7x, 32 devices: a whole 2x2x4 slice. The times are simulated.
32 devices in a mesh: fsdp: 4 (over y, x), tensor: 8 (over z, core).
Axes of the slice: x: 2, y: 2, z: 4, core: 2. Of those that a mesh axis runs over, the one named last changes fastest.
Arguments:
- tokens: bfloat16 [2, 4, 1024, 2048], P(None, 'fsdp', 'tensor'), may hold values from -6 to 6
- lengths: int32 [2, 4], P(None, 'fsdp'), may hold values from 256 to 1024, as said below
- routes: int32 [2, 4, 1024, 4], P(None, 'fsdp'), may hold values from 0 to 7, all different within a row; in each aligned block of 128 rows (0 to 127, 128 to 255, ..., all dimensions but the last counted through in order) at most 96 rows name the same one
- norm1_gain: bfloat16 [2048], P(('fsdp', 'tensor')), may hold values from 0.5 to 1.5
- w_query: bfloat16 [2048, 2048], P('fsdp', 'tensor'), may hold values from -0.125 to 0.125
- w_key: bfloat16 [2048, 2048], P('fsdp', 'tensor'), may hold values from -0.125 to 0.125
- w_value: bfloat16 [2048, 2048], P('fsdp', 'tensor'), may hold values from -0.125 to 0.125
- b_query: bfloat16 [16, 128], P('tensor', 'fsdp'), may hold values from -3 to 3
- b_key: bfloat16 [16, 128], P('tensor', 'fsdp'), may hold values from -3 to 3
- b_value: bfloat16 [16, 128], P('tensor', 'fsdp'), may hold values from -3 to 3
- w_out: bfloat16 [2048, 2048], P('tensor', 'fsdp'), may hold values from -1.5 to 1.5
- norm2_gain: bfloat16 [2048], P(('fsdp', 'tensor')), may hold values from 0.5 to 1.5
- router: bfloat16 [2048, 8], P(('fsdp', 'tensor')), may hold values from -0.25 to 0.25
- shared_gate_vec: bfloat16 [2048], P(('fsdp', 'tensor')), may hold values from -0.125 to 0.125
- shared_gate: bfloat16 [2048, 5632], P('fsdp', 'tensor'), may hold values from -0.125 to 0.125
- shared_up: bfloat16 [2048, 5632], P('fsdp', 'tensor'), may hold values from -0.125 to 0.125
- shared_down: bfloat16 [5632, 2048], P('tensor', 'fsdp'), may hold values from -0.625 to 0.625
- expert_gate: bfloat16 [8, 2048, 1408], P('tensor', 'fsdp'), may hold values from -0.125 to 0.125
- expert_up: bfloat16 [8, 2048, 1408], P('tensor', 'fsdp'), may hold values from -0.125 to 0.125
- expert_down: bfloat16 [8, 1408, 2048], P('tensor', None, 'fsdp'), may hold values from -1.25 to 1.25
- cotangent: bfloat16 [2, 4, 1024, 2048], P(None, 'fsdp', 'tensor'), may hold values from -6 to 6
Outputs:
- layer_out: bfloat16 [2, 4, 1024, 2048], P(None, 'fsdp', 'tensor')
- grad_tokens: bfloat16 [2, 4, 1024, 2048], P(None, 'fsdp', 'tensor')
- grad_norm1_gain: float32 [2048], P(('fsdp', 'tensor'))
- grad_w_query: float32 [2048, 2048], P('fsdp', 'tensor')
- grad_w_key: float32 [2048, 2048], P('fsdp', 'tensor')
- grad_w_value: float32 [2048, 2048], P('fsdp', 'tensor')
- grad_b_query: float32 [16, 128], P('tensor', 'fsdp')
- grad_b_key: float32 [16, 128], P('tensor', 'fsdp')
- grad_b_value: float32 [16, 128], P('tensor', 'fsdp')
- grad_w_out: float32 [2048, 2048], P('tensor', 'fsdp')
- grad_norm2_gain: float32 [2048], P(('fsdp', 'tensor'))
- grad_router: float32 [2048, 8], P(('fsdp', 'tensor'))
- grad_shared_gate_vec: float32 [2048], P(('fsdp', 'tensor'))
- grad_shared_gate: float32 [2048, 5632], P('fsdp', 'tensor')
- grad_shared_up: float32 [2048, 5632], P('fsdp', 'tensor')
- grad_shared_down: float32 [5632, 2048], P('tensor', 'fsdp')
- grad_expert_gate: float32 [8, 2048, 1408], P('tensor', 'fsdp')
- grad_expert_up: float32 [8, 2048, 1408], P('tensor', 'fsdp')
- grad_expert_down: float32 [8, 1408, 2048], P('tensor', None, 'fsdp')
Inputs may be any that keep to these rules, and one draw needn't show every extreme that they name: `lengths`: one sequence of every draw has exactly 1024 valid tokens. `routes`: each row names 4 different experts; among the 128 rows of one device within a sequence no expert is named by more than 96 rows, and in every draw some expert is named by exactly 96 of them.
All inputs are finite; a program needn't handle non-finite values.
Results may differ from a plain program's by a relative error of at most 0.03.
The roundings to bfloat16 on the way count: a program that leaves them out, or rounds other values in their place, can miss the bound.
Values may be sent and summed in bfloat16 or wider, within the bound.
A program may use at most 320 MiB of HBM per device.

v0:
```python
import jax
import jax.numpy as jnp
from jax import lax
from jax.sharding import PartitionSpec as P

HD = 128
TOP = 4


EPSILON = 1e-06
ROPE_BASE = 1000000.0
HIGHEST = lax.Precision.HIGHEST


def matmul(left, right):
    return jnp.dot(left, right, preferred_element_type=jnp.float32)


def contract_rows(left, right):
    return lax.dot_general(
        left, right, (((0,), (0,)), ((), ())), preferred_element_type=jnp.float32
    )


def contract_cols(left, right):
    return lax.dot_general(
        left, right, (((1,), (1,)), ((), ())), preferred_element_type=jnp.float32
    )


def normalize(values):
    inverse = lax.rsqrt(jnp.mean(values * values, axis=-1, keepdims=True) + EPSILON)
    return (values * inverse, inverse)


def norm_back(grad_normed, unit, inverse, gain):
    grad_unit = grad_normed * gain
    grad_values = inverse * (grad_unit - unit * jnp.mean(grad_unit * unit, axis=-1, keepdims=True))
    return (grad_values, jnp.sum(grad_normed * unit, axis=0))


def rotary(values, positions, direction):
    half_dim = values.shape[-1] // 2
    frequency = ROPE_BASE ** (-(2.0 * jnp.arange(half_dim, dtype=jnp.float32)) / values.shape[-1])
    angles = positions.astype(jnp.float32)[:, None] * frequency[None, :]
    cosine_part = jnp.cos(angles)[:, None, :]
    sine_part = direction * jnp.sin(angles)[:, None, :]
    first_half = values[..., :half_dim]
    second_half = values[..., half_dim:]
    return jnp.concatenate(
        [
            first_half * cosine_part - second_half * sine_part,
            second_half * cosine_part + first_half * sine_part,
        ],
        axis=-1,
    )


def swiglu(gate_act, up_act):
    return (jax.nn.silu(gate_act) * up_act).astype(jnp.bfloat16)


def swiglu_back(grad_hidden, gate_act, up_act):
    sigmoid_gate = jax.nn.sigmoid(gate_act)
    grad_gate = grad_hidden * up_act * sigmoid_gate * (1.0 + gate_act * (1.0 - sigmoid_gate))
    grad_up = grad_hidden * gate_act * sigmoid_gate
    return (grad_gate.astype(jnp.bfloat16), grad_up.astype(jnp.bfloat16))


def pick_slots(route_rows, expert_id, slot_total):
    chosen = jnp.any(route_rows == expert_id, axis=1)
    rank_of = jnp.cumsum(chosen.astype(jnp.int32)) - 1
    target = jnp.where(chosen, rank_of, slot_total)
    token_ids = jnp.arange(route_rows.shape[0], dtype=jnp.int32)
    slot_index = jnp.zeros((slot_total,), jnp.int32).at[target].set(token_ids, mode="drop")
    filled = jnp.sum(chosen.astype(jnp.int32))
    slot_used = (jnp.arange(slot_total, dtype=jnp.int32) < filled).astype(jnp.float32)
    return (slot_index, slot_used)


def block_scores(query_block, key_rows, first_row, length):
    block_len = query_block.shape[0]
    score_scale = query_block.shape[-1] ** (-0.5)
    key_pos = jnp.arange(key_rows.shape[0], dtype=jnp.int32)
    scores = (
        jnp.einsum("qhd,khd->hqk", query_block, key_rows, preferred_element_type=jnp.float32)
        * score_scale
    )
    row_pos = first_row + jnp.arange(block_len, dtype=jnp.int32)
    allowed = (key_pos[None, :] <= row_pos[:, None]) & (key_pos[None, :] < length)
    return jnp.where(allowed[None], scores, -1e30)


def attend_forward(query_rows, key_rows, values, length):
    seq_len = query_rows.shape[0]
    block_len = min(512, seq_len)
    starts = jnp.arange(seq_len // block_len, dtype=jnp.int32) * block_len

    def one_block(first_row):
        query_block = lax.dynamic_slice_in_dim(query_rows, first_row, block_len, 0)
        scores = block_scores(query_block, key_rows, first_row, length)
        top_score = jnp.max(scores, axis=-1, keepdims=True)
        exp_scores = jnp.exp(scores - top_score)
        totals = jnp.sum(exp_scores, axis=-1, keepdims=True)
        weights = (exp_scores / totals).astype(jnp.bfloat16)
        mixed_block = jnp.einsum(
            "hqk,khd->qhd", weights, values, preferred_element_type=jnp.float32
        )
        return (mixed_block.astype(jnp.bfloat16), (top_score + jnp.log(totals))[..., 0])

    mixed_blocks, log_totals = lax.map(one_block, starts)
    return (mixed_blocks.reshape(seq_len, -1), log_totals)


def attend_backward(query_rows, key_rows, values, length, grad_mixed, log_totals):
    seq_len = query_rows.shape[0]
    block_len = min(512, seq_len)
    score_scale = query_rows.shape[-1] ** (-0.5)
    starts = jnp.arange(seq_len // block_len, dtype=jnp.int32) * block_len

    def one_block(carried, block_item):
        first_row, block_lse = block_item
        query_block = lax.dynamic_slice_in_dim(query_rows, first_row, block_len, 0)
        grad_block = lax.dynamic_slice_in_dim(grad_mixed, first_row, block_len, 0)
        scores = block_scores(query_block, key_rows, first_row, length)
        weights = jnp.exp(scores - block_lse[..., None])
        grad_weights = jnp.einsum(
            "qhd,khd->hqk", grad_block, values, preferred_element_type=jnp.float32
        )
        inner = jnp.sum(weights * grad_weights, axis=-1, keepdims=True)
        grad_scores = (score_scale * weights * (grad_weights - inner)).astype(jnp.bfloat16)
        grad_query = jnp.einsum(
            "hqk,khd->qhd", grad_scores, key_rows, preferred_element_type=jnp.float32
        )
        grad_key = carried[0] + jnp.einsum(
            "hqk,qhd->khd", grad_scores, query_block, preferred_element_type=jnp.float32
        )
        grad_value = carried[1] + jnp.einsum(
            "hqk,qhd->khd",
            weights.astype(jnp.bfloat16),
            grad_block,
            preferred_element_type=jnp.float32,
        )
        return ((grad_key, grad_value), grad_query)

    zeros_kv = jnp.zeros(key_rows.shape, jnp.float32)
    (grad_key, grad_value), grad_query = lax.scan(
        one_block, (zeros_kv, zeros_kv), (starts, log_totals)
    )
    return (grad_query.reshape(query_rows.shape), grad_key, grad_value)


def gather_layer(
    w_query,
    w_key,
    w_value,
    b_query,
    b_key,
    b_value,
    w_out,
    shared_gate,
    shared_up,
    shared_down,
    expert_gate,
    expert_up,
    expert_down,
):
    return (
        lax.all_gather(w_query, "fsdp", axis=0, tiled=True),
        lax.all_gather(w_key, "fsdp", axis=0, tiled=True),
        lax.all_gather(w_value, "fsdp", axis=0, tiled=True),
        lax.all_gather(b_query, "fsdp", axis=1, tiled=True),
        lax.all_gather(b_key, "fsdp", axis=1, tiled=True),
        lax.all_gather(b_value, "fsdp", axis=1, tiled=True),
        lax.all_gather(w_out, "fsdp", axis=1, tiled=True),
        lax.all_gather(shared_gate, "fsdp", axis=0, tiled=True),
        lax.all_gather(shared_up, "fsdp", axis=0, tiled=True),
        lax.all_gather(shared_down, "fsdp", axis=1, tiled=True),
        lax.all_gather(expert_gate, "fsdp", axis=1, tiled=True),
        lax.all_gather(expert_up, "fsdp", axis=1, tiled=True),
        lax.all_gather(expert_down, "fsdp", axis=2, tiled=True),
    )


def local(
    tokens,
    lengths,
    routes,
    norm1_gain,
    w_query,
    w_key,
    w_value,
    b_query,
    b_key,
    b_value,
    w_out,
    norm2_gain,
    router,
    shared_gate_vec,
    shared_gate,
    shared_up,
    shared_down,
    expert_gate,
    expert_up,
    expert_down,
    cotangent,
):
    tensor_size = lax.axis_size("tensor")
    tensor_rank = lax.axis_index("tensor")
    micro_count = tokens.shape[0]
    local_rows = tokens.shape[2]
    seq_len = local_rows * tensor_size
    heads_here = w_query.shape[1] // HD
    experts_here = expert_gate.shape[0]
    expert_total = experts_here * tensor_size
    capacity = local_rows * TOP * 3 // (2 * expert_total)
    slot_total = tensor_size * capacity
    own_first = tensor_rank * local_rows
    positions = jnp.arange(seq_len, dtype=jnp.int32)
    local_pos = own_first + jnp.arange(local_rows, dtype=jnp.int32)
    small_full = (
        lax.all_gather(norm1_gain, ("fsdp", "tensor"), axis=0, tiled=True),
        lax.all_gather(norm2_gain, ("fsdp", "tensor"), axis=0, tiled=True),
        lax.all_gather(router, ("fsdp", "tensor"), axis=0, tiled=True),
        lax.all_gather(shared_gate_vec, ("fsdp", "tensor"), axis=0, tiled=True),
    )
    gain_one = small_full[0].astype(jnp.float32)
    gain_two = small_full[1].astype(jnp.float32)
    router_full = small_full[2]
    gate_vec = small_full[3]
    grad_gain_one = jnp.zeros(gain_one.shape, jnp.float32)
    grad_gain_two = jnp.zeros(gain_two.shape, jnp.float32)
    grad_router_w = jnp.zeros(router_full.shape, jnp.float32)
    grad_gate_vec = jnp.zeros(gate_vec.shape, jnp.float32)
    layer_outs = []
    input_grads = []
    for micro_id in range(micro_count):
        forward_weights = gather_layer(
            w_query,
            w_key,
            w_value,
            b_query,
            b_key,
            b_value,
            w_out,
            shared_gate,
            shared_up,
            shared_down,
            expert_gate,
            expert_up,
            expert_down,
        )
        (
            full_wq,
            full_wk,
            full_wv,
            full_bq,
            full_bk,
            full_bv,
            full_wo,
            full_sg,
            full_su,
            full_sd,
            full_eg,
            full_eu,
            full_ed,
        ) = forward_weights
        length = lengths[micro_id, 0]
        route_rows = routes[micro_id, 0]
        inputs = tokens[micro_id, 0].astype(jnp.float32)
        unit_one, inverse_one = normalize(inputs)
        normed_one = (unit_one * gain_one).astype(jnp.bfloat16)
        rows_one = lax.all_gather(normed_one, "tensor", axis=0, tiled=True)
        query_pre = matmul(rows_one, full_wq) + full_bq.reshape(-1).astype(jnp.float32)
        key_pre = matmul(rows_one, full_wk) + full_bk.reshape(-1).astype(jnp.float32)
        query_rows = rotary(query_pre.reshape(seq_len, heads_here, HD), positions, 1.0).astype(
            jnp.bfloat16
        )
        key_rows = rotary(key_pre.reshape(seq_len, heads_here, HD), positions, 1.0).astype(
            jnp.bfloat16
        )
        value_rows = (matmul(rows_one, full_wv) + full_bv.reshape(-1).astype(jnp.float32)).astype(
            jnp.bfloat16
        )
        value_rows = value_rows.reshape(seq_len, heads_here, HD)
        mixed_heads, log_totals = attend_forward(query_rows, key_rows, value_rows, length)
        attended = lax.psum_scatter(
            matmul(mixed_heads, full_wo), "tensor", scatter_dimension=0, tiled=True
        )
        hidden_one = inputs + attended
        unit_two, inverse_two = normalize(hidden_one)
        normed_two = (unit_two * gain_two).astype(jnp.bfloat16)
        rows_two = lax.all_gather(normed_two, "tensor", axis=0, tiled=True)
        router_probs = jax.nn.softmax(matmul(rows_two, router_full), axis=-1)
        shared_scale = jax.nn.sigmoid(matmul(rows_two, gate_vec))
        shared_gate_act = matmul(rows_two, full_sg)
        shared_up_act = matmul(rows_two, full_su)
        shared_hidden = swiglu(shared_gate_act, shared_up_act)
        shared_result = matmul(shared_hidden, full_sd)
        combined = shared_scale[:, None] * shared_result
        expert_j = 0
        expert_id = tensor_rank * experts_here + expert_j
        slot_index, slot_used = pick_slots(route_rows, expert_id, slot_total)
        expert_in = rows_two[slot_index]
        expert_gate_act = matmul(expert_in, full_eg[expert_j])
        expert_up_act = matmul(expert_in, full_eu[expert_j])
        expert_hidden = swiglu(expert_gate_act, expert_up_act)
        expert_result = matmul(expert_hidden, full_ed[expert_j])
        prob_column = lax.dynamic_slice_in_dim(router_probs, expert_id, 1, 1)[:, 0]
        slot_weight = prob_column[slot_index] * slot_used
        combined = combined.at[slot_index].add(slot_weight[:, None] * expert_result)
        expert_saved = [
            (
                expert_id,
                slot_index,
                slot_used,
                expert_in,
                expert_gate_act,
                expert_up_act,
                expert_hidden,
                expert_result,
                slot_weight,
            )
        ]
        mixed_ffn = lax.psum_scatter(combined, "tensor", scatter_dimension=0, tiled=True)
        inside = (local_pos < length).astype(jnp.float32)
        layer_outs.append((inside[:, None] * (hidden_one + mixed_ffn)).astype(jnp.bfloat16))
        backward_weights = gather_layer(
            w_query,
            w_key,
            w_value,
            b_query,
            b_key,
            b_value,
            w_out,
            shared_gate,
            shared_up,
            shared_down,
            expert_gate,
            expert_up,
            expert_down,
        )
        (
            full_wq,
            full_wk,
            full_wv,
            full_bq,
            full_bk,
            full_bv,
            full_wo,
            full_sg,
            full_su,
            full_sd,
            full_eg,
            full_eu,
            full_ed,
        ) = backward_weights
        grad_out = inside[:, None] * cotangent[micro_id, 0].astype(jnp.float32)
        grad_all = lax.all_gather(
            grad_out.astype(jnp.bfloat16), "tensor", axis=0, tiled=True
        ).astype(jnp.float32)
        grad_shared_res = (shared_scale[:, None] * grad_all).astype(jnp.bfloat16)
        grad_scale_part = jnp.sum(grad_all * shared_result, axis=1)
        grad_shared_hidden = contract_cols(grad_shared_res, full_sd)
        grad_sg_act, grad_su_act = swiglu_back(grad_shared_hidden, shared_gate_act, shared_up_act)
        grad_sd = contract_rows(shared_hidden, grad_shared_res)
        grad_sg = contract_rows(rows_two, grad_sg_act)
        grad_su = contract_rows(rows_two, grad_su_act)
        grad_rows_two = contract_cols(grad_sg_act, full_sg) + contract_cols(grad_su_act, full_su)
        grad_eg = jnp.zeros(full_eg.shape, jnp.float32)
        grad_eu = jnp.zeros(full_eu.shape, jnp.float32)
        grad_ed = jnp.zeros(full_ed.shape, jnp.float32)
        expert_cols = jnp.arange(expert_total, dtype=jnp.int32)
        expert_j = 0
        (
            expert_id,
            slot_index,
            slot_used,
            expert_in,
            expert_gate_act,
            expert_up_act,
            expert_hidden,
            expert_result,
            slot_weight,
        ) = expert_saved[expert_j]
        slot_grads = grad_all[slot_index]
        grad_result = (slot_weight[:, None] * slot_grads).astype(jnp.bfloat16)
        weight_grad = jnp.sum(slot_grads * expert_result, axis=1) * slot_used
        token_grad = jnp.zeros((seq_len,), jnp.float32).at[slot_index].add(weight_grad)
        grad_probs = token_grad[:, None] * (expert_cols == expert_id).astype(jnp.float32)[None, :]
        grad_e_hidden = contract_cols(grad_result, full_ed[expert_j])
        grad_e_gate, grad_e_up = swiglu_back(grad_e_hidden, expert_gate_act, expert_up_act)
        grad_ed = grad_ed.at[expert_j].add(contract_rows(expert_hidden, grad_result))
        grad_eg = grad_eg.at[expert_j].add(contract_rows(expert_in, grad_e_gate))
        grad_eu = grad_eu.at[expert_j].add(contract_rows(expert_in, grad_e_up))
        grad_in_slots = contract_cols(grad_e_gate, full_eg[expert_j]) + contract_cols(
            grad_e_up, full_eu[expert_j]
        )
        grad_rows_two = grad_rows_two.at[slot_index].add(grad_in_slots)
        grad_two, grad_scale, grad_router_rows = (
            lax.psum_scatter(grad_rows_two, "tensor", scatter_dimension=0, tiled=True),
            lax.psum_scatter(grad_scale_part, "tensor", scatter_dimension=0, tiled=True),
            lax.psum_scatter(grad_probs, "tensor", scatter_dimension=0, tiled=True),
        )
        scale_here = lax.dynamic_slice_in_dim(shared_scale, own_first, local_rows, 0)
        probs_here = lax.dynamic_slice_in_dim(router_probs, own_first, local_rows, 0)
        grad_gate_logit = grad_scale * scale_here * (1.0 - scale_here)
        grad_logits = probs_here * (
            grad_router_rows - jnp.sum(grad_router_rows * probs_here, axis=1, keepdims=True)
        )
        normed_two_wide = normed_two.astype(jnp.float32)
        grad_normed_two = (
            grad_two
            + grad_gate_logit[:, None] * gate_vec.astype(jnp.float32)[None, :]
            + jnp.dot(grad_logits, router_full.astype(jnp.float32).T, precision=HIGHEST)
        )
        grad_gate_vec = grad_gate_vec + jnp.dot(grad_gate_logit, normed_two_wide, precision=HIGHEST)
        grad_router_w = grad_router_w + jnp.dot(normed_two_wide.T, grad_logits, precision=HIGHEST)
        grad_hidden_one, gain_part = norm_back(grad_normed_two, unit_two, inverse_two, gain_two)
        grad_gain_two = grad_gain_two + gain_part
        grad_hidden_one = grad_hidden_one + grad_out
        grad_attn_rows = lax.all_gather(
            grad_hidden_one.astype(jnp.bfloat16), "tensor", axis=0, tiled=True
        )
        grad_wo = contract_rows(mixed_heads, grad_attn_rows)
        grad_mixed = (
            contract_cols(grad_attn_rows, full_wo)
            .astype(jnp.bfloat16)
            .reshape(seq_len, heads_here, HD)
        )
        grad_q_rot, grad_k_rot, grad_v_wide = attend_backward(
            query_rows, key_rows, value_rows, length, grad_mixed, log_totals
        )
        grad_q = (
            rotary(grad_q_rot, positions, -1.0)
            .astype(jnp.bfloat16)
            .reshape(seq_len, heads_here * HD)
        )
        grad_k = (
            rotary(grad_k_rot, positions, -1.0)
            .astype(jnp.bfloat16)
            .reshape(seq_len, heads_here * HD)
        )
        grad_v = grad_v_wide.astype(jnp.bfloat16).reshape(seq_len, heads_here * HD)
        grad_wq = contract_rows(rows_one, grad_q)
        grad_wk = contract_rows(rows_one, grad_k)
        grad_wv = contract_rows(rows_one, grad_v)
        grad_bq = jnp.sum(grad_q.astype(jnp.float32), axis=0).reshape(heads_here, HD)
        grad_bk = jnp.sum(grad_k.astype(jnp.float32), axis=0).reshape(heads_here, HD)
        grad_bv = jnp.sum(grad_v.astype(jnp.float32), axis=0).reshape(heads_here, HD)
        grad_rows_one = (
            contract_cols(grad_q, full_wq)
            + contract_cols(grad_k, full_wk)
            + contract_cols(grad_v, full_wv)
        )
        grad_normed_one = lax.psum_scatter(grad_rows_one, "tensor", scatter_dimension=0, tiled=True)
        grad_inputs, gain_part = norm_back(grad_normed_one, unit_one, inverse_one, gain_one)
        grad_gain_one = grad_gain_one + gain_part
        input_grads.append((grad_inputs + grad_hidden_one).astype(jnp.bfloat16))
        micro_grads = (
            grad_wq,
            grad_wk,
            grad_wv,
            grad_bq,
            grad_bk,
            grad_bv,
            grad_wo,
            grad_sg,
            grad_su,
            grad_sd,
            grad_eg,
            grad_eu,
            grad_ed,
        )
        if micro_id == 0:
            full_totals = micro_grads
        else:
            full_totals = jax.tree.map(jnp.add, full_totals, micro_grads)
    (
        total_wq,
        total_wk,
        total_wv,
        total_bq,
        total_bk,
        total_bv,
        total_wo,
        total_sg,
        total_su,
        total_sd,
        total_eg,
        total_eu,
        total_ed,
    ) = full_totals
    final_grads = (
        lax.psum_scatter(total_wq, "fsdp", scatter_dimension=0, tiled=True),
        lax.psum_scatter(total_wk, "fsdp", scatter_dimension=0, tiled=True),
        lax.psum_scatter(total_wv, "fsdp", scatter_dimension=0, tiled=True),
        lax.psum_scatter(total_bq, "fsdp", scatter_dimension=1, tiled=True),
        lax.psum_scatter(total_bk, "fsdp", scatter_dimension=1, tiled=True),
        lax.psum_scatter(total_bv, "fsdp", scatter_dimension=1, tiled=True),
        lax.psum_scatter(total_wo, "fsdp", scatter_dimension=1, tiled=True),
        lax.psum_scatter(total_sg, "fsdp", scatter_dimension=0, tiled=True),
        lax.psum_scatter(total_su, "fsdp", scatter_dimension=0, tiled=True),
        lax.psum_scatter(total_sd, "fsdp", scatter_dimension=1, tiled=True),
        lax.psum_scatter(total_eg, "fsdp", scatter_dimension=1, tiled=True),
        lax.psum_scatter(total_eu, "fsdp", scatter_dimension=1, tiled=True),
        lax.psum_scatter(total_ed, "fsdp", scatter_dimension=2, tiled=True),
    )
    small_sums = (
        lax.psum_scatter(grad_gain_one, ("fsdp", "tensor"), scatter_dimension=0, tiled=True),
        lax.psum_scatter(grad_gain_two, ("fsdp", "tensor"), scatter_dimension=0, tiled=True),
        lax.psum_scatter(grad_router_w, ("fsdp", "tensor"), scatter_dimension=0, tiled=True),
        lax.psum_scatter(grad_gate_vec, ("fsdp", "tensor"), scatter_dimension=0, tiled=True),
    )
    layer_out = jnp.stack(layer_outs)[:, None]
    grad_tokens = jnp.stack(input_grads)[:, None]
    return (
        layer_out,
        grad_tokens,
        small_sums[0],
        final_grads[0],
        final_grads[1],
        final_grads[2],
        final_grads[3],
        final_grads[4],
        final_grads[5],
        final_grads[6],
        small_sums[1],
        small_sums[2],
        small_sums[3],
        final_grads[7],
        final_grads[8],
        final_grads[9],
        final_grads[10],
        final_grads[11],
        final_grads[12],
    )


def solution(mesh):
    in_specs = (
        P(None, "fsdp", "tensor", None),
        P(None, "fsdp"),
        P(None, "fsdp", None, None),
        P(("fsdp", "tensor")),
        P("fsdp", "tensor"),
        P("fsdp", "tensor"),
        P("fsdp", "tensor"),
        P("tensor", "fsdp"),
        P("tensor", "fsdp"),
        P("tensor", "fsdp"),
        P("tensor", "fsdp"),
        P(("fsdp", "tensor")),
        P(("fsdp", "tensor"), None),
        P(("fsdp", "tensor")),
        P("fsdp", "tensor"),
        P("fsdp", "tensor"),
        P("tensor", "fsdp"),
        P("tensor", "fsdp", None),
        P("tensor", "fsdp", None),
        P("tensor", None, "fsdp"),
        P(None, "fsdp", "tensor", None),
    )
    out_specs = (
        P(None, "fsdp", "tensor", None),
        P(None, "fsdp", "tensor", None),
        P(("fsdp", "tensor")),
        P("fsdp", "tensor"),
        P("fsdp", "tensor"),
        P("fsdp", "tensor"),
        P("tensor", "fsdp"),
        P("tensor", "fsdp"),
        P("tensor", "fsdp"),
        P("tensor", "fsdp"),
        P(("fsdp", "tensor")),
        P(("fsdp", "tensor"), None),
        P(("fsdp", "tensor")),
        P("fsdp", "tensor"),
        P("fsdp", "tensor"),
        P("tensor", "fsdp"),
        P("tensor", "fsdp", None),
        P("tensor", "fsdp", None),
        P("tensor", None, "fsdp"),
    )
    return jax.shard_map(local, mesh=mesh, in_specs=in_specs, out_specs=out_specs, check_vma=False)
```

profile of v0, /device:TPU:0, one launch (start us, length us, event | category | flops | bytes accessed | tf_op | source)
XLA Modules:
  0.0 2578.7 jit_solution(684672944130913339)
XLA Ops:
  10.6 42.2 %all-reduce.10 = (bf16[2048]{0:T(1024)(128)(2,1)S(1)}, bf16[2048]{0:T(1024)(128)(2,1)S(1)}, bf16[2048]{0:T(1024)(128)(2,1)S(1)}) all-reduce(bf16[2048]{0:T(1024)(128)(2,1)S(1)} %dynamic-update-slice.12, bf16[2048]{0:T(1024)(128)(2,1)S(1)} %dynamic-update-slice.13, ...), channel_id=1, replica_groups=mesh['fsdp'=4,'tensor'=8] {'fsdp','tensor'}, use_global_device_ids=true, to_apply=%add | all-reduce | flops 6144 | bytes 24576
  85.6 18.3 all-gather.23.cloned.1.call-done
  107.8 44.2 %all-gather.47.cloned.1.call-done = bf16[1024,2048]{1,0:T(8,128)(2,1)} async-done(((bf16[128,2048]{1,0:T(8,128)(2,1)}), bf16[1024,2048]{1,0:T(8,128)(2,1)}) %all-gather.47.cloned.1.call-update) | async-done | bytes 4194320 | tf_op jit(solution)/shard_map/all_gather | solution.py:273
  155.5 23.6 all-gather.27.cloned.1.call-done
  188.0 19.4 all-gather.29.cloned.1.call-done
  211.8 17.3 while.61
  247.2 17.4 while.60
  272.7 58.7 %reduce-scatter.37.cloned.1.call-done = f32[128,2048]{1,0:T(8,128)} async-done(((f32[1024,2048]{1,0:T(8,128)}), f32[128,2048]{1,0:T(8,128)}) %reduce-scatter.37.cloned.1.call-update) | async-done | bytes 1048592 | tf_op jit(solution)/shard_map/reduce_scatter | solution.py:287
  331.4 90.2 %reduce-scatter.33.cloned.1.call-done = f32[128,2048]{1,0:T(8,128)} async-done(((f32[1024,2048]{1,0:T(8,128)}), f32[128,2048]{1,0:T(8,128)}) %reduce-scatter.33.cloned.1.call-update) | async-done | bytes 1048592 | tf_op jit(solution)/shard_map/reduce_scatter | solution.py:287
  431.9 40.0 %all-gather.3 = bf16[32,64,8]{1,2,0:T(8,128)(2,1)S(1)} all-gather(bf16[1,64,8]{1,2,0:T(8,128)(2,1)S(1)} %bitcast.448), channel_id=1, replica_groups=mesh['fsdp'=4,'tensor'=8] {'fsdp','tensor'}, dimensions={0}, use_global_device_ids=true | all-gather | bytes 33792 | tf_op jit(solution)/shard_map/all_gather | solution.py:224
  489.0 11.0 gather_fusion.4
  500.0 17.9 all-gather.55.cloned.1.call-done
  524.5 11.1 gather_fusion.5
  535.7 29.7 %all-gather.33.cloned.1.call-done = bf16[1024,2048]{1,0:T(8,128)(2,1)} async-done(((bf16[128,2048]{1,0:T(8,128)(2,1)}), bf16[1024,2048]{1,0:T(8,128)(2,1)}) %all-gather.33.cloned.1.call-update) | async-done | bytes 4194320 | tf_op jit(solution)/shard_map/all_gather | solution.py:293
  572.6 40.1 %all-gather.49.cloned.1.call-done = bf16[1024,2048]{1,0:T(8,128)(2,1)} async-done(((bf16[128,2048]{1,0:T(8,128)(2,1)}), bf16[1024,2048]{1,0:T(8,128)(2,1)}) %all-gather.49.cloned.1.call-update) | async-done | bytes 4194320 | tf_op jit(solution)/shard_map/all_gather | solution.py:293
  630.2 49.0 %all-gather.41.cloned.1.call-done = bf16[1,2048,1408]{2,1,0:T(8,128)(2,1)} async-done(((bf16[1,512,1408]{2,1,0:T(8,128)(2,1)}), bf16[1,2048,1408]{2,1,0:T(8,128)(2,1)}) %all-gather.41.cloned.1.call-update) | async-done | bytes 5767184 | tf_op jit(solution)/shard_map/all_gather | solution.py:179
  688.3 58.4 %all-gather.43.cloned.1.call-done = bf16[1,2048,1408]{2,1,0:T(8,128)(2,1)} async-done(((bf16[1,512,1408]{2,1,0:T(8,128)(2,1)}), bf16[1,2048,1408]{2,1,0:T(8,128)(2,1)}) %all-gather.43.cloned.1.call-update) | async-done | bytes 5767184 | tf_op jit(solution)/shard_map/all_gather | solution.py:180
  756.1 58.0 %all-gather.45.cloned.1.call-done = bf16[1,1408,2048]{2,1,0:T(8,128)(2,1)} async-done(((bf16[1,1408,512]{2,1,0:T(8,128)(2,1)}), bf16[1,1408,2048]{2,1,0:T(8,128)(2,1)}) %all-gather.45.cloned.1.call-update) | async-done | bytes 5767184 | tf_op jit(solution)/shard_map/all_gather | solution.py:181
  814.1 13.7 multiply_convert_fusion.8
  844.6 10.4 gather_fusion.3
  874.7 12.5 multiply_convert_fusion.6
  963.0 23.9 scatter_custom_fusion.6
  1028.6 23.8 scatter_custom_fusion.4
  1052.5 10.9 multiply_reduce_fusion.3
  1063.4 22.7 scatter_custom_fusion.1
  1095.0 22.1 scatter_custom_fusion.3
  1119.0 18.0 all-reduce.9
  1140.6 48.4 %reduce-scatter.41.cloned.1.call-done = f32[128,2048]{1,0:T(8,128)} async-done(((f32[1024,2048]{1,0:T(8,128)}), f32[128,2048]{1,0:T(8,128)}) %reduce-scatter.41.cloned.1.call-update) | async-done | bytes 1048592 | tf_op jit(solution)/shard_map/reduce_scatter | solution.py:401
  1192.9 86.3 %reduce-scatter.35.cloned.1.call-done = f32[128,2048]{1,0:T(8,128)} async-done(((f32[1024,2048]{1,0:T(8,128)}), f32[128,2048]{1,0:T(8,128)}) %reduce-scatter.35.cloned.1.call-update) | async-done | bytes 1048592 | tf_op jit(solution)/shard_map/reduce_scatter | solution.py:325
  1279.2 90.1 %reduce-scatter.39.cloned.1.call-done = f32[128,2048]{1,0:T(8,128)} async-done(((f32[1024,2048]{1,0:T(8,128)}), f32[128,2048]{1,0:T(8,128)}) %reduce-scatter.39.cloned.1.call-update) | async-done | bytes 1048592 | tf_op jit(solution)/shard_map/reduce_scatter | solution.py:325
  1379.4 40.8 %all-gather.57.cloned.1.call-done = bf16[1024,2048]{1,0:T(8,128)(2,1)} async-done(((bf16[128,2048]{1,0:T(8,128)(2,1)}), bf16[1024,2048]{1,0:T(8,128)(2,1)}) %all-gather.57.cloned.1.call-update) | async-done | bytes 4194320 | tf_op jit(solution)/shard_map/all_gather | solution.py:422
  1423.7 35.5 %while.63 = (s32[]{:T(128)}, f32[1024,2,128]{0,2,1:T(8,128)}, f32[1024,2,128]{0,2,1:T(8,128)}, f32[2,512,2,128]{3,1,0,2:T(8,128)}, s32[2]{0:T(128)S(1)}, /*index...) while((s32[]{:T(128)}, f32[1024,2,128]{0,2,1:T(8,128)}, ...), condition=%wide.region_57.58_spmd.clone, body=%wide.region_55.57_spmd.clone.sunk | while | flops 1361052160 | bytes 80776056 | solution.py:147
  1471.9 60.2 %while.62 = (s32[]{:T(128)}, f32[1024,2,128]{0,2,1:T(8,128)}, f32[1024,2,128]{0,2,1:T(8,128)}, f32[2,512,2,128]{1,0,3,2:T(2,128)}, s32[2]{0:T(128)S(1)}, /*index...) while((s32[]{:T(128)}, f32[1024,2,128]{0,2,1:T(8,128)}, ...), condition=%wide.region_43.44_spmd.clone, body=%wide.region_41.43_spmd.clone.sunk | while | flops 1361052160 | bytes 82872696 | solution.py:147
  1514.9 10.3 dynamic_update_slice.38
  1609.5 11.0 add_bitcast_fusion
  1688.6 83.1 %reduce-scatter.51.cloned.1.call-done = f32[128,2048]{1,0:T(8,128)} async-done(((f32[1024,2048]{1,0:T(8,128)}), f32[128,2048]{1,0:T(8,128)}) %reduce-scatter.51.cloned.1.call-update) | async-done | bytes 1048592 | tf_op jit(solution)/shard_map/reduce_scatter | solution.py:456
  1771.7 90.3 %reduce-scatter.45.cloned.1.call-done = f32[128,2048]{1,0:T(8,128)} async-done(((f32[1024,2048]{1,0:T(8,128)}), f32[128,2048]{1,0:T(8,128)}) %reduce-scatter.45.cloned.1.call-update) | async-done | bytes 1048592 | tf_op jit(solution)/shard_map/reduce_scatter | solution.py:456
  1864.2 38.5 %all-reduce.8 = (f32[2048]{0:T(1024)S(1)}, f32[2048]{0:T(1024)S(1)}, f32[2048]{0:T(1024)S(1)}) all-reduce(f32[2048]{0:T(1024)S(1)} %add.598, f32[2048]{0:T(1024)S(1)} %add.606, f32[2048]{0:T(1024)S(1)} %add.608), channel_id=14, replica_groups=mesh['fsdp'=4,'tensor'=8] {'fsdp','tensor'}, use_global_device_ids=true, to_apply=%region_62.63.clone | all-reduce | flops 6144 | bytes 49152
  1907.7 22.8 reduce-scatter.65.cloned.1.call-done
  1930.5 69.4 %reduce-scatter.61.cloned.1.call-done = f32[512,704]{0,1:T(8,128)} async-done(((f32[2048,704]{0,1:T(8,128)}), f32[512,704]{0,1:T(8,128)}) %reduce-scatter.61.cloned.1.call-update) | async-done | bytes 1441808 | tf_op jit(solution)/shard_map/reduce_scatter | solution.py:502
  1999.9 69.4 %reduce-scatter.63.cloned.1.call-done = f32[512,704]{0,1:T(8,128)} async-done(((f32[2048,704]{0,1:T(8,128)}), f32[512,704]{0,1:T(8,128)}) %reduce-scatter.63.cloned.1.call-update) | async-done | bytes 1441808 | tf_op jit(solution)/shard_map/reduce_scatter | solution.py:503
  2069.3 115.7 %reduce-scatter.71.cloned.1.call-done = f32[1,1408,512]{2,1,0:T(8,128)} async-done(((f32[1,1408,2048]{2,1,0:T(8,128)}), f32[1,1408,512]{2,1,0:T(8,128)}) %reduce-scatter.71.cloned.1.call-update) | async-done | bytes 2883600 | tf_op jit(solution)/shard_map/reduce_scatter | solution.py:507
  2184.9 115.7 %reduce-scatter.67.cloned.1.call-done = f32[1,512,1408]{2,1,0:T(8,128)} async-done(((f32[1,2048,1408]{2,1,0:T(8,128)}), f32[1,512,1408]{2,1,0:T(8,128)}) %reduce-scatter.67.cloned.1.call-update) | async-done | bytes 2883600 | tf_op jit(solution)/shard_map/reduce_scatter | solution.py:505
  2300.6 115.8 %reduce-scatter.69.cloned.1.call-done = f32[1,512,1408]{2,1,0:T(8,128)} async-done(((f32[1,2048,1408]{2,1,0:T(8,128)}), f32[1,512,1408]{2,1,0:T(8,128)}) %reduce-scatter.69.cloned.1.call-update) | async-done | bytes 2883600 | tf_op jit(solution)/shard_map/reduce_scatter | solution.py:506
  2416.4 38.6 %reduce-scatter.59.cloned.1.call-done = f32[256,512]{1,0:T(8,128)} async-done(((f32[256,2048]{1,0:T(8,128)}), f32[256,512]{1,0:T(8,128)}) %reduce-scatter.59.cloned.1.call-update) | async-done | bytes 524304 | tf_op jit(solution)/shard_map/reduce_scatter | solution.py:501
  2455.0 39.0 %reduce-scatter.57.cloned.1.call-done = f32[512,256]{1,0:T(8,128)} async-done(((f32[2048,256]{1,0:T(8,128)}), f32[512,256]{1,0:T(8,128)}) %reduce-scatter.57.cloned.1.call-update) | async-done | bytes 524304 | tf_op jit(solution)/shard_map/reduce_scatter | solution.py:497
  2494.1 38.7 %reduce-scatter.55.cloned.1.call-done = f32[512,256]{1,0:T(8,128)} async-done(((f32[2048,256]{1,0:T(8,128)}), f32[512,256]{1,0:T(8,128)}) %reduce-scatter.55.cloned.1.call-update) | async-done | bytes 524304 | tf_op jit(solution)/shard_map/reduce_scatter | solution.py:496
  2532.8 39.1 %reduce-scatter.53.cloned.1.call-done = f32[512,256]{1,0:T(8,128)} async-done(((f32[2048,256]{1,0:T(8,128)}), f32[512,256]{1,0:T(8,128)}) %reduce-scatter.53.cloned.1.call-update) | async-done | bytes 524304 | tf_op jit(solution)/shard_map/reduce_scatter | solution.py:495
  (747 shorter events, 611.3 us)
Async XLA Ops:
  7.2 78.3 %all-gather.25.cloned.1.call-start = ((), (), s32[]{:S(2)}) async-start(), calls=%async_computation.25 | async-start | bytes 1310720 | tf_op jit(solution)/shard_map/all_gather | solution.py:169
  8.0 96.0 %all-gather.23.cloned.1.call-start = ((), (), s32[]{:S(2)}) async-start(), calls=%async_computation.24 | async-start | bytes 4718592 | tf_op jit(solution)/shard_map/all_gather | solution.py:273
  52.8 429.1 %copy-start.95 = (bf16[2048]{0:T(1024)(128)(2,1)}, bf16[2048]{0:T(1024)(128)(2,1)S(1)}, u32[]{:S(2)}) copy-start(bf16[2048]{0:T(1024)(128)(2,1)S(1)} %get-tuple-element.759) | copy-start | bytes 12292
  56.8 95.2 %all-gather.47.cloned.1.call-start = ((), (), s32[]{:S(2)}) async-start(), calls=%async_computation.38 | async-start | bytes 4718592 | tf_op jit(solution)/shard_map/all_gather | solution.py:273
  57.5 121.6 %all-gather.27.cloned.1.call-start = ((), (), s32[]{:S(2)}) async-start(), calls=%async_computation.26 | async-start | bytes 1310720 | tf_op jit(solution)/shard_map/all_gather | solution.py:170
  58.1 149.3 %all-gather.29.cloned.1.call-start = ((), (), s32[]{:S(2)}) async-start(), calls=%async_computation.27 | async-start | bytes 1310720 | tf_op jit(solution)/shard_map/all_gather | solution.py:171
  58.7 176.9 %all-gather.31.cloned.1.call-start = ((), (), s32[]{:S(2)}) async-start(), calls=%async_computation.28 | async-start | bytes 1310720 | tf_op jit(solution)/shard_map/all_gather | solution.py:175
  59.3 272.1 %reduce-scatter.37.cloned.1.call-start = ((), (), s32[]{:S(2)}) async-start(), calls=%async_computation.39 | async-start | bytes 9437184 | tf_op jit(solution)/shard_map/reduce_scatter | solution.py:287
  241.6 180.0 %reduce-scatter.33.cloned.1.call-start = ((), (), s32[]{:S(2)}) async-start(), calls=%async_computation.29 | async-start | bytes 9437184 | tf_op jit(solution)/shard_map/reduce_scatter | solution.py:287
  269.2 213.3 %all-gather.51.cloned.1.call-start = ((), (), s32[]{:S(2)}) async-start(), calls=%async_computation.42 | async-start | bytes 4718592 | tf_op jit(solution)/shard_map/all_gather | solution.py:359
  272.0 245.9 %all-gather.55.cloned.1.call-start = ((), (), s32[]{:S(2)}) async-start(), calls=%async_computation.47 | async-start | bytes 4718592 | tf_op jit(solution)/shard_map/all_gather | solution.py:359
  272.6 292.8 %all-gather.33.cloned.1.call-start = ((), (), s32[]{:S(2)}) async-start(), calls=%async_computation.30 | async-start | bytes 4718592 | tf_op jit(solution)/shard_map/all_gather | solution.py:293
  425.7 187.0 %all-gather.49.cloned.1.call-start = ((), (), s32[]{:S(2)}) async-start(), calls=%async_computation.40 | async-start | bytes 4718592 | tf_op jit(solution)/shard_map/all_gather | solution.py:293
  426.3 252.9 %all-gather.41.cloned.1.call-start = ((), (), s32[]{:S(2)}) async-start(), calls=%async_computation.34 | async-start | bytes 7208960 | tf_op jit(solution)/shard_map/all_gather | solution.py:179
  427.1 319.6 %all-gather.43.cloned.1.call-start = ((), (), s32[]{:S(2)}) async-start(), calls=%async_computation.35 | async-start | bytes 7208960 | tf_op jit(solution)/shard_map/all_gather | solution.py:180
  427.6 386.4 %all-gather.45.cloned.1.call-start = ((), (), s32[]{:S(2)}) async-start(), calls=%async_computation.36 | async-start | bytes 7208960 | tf_op jit(solution)/shard_map/all_gather | solution.py:181
  428.2 478.8 %all-gather.35.cloned.1.call-start = ((), (), s32[]{:S(2)}) async-start(), calls=%async_computation.31 | async-start | bytes 3604480 | tf_op jit(solution)/shard_map/all_gather | solution.py:176
  428.8 486.5 %all-gather.37.cloned.1.call-start = ((), (), s32[]{:S(2)}) async-start(), calls=%async_computation.32 | async-start | bytes 3604480 | tf_op jit(solution)/shard_map/all_gather | solution.py:177
  429.4 514.8 %all-gather.39.cloned.1.call-start = ((), (), s32[]{:S(2)}) async-start(), calls=%async_computation.33 | async-start | bytes 3604480 | tf_op jit(solution)/shard_map/all_gather | solution.py:178
  430.0 707.2 %reduce-scatter.43.cloned.1.call-start = ((), (), s32[]{:S(2)}) async-start(), calls=%async_computation.44 | async-start | bytes 36864 | tf_op jit(solution)/shard_map/reduce_scatter | solution.py:403
  477.5 361.2 %copy-start.98 = (s32[768]{0:T(1024)}, s32[768]{0:T(1024)S(1)}, u32[]{:S(2)}) copy-start(s32[768]{0:T(1024)S(1)} %compare_select_fusion.3) | copy-start | bytes 9220
  903.3 234.6 %reduce-scatter.49.cloned.1.call-start = ((), (), s32[]{:S(2)}) async-start(), calls=%async_computation.49 | async-start | bytes 36864 | tf_op jit(solution)/shard_map/reduce_scatter | solution.py:403
  906.8 231.8 %reduce-scatter.47.cloned.1.call-start = ((), (), s32[]{:S(2)}) async-start(), calls=%async_computation.48 | async-start | bytes 9437184 | tf_op jit(solution)/shard_map/reduce_scatter | solution.py:401
  986.9 202.0 %reduce-scatter.41.cloned.1.call-start = ((), (), s32[]{:S(2)}) async-start(), calls=%async_computation.43 | async-start | bytes 9437184 | tf_op jit(solution)/shard_map/reduce_scatter | solution.py:401
  1052.5 226.8 %reduce-scatter.35.cloned.1.call-start = ((), (), s32[]{:S(2)}) async-start(), calls=%async_computation.37 | async-start | bytes 9437184 | tf_op jit(solution)/shard_map/reduce_scatter | solution.py:325
  1086.1 283.3 %reduce-scatter.39.cloned.1.call-start = ((), (), s32[]{:S(2)}) async-start(), calls=%async_computation.41 | async-start | bytes 9437184 | tf_op jit(solution)/shard_map/reduce_scatter | solution.py:325
  1117.2 252.2 %copy-start.122 = (f32[128]{0:T(128)S(1)}, f32[128]{0:T(128)}, u32[]{:S(2)}) copy-start(f32[128]{0:T(128)} %copy-done.121) | copy-start | bytes 1540
  1117.2 252.2 %copy-start.124 = (f32[128]{0:T(128)S(1)}, f32[128]{0:T(128)}, u32[]{:S(2)}) copy-start(f32[128]{0:T(128)} %copy-done.123) | copy-start | bytes 1540
  1117.2 302.9 %all-gather.57.cloned.1.call-start = ((), (), s32[]{:S(2)}) async-start(), calls=%async_computation.50 | async-start | bytes 4718592 | tf_op jit(solution)/shard_map/all_gather | solution.py:422
  1137.1 237.3 %copy-start.117 = (f32[128]{0:T(128)}, f32[128]{0:T(128)S(1)}, u32[]{:S(2)}) copy-start(f32[128]{0:T(128)S(1)} %fusion.178) | copy-start | bytes 1540
  1137.2 237.3 %copy-start.119 = (f32[128]{0:T(128)}, f32[128]{0:T(128)S(1)}, u32[]{:S(2)}) copy-start(f32[128]{0:T(128)S(1)} %fusion.179) | copy-start | bytes 1540
  1374.5 93.6 %all-gather.53.cloned.1.call-start = ((), (), s32[]{:S(2)}) async-start(), calls=%async_computation.45 | async-start | bytes 4718592 | tf_op jit(solution)/shard_map/all_gather | solution.py:422
  1375.1 305.6 %reduce-scatter.79.cloned.1.call-start = ((), (), s32[]{:S(2)}) async-start(), calls=%async_computation.65 | async-start | bytes 1081344
  1379.3 305.2 %reduce-scatter.77.cloned.1.call-start = ((), (), s32[]{:S(2)}) async-start(), calls=%async_computation.64 | async-start | bytes 81920
  1542.2 143.6 %reduce-scatter.75.cloned.1.call-start = ((), (), s32[]{:S(2)}) async-start(), calls=%async_computation.63 | async-start | bytes 81920
  1546.4 140.8 %reduce-scatter.73.cloned.1.call-start = ((), (), s32[]{:S(2)}) async-start(), calls=%async_computation.62 | async-start | bytes 81920
  1550.5 221.2 %reduce-scatter.51.cloned.1.call-start = ((), (), s32[]{:S(2)}) async-start(), calls=%async_computation.51 | async-start | bytes 9437184 | tf_op jit(solution)/shard_map/reduce_scatter | solution.py:456
  1559.4 302.5 %reduce-scatter.45.cloned.1.call-start = ((), (), s32[]{:S(2)}) async-start(), calls=%async_computation.46 | async-start | bytes 9437184 | tf_op jit(solution)/shard_map/reduce_scatter | solution.py:456
  1567.9 362.5 %reduce-scatter.65.cloned.1.call-start = ((), (), s32[]{:S(2)}) async-start(), calls=%async_computation.58 | async-start | bytes 7208960 | tf_op jit(solution)/shard_map/reduce_scatter | solution.py:504
  1579.6 420.3 %reduce-scatter.61.cloned.1.call-start = ((), (), s32[]{:S(2)}) async-start(), calls=%async_computation.56 | async-start | bytes 7208960 | tf_op jit(solution)/shard_map/reduce_scatter | solution.py:502
  1590.4 478.9 %reduce-scatter.63.cloned.1.call-start = ((), (), s32[]{:S(2)}) async-start(), calls=%async_computation.57 | async-start | bytes 7208960 | tf_op jit(solution)/shard_map/reduce_scatter | solution.py:503
  1601.0 584.0 %reduce-scatter.71.cloned.1.call-start = ((), (), s32[]{:S(2)}) async-start(), calls=%async_computation.61 | async-start | bytes 14417920 | tf_op jit(solution)/shard_map/reduce_scatter | solution.py:507
  1620.4 680.2 %reduce-scatter.67.cloned.1.call-start = ((), (), s32[]{:S(2)}) async-start(), calls=%async_computation.59 | async-start | bytes 14417920 | tf_op jit(solution)/shard_map/reduce_scatter | solution.py:505
  1636.6 779.9 %reduce-scatter.69.cloned.1.call-start = ((), (), s32[]{:S(2)}) async-start(), calls=%async_computation.60 | async-start | bytes 14417920 | tf_op jit(solution)/shard_map/reduce_scatter | solution.py:506
  1652.5 802.6 %reduce-scatter.59.cloned.1.call-start = ((), (), s32[]{:S(2)}) async-start(), calls=%async_computation.55 | async-start | bytes 2621440 | tf_op jit(solution)/shard_map/reduce_scatter | solution.py:501
  1659.8 834.3 %reduce-scatter.57.cloned.1.call-start = ((), (), s32[]{:S(2)}) async-start(), calls=%async_computation.54 | async-start | bytes 2621440 | tf_op jit(solution)/shard_map/reduce_scatter | solution.py:497
  1666.6 866.2 %reduce-scatter.55.cloned.1.call-start = ((), (), s32[]{:S(2)}) async-start(), calls=%async_computation.53 | async-start | bytes 2621440 | tf_op jit(solution)/shard_map/reduce_scatter | solution.py:496
  1673.2 898.7 %reduce-scatter.53.cloned.1.call-start = ((), (), s32[]{:S(2)}) async-start(), calls=%async_computation.52 | async-start | bytes 2621440 | tf_op jit(solution)/shard_map/reduce_scatter | solution.py:495
  (170 other events, 4602.2 us)
Sparse Core Ops, SparseCore 0:
  9.9 29.4 all-gather.24
  56.9 46.9 all-gather.22
  106.1 45.8 all-gather.46
  153.7 25.3 all-gather.26
  180.8 26.6 all-gather.28
  209.1 26.4 all-gather.30
  241.7 89.6 reduce-scatter.36
  333.7 87.8 reduce-scatter.32
  423.8 46.0 all-gather.50
  471.9 45.9 all-gather.54
  519.5 45.8 all-gather.32
  566.9 45.8 all-gather.48
  614.6 64.5 all-gather.40
  680.9 65.7 all-gather.42
  748.4 65.6 all-gather.44
  815.7 41.6 all-gather.34
  859.1 41.6 all-gather.36
  902.5 41.6 all-gather.38
  947.0 29.9 reduce-scatter.42
  979.8 28.1 reduce-scatter.48
  1010.3 87.6 reduce-scatter.46
  1100.3 88.5 reduce-scatter.40
  1191.3 87.9 reduce-scatter.34
  1281.4 87.9 reduce-scatter.38
  1374.6 45.4 all-gather.56
  1422.2 45.8 all-gather.52
  1470.2 133.5 reduce-scatter.78
  1606.7 20.0 reduce-scatter.76
  1629.5 23.6 reduce-scatter.74
  1656.0 23.6 reduce-scatter.72
  1682.0 89.5 reduce-scatter.50
  1774.0 87.9 reduce-scatter.44
  1865.4 65.0 reduce-scatter.64
  1934.0 65.8 reduce-scatter.60
  2003.4 65.8 reduce-scatter.62
  2072.8 112.0 reduce-scatter.70
  2188.5 112.0 reduce-scatter.66
  2304.3 112.0 reduce-scatter.68
  2419.8 35.1 reduce-scatter.58
  2458.9 35.1 reduce-scatter.56
  2497.6 35.1 reduce-scatter.54
  2536.6 35.2 reduce-scatter.52
where the time goes:
time: 2590 us; the launch traced here: 2580 us
  waiting for transfers between devices  1640 us (63%)
  matrix products  433 us (17%)
  other arithmetic  187 us (7%)
  blocking collectives  162 us (6%)
  local copies, waits for them, and re-layouts  122 us (5%)
    reduce_scatter x2, waiting for transfers between devices, local(): lax.psum_scatter(combined, 'tensor', scatter_dimension=0, tiled=True)  176 us
    reduce_scatter x2, waiting for transfers between devices, local(): lax.psum_scatter(grad_rows_one, 'tensor', scatter_dimension=0, tiled=True)  173 us
    reduce_scatter x2, waiting for transfers between devices, local(): lax.psum_scatter(matmul(mixed_heads, full_wo), 'tensor', scatter_dimensio...  149 us
    dot_general x24, matrix products, matmul(): return jnp.dot(left, right, preferred_element_type=jnp.float32)  144 us
    reduce_scatter x1, waiting for transfers between devices, local(): lax.psum_scatter(total_eu, 'fsdp', scatter_dimension=1, tiled=True)  116 us
    reduce_scatter x1, waiting for transfers between devices, local(): lax.psum_scatter(total_eg, 'fsdp', scatter_dimension=1, tiled=True)  116 us
    reduce_scatter x1, waiting for transfers between devices, local(): lax.psum_scatter(total_ed, 'fsdp', scatter_dimension=2, tiled=True)  116 us
    dot_general x20, matrix products, contract_cols(): lax.dot_general(left, right, (((1,), (1,)), ((), ())), preferred_element_...  114 us
  transfers between devices with their start and end apart: 42, of which 31 were waited for; matrix products, arithmetic and copies ran while one was open for 28% of the time, Pallas kernels for 0%

commit v1 on v0

v1 whole, which is shorter than its diff:
```python
import functools

import jax
import jax.numpy as jnp
from jax import lax
from jax.experimental import pallas as pl
from jax.experimental.pallas import tpu as pltpu
from jax.sharding import PartitionSpec as P

HD = 128
EPSILON = 1e-06
ROPE_BASE = 1000000.0
BF = jnp.bfloat16
F32 = jnp.float32
QB = 256


def dot(left, right, left_dims, right_dims):
    return lax.dot_general(
        left, right, ((left_dims, right_dims), ((), ())), preferred_element_type=F32
    )


def normalize(values):
    inverse = lax.rsqrt(jnp.mean(values * values, axis=-1, keepdims=True) + EPSILON)
    return (values * inverse, inverse)


def norm_back(grad_normed, unit, inverse, gain):
    grad_unit = grad_normed * gain
    grad_values = inverse * (grad_unit - unit * jnp.mean(grad_unit * unit, axis=-1, keepdims=True))
    return (grad_values, jnp.sum(grad_normed * unit, axis=0))


def line_pairs(size, chips):
    return [(2 * z + c, 2 * (z + size) + c) for z in chips for c in range(2)]


def swap_cores(values, ranks):
    return lax.ppermute(values, "tensor", [(t, t ^ 1) for t in range(ranks)])


def gather_rows(block, ranks):
    chips = ranks // 2
    rank = lax.axis_index("tensor")
    chip, core = rank // 2, rank % 2
    pieces = []
    upward = downward = block
    for step in range(1, chips):
        upward = lax.ppermute(upward, "tensor", line_pairs(1, range(step - 1, chips - 1)))
        downward = lax.ppermute(downward, "tensor", line_pairs(-1, range(1, chips - step + 1)))
        from_below, from_above = chip >= step, chip < chips - step
        if 2 * step > chips - 1:
            place = jnp.where(from_below, chip - step, jnp.where(from_above, chip + step, chip))
            pieces.append((jnp.where(from_below, upward, downward), place))
        else:
            pieces.append((upward, jnp.where(from_below, chip - step, chip)))
            pieces.append((downward, jnp.where(from_above, chip + step, chip)))
    pieces.append((block, chip))
    whole = jnp.zeros((chips, 2) + block.shape, block.dtype)
    rest = (0,) * block.ndim
    for piece, place in pieces:
        whole = lax.dynamic_update_slice(whole, piece[None, None], (place, core) + rest)
        other = swap_cores(piece, ranks)
        whole = lax.dynamic_update_slice(whole, other[None, None], (place, 1 - core) + rest)
    return whole.reshape((ranks * block.shape[0],) + block.shape[1:])


def scatter_rows(partial, ranks):
    chips = ranks // 2
    rank = lax.axis_index("tensor")
    chip, core = rank // 2, rank % 2
    rows = partial.shape[0] // ranks
    halves = partial.reshape(chips, 2, rows, -1)
    kept = lax.dynamic_index_in_dim(halves, core, 1, False)
    given = lax.dynamic_index_in_dim(halves, 1 - core, 1, False)
    both = kept.astype(F32) + swap_cores(given, ranks).astype(F32)
    narrow = both.astype(BF)

    def pick(index):
        return lax.dynamic_index_in_dim(narrow, jnp.clip(index, 0, chips - 1), 0, False)

    upward = pick(chip + chips - 1)
    downward = pick(chip - chips + 1)
    for step in range(1, chips):
        upward = lax.ppermute(upward, "tensor", line_pairs(1, range(0, step)))
        downward = lax.ppermute(downward, "tensor", line_pairs(-1, range(chips - step, chips)))
        if step < chips - 1:
            following = chips - step - 1
            upward = (upward.astype(F32) + pick(chip + following).astype(F32)).astype(BF)
            downward = (downward.astype(F32) + pick(chip - following).astype(F32)).astype(BF)
    own = lax.dynamic_index_in_dim(both, chip, 0, False)
    return own + upward.astype(F32) + downward.astype(F32)


def rope_tables(seq_len):
    half = HD // 2
    frequency = ROPE_BASE ** (-(2.0 * jnp.arange(half, dtype=F32)) / HD)
    angles = jnp.arange(seq_len, dtype=F32)[:, None] * frequency[None, :]
    cosine, sine = jnp.cos(angles), jnp.sin(angles)
    return (
        jnp.concatenate([cosine, cosine], axis=1),
        jnp.concatenate([-sine, sine], axis=1),
    )


def swap_halves(values):
    half = HD // 2
    return jnp.concatenate([values[:, half:], values[:, :half]], axis=1)


def block_weights(query, keys, first_row, length):
    scores = dot(query, keys, (1,), (1,)) * (HD ** (-0.5))
    rows = first_row + lax.broadcasted_iota(jnp.int32, scores.shape, 0)
    cols = lax.broadcasted_iota(jnp.int32, scores.shape, 1)
    scores = jnp.where((cols <= rows) & (cols < length), scores, -1e30)
    exps = jnp.exp(scores - jnp.max(scores, axis=1, keepdims=True))
    return exps / jnp.sum(exps, axis=1, keepdims=True)


def attend_kernel(heads, length_ref, pre_ref, bias_ref, cos_ref, sin_ref, qkv_ref, out_ref):
    seq_len = pre_ref.shape[0]
    length = length_ref[0]
    for head in range(heads):
        for which in range(3):
            at = (which * heads + head) * HD
            for row in range(0, seq_len, QB):
                part = pre_ref[row : row + QB, at : at + HD] + bias_ref[:, at : at + HD]
                if which < 2:
                    part = (
                        part * cos_ref[row : row + QB, :]
                        + swap_halves(part) * sin_ref[row : row + QB, :]
                    )
                qkv_ref[row : row + QB, at : at + HD] = part.astype(BF)
        q_at, k_at, v_at = (head * HD, (heads + head) * HD, (2 * heads + head) * HD)
        for row in range(0, seq_len, QB):
            end = row + QB
            weights = block_weights(
                qkv_ref[row:end, q_at : q_at + HD], qkv_ref[:end, k_at : k_at + HD], row, length
            )
            mixed = dot(weights.astype(BF), qkv_ref[:end, v_at : v_at + HD], (1,), (0,))
            out_ref[row:end, q_at : q_at + HD] = mixed.astype(BF)


def attend_back_kernel(
    heads, length_ref, qkv_ref, grad_ref, cos_ref, sin_ref, out_ref, sums_ref, key_acc, value_acc
):
    seq_len = qkv_ref.shape[0]
    length = length_ref[0]
    scale = HD ** (-0.5)
    for head in range(heads):
        q_at, k_at, v_at = (head * HD, (heads + head) * HD, (2 * heads + head) * HD)
        key_acc[...] = jnp.zeros_like(key_acc)
        value_acc[...] = jnp.zeros_like(value_acc)
        q_sum = jnp.zeros((1, HD), F32)
        for row in range(0, seq_len, QB):
            end = row + QB
            query = qkv_ref[row:end, q_at : q_at + HD]
            keys = qkv_ref[:end, k_at : k_at + HD]
            grad = grad_ref[row:end, q_at : q_at + HD]
            weights = block_weights(query, keys, row, length)
            grad_weights = dot(grad, qkv_ref[:end, v_at : v_at + HD], (1,), (1,))
            inner = jnp.sum(weights * grad_weights, axis=1, keepdims=True)
            grad_scores = (scale * weights * (grad_weights - inner)).astype(BF)
            turned = dot(grad_scores, keys, (1,), (0,))
            grad_query = (
                turned * cos_ref[row:end, :] - swap_halves(turned) * sin_ref[row:end, :]
            ).astype(BF)
            out_ref[row:end, q_at : q_at + HD] = grad_query
            q_sum = q_sum + jnp.sum(grad_query.astype(F32), axis=0, keepdims=True)
            key_acc[:end, :] += dot(grad_scores, query, (0,), (0,))
            value_acc[:end, :] += dot(weights.astype(BF), grad, (0,), (0,))
        k_sum = jnp.zeros((1, HD), F32)
        v_sum = jnp.zeros((1, HD), F32)
        for row in range(0, seq_len, QB):
            end = row + QB
            turned = key_acc[row:end, :]
            grad_key = (
                turned * cos_ref[row:end, :] - swap_halves(turned) * sin_ref[row:end, :]
            ).astype(BF)
            grad_value = value_acc[row:end, :].astype(BF)
            out_ref[row:end, k_at : k_at + HD] = grad_key
            out_ref[row:end, v_at : v_at + HD] = grad_value
            k_sum = k_sum + jnp.sum(grad_key.astype(F32), axis=0, keepdims=True)
            v_sum = v_sum + jnp.sum(grad_value.astype(F32), axis=0, keepdims=True)
        sums_ref[:, q_at : q_at + HD] = q_sum
        sums_ref[:, k_at : k_at + HD] = k_sum
        sums_ref[:, v_at : v_at + HD] = v_sum


def in_vmem(count):
    return [pl.BlockSpec(memory_space=pltpu.VMEM)] * count


def attend(length, pre, bias, cosine, sine):
    seq_len, width = pre.shape
    heads = width // (3 * HD)
    return pl.pallas_call(
        functools.partial(attend_kernel, heads),
        out_shape=(
            jax.ShapeDtypeStruct((seq_len, width), BF),
            jax.ShapeDtypeStruct((seq_len, heads * HD), BF),
        ),
        in_specs=[pl.BlockSpec(memory_space=pltpu.SMEM)] + in_vmem(4),
        out_specs=tuple(in_vmem(2)),
        compiler_params=pltpu.CompilerParams(vmem_limit_bytes=32 << 20),
        cost_estimate=pl.CostEstimate(
            flops=3 * heads * HD * seq_len * seq_len,
            bytes_accessed=10 * seq_len * width,
            transcendentals=heads * seq_len * seq_len,
        ),
    )(length, pre, bias, cosine, sine)


def attend_back(length, qkv, grad, cosine, sine):
    seq_len, width = qkv.shape
    heads = width // (3 * HD)
    return pl.pallas_call(
        functools.partial(attend_back_kernel, heads),
        out_shape=(
            jax.ShapeDtypeStruct((seq_len, width), BF),
            jax.ShapeDtypeStruct((1, width), F32),
        ),
        in_specs=[pl.BlockSpec(memory_space=pltpu.SMEM)] + in_vmem(4),
        out_specs=tuple(in_vmem(2)),
        scratch_shapes=[pltpu.VMEM((seq_len, HD), F32), pltpu.VMEM((seq_len, HD), F32)],
        compiler_params=pltpu.CompilerParams(vmem_limit_bytes=32 << 20),
        cost_estimate=pl.CostEstimate(
            flops=8 * heads * HD * seq_len * seq_len,
            bytes_accessed=8 * seq_len * width,
            transcendentals=heads * seq_len * seq_len,
        ),
    )(length, qkv, grad, cosine, sine)


def local(
    tokens,
    lengths,
    routes,
    norm1_gain,
    w_query,
    w_key,
    w_value,
    b_query,
    b_key,
    b_value,
    w_out,
    norm2_gain,
    router,
    shared_gate_vec,
    shared_gate,
    shared_up,
    shared_down,
    expert_gate,
    expert_up,
    expert_down,
    cotangent,
):
    ranks = lax.axis_size("tensor")
    groups = lax.axis_size("fsdp")
    rank = lax.axis_index("tensor")
    micros, _, rows, width = tokens.shape
    seq_len = rows * ranks
    heads = w_query.shape[1] // HD
    span = heads * HD
    experts = ranks * expert_gate.shape[0]
    shared_units = shared_gate.shape[1]
    own_first = rank * rows
    positions = jnp.arange(seq_len, dtype=jnp.int32)
    local_pos = own_first + jnp.arange(rows, dtype=jnp.int32)

    per_device = norm1_gain.shape[0]
    small = jnp.concatenate(
        [
            norm1_gain,
            norm2_gain,
            shared_gate_vec,
            router.reshape(-1),
            b_query.reshape(-1),
            b_key.reshape(-1),
            b_value.reshape(-1),
        ]
    )
    small_all = lax.all_gather(small, ("fsdp", "tensor"), axis=0, tiled=False)
    gain_one = small_all[:, :per_device].reshape(-1).astype(F32)
    gain_two = small_all[:, per_device : 2 * per_device].reshape(-1).astype(F32)
    gate_vec = small_all[:, 2 * per_device : 3 * per_device].reshape(-1)
    bias_at = per_device * (3 + experts)
    router_full = small_all[:, 3 * per_device : bias_at].reshape(width, experts)
    router_wide = jnp.concatenate([router_full, gate_vec[:, None]], axis=1)
    own_bias = lax.dynamic_index_in_dim(
        small_all.reshape(groups, ranks, -1), rank, 1, False
    )[:, bias_at:].reshape(groups, 3, heads, HD // groups)
    bias = own_bias.transpose(1, 2, 0, 3).reshape(1, 3 * span).astype(F32)

    qkv_w = lax.all_gather(
        jnp.concatenate([w_query, w_key, w_value], axis=1), "fsdp", axis=0, tiled=True
    )
    out_w = lax.all_gather(w_out, "fsdp", axis=1, tiled=True)
    gate_w = lax.all_gather(
        jnp.concatenate([shared_gate, expert_gate[0]], axis=1), "fsdp", axis=0, tiled=True
    )
    up_w = lax.all_gather(
        jnp.concatenate([shared_up, expert_up[0]], axis=1), "fsdp", axis=0, tiled=True
    )
    down_w = lax.all_gather(
        jnp.concatenate([shared_down, expert_down[0]], axis=0), "fsdp", axis=1, tiled=True
    )

    cosine, sine = rope_tables(seq_len)
    token_rows = [gather_rows(tokens[m, 0], ranks) for m in range(micros)]
    grads_own = []
    for m in range(micros):
        inside = (local_pos < lengths[m, 0])[:, None]
        grads_own.append(jnp.where(inside, cotangent[m, 0], jnp.zeros((), BF)))
    grad_rows = [gather_rows(grads_own[m], ranks) for m in range(micros)]

    saved = []
    layer_outs = []
    for m in range(micros):
        length = lengths[m]
        normed_one = (normalize(token_rows[m].astype(F32))[0] * gain_one).astype(BF)
        pre = dot(normed_one, qkv_w, (1,), (0,))
        qkv, mixed = attend(length, pre, bias, cosine, sine)
        attended = scatter_rows(dot(mixed, out_w, (1,), (0,)).astype(BF), ranks)
        hidden = tokens[m, 0].astype(F32) + attended
        unit_two, inverse_two = normalize(hidden)
        rows_two = gather_rows((unit_two * gain_two).astype(BF), ranks)
        saved.append((normed_one, qkv, mixed, hidden, rows_two))

    ffn = []
    for m in range(micros):
        normed_one, qkv, mixed, hidden, rows_two = saved[m]
        logits = dot(rows_two, router_wide, (1,), (0,))
        probs = jax.nn.softmax(logits[:, :experts], axis=-1)
        shared_scale = jax.nn.sigmoid(logits[:, experts:])
        chosen = jnp.any(routes[m, 0] == rank, axis=1, keepdims=True)
        own_expert = (jnp.arange(experts, dtype=jnp.int32) == rank)[None, :]
        prob = jnp.sum(jnp.where(own_expert, probs, 0.0), axis=1, keepdims=True)
        expert_scale = jnp.where(chosen, prob, 0.0)
        is_shared = (jnp.arange(gate_w.shape[1]) < shared_units)[None, :]
        scale = jnp.where(is_shared, shared_scale, expert_scale)
        gate_act = dot(rows_two, gate_w, (1,), (0,))
        up_act = dot(rows_two, up_w, (1,), (0,))
        sigmoid = jax.nn.sigmoid(gate_act)
        unit_hidden = (gate_act * sigmoid * up_act).astype(BF)
        scaled = (scale * unit_hidden.astype(F32)).astype(BF)
        moved = scatter_rows(dot(scaled, down_w, (1,), (0,)).astype(BF), ranks)
        inside = (local_pos < lengths[m, 0]).astype(F32)[:, None]
        layer_outs.append((inside * (hidden + moved)).astype(BF))
        back = dot(grad_rows[m], down_w, (1,), (1,))
        product = unit_hidden.astype(F32) * back
        shared_grad = jnp.sum(jnp.where(is_shared, product, 0.0), axis=1, keepdims=True)
        expert_grad = jnp.sum(jnp.where(is_shared, 0.0, product), axis=1, keepdims=True)
        grad_hidden = scale * back
        grad_gate = (grad_hidden * up_act * sigmoid * (1.0 + gate_act * (1.0 - sigmoid))).astype(BF)
        grad_up = (grad_hidden * gate_act * sigmoid).astype(BF)
        expert_grad = jnp.where(chosen, expert_grad, 0.0)
        grad_logits = probs * (jnp.where(own_expert, expert_grad, 0.0) - expert_grad * prob)
        grad_gate_logit = shared_grad * shared_scale * (1.0 - shared_scale)
        grad_wide = jnp.concatenate([grad_logits, grad_gate_logit], axis=1).astype(BF)
        partial = (
            dot(grad_gate, gate_w, (1,), (1,))
            + dot(grad_up, up_w, (1,), (1,))
            + dot(grad_wide, router_wide, (1,), (1,))
        )
        ffn.append((scaled, grad_gate, grad_up, grad_wide, scatter_rows(partial.astype(BF), ranks)))

    rows_both = jnp.concatenate([saved[m][4] for m in range(micros)], axis=0)
    total_down = dot(
        jnp.concatenate([ffn[m][0] for m in range(micros)], axis=0),
        jnp.concatenate(grad_rows, axis=0),
        (0,),
        (0,),
    )
    total_gate = dot(rows_both, jnp.concatenate([ffn[m][1] for m in range(micros)], axis=0), (0,), (0,))
    total_up = dot(rows_both, jnp.concatenate([ffn[m][2] for m in range(micros)], axis=0), (0,), (0,))
    total_wide = dot(rows_both, jnp.concatenate([ffn[m][3] for m in range(micros)], axis=0), (0,), (0,))
    down_g = lax.psum_scatter(total_down.astype(BF), "fsdp", scatter_dimension=1, tiled=True)
    gate_g = lax.psum_scatter(total_gate.astype(BF), "fsdp", scatter_dimension=0, tiled=True)
    up_g = lax.psum_scatter(total_up.astype(BF), "fsdp", scatter_dimension=0, tiled=True)

    grad_gain_two = jnp.zeros((width,), F32)
    backs = []
    for m in range(micros):
        normed_one, qkv, mixed, hidden, rows_two = saved[m]
        unit_two, inverse_two = normalize(hidden)
        grad_hidden, gain_part = norm_back(ffn[m][4], unit_two, inverse_two, gain_two)
        grad_gain_two = grad_gain_two + gain_part
        grad_hidden = grad_hidden + grads_own[m].astype(F32)
        attn_grad = gather_rows(grad_hidden.astype(BF), ranks)
        backs.append((grad_hidden, attn_grad))

    grad_gain_one = jnp.zeros((width,), F32)
    bias_sums = jnp.zeros((1, 3 * span), F32)
    grad_qkvs = []
    input_grads = []
    for m in range(micros):
        normed_one, qkv, mixed, hidden, rows_two = saved[m]
        grad_hidden, attn_grad = backs[m]
        grad_mixed = dot(attn_grad, out_w, (1,), (1,)).astype(BF)
        grad_qkv, sums = attend_back(lengths[m], qkv, grad_mixed, cosine, sine)
        bias_sums = bias_sums + sums
        grad_qkvs.append(grad_qkv)
        grad_normed = scatter_rows(dot(grad_qkv, qkv_w, (1,), (1,)).astype(BF), ranks)
        unit_one, inverse_one = normalize(tokens[m, 0].astype(F32))
        grad_inputs, gain_part = norm_back(grad_normed, unit_one, inverse_one, gain_one)
        grad_gain_one = grad_gain_one + gain_part
        input_grads.append((grad_inputs + grad_hidden).astype(BF))

    total_out = dot(
        jnp.concatenate([saved[m][2] for m in range(micros)], axis=0),
        jnp.concatenate([backs[m][1] for m in range(micros)], axis=0),
        (0,),
        (0,),
    )
    total_qkv = dot(
        jnp.concatenate([saved[m][0] for m in range(micros)], axis=0),
        jnp.concatenate(grad_qkvs, axis=0),
        (0,),
        (0,),
    )
    out_g = lax.psum_scatter(total_out.astype(BF), "fsdp", scatter_dimension=1, tiled=True).astype(F32)
    qkv_g = lax.psum_scatter(total_qkv.astype(BF), "fsdp", scatter_dimension=0, tiled=True).astype(F32)

    early = jnp.concatenate([grad_gain_two[:, None], total_wide], axis=1)
    early = lax.psum_scatter(early, ("fsdp", "tensor"), scatter_dimension=0, tiled=True)
    slots = (jnp.arange(ranks, dtype=jnp.int32) == rank).astype(F32)[:, None]
    late = jnp.concatenate([grad_gain_one, (slots * bias_sums).reshape(-1)])
    late = lax.psum(late, ("fsdp", "tensor"))
    place = lax.axis_index("fsdp") * ranks + rank
    gain_one_g = lax.dynamic_slice_in_dim(late, place * per_device, per_device, 0)
    bias_g = lax.dynamic_slice_in_dim(late, width + rank * 3 * span, 3 * span, 0)
    part = HD // groups
    bias_g = lax.dynamic_slice_in_dim(
        bias_g.reshape(3, heads, HD), lax.axis_index("fsdp") * part, part, 2
    )

    return (
        jnp.stack(layer_outs)[:, None],
        jnp.stack(input_grads)[:, None],
        gain_one_g,
        qkv_g[:, :span],
        qkv_g[:, span : 2 * span],
        qkv_g[:, 2 * span :],
        bias_g[0],
        bias_g[1],
        bias_g[2],
        out_g,
        early[:, 0],
        early[:, 1 : 1 + experts],
        early[:, 1 + experts],
        gate_g[:, :shared_units].astype(F32),
        up_g[:, :shared_units].astype(F32),
        down_g[:shared_units].astype(F32),
        gate_g[None, :, shared_units:].astype(F32),
        up_g[None, :, shared_units:].astype(F32),
        down_g[None, shared_units:].astype(F32),
    )


def solution(mesh):
    in_specs = (
        P(None, "fsdp", "tensor", None),
        P(None, "fsdp"),
        P(None, "fsdp", None, None),
        P(("fsdp", "tensor")),
        P("fsdp", "tensor"),
        P("fsdp", "tensor"),
        P("fsdp", "tensor"),
        P("tensor", "fsdp"),
        P("tensor", "fsdp"),
        P("tensor", "fsdp"),
        P("tensor", "fsdp"),
        P(("fsdp", "tensor")),
        P(("fsdp", "tensor"), None),
        P(("fsdp", "tensor")),
        P("fsdp", "tensor"),
        P("fsdp", "tensor"),
        P("tensor", "fsdp"),
        P("tensor", "fsdp", None),
        P("tensor", "fsdp", None),
        P("tensor", None, "fsdp"),
        P(None, "fsdp", "tensor", None),
    )
    out_specs = (
        P(None, "fsdp", "tensor", None),
        P(None, "fsdp", "tensor", None),
        P(("fsdp", "tensor")),
        P("fsdp", "tensor"),
        P("fsdp", "tensor"),
        P("fsdp", "tensor"),
        P("tensor", "fsdp"),
        P("tensor", "fsdp"),
        P("tensor", "fsdp"),
        P("tensor", "fsdp"),
        P(("fsdp", "tensor")),
        P(("fsdp", "tensor"), None),
        P(("fsdp", "tensor")),
        P("fsdp", "tensor"),
        P("fsdp", "tensor"),
        P("tensor", "fsdp"),
        P("tensor", "fsdp", None),
        P("tensor", "fsdp", None),
        P("tensor", None, "fsdp"),
    )
    return jax.shard_map(local, mesh=mesh, in_specs=in_specs, out_specs=out_specs, check_vma=False)
```

time: 2590 us -> 1260 us (0.49)
  waiting for transfers between devices: 1640 us -> 396 us
  starting transfers between devices: 3.26 us -> 218 us
  matrix products: 433 us -> 311 us
  blocking collectives: 162 us -> 85.5 us
  other arithmetic: 187 us -> 131 us
  local copies, waits for them, and re-layouts: 122 us -> 71 us
  Pallas kernels: 0 us -> 27.3 us
    reduce_scatter x20 -> x5, waiting for transfers between devices: 1210 us -> 49.1 us  [the longest x1 49 us: local(): lax.psum_scatter(total_down.astype(BF), 'fsdp', scatter_dimension=1, tile...]
    all_gather x18 -> x5, waiting for transfers between devices: 417 us -> 0.03 us  [the longest x1 0.02 us: local(): out_w = lax.all_gather(w_out, 'fsdp', axis=1, tiled=True)]
    ppermute x0 -> x144, waiting for transfers between devices: none -> 346 us  [the longest x24 200 us: gather_rows(): lax.ppermute(downward, 'tensor', line_pairs(-1, range(1, chips - step + 1)))]
    ppermute x0 -> x144, starting transfers between devices: none -> 217 us  [the longest x24 95.6 us: scatter_rows(): upward = lax.ppermute(upward, 'tensor', line_pairs(1, range(0, step)))]
    dot_general x98 -> x30, matrix products: 433 us -> 311 us  [dot(): lax.dot_general(left, right, ((left_dims, right_dims), ((), ())), preferr...]
    scatter-add x6 -> x0, other arithmetic: 104 us -> none  [the longest x2 47.7 us: local(): grad_rows_two = grad_rows_two.at[slot_index].add(grad_in_slots)]
    unnamed x3 -> x0, blocking collectives: 98.7 us -> none
    convert_element_type x21 -> x37, other arithmetic: 31 us -> 88.1 us  [the longest x1 29.5 us: local(): grad_up = (grad_hidden * gate_act * sigmoid).astype(BF)]
  transfers between devices with their start and end apart: 42 -> 155, of which waited for: 31 -> 51; matrix products, arithmetic and copies ran while one was open for 28% -> 30% of each run, Pallas kernels for 0% -> 2%
where the time goes in v1:
time: 1260 us
  waiting for transfers between devices  396 us (31%)
  matrix products  311 us (25%)
  starting transfers between devices  218 us (17%)
  other arithmetic  131 us (10%)
  blocking collectives  85.5 us (7%)
  local copies, waits for them, and re-layouts  71 us (6%)
  Pallas kernels  27.3 us (2%)
  between operations  18 us (1%)
    dot_general x30, matrix products, dot(): lax.dot_general(left, right, ((left_dims, right_dims), ((), ())), preferr...  311 us
    ppermute x24, waiting for transfers between devices, gather_rows(): lax.ppermute(downward, 'tensor', line_pairs(-1, range(1, chips - step + 1)))  200 us
    ppermute x24, waiting for transfers between devices, scatter_rows(): upward = lax.ppermute(upward, 'tensor', line_pairs(1, range(0, step)))  96.8 us
    ppermute x24, starting transfers between devices, scatter_rows(): upward = lax.ppermute(upward, 'tensor', line_pairs(1, range(0, step)))  95.6 us
    reduce_scatter x1, waiting for transfers between devices, local(): lax.psum_scatter(total_down.astype(BF), 'fsdp', scatter_dimension=1, tile...  49 us
    ppermute x24, starting transfers between devices, gather_rows(): lax.ppermute(upward, 'tensor', line_pairs(1, range(step - 1, chips - 1)))  47.9 us
    all_gather x1, blocking collectives, local(): small_all = lax.all_gather(small, ('fsdp', 'tensor'), axis=0, tiled=False)  44.1 us
    ppermute x24, starting transfers between devices, gather_rows(): lax.ppermute(downward, 'tensor', line_pairs(-1, range(1, chips - step + 1)))  43.8 us
  transfers between devices with their start and end apart: 155, of which 51 were waited for; matrix products, arithmetic and copies ran while one was open for 30% of the time, Pallas kernels for 2%

profile of v1, /device:TPU:0, one launch (start us, length us, event | category | flops | bytes accessed | tf_op | source)
XLA Modules:
  0.0 1257.1 jit_solution(4514429840141334299)
XLA Ops:
  40.5 44.1 %all-gather.1 = bf16[32,1,896]{2,1,0:T(2,128)(2,1)S(1)} all-gather(bf16[1,1,896]{2,1,0:T(2,128)(2,1)S(1)} %reshape.493), channel_id=2, replica_groups=mesh['fsdp'=4,'tensor'=8] {'fsdp','tensor'}, dimensions={0}, use_global_device_ids=true | all-gather | bytes 59136 | tf_op jit(solution)/shard_map/all_gather | solution.py:284
  99.7 7.4 collective-permute-done.72
  112.0 13.0 %collective-permute-done.5 = bf16[128,2048]{1,0:T(8,128)(2,1)S(1)} collective-permute-done((bf16[128,2048]{1,0:T(8,128)(2,1)}, bf16[128,2048]{1,0:T(8,128)(2,1)S(1)}, u32[]{:S(2)}, u32[]{:S(2)}) %collective-permute-start.5) | collective-permute-done | bytes 524320 | tf_op jit(solution)/shard_map/ppermute | solution.py:51
  130.5 16.8 %collective-permute-done.8 = bf16[128,2048]{1,0:T(8,128)(2,1)S(1)} collective-permute-done((bf16[128,2048]{1,0:T(8,128)(2,1)S(1)}, bf16[128,2048]{1,0:T(8,128)(2,1)S(1)}, u32[]{:S(2)}, u32[]{:S(2)}) %collective-permute-start.8) | collective-permute-done | bytes 524320 | tf_op jit(solution)/shard_map/ppermute | solution.py:51
  150.2 13.2 %collective-permute-done.113 = bf16[128,2048]{1,0:T(8,128)(2,1)} collective-permute-done((bf16[128,2048]{1,0:T(8,128)(2,1)}, bf16[128,2048]{1,0:T(8,128)(2,1)}, u32[]{:S(2)}, u32[]{:S(2)}) %collective-permute-start.113) | collective-permute-done | bytes 524320 | tf_op jit(solution)/shard_map/ppermute | solution.py:51
  168.5 10.5 collective-permute-done.36
  183.8 14.1 %collective-permute-start.41 = (bf16[128,2048]{1,0:T(8,128)(2,1)S(1)}, bf16[128,2048]{1,0:T(8,128)(2,1)S(1)}, u32[]{:S(2)}, u32[]{:S(2)}) collective-permute-start(bf16[128,2048]{1,0:T(8,128)(2,1)S(1)} %collective-permute-done.38), channel_id=1, source_target_pairs={{2,0},{3,1},{4,2},{5,3},{10,8},{11,9},{12,10},{13,11},{18,16},{19,... | collective-permute-start | bytes 1572872 | tf_op jit(solution)/shard_map/ppermute | solution.py:51
  200.0 13.2 %collective-permute-done.41 = bf16[128,2048]{1,0:T(8,128)(2,1)S(1)} collective-permute-done((bf16[128,2048]{1,0:T(8,128)(2,1)S(1)}, bf16[128,2048]{1,0:T(8,128)(2,1)S(1)}, u32[]{:S(2)}, u32[]{:S(2)}) %collective-permute-start.41) | collective-permute-done | bytes 524320 | tf_op jit(solution)/shard_map/ppermute | solution.py:51
  213.5 10.6 collective-permute-done.77
  231.1 11.3 collective-permute-done.44
  251.7 6.1 fusion.187.pre_ref
  308.7 6.4 collective-permute-done.12
  326.8 9.9 collective-permute-start.50
  382.5 6.8 collective-permute-done.18
  394.9 14.2 %collective-permute-done.59 = bf16[128,2048]{1,0:T(8,128)(2,1)S(1)} collective-permute-done((bf16[128,2048]{1,0:T(8,128)(2,1)S(1)}, bf16[128,2048]{1,0:T(8,128)(2,1)S(1)}, u32[]{:S(2)}, u32[]{:S(2)}) %collective-permute-start.59) | collective-permute-done | bytes 524320 | tf_op jit(solution)/shard_map/ppermute | solution.py:51
  412.1 13.5 %collective-permute-done.23 = bf16[128,2048]{1,0:T(8,128)(2,1)S(1)} collective-permute-done((bf16[128,2048]{1,0:T(8,128)(2,1)S(1)}, bf16[128,2048]{1,0:T(8,128)(2,1)S(1)}, u32[]{:S(2)}, u32[]{:S(2)}) %collective-permute-start.23) | collective-permute-done | bytes 524320 | tf_op jit(solution)/shard_map/ppermute | solution.py:51
  427.8 13.1 %collective-permute-done.62 = bf16[128,2048]{1,0:T(8,128)(2,1)S(1)} collective-permute-done((bf16[128,2048]{1,0:T(8,128)(2,1)S(1)}, bf16[128,2048]{1,0:T(8,128)(2,1)S(1)}, u32[]{:S(2)}, u32[]{:S(2)}) %collective-permute-start.62) | collective-permute-done | bytes 524320 | tf_op jit(solution)/shard_map/ppermute | solution.py:51
  442.7 12.8 %collective-permute-done.26 = bf16[128,2048]{1,0:T(8,128)(2,1)S(1)} collective-permute-done((bf16[128,2048]{1,0:T(8,128)(2,1)S(1)}, bf16[128,2048]{1,0:T(8,128)(2,1)S(1)}, u32[]{:S(2)}, u32[]{:S(2)}) %collective-permute-start.26) | collective-permute-done | bytes 524320 | tf_op jit(solution)/shard_map/ppermute | solution.py:51
  461.9 15.8 %fusion.185 = f32[1024,2112]{0,1:T(8,128)} fusion(bf16[1024,2048]{1,0:T(8,128)(2,1)} %bitcast.570, bf16[2048,2112]{1,0:T(8,128)(2,1)} %all-gather.12.cloned.1.call-done), kind=kOutput, calls=%fused_computation.459 | convolution fusion | flops 8858370048 | bytes 21495808 | tf_op jit(solution)/shard_map/dot_general | solution.py:19
  477.7 14.4 %fusion.188 = f32[1024,2112]{0,1:T(8,128)} fusion(bf16[1024,2048]{1,0:T(8,128)(2,1)S(1)} %bitcast.566, bf16[2048,2112]{1,0:T(8,128)(2,1)} %all-gather.12.cloned.1.call-done), kind=kOutput, calls=%fused_computation.462 | convolution fusion | flops 8858370048 | bytes 21495808 | tf_op jit(solution)/shard_map/dot_general | solution.py:19
  492.2 16.0 %fusion.186 = f32[1024,2112]{0,1:T(8,128)} fusion(bf16[1024,2048]{1,0:T(8,128)(2,1)} %bitcast.571, bf16[2048,2112]{1,0:T(8,128)(2,1)} %all-gather.14.cloned.1.call-done), kind=kOutput, calls=%fused_computation.460 | convolution fusion | flops 8858370048 | bytes 21495808 | tf_op jit(solution)/shard_map/dot_general | solution.py:19
  508.2 14.5 %fusion.189 = f32[1024,2112]{0,1:T(8,128)} fusion(bf16[1024,2048]{1,0:T(8,128)(2,1)S(1)} %bitcast.567, bf16[2048,2112]{1,0:T(8,128)(2,1)} %all-gather.14.cloned.1.call-done), kind=kOutput, calls=%fused_computation.463 | convolution fusion | flops 8858370048 | bytes 21495808 | tf_op jit(solution)/shard_map/dot_general | solution.py:19
  522.7 15.5 %fusion.192 = f32[1024,2112]{0,1:T(8,128)} fusion(bf16[1024,2048]{1,0:T(8,128)(2,1)} %bitcast.583, bf16[2112,2048]{1,0:T(8,128)(2,1)} %all-gather.16.cloned.1.call-done), kind=kOutput, calls=%fused_computation.466 | convolution fusion | flops 8858370048 | bytes 21495808 | tf_op jit(solution)/shard_map/dot_general | solution.py:19
  538.3 31.9 %select_reduce_fusion.3 = (f32[1024]{0:T(1024)S(1)}, f32[1024]{0:T(1024)S(1)}, f32[1024]{0:T(1024)S(1)}, f32[1024]{0:T(1024)S(1)}, bf16[1024,2112]{0,1:T(8,128)(...) fusion(pred[2112]{0:T(1024)(128)(4,1)S(1)} %copy-done.83, f32[1024,2112]{0,1:T(8,128)} %fusion.192, ...), kind=kOutput, calls=%fused_computation.25 | convolution fusion | flops 8910270464 | bytes 73418816 | tf_op jit(solution)/shard_map/dot_general | solution.py:19
  570.4 29.5 %multiply_convert_fusion = (bf16[1024,2112]{0,1:T(8,128)(2,1)}, bf16[1024,2112]{0,1:T(8,128)(2,1)S(1)}, bf16[1024,2112]{0,1:T(8,128)(2,1)}, bf16[1024,2112]{0,1:...) fusion(f32[1024,2112]{0,1:T(8,128)} %fusion.188, f32[1024,2112]{0,1:T(8,128)} %fusion.192, ...), kind=kLoop, calls=%fused_computation.22 | loop fusion | flops 77856768 | bytes 86526016 | tf_op jit(solution)/shard_map/convert_element_type | solution.py:357
  600.0 14.1 %fusion.193 = f32[1024,2048]{1,0:T(8,128)S(1)} fusion(bf16[1024,2112]{0,1:T(8,128)(2,1)S(1)} %get-tuple-element.185, bf16[2048,2112]{1,0:T(8,128)(2,1)} %all-gather.12.cloned.1.call-done), kind=kOutput, calls=%fused_computation.467 | convolution fusion | flops 8858370048 | bytes 21364736 | tf_op jit(solution)/shard_map/dot_general | solution.py:19
  614.2 14.0 %fusion.194 = f32[1024,2048]{1,0:T(8,128)S(1)} fusion(bf16[1024,2112]{0,1:T(8,128)(2,1)} %get-tuple-element.184, bf16[2048,2112]{1,0:T(8,128)(2,1)} %all-gather.14.cloned.1.call-done), kind=kOutput, calls=%fused_computation.468 | convolution fusion | flops 8858370048 | bytes 21364736 | tf_op jit(solution)/shard_map/dot_general | solution.py:19
  631.5 13.9 %fusion.191 = f32[1024,2048]{1,0:T(8,128)S(1)} fusion(bf16[1024,2112]{0,1:T(8,128)(2,1)} %get-tuple-element.274, bf16[2048,2112]{1,0:T(8,128)(2,1)} %all-gather.14.cloned.1.call-done), kind=kOutput, calls=%fused_computation.465 | convolution fusion | flops 8858370048 | bytes 21364736 | tf_op jit(solution)/shard_map/dot_general | solution.py:19
  645.4 14.9 %fusion.190 = f32[1024,2048]{1,0:T(8,128)} fusion(bf16[1024,2112]{0,1:T(8,128)(2,1)S(1)} %bitcast.580, bf16[2048,2112]{1,0:T(8,128)(2,1)} %all-gather.12.cloned.1.call-done), kind=kOutput, calls=%fused_computation.464 | convolution fusion | flops 8858370048 | bytes 21364736 | tf_op jit(solution)/shard_map/dot_general | solution.py:19
  673.6 8.3 collective-permute-done.120
  727.4 9.9 collective-permute-done.86
  772.3 13.5 %collective-permute-done.131 = bf16[128,2048]{1,0:T(8,128)(2,1)S(1)} collective-permute-done((bf16[128,2048]{1,0:T(8,128)(2,1)}, bf16[128,2048]{1,0:T(8,128)(2,1)S(1)}, u32[]{:S(2)}, u32[]{:S(2)}) %collective-permute-start.131) | collective-permute-done | bytes 524320 | tf_op jit(solution)/shard_map/ppermute | solution.py:51
  789.7 14.2 %collective-permute-done.95 = bf16[128,2048]{1,0:T(8,128)(2,1)S(1)} collective-permute-done((bf16[128,2048]{1,0:T(8,128)(2,1)}, bf16[128,2048]{1,0:T(8,128)(2,1)S(1)}, u32[]{:S(2)}, u32[]{:S(2)}) %collective-permute-start.95) | collective-permute-done | bytes 524320 | tf_op jit(solution)/shard_map/ppermute | solution.py:51
  806.2 14.3 %collective-permute-done.134 = bf16[128,2048]{1,0:T(8,128)(2,1)S(1)} collective-permute-done((bf16[128,2048]{1,0:T(8,128)(2,1)S(1)}, bf16[128,2048]{1,0:T(8,128)(2,1)S(1)}, u32[]{:S(2)}, u32[]{:S(2)}) %collective-permute-start.134) | collective-permute-done | bytes 524320 | tf_op jit(solution)/shard_map/ppermute | solution.py:51
  822.1 13.9 %collective-permute-done.98 = bf16[128,2048]{1,0:T(8,128)(2,1)S(1)} collective-permute-done((bf16[128,2048]{1,0:T(8,128)(2,1)S(1)}, bf16[128,2048]{1,0:T(8,128)(2,1)S(1)}, u32[]{:S(2)}, u32[]{:S(2)}) %collective-permute-start.98) | collective-permute-done | bytes 524320 | tf_op jit(solution)/shard_map/ppermute | solution.py:51
  850.1 7.9 shard_map.351
  860.0 9.0 shard_map.350
  870.1 8.2 fusion.26
  878.4 24.3 %convolution_convert_fusion = bf16[2048,2112]{0,1:T(8,128)(2,1)} fusion(bf16[1024,2112]{0,1:T(8,128)(2,1)} %get-tuple-element.184, bf16[1024,2112]{0,1:T(8,128)(2,1)} %get-tuple-element.274, bf16[1024,2048]{1,0:T(8,128)(2,1)} %bitcast.564, bf16[1024,2048]{1,0:T(8,128)(2,1)} %bitcast.572), kind=kOutput, calls=%fused_computation.4 | convolution fusion | flops 17755144192 | bytes 25690112 | tf_op jit(solution)/shard_map/dot_general | solution.py:19
  903.0 24.3 %convolution_convert_fusion.1 = bf16[2048,2112]{0,1:T(8,128)(2,1)} fusion(bf16[1024,2112]{0,1:T(8,128)(2,1)} %copy-done.35, bf16[1024,2112]{0,1:T(8,128)(2,1)} %get-tuple-element.273, bf16[1024,2048]{1,0:T(8,128)(2,1)} %bitcast.565, bf16[1024,2048]{1,0:T(8,128)(2,1)} %bitcast.573), kind=kOutput, calls=%fused_computation.5 | convolution fusion | flops 17755144192 | bytes 25690112 | tf_op jit(solution)/shard_map/dot_general | solution.py:19
  927.4 14.0 %convolution_convert_fusion.4 = bf16[1024,2048]{1,0:T(8,128)(2,1)S(1)} fusion(bf16[1024,2112]{0,1:T(8,128)(2,1)} %get-tuple-element.272, bf16[2112,2048]{1,0:T(8,128)(2,1)} %all-gather.16.cloned.1.call-done), kind=kOutput, calls=%fused_computation.63 | convolution fusion | flops 8860467200 | bytes 17170432 | tf_op jit(solution)/shard_map/dot_general | solution.py:19
  945.9 21.7 %convolution_convert_fusion.2 = bf16[2112,2048]{1,0:T(8,128)(2,1)} fusion(bf16[1024,2112]{0,1:T(8,128)(2,1)} %get-tuple-element.260, bf16[1024,2112]{0,1:T(8,128)(2,1)} %get-tuple-element.272, bf16[1024,2048]{1,0:T(8,128)(2,1)S(1)} %bitcast.584, bf16[1024,2048]{1,0:T(8,128)(2,1)S(1)} %bitcast.586), kind=kOutput, calls=%fused_computation.6 | convolution fusion | flops 17755144192 | bytes 25690112 | tf_op jit(solution)/shard_map/dot_general | solution.py:19
  967.7 14.3 %convolution_convert_fusion.3 = bf16[1024,2048]{1,0:T(8,128)(2,1)S(1)} fusion(bf16[1024,2112]{0,1:T(8,128)(2,1)} %get-tuple-element.260, bf16[2112,2048]{1,0:T(8,128)(2,1)} %all-gather.16.cloned.1.call-done), kind=kOutput, calls=%fused_computation.62 | convolution fusion | flops 8860467200 | bytes 17170432 | tf_op jit(solution)/shard_map/dot_general | solution.py:19
  1038.3 12.3 collective-permute-done.138
  1071.9 12.3 collective-permute-done.139
  1110.3 6.0 collective-permute-start.68
  1123.9 41.4 %psum.7 = f32[8192]{0:T(1024)S(1)} all-reduce(f32[8192]{0:T(1024)S(1)} %pad_maximum_fusion.12), channel_id=1, replica_groups=mesh['fsdp'=4,'tensor'=8] {'fsdp','tensor'}, use_global_device_ids=true, to_apply=%region_24.25 | all-reduce | flops 8192 | bytes 65536 | tf_op jit(solution)/shard_map/psum | solution.py:430
  1190.8 49.0 %reduce-scatter.17.cloned.1.call-done = bf16[2112,512]{1,0:T(8,128)(2,1)} async-done(((bf16[2112,2048]{1,0:T(8,128)(2,1)}), bf16[2112,512]{1,0:T(8,128)(2,1)}) %reduce-scatter.17.cloned.1.call-update) | async-done | bytes 2162704 | tf_op jit(solution)/shard_map/reduce_scatter | solution.py:379
  (765 shorter events, 489.0 us)
Async XLA Ops:
  7.2 244.5 %all-gather.8.cloned.1.call-start = ((), (), s32[]{:S(2)}) async-start(), calls=%async_computation.6 | async-start | bytes 3932160 | tf_op jit(solution)/shard_map/all_gather | solution.py:296
  9.4 253.6 %all-gather.10.cloned.1.call-start = ((), (), s32[]{:S(2)}) async-start(), calls=%async_computation.7 | async-start | bytes 1310720 | tf_op jit(solution)/shard_map/all_gather | solution.py:299
  10.2 451.7 %all-gather.12.cloned.1.call-start = ((), (), s32[]{:S(2)}) async-start(), calls=%async_computation.8 | async-start | bytes 11141120 | tf_op jit(solution)/shard_map/all_gather | solution.py:300
  13.8 478.4 %all-gather.14.cloned.1.call-start = ((), (), s32[]{:S(2)}) async-start(), calls=%async_computation.9 | async-start | bytes 11141120 | tf_op jit(solution)/shard_map/all_gather | solution.py:303
  18.9 503.9 %all-gather.16.cloned.1.call-start = ((), (), s32[]{:S(2)}) async-start(), calls=%async_computation.10 | async-start | bytes 10813440 | tf_op jit(solution)/shard_map/all_gather | solution.py:306
  19.8 71.7 %collective-permute-start = (bf16[128,2048]{1,0:T(8,128)(2,1)}, bf16[128,2048]{1,0:T(8,128)(2,1)}, u32[]{:S(2)}, u32[]{:S(2)}) collective-permute-start(bf16[128,2048]{1,0:T(8,128)(2,1)} %slice_bitcast_fusion.4), channel_id=1, source_target_pairs={{0,2},{1,3},{2,4},{3,5},{4,6},{5,7},{8,10},{9,11},{10,12},{11,13},... | collective-permute-start | bytes 1572872 | tf_op jit(solution)/shard_map/ppermute | solution.py:50
  25.5 73.5 %collective-permute-start.2 = (bf16[128,2048]{1,0:T(8,128)(2,1)}, bf16[128,2048]{1,0:T(8,128)(2,1)}, u32[]{:S(2)}, u32[]{:S(2)}) collective-permute-start(bf16[128,2048]{1,0:T(8,128)(2,1)} %slice_bitcast_fusion.4), channel_id=1, source_target_pairs={{2,0},{3,1},{4,2},{5,3},{6,4},{7,5},{10,8},{11,9},{12,10},{13,11},... | collective-permute-start | bytes 1572872 | tf_op jit(solution)/shard_map/ppermute | solution.py:51
  26.8 199.0 %collective-permute-start.10 = (bf16[128,2048]{1,0:T(8,128)(2,1)}, bf16[128,2048]{1,0:T(8,128)(2,1)}, u32[]{:S(2)}, u32[]{:S(2)}) collective-permute-start(bf16[128,2048]{1,0:T(8,128)(2,1)} %slice_bitcast_fusion.4), channel_id=1, source_target_pairs={{0,1},{1,0},{2,3},{3,2},{4,5},{5,4},{6,7},{7,6},{8,9},{9,8},{10,11... | collective-permute-start | bytes 1572872 | tf_op jit(solution)/shard_map/ppermute | solution.py:40
  29.6 67.6 %collective-permute-start.108 = (bf16[128,2048]{1,0:T(8,128)(2,1)S(1)}, bf16[128,2048]{1,0:T(8,128)(2,1)}, u32[]{:S(2)}, u32[]{:S(2)}) collective-permute-start(bf16[128,2048]{1,0:T(8,128)(2,1)S(1)} %get-tuple-element.248), channel_id=1, source_target_pairs={{0,2},{1,3},{2,4},{3,5},{4,6},{5,7},{8,10},{9,11},{10,12},{11,13},... | collective-permute-start | bytes 1572872 | tf_op jit(solution)/shard_map/ppermute | solution.py:50
  34.9 91.1 %collective-permute-start.110 = (bf16[128,2048]{1,0:T(8,128)(2,1)S(1)}, bf16[128,2048]{1,0:T(8,128)(2,1)}, u32[]{:S(2)}, u32[]{:S(2)}) collective-permute-start(bf16[128,2048]{1,0:T(8,128)(2,1)S(1)} %get-tuple-element.248), channel_id=1, source_target_pairs={{2,0},{3,1},{4,2},{5,3},{6,4},{7,5},{10,8},{11,9},{12,10},{13,11},... | collective-permute-start | bytes 1572872 | tf_op jit(solution)/shard_map/ppermute | solution.py:51
  39.3 1064.1 %reduce-scatter.19.cloned.1.call-start = ((), (), s32[]{:S(2)}) async-start(), calls=%async_computation.16 | async-start | bytes 1081344
  110.7 38.2 %collective-permute-start.74 = (bf16[128,2048]{1,0:T(8,128)(2,1)S(1)}, bf16[128,2048]{1,0:T(8,128)(2,1)S(1)}, u32[]{:S(2)}, u32[]{:S(2)}) collective-permute-start(bf16[128,2048]{1,0:T(8,128)(2,1)S(1)} %get-tuple-element.249), channel_id=1, source_target_pairs={{2,0},{3,1},{4,2},{5,3},{6,4},{7,5},{10,8},{11,9},{12,10},{13,11},... | collective-permute-start | bytes 1572872 | tf_op jit(solution)/shard_map/ppermute | solution.py:51
  149.5 64.0 %collective-permute-start.76 = (bf16[128,2048]{1,0:T(8,128)(2,1)S(1)}, bf16[128,2048]{1,0:T(8,128)(2,1)S(1)}, u32[]{:S(2)}, u32[]{:S(2)}) collective-permute-start(bf16[128,2048]{1,0:T(8,128)(2,1)S(1)} %collective-permute-done.72), channel_id=1, source_target_pairs={{2,4},{3,5},{4,6},{5,7},{10,12},{11,13},{12,14},{13,15},{18,20},{1... | collective-permute-start | bytes 1572872 | tf_op jit(solution)/shard_map/ppermute | solution.py:50
  183.8 29.4 %collective-permute-start.41 = (bf16[128,2048]{1,0:T(8,128)(2,1)S(1)}, bf16[128,2048]{1,0:T(8,128)(2,1)S(1)}, u32[]{:S(2)}, u32[]{:S(2)}) collective-permute-start(bf16[128,2048]{1,0:T(8,128)(2,1)S(1)} %collective-permute-done.38), channel_id=1, source_target_pairs={{2,0},{3,1},{4,2},{5,3},{10,8},{11,9},{12,10},{13,11},{18,16},{19,... | collective-permute-start | bytes 1572872 | tf_op jit(solution)/shard_map/ppermute | solution.py:51
  198.0 26.0 %collective-permute-start.77 = (bf16[128,2048]{1,0:T(8,128)(2,1)S(1)}, bf16[128,2048]{1,0:T(8,128)(2,1)S(1)}, u32[]{:S(2)}, u32[]{:S(2)}) collective-permute-start(bf16[128,2048]{1,0:T(8,128)(2,1)S(1)} %collective-permute-done.74), channel_id=1, source_target_pairs={{2,0},{3,1},{4,2},{5,3},{10,8},{11,9},{12,10},{13,11},{18,16},{19,... | collective-permute-start | bytes 1572872 | tf_op jit(solution)/shard_map/ppermute | solution.py:51
  199.4 78.0 %collective-permute-start.114 = (bf16[128,2048]{1,0:T(8,128)(2,1)}, bf16[128,2048]{1,0:T(8,128)(2,1)}, u32[]{:S(2)}, u32[]{:S(2)}) collective-permute-start(bf16[128,2048]{1,0:T(8,128)(2,1)} %get-tuple-element.151), channel_id=1, source_target_pairs={{0,1},{1,0},{2,3},{3,2},{4,5},{5,4},{6,7},{7,6},{8,9},{9,8},{10,11... | collective-permute-start | bytes 1572872 | tf_op jit(solution)/shard_map/ppermute | solution.py:40
  225.0 54.5 %collective-permute-start.78 = (bf16[128,2048]{1,0:T(8,128)(2,1)}, bf16[128,2048]{1,0:T(8,128)(2,1)}, u32[]{:S(2)}, u32[]{:S(2)}) collective-permute-start(bf16[128,2048]{1,0:T(8,128)(2,1)} %get-tuple-element.147), channel_id=1, source_target_pairs={{0,1},{1,0},{2,3},{3,2},{4,5},{5,4},{6,7},{7,6},{8,9},{9,8},{10,11... | collective-permute-start | bytes 1572872 | tf_op jit(solution)/shard_map/ppermute | solution.py:40
  228.3 53.5 %collective-permute-start.115 = (bf16[128,2048]{1,0:T(8,128)(2,1)}, bf16[128,2048]{1,0:T(8,128)(2,1)}, u32[]{:S(2)}, u32[]{:S(2)}) collective-permute-start(bf16[128,2048]{1,0:T(8,128)(2,1)} %collective-permute-done.112), channel_id=1, source_target_pairs={{4,6},{5,7},{12,14},{13,15},{20,22},{21,23},{28,30},{29,31}} | collective-permute-start | bytes 1572872 | tf_op jit(solution)/shard_map/ppermute | solution.py:50
  229.8 52.7 %collective-permute-start.116 = (bf16[128,2048]{1,0:T(8,128)(2,1)}, bf16[128,2048]{1,0:T(8,128)(2,1)}, u32[]{:S(2)}, u32[]{:S(2)}) collective-permute-start(bf16[128,2048]{1,0:T(8,128)(2,1)} %collective-permute-done.113), channel_id=1, source_target_pairs={{2,0},{3,1},{10,8},{11,9},{18,16},{19,17},{26,24},{27,25}} | collective-permute-start | bytes 1572872 | tf_op jit(solution)/shard_map/ppermute | solution.py:51
  279.5 90.0 %collective-permute-start.118 = (bf16[128,2048]{1,0:T(8,128)(2,1)S(1)}, bf16[128,2048]{1,0:T(8,128)(2,1)S(1)}, u32[]{:S(2)}, u32[]{:S(2)}) collective-permute-start(bf16[128,2048]{1,0:T(8,128)(2,1)S(1)} %copy-done.32), channel_id=1, source_target_pairs={{0,1},{1,0},{2,3},{3,2},{4,5},{5,4},{6,7},{7,6},{8,9},{9,8},{10,11... | collective-permute-start | bytes 1572872 | tf_op jit(solution)/shard_map/ppermute | solution.py:40
  304.3 22.1 %collective-permute-start.49 = (bf16[128,2048]{1,0:T(8,128)(2,1)S(1)}, bf16[128,2048]{1,0:T(8,128)(2,1)S(1)}, u32[]{:S(2)}, u32[]{:S(2)}) collective-permute-start(bf16[128,2048]{1,0:T(8,128)(2,1)S(1)} %get-tuple-element.232), channel_id=1, source_target_pairs={{0,2},{1,3},{2,4},{3,5},{8,10},{9,11},{10,12},{11,13},{16,18},{17,... | collective-permute-start | bytes 1572872 | tf_op jit(solution)/shard_map/ppermute | solution.py:86
  326.8 22.2 %collective-permute-start.50 = (bf16[128,2048]{1,0:T(8,128)(2,1)S(1)}, bf16[128,2048]{1,0:T(8,128)(2,1)S(1)}, u32[]{:S(2)}, u32[]{:S(2)}) collective-permute-start(bf16[128,2048]{1,0:T(8,128)(2,1)S(1)} %get-tuple-element.230), channel_id=1, source_target_pairs={{0,2},{1,3},{2,4},{3,5},{4,6},{5,7},{8,10},{9,11},{10,12},{11,13},... | collective-permute-start | bytes 1572872 | tf_op jit(solution)/shard_map/ppermute | solution.py:86
  349.0 27.2 %collective-permute-start.82 = (bf16[128,2048]{1,0:T(8,128)(2,1)S(1)}, bf16[128,2048]{1,0:T(8,128)(2,1)S(1)}, u32[]{:S(2)}, u32[]{:S(2)}) collective-permute-start(bf16[128,2048]{1,0:T(8,128)(2,1)S(1)} %copy-done.29), channel_id=1, source_target_pairs={{0,1},{1,0},{2,3},{3,2},{4,5},{5,4},{6,7},{7,6},{8,9},{9,8},{10,11... | collective-permute-start | bytes 1572872 | tf_op jit(solution)/shard_map/ppermute | solution.py:40
  378.4 79.4 %collective-permute-start.28 = (bf16[128,2048]{1,0:T(8,128)(2,1)S(1)}, bf16[128,2048]{1,0:T(8,128)(2,1)S(1)}, u32[]{:S(2)}, u32[]{:S(2)}) collective-permute-start(bf16[128,2048]{1,0:T(8,128)(2,1)S(1)} %get-tuple-element.264), channel_id=1, source_target_pairs={{0,1},{1,0},{2,3},{3,2},{4,5},{5,4},{6,7},{7,6},{8,9},{9,8},{10,11... | collective-permute-start | bytes 1572872 | tf_op jit(solution)/shard_map/ppermute | solution.py:40
  394.2 61.6 %collective-permute-start.64 = (bf16[128,2048]{1,0:T(8,128)(2,1)S(1)}, bf16[128,2048]{1,0:T(8,128)(2,1)S(1)}, u32[]{:S(2)}, u32[]{:S(2)}) collective-permute-start(bf16[128,2048]{1,0:T(8,128)(2,1)S(1)} %get-tuple-element.263), channel_id=1, source_target_pairs={{0,1},{1,0},{2,3},{3,2},{4,5},{5,4},{6,7},{7,6},{8,9},{9,8},{10,11... | collective-permute-start | bytes 1572872 | tf_op jit(solution)/shard_map/ppermute | solution.py:40
  631.0 34.6 %collective-permute-start.119 = (bf16[4,128,2048]{2,1,0:T(8,128)(2,1)}, bf16[4,128,2048]{2,1,0:T(8,128)(2,1)}, u32[]{:S(2)}, u32[]{:S(2)}) collective-permute-start(bf16[4,128,2048]{2,1,0:T(8,128)(2,1)} %dynamic-slice_bitcast_fusion.1), channel_id=1, source_target_pairs={{0,1},{1,0},{2,3},{3,2},{4,5},{5,4},{6,7},{7,6},{8,9},{9,8},{10,11... | collective-permute-start | bytes 6291464 | tf_op jit(solution)/shard_map/ppermute | solution.py:40
  682.3 22.1 %collective-permute-start.121 = (bf16[128,2048]{1,0:T(8,128)(2,1)S(1)}, bf16[128,2048]{1,0:T(8,128)(2,1)S(1)}, u32[]{:S(2)}, u32[]{:S(2)}) collective-permute-start(bf16[128,2048]{1,0:T(8,128)(2,1)S(1)} %get-tuple-element.196), channel_id=1, source_target_pairs={{0,2},{1,3},{2,4},{3,5},{8,10},{9,11},{10,12},{11,13},{16,18},{17,... | collective-permute-start | bytes 1572872 | tf_op jit(solution)/shard_map/ppermute | solution.py:86
  745.3 92.9 %collective-permute-start.136 = (bf16[128,2048]{1,0:T(8,128)(2,1)}, bf16[128,2048]{1,0:T(8,128)(2,1)}, u32[]{:S(2)}, u32[]{:S(2)}) collective-permute-start(bf16[128,2048]{1,0:T(8,128)(2,1)} %get-tuple-element.262), channel_id=1, source_target_pairs={{0,1},{1,0},{2,3},{3,2},{4,5},{5,4},{6,7},{7,6},{8,9},{9,8},{10,11... | collective-permute-start | bytes 1572872 | tf_op jit(solution)/shard_map/ppermute | solution.py:40
  753.9 353.2 %reduce-scatter.11.cloned.1.call-start = ((), (), s32[]{:S(2)}) async-start(), calls=%async_computation.12 | async-start | bytes 1310720 | tf_op jit(solution)/shard_map/reduce_scatter | solution.py:423
  771.6 67.8 %collective-permute-start.100 = (bf16[128,2048]{1,0:T(8,128)(2,1)S(1)}, bf16[128,2048]{1,0:T(8,128)(2,1)S(1)}, u32[]{:S(2)}, u32[]{:S(2)}) collective-permute-start(bf16[128,2048]{1,0:T(8,128)(2,1)S(1)} %fusion.158), channel_id=1, source_target_pairs={{0,1},{1,0},{2,3},{3,2},{4,5},{5,4},{6,7},{7,6},{8,9},{9,8},{10,11... | collective-permute-start | bytes 1572872 | tf_op jit(solution)/shard_map/ppermute | solution.py:40
  846.0 328.7 %reduce-scatter.9.cloned.1.call-start = ((), (), s32[]{:S(2)}) async-start(), calls=%async_computation.11 | async-start | bytes 3932160 | tf_op jit(solution)/shard_map/reduce_scatter | solution.py:424
  878.4 298.6 %reduce-scatter.15.cloned.1.call-start = ((), (), s32[]{:S(2)}) async-start(), calls=%async_computation.14 | async-start | bytes 10813440 | tf_op jit(solution)/shard_map/reduce_scatter | solution.py:381
  902.8 281.0 %reduce-scatter.13.cloned.1.call-start = ((), (), s32[]{:S(2)}) async-start(), calls=%async_computation.13 | async-start | bytes 10813440 | tf_op jit(solution)/shard_map/reduce_scatter | solution.py:380
  927.4 312.5 %reduce-scatter.17.cloned.1.call-start = ((), (), s32[]{:S(2)}) async-start(), calls=%async_computation.15 | async-start | bytes 10813440 | tf_op jit(solution)/shard_map/reduce_scatter | solution.py:379
  945.1 40.5 %collective-permute-start.29 = (bf16[4,128,2048]{2,1,0:T(8,128)(2,1)}, bf16[4,128,2048]{2,1,0:T(8,128)(2,1)}, u32[]{:S(2)}, u32[]{:S(2)}) collective-permute-start(bf16[4,128,2048]{2,1,0:T(8,128)(2,1)} %dynamic-slice_bitcast_fusion.6), channel_id=1, source_target_pairs={{0,1},{1,0},{2,3},{3,2},{4,5},{5,4},{6,7},{7,6},{8,9},{9,8},{10,11... | collective-permute-start | bytes 6291464 | tf_op jit(solution)/shard_map/ppermute | solution.py:40
  1011.7 23.1 %collective-permute-start.31 = (bf16[128,2048]{1,0:T(8,128)(2,1)S(1)}, bf16[128,2048]{1,0:T(8,128)(2,1)S(1)}, u32[]{:S(2)}, u32[]{:S(2)}) collective-permute-start(bf16[128,2048]{1,0:T(8,128)(2,1)S(1)} %get-tuple-element.214), channel_id=1, source_target_pairs={{0,2},{1,3},{2,4},{3,5},{8,10},{9,11},{10,12},{11,13},{16,18},{17,... | collective-permute-start | bytes 1572872 | tf_op jit(solution)/shard_map/ppermute | solution.py:86
  1017.9 49.4 %collective-permute-start.67 = (bf16[128,2048]{1,0:T(8,128)(2,1)S(1)}, bf16[128,2048]{1,0:T(8,128)(2,1)S(1)}, u32[]{:S(2)}, u32[]{:S(2)}) collective-permute-start(bf16[128,2048]{1,0:T(8,128)(2,1)S(1)} %get-tuple-element.220), channel_id=1, source_target_pairs={{0,2},{1,3},{2,4},{3,5},{8,10},{9,11},{10,12},{11,13},{16,18},{17,... | collective-permute-start | bytes 1572872 | tf_op jit(solution)/shard_map/ppermute | solution.py:86
  1026.2 24.4 %collective-permute-start.138 = (bf16[128,2048]{1,0:T(8,128)(2,1)S(1)}, bf16[128,2048]{1,0:T(8,128)(2,1)S(1)}, u32[]{:S(2)}, u32[]{:S(2)}) collective-permute-start(bf16[128,2048]{1,0:T(8,128)(2,1)S(1)} %get-tuple-element.192), channel_id=1, source_target_pairs={{0,2},{1,3},{8,10},{9,11},{16,18},{17,19},{24,26},{25,27}} | collective-permute-start | bytes 1572872 | tf_op jit(solution)/shard_map/ppermute | solution.py:86
  1034.8 27.0 %collective-permute-start.102 = (bf16[128,2048]{1,0:T(8,128)(2,1)S(1)}, bf16[128,2048]{1,0:T(8,128)(2,1)S(1)}, u32[]{:S(2)}, u32[]{:S(2)}) collective-permute-start(bf16[128,2048]{1,0:T(8,128)(2,1)S(1)} %get-tuple-element.204), channel_id=1, source_target_pairs={{0,2},{1,3},{8,10},{9,11},{16,18},{17,19},{24,26},{25,27}} | collective-permute-start | bytes 1572872 | tf_op jit(solution)/shard_map/ppermute | solution.py:86
  1036.1 30.1 %collective-permute-start.105 = (bf16[128,2048]{1,0:T(8,128)(2,1)S(1)}, bf16[128,2048]{1,0:T(8,128)(2,1)S(1)}, u32[]{:S(2)}, u32[]{:S(2)}) collective-permute-start(bf16[128,2048]{1,0:T(8,128)(2,1)S(1)} %get-tuple-element.205), channel_id=1, source_target_pairs={{6,4},{7,5},{14,12},{15,13},{22,20},{23,21},{30,28},{31,29}} | collective-permute-start | bytes 1572872 | tf_op jit(solution)/shard_map/ppermute | solution.py:87
  1051.2 115.4 %collective-permute-start.32 = (bf16[128,2048]{1,0:T(8,128)(2,1)}, bf16[128,2048]{1,0:T(8,128)(2,1)}, u32[]{:S(2)}, u32[]{:S(2)}) collective-permute-start(bf16[128,2048]{1,0:T(8,128)(2,1)} %get-tuple-element.212), channel_id=1, source_target_pairs={{0,2},{1,3},{2,4},{3,5},{4,6},{5,7},{8,10},{9,11},{10,12},{11,13},... | collective-permute-start | bytes 1572872 | tf_op jit(solution)/shard_map/ppermute | solution.py:86
  1061.8 22.5 %collective-permute-start.139 = (bf16[128,2048]{1,0:T(8,128)(2,1)S(1)}, bf16[128,2048]{1,0:T(8,128)(2,1)S(1)}, u32[]{:S(2)}, u32[]{:S(2)}) collective-permute-start(bf16[128,2048]{1,0:T(8,128)(2,1)S(1)} %get-tuple-element.190), channel_id=1, source_target_pairs={{0,2},{1,3},{2,4},{3,5},{8,10},{9,11},{10,12},{11,13},{16,18},{17,... | collective-permute-start | bytes 1572872 | tf_op jit(solution)/shard_map/ppermute | solution.py:86
  1067.3 28.2 %collective-permute-start.103 = (bf16[128,2048]{1,0:T(8,128)(2,1)S(1)}, bf16[128,2048]{1,0:T(8,128)(2,1)S(1)}, u32[]{:S(2)}, u32[]{:S(2)}) collective-permute-start(bf16[128,2048]{1,0:T(8,128)(2,1)S(1)} %get-tuple-element.202), channel_id=1, source_target_pairs={{0,2},{1,3},{2,4},{3,5},{8,10},{9,11},{10,12},{11,13},{16,18},{17,... | collective-permute-start | bytes 1572872 | tf_op jit(solution)/shard_map/ppermute | solution.py:86
  1069.8 25.6 %collective-permute-start.106 = (bf16[128,2048]{1,0:T(8,128)(2,1)S(1)}, bf16[128,2048]{1,0:T(8,128)(2,1)S(1)}, u32[]{:S(2)}, u32[]{:S(2)}) collective-permute-start(bf16[128,2048]{1,0:T(8,128)(2,1)S(1)} %get-tuple-element.203), channel_id=1, source_target_pairs={{4,2},{5,3},{6,4},{7,5},{12,10},{13,11},{14,12},{15,13},{20,18},{2... | collective-permute-start | bytes 1572872 | tf_op jit(solution)/shard_map/ppermute | solution.py:87
  1085.6 23.3 %collective-permute-start.140 = (bf16[128,2048]{1,0:T(8,128)(2,1)}, bf16[128,2048]{1,0:T(8,128)(2,1)S(1)}, u32[]{:S(2)}, u32[]{:S(2)}) collective-permute-start(bf16[128,2048]{1,0:T(8,128)(2,1)} %get-tuple-element.188), channel_id=1, source_target_pairs={{0,2},{1,3},{2,4},{3,5},{4,6},{5,7},{8,10},{9,11},{10,12},{11,13},... | collective-permute-start | bytes 1572872 | tf_op jit(solution)/shard_map/ppermute | solution.py:86
  1109.0 57.7 %collective-permute-start.35 = (bf16[128,2048]{1,0:T(8,128)(2,1)}, bf16[128,2048]{1,0:T(8,128)(2,1)}, u32[]{:S(2)}, u32[]{:S(2)}) collective-permute-start(bf16[128,2048]{1,0:T(8,128)(2,1)} %get-tuple-element.213), channel_id=1, source_target_pairs={{2,0},{3,1},{4,2},{5,3},{6,4},{7,5},{10,8},{11,9},{12,10},{13,11},... | collective-permute-start | bytes 1572872 | tf_op jit(solution)/shard_map/ppermute | solution.py:87
  1110.3 59.8 %collective-permute-start.68 = (bf16[128,2048]{1,0:T(8,128)(2,1)}, bf16[128,2048]{1,0:T(8,128)(2,1)}, u32[]{:S(2)}, u32[]{:S(2)}) collective-permute-start(bf16[128,2048]{1,0:T(8,128)(2,1)} %get-tuple-element.218), channel_id=1, source_target_pairs={{0,2},{1,3},{2,4},{3,5},{4,6},{5,7},{8,10},{9,11},{10,12},{11,13},... | collective-permute-start | bytes 1572872 | tf_op jit(solution)/shard_map/ppermute | solution.py:86
  1118.1 52.0 %collective-permute-start.71 = (bf16[128,2048]{1,0:T(8,128)(2,1)}, bf16[128,2048]{1,0:T(8,128)(2,1)}, u32[]{:S(2)}, u32[]{:S(2)}) collective-permute-start(bf16[128,2048]{1,0:T(8,128)(2,1)} %get-tuple-element.219), channel_id=1, source_target_pairs={{2,0},{3,1},{4,2},{5,3},{6,4},{7,5},{10,8},{11,9},{12,10},{13,11},... | collective-permute-start | bytes 1572872 | tf_op jit(solution)/shard_map/ppermute | solution.py:87
  (222 other events, 5337.3 us)
Sparse Core Ops, SparseCore 0:
  10.4 46.8 all-gather.7
  59.1 26.6 all-gather.9
  88.2 91.8 all-gather.11
  182.4 91.9 all-gather.13
  276.6 89.6 all-gather.15
  754.0 134.6 reduce-scatter.18
  892.4 24.2 reduce-scatter.10
  919.7 43.9 reduce-scatter.8
  966.8 88.5 reduce-scatter.14
  1058.3 89.1 reduce-scatter.12
  1150.7 89.0 reduce-scatter.16

commit v2 on v1

v2 whole, which is shorter than its diff:
```python
import functools

import jax
import jax.numpy as jnp
from jax import lax
from jax.experimental import pallas as pl
from jax.experimental.layout import Layout, with_layout_constraint
from jax.experimental.pallas import tpu as pltpu
from jax.sharding import PartitionSpec as P

HD = 128
EPSILON = 1e-06
ROPE_BASE = 1000000.0
BF = jnp.bfloat16
F32 = jnp.float32
MESH = pl.DeviceIdType.MESH
QB = 256
LANES = 128
CHUNKS = 2
STRIP = 16
ROW_BLOCK = 256
VMEM_BYTES = 60 << 20


def dot(left, right, left_dims, right_dims):
    return lax.dot_general(
        left, right, ((left_dims, right_dims), ((), ())), preferred_element_type=F32
    )


def normalize(values):
    inverse = lax.rsqrt(jnp.mean(values * values, axis=-1, keepdims=True) + EPSILON)
    return (values * inverse, inverse)


def norm_back(grad_normed, unit, inverse, gain):
    grad_unit = grad_normed * gain
    grad_values = inverse * (grad_unit - unit * jnp.mean(grad_unit * unit, axis=-1, keepdims=True))
    return (grad_values, jnp.sum(grad_normed * unit, axis=0))


def after(value, *others):
    return lax.optimization_barrier((value,) + others)[0]


def remote(src, dst, sems, at, target):
    return pltpu.make_async_remote_copy(
        src_ref=src,
        dst_ref=dst,
        send_sem=sems[0].at[at],
        recv_sem=sems[1].at[at],
        device_id={"tensor": target},
        device_id_type=MESH,
    )


class Place:
    def __init__(self, ranks):
        rank = lax.axis_index("tensor")
        self.chips = ranks // 2
        self.chip, self.core = rank // 2, rank % 2
        self.partner = rank + 1 - 2 * self.core
        self.above, self.below = rank + 2, rank - 2
        self.not_top = self.chip < self.chips - 1
        self.not_bottom = self.chip > 0

    def meet(self):
        barrier = pltpu.get_barrier_semaphore()

        def greet(target):
            pl.semaphore_signal(barrier, 1, device_id={"tensor": target}, device_id_type=MESH)

        greet(self.partner)
        pl.when(self.not_top)(lambda: greet(self.above))
        pl.when(self.not_bottom)(lambda: greet(self.below))
        peers = 1 + self.not_top.astype(jnp.int32) + self.not_bottom.astype(jnp.int32)
        pl.semaphore_wait(barrier, peers)


def gather_scratch(ranks):
    chips = ranks // 2
    pair = [pltpu.SemaphoreType.DMA((chips, CHUNKS))] * 2
    cross = [pltpu.SemaphoreType.DMA((2 * chips, CHUNKS))] * 2
    return [pltpu.SemaphoreType.DMA] + pair + pair + cross


def gather_steps(place, block, whole, local_sem, up_s, up_r, down_s, down_r, cross_s, cross_r):
    chips, chip, core = place.chips, place.chip, place.core
    rows = block.shape[0]
    part = rows // CHUNKS
    up, down, cross = (up_s, up_r), (down_s, down_r), (cross_s, cross_r)

    def at(owner, chunk):
        first = pl.multiple_of((2 * owner + core) * rows + chunk * part, part)
        return whole.at[pl.ds(first, part)]

    def theirs(owner, chunk):
        first = pl.multiple_of((2 * owner + 1 - core) * rows + chunk * part, part)
        return whole.at[pl.ds(first, part)]

    def own(chunk):
        return block.at[pl.ds(chunk * part, part)]

    def upward(step, chunk):
        source = own(chunk) if step == 0 else at(chip - step, chunk)
        return remote(source, at(chip - step, chunk), up, (step, chunk), place.above)

    def downward(step, chunk):
        source = own(chunk) if step == 0 else at(chip + step, chunk)
        return remote(source, at(chip + step, chunk), down, (step, chunk), place.below)

    def across(slot, owner, chunk):
        source = own(chunk) if slot == 0 else at(owner, chunk)
        return remote(source, at(owner, chunk), cross, (slot, chunk), place.partner)

    def arrived(slot, owner, chunk):
        return remote(theirs(owner, chunk), theirs(owner, chunk), cross, (slot, chunk), place.partner)

    def arrived_up(step, chunk):
        return remote(at(chip - step, chunk), at(chip - step, chunk), up, (step - 1, chunk), place.above)

    def arrived_down(step, chunk):
        return remote(at(chip + step, chunk), at(chip + step, chunk), down, (step - 1, chunk), place.below)

    both = range(CHUNKS)

    def mine():
        first = pl.multiple_of((2 * chip + core) * rows, rows)
        return pltpu.make_async_copy(block, whole.at[pl.ds(first, rows)], local_sem)

    for chunk in both:
        pl.when(place.not_top)(lambda: upward(0, chunk).start())
        pl.when(place.not_bottom)(lambda: downward(0, chunk).start())
    for chunk in both:
        across(0, chip, chunk).start()
    mine().start()
    yield
    for step in range(1, chips):
        for chunk in both:

            @pl.when(chip >= step)
            def _():
                arrived_up(step, chunk).wait_recv()
                pl.when(place.not_top)(lambda: upward(step, chunk).start())
                across(2 * step - 1, chip - step, chunk).start()

            @pl.when(chip < chips - step)
            def _():
                arrived_down(step, chunk).wait_recv()
                pl.when(place.not_bottom)(lambda: downward(step, chunk).start())
                across(2 * step, chip + step, chunk).start()

        yield
    mine().wait()
    for step in range(chips):
        for chunk in both:
            if step == 0:
                arrived(0, chip, chunk).wait_recv()
                across(0, chip, chunk).wait_send()
            else:

                @pl.when(chip >= step)
                def _():
                    arrived(2 * step - 1, chip - step, chunk).wait_recv()
                    across(2 * step - 1, chip - step, chunk).wait_send()

                @pl.when(chip < chips - step)
                def _():
                    arrived(2 * step, chip + step, chunk).wait_recv()
                    across(2 * step, chip + step, chunk).wait_send()

            @pl.when(place.not_top & (chip >= step))
            def _():
                upward(step, chunk).wait_send()

            @pl.when(place.not_bottom & (chip < chips - step))
            def _():
                downward(step, chunk).wait_send()


def scatter_scratch(ranks, rows, width):
    chips = ranks // 2
    line = [pltpu.SemaphoreType.DMA((chips, CHUNKS))] * 2
    buffers = [pltpu.VMEM((chips, rows, width), BF)] * 5
    return buffers + [pltpu.SemaphoreType.DMA((chips,))] + line * 3


def scatter_steps(
    place, partial, total, kept, pair, held, up_in, down_in, keep_sem,
    up_s, up_r, down_s, down_r, cross_s, cross_r,
):
    chips, chip, core = place.chips, place.chip, place.core
    rows = total.shape[0]
    part = rows // CHUNKS
    up, down, cross = (up_s, up_r), (down_s, down_r), (cross_s, cross_r)
    both = range(CHUNKS)

    def keep(k):
        first = pl.multiple_of((2 * k + core) * rows, rows)
        return pltpu.make_async_copy(partial.at[pl.ds(first, rows)], kept.at[k], keep_sem.at[k])

    def across(k, chunk):
        first = pl.multiple_of((2 * k + 1 - core) * rows + chunk * part, part)
        return remote(
            partial.at[pl.ds(first, part)],
            pair.at[k, pl.ds(chunk * part, part)],
            cross,
            (k, chunk),
            place.partner,
        )

    def upward(step, k, chunk):
        cut = pl.ds(chunk * part, part)
        return remote(held.at[k, cut], up_in.at[step, cut], up, (step, chunk), place.above)

    def downward(step, k, chunk):
        cut = pl.ds(chunk * part, part)
        return remote(held.at[k, cut], down_in.at[step, cut], down, (step, chunk), place.below)

    def add(k, chunk, target, others):
        def strip(i, carry):
            cut = pl.ds(chunk * part + i * STRIP, STRIP)
            value = kept[k, cut].astype(F32) + pair[k, cut].astype(F32)
            for ref, slot in others:
                value = value + ref[slot, cut].astype(F32)
            if target is None:
                total[cut] = value
            else:
                target[k, cut] = value.astype(BF)
            return carry

        lax.fori_loop(0, part // STRIP, strip, 0)

    order = []
    for i in range(chips):
        for k in (chips - 1 - i, i):
            if k not in order:
                order.append(k)
    for k in order:
        keep(k).start()
        for chunk in both:
            across(k, chunk).start()
    yield
    for step in range(1, chips):
        for chunk in both:

            @pl.when(place.not_top & (chip <= step - 1))
            def _():
                k = chip + chips - step
                if chunk == 0:
                    keep(k).wait()
                across(k, chunk).wait_recv()

                @pl.when(place.not_bottom)
                def _():
                    upward(step - 1, k, chunk).wait_recv()
                    add(k, chunk, held, [(up_in, step - 1)])

                pl.when(jnp.logical_not(place.not_bottom))(lambda: add(k, chunk, held, []))
                upward(step, k, chunk).start()

            @pl.when(place.not_bottom & (chip >= chips - step))
            def _():
                k = chip - (chips - step)
                if chunk == 0:
                    keep(k).wait()
                across(k, chunk).wait_recv()

                @pl.when(place.not_top)
                def _():
                    downward(step - 1, k, chunk).wait_recv()
                    add(k, chunk, held, [(down_in, step - 1)])

                pl.when(jnp.logical_not(place.not_top))(lambda: add(k, chunk, held, []))
                downward(step, k, chunk).start()

        yield
    keep(chip).wait()
    last = chips - 1
    for chunk in both:
        across(chip, chunk).wait_recv()

        @pl.when(place.not_top & place.not_bottom)
        def _():
            upward(last, chip, chunk).wait_recv()
            downward(last, chip, chunk).wait_recv()
            add(chip, chunk, None, [(up_in, last), (down_in, last)])

        @pl.when(jnp.logical_not(place.not_top))
        def _():
            upward(last, chip, chunk).wait_recv()
            add(chip, chunk, None, [(up_in, last)])

        @pl.when(jnp.logical_not(place.not_bottom))
        def _():
            downward(last, chip, chunk).wait_recv()
            add(chip, chunk, None, [(down_in, last)])

    for chunk in both:
        for k in range(chips):
            across(k, chunk).wait_send()
        for step in range(1, chips):

            @pl.when(place.not_top & (chip <= step - 1))
            def _():
                upward(step, chip + chips - step, chunk).wait_send()

            @pl.when(place.not_bottom & (chip >= chips - step))
            def _():
                downward(step, chip - (chips - step), chunk).wait_send()


GATHER_REFS, SCATTER_REFS = 7, 12


class Transfers:
    def __init__(self, ranks, ident, blocks=(), partials=(), needed=()):
        self.ranks, self.ident = ranks, ident
        self.blocks, self.partials = list(blocks), list(partials)
        self.inputs = self.blocks + self.partials + list(needed)
        self.moves = len(self.blocks) + len(self.partials)
        self.shapes, self.out_specs, self.scratch = [], [], []
        anywhere = pl.BlockSpec(memory_space=pl.ANY)
        self.in_specs = [anywhere] * len(self.inputs)
        for block in self.blocks:
            self.shapes.append(
                jax.ShapeDtypeStruct((ranks * block.shape[0], block.shape[1]), BF)
            )
            self.out_specs.append(anywhere)
            self.scratch += gather_scratch(ranks)
        for partial in self.partials:
            rows, width = partial.shape[0] // ranks, partial.shape[1]
            self.shapes.append(jax.ShapeDtypeStruct((rows, width), F32))
            self.out_specs.append(pl.BlockSpec(memory_space=pltpu.VMEM))
            self.scratch += scatter_scratch(ranks, rows, width)

    def params(self):
        if not self.moves:
            return pltpu.CompilerParams(vmem_limit_bytes=VMEM_BYTES)
        return pltpu.CompilerParams(
            collective_id=self.ident, has_side_effects=True, vmem_limit_bytes=VMEM_BYTES
        )

    def begin(self, inputs, outputs, scratch):
        if not self.moves:
            return lambda: False
        place = Place(self.ranks)
        scratch = list(scratch)
        running = []
        for i in range(self.moves):
            gathers = i < len(self.blocks)
            count = GATHER_REFS if gathers else SCATTER_REFS
            taken, scratch = scratch[:count], scratch[count:]
            steps = gather_steps if gathers else scatter_steps
            running.append(steps(place, inputs[i], outputs[i], *taken))
        state = {"met": False, "running": running}

        def phase():
            if not state["met"]:
                place.meet()
                state["met"] = True
            still = []
            for steps in state["running"]:
                if next(steps, True) is None:
                    still.append(steps)
            state["running"] = still
            return bool(still)

        return phase


def finish(phase):
    while phase():
        pass


def exchange_kernel(transfers, *refs):
    count, moves = len(transfers.inputs), transfers.moves
    finish(transfers.begin(refs[:moves], refs[count : count + moves], refs[count + moves :]))


def exchange(ranks, ident, blocks=(), partials=(), needed=()):
    transfers = Transfers(ranks, ident, blocks, partials, needed)
    return pl.pallas_call(
        functools.partial(exchange_kernel, transfers),
        out_shape=tuple(transfers.shapes),
        in_specs=transfers.in_specs,
        out_specs=tuple(transfers.out_specs),
        scratch_shapes=transfers.scratch,
        compiler_params=transfers.params(),
    )(*transfers.inputs)


def beside(phase, at, grid_steps, work):
    step = pl.program_id(0)
    for when in at:
        pl.when(step == when)(lambda: phase() and None)
    work()
    pl.when(step == grid_steps - 1)(lambda: finish(phase))


def spread_kernel(groups, ranks, reduces, value_ref, *refs):
    out_ref, landing, send_sem, recv_sem, own_sem = refs[-5:]
    devices = groups * ranks
    me = lax.axis_index("fsdp") * ranks + lax.axis_index("tensor")
    barrier = pltpu.get_barrier_semaphore()

    def name(device):
        return {"fsdp": device // ranks, "tensor": device % ranks}

    def greet(i, carry):
        target = lax.rem(me + i, devices)
        pl.semaphore_signal(barrier, 1, device_id=name(target), device_id_type=MESH)
        return carry

    lax.fori_loop(1, devices, greet, 0)
    pl.semaphore_wait(barrier, devices - 1)

    def copy(i):
        target = lax.rem(me + i, devices)
        return pltpu.make_async_remote_copy(
            src_ref=value_ref.at[target] if reduces else value_ref.at[0],
            dst_ref=landing.at[me],
            send_sem=send_sem.at[i],
            recv_sem=recv_sem.at[i],
            device_id=name(target),
            device_id_type=MESH,
        )

    def arrival(i):
        source = lax.rem(me - i + devices, devices)
        return pltpu.make_async_remote_copy(
            src_ref=landing.at[source],
            dst_ref=landing.at[source],
            send_sem=send_sem.at[i],
            recv_sem=recv_sem.at[i],
            device_id=name(source),
            device_id_type=MESH,
        )

    def send(i, carry):
        copy(i).start()
        return carry

    def receive(i, carry):
        arrival(i).wait_recv()
        copy(i).wait_send()
        return carry

    own = pltpu.make_async_copy(
        value_ref.at[me] if reduces else value_ref.at[0], landing.at[me], own_sem
    )
    own.start()
    lax.fori_loop(1, devices, send, 0)
    lax.fori_loop(1, devices, receive, 0)
    own.wait()
    if reduces:
        out_ref[...] = jnp.sum(landing[...], axis=0)
    else:
        out_ref[...] = landing[...]


def spread(groups, ranks, ident, values, reduces, needed=()):
    devices = groups * ranks
    tail = values.shape[1:]
    vmem = pl.BlockSpec(memory_space=pltpu.VMEM)
    return pl.pallas_call(
        functools.partial(spread_kernel, groups, ranks, reduces),
        out_shape=jax.ShapeDtypeStruct(tail if reduces else (devices,) + tail, values.dtype),
        in_specs=[vmem] + [pl.BlockSpec(memory_space=pl.ANY)] * len(needed),
        out_specs=vmem,
        scratch_shapes=[
            pltpu.VMEM((devices,) + tail, values.dtype),
            pltpu.SemaphoreType.DMA((devices,)),
            pltpu.SemaphoreType.DMA((devices,)),
            pltpu.SemaphoreType.DMA,
        ],
        compiler_params=pltpu.CompilerParams(collective_id=ident, has_side_effects=True),
    )(values, *needed)


def ffn_kernel(transfers, at, grid_steps, first, *refs):
    refs = list(refs)

    def take(count):
        taken = refs[:count]
        del refs[:count]
        return taken

    rows_ref, grad_ref, scale_ref, w_ref = take(4)
    before = () if first else take(2)
    sent = take(len(transfers.inputs))
    hidden_ref, gate_ref, up_ref, out_ref, back_ref, dots_ref = take(6)
    landed = take(transfers.moves)
    phase = transfers.begin(sent, landed, refs)

    def work():
        groups, _, depth, units = w_ref.shape
        gate_w, up_w, down_w = [w_ref[:, i].reshape(groups * depth, units) for i in range(3)]
        rows, grad, scale = rows_ref[...], grad_ref[...], scale_ref[...]
        gate_act = dot(rows, gate_w, (1,), (0,))
        up_act = dot(rows, up_w, (1,), (0,))
        back = dot(grad, down_w, (1,), (0,))
        sigmoid = 1.0 / (1.0 + jnp.exp(-gate_act))
        silu = gate_act * sigmoid
        hidden = (silu * up_act).astype(BF).astype(F32)
        dots_ref[...] = jnp.sum(hidden * back, axis=1, keepdims=True)
        scaled = (scale * hidden).astype(BF)
        hidden_ref[...] = scaled
        grad_hidden = scale * back
        grad_gate = (grad_hidden * up_act * (sigmoid * (1.0 + gate_act * (1.0 - sigmoid)))).astype(BF)
        gate_ref[...] = grad_gate
        grad_up = (grad_hidden * silu).astype(BF)
        up_ref[...] = grad_up
        moved = dot(scaled, down_w, (1,), (1,))
        turned = dot(grad_gate, gate_w, (1,), (1,)) + dot(grad_up, up_w, (1,), (1,))
        if not first:
            moved = moved + before[0][...].astype(F32)
            turned = turned + before[1][...].astype(F32)
        out_ref[...] = moved.astype(BF)
        back_ref[...] = turned.astype(BF)

    beside(phase, at, grid_steps, work)


def ffn(rows, grads, scale, weights, before, transfers, at=()):
    count, width = rows.shape
    units = weights.shape[3]
    first = before is None
    steps = count // ROW_BLOCK

    def block(size):
        return pl.BlockSpec((ROW_BLOCK, size), lambda i: (i, 0))

    whole = pl.BlockSpec(weights.shape, lambda i: (0, 0, 0, 0), pipeline_mode=pl.Buffered(1))
    given = [] if first else list(before)
    narrow = [jax.ShapeDtypeStruct((count, units), BF)] * 3
    wide = [jax.ShapeDtypeStruct((count, width), BF)] * 2
    dots = [jax.ShapeDtypeStruct((count, 1), F32)]
    results = pl.pallas_call(
        functools.partial(ffn_kernel, transfers, at, steps, first),
        grid=(steps,),
        in_specs=[block(width), block(width), block(1), whole]
        + [block(width)] * len(given)
        + transfers.in_specs,
        out_specs=tuple(
            [block(units)] * 3 + [block(width)] * 2 + [block(1)] + transfers.out_specs
        ),
        out_shape=tuple(narrow + wide + dots + transfers.shapes),
        scratch_shapes=transfers.scratch,
        compiler_params=transfers.params(),
        cost_estimate=pl.CostEstimate(
            flops=12 * count * width * units,
            bytes_accessed=2 * (3 * width * units + 4 * count * width + 3 * count * units),
            transcendentals=count * units,
        ),
    )(rows, grads, scale, weights, *given, *transfers.inputs)
    return results[:3], results[3:5], results[5], results[6:]


def ffn_grads_kernel(transfers, at, grid_steps, micros, *refs):
    refs = list(refs)

    def take(count):
        taken = refs[:count]
        del refs[:count]
        return taken

    per_micro = [take(5) for _ in range(micros)]
    sent = take(len(transfers.inputs))
    (out_ref,) = take(1)
    landed = take(transfers.moves)
    phase = transfers.begin(sent, landed, refs)

    def work():
        for which, left in ((0, 0), (1, 0), (2, 1)):
            total = None
            for one in per_micro:
                product = dot(one[left][...], one[2 + which][...], (0,), (0,))
                total = product if total is None else total + product
            out_ref[0, which] = total.astype(BF)

    beside(phase, at, grid_steps, work)


def ffn_grads(groups, per_micro, transfers, at=()):
    count, width = per_micro[0][0].shape
    units = per_micro[0][2].shape[1]
    depth = width // groups
    columns = pl.BlockSpec((count, depth), lambda i: (0, i))
    whole = pl.BlockSpec((count, units), lambda i: (0, 0), pipeline_mode=pl.Buffered(1))
    results = pl.pallas_call(
        functools.partial(ffn_grads_kernel, transfers, at, groups, len(per_micro)),
        grid=(groups,),
        in_specs=[columns, columns, whole, whole, whole] * len(per_micro) + transfers.in_specs,
        out_specs=tuple(
            [pl.BlockSpec((1, 3, depth, units), lambda i: (i, 0, 0, 0))] + transfers.out_specs
        ),
        out_shape=tuple(
            [jax.ShapeDtypeStruct((groups, 3, depth, units), BF)] + transfers.shapes
        ),
        scratch_shapes=transfers.scratch,
        compiler_params=transfers.params(),
        cost_estimate=pl.CostEstimate(
            flops=6 * len(per_micro) * count * width * units,
            bytes_accessed=2 * len(per_micro) * (2 * count * width + 3 * count * units)
            + 6 * width * units,
            transcendentals=0,
        ),
    )(*[array for one in per_micro for array in one], *transfers.inputs)
    return results[0], results[1:]


def rope_tables(seq_len):
    half = HD // 2
    frequency = ROPE_BASE ** (-(2.0 * jnp.arange(half, dtype=F32)) / HD)
    angles = jnp.arange(seq_len, dtype=F32)[:, None] * frequency[None, :]
    cosine, sine = jnp.cos(angles), jnp.sin(angles)
    return (
        jnp.concatenate([cosine, cosine], axis=1),
        jnp.concatenate([-sine, sine], axis=1),
    )


def swap_halves(values):
    half = HD // 2
    return jnp.concatenate([values[:, half:], values[:, :half]], axis=1)


def block_weights(query, keys, first_row, length):
    scores = dot(query, keys, (1,), (1,)) * (HD ** (-0.5))
    rows = first_row + lax.broadcasted_iota(jnp.int32, scores.shape, 0)
    cols = lax.broadcasted_iota(jnp.int32, scores.shape, 1)
    scores = jnp.where((cols <= rows) & (cols < length), scores, -1e30)
    exps = jnp.exp(scores - jnp.max(scores, axis=1, keepdims=True))
    return exps / jnp.sum(exps, axis=1, keepdims=True)


def attend_kernel(heads, length_ref, pre_ref, bias_ref, cos_ref, sin_ref, qkv_ref, out_ref):
    seq_len = pre_ref.shape[0]
    length = length_ref[0]
    for head in range(heads):
        for which in range(3):
            at = (which * heads + head) * HD
            for row in range(0, seq_len, QB):
                part = pre_ref[row : row + QB, at : at + HD] + bias_ref[:, at : at + HD]
                if which < 2:
                    part = (
                        part * cos_ref[row : row + QB, :]
                        + swap_halves(part) * sin_ref[row : row + QB, :]
                    )
                qkv_ref[row : row + QB, at : at + HD] = part.astype(BF)
        q_at, k_at, v_at = (head * HD, (heads + head) * HD, (2 * heads + head) * HD)
        for row in range(0, seq_len, QB):
            end = row + QB
            weights = block_weights(
                qkv_ref[row:end, q_at : q_at + HD], qkv_ref[:end, k_at : k_at + HD], row, length
            )
            mixed = dot(weights.astype(BF), qkv_ref[:end, v_at : v_at + HD], (1,), (0,))
            out_ref[row:end, q_at : q_at + HD] = mixed.astype(BF)


def attend_back_kernel(
    heads, length_ref, qkv_ref, grad_ref, cos_ref, sin_ref, out_ref, sums_ref, key_acc, value_acc
):
    seq_len = qkv_ref.shape[0]
    length = length_ref[0]
    scale = HD ** (-0.5)
    for head in range(heads):
        q_at, k_at, v_at = (head * HD, (heads + head) * HD, (2 * heads + head) * HD)
        key_acc[...] = jnp.zeros_like(key_acc)
        value_acc[...] = jnp.zeros_like(value_acc)
        q_sum = jnp.zeros((1, HD), F32)
        for row in range(0, seq_len, QB):
            end = row + QB
            query = qkv_ref[row:end, q_at : q_at + HD]
            keys = qkv_ref[:end, k_at : k_at + HD]
            grad = grad_ref[row:end, q_at : q_at + HD]
            weights = block_weights(query, keys, row, length)
            grad_weights = dot(grad, qkv_ref[:end, v_at : v_at + HD], (1,), (1,))
            inner = jnp.sum(weights * grad_weights, axis=1, keepdims=True)
            grad_scores = (scale * weights * (grad_weights - inner)).astype(BF)
            turned = dot(grad_scores, keys, (1,), (0,))
            grad_query = (
                turned * cos_ref[row:end, :] - swap_halves(turned) * sin_ref[row:end, :]
            ).astype(BF)
            out_ref[row:end, q_at : q_at + HD] = grad_query
            q_sum = q_sum + jnp.sum(grad_query.astype(F32), axis=0, keepdims=True)
            key_acc[:end, :] += dot(grad_scores, query, (0,), (0,))
            value_acc[:end, :] += dot(weights.astype(BF), grad, (0,), (0,))
        k_sum = jnp.zeros((1, HD), F32)
        v_sum = jnp.zeros((1, HD), F32)
        for row in range(0, seq_len, QB):
            end = row + QB
            turned = key_acc[row:end, :]
            grad_key = (
                turned * cos_ref[row:end, :] - swap_halves(turned) * sin_ref[row:end, :]
            ).astype(BF)
            grad_value = value_acc[row:end, :].astype(BF)
            out_ref[row:end, k_at : k_at + HD] = grad_key
            out_ref[row:end, v_at : v_at + HD] = grad_value
            k_sum = k_sum + jnp.sum(grad_key.astype(F32), axis=0, keepdims=True)
            v_sum = v_sum + jnp.sum(grad_value.astype(F32), axis=0, keepdims=True)
        sums_ref[:, q_at : q_at + HD] = q_sum
        sums_ref[:, k_at : k_at + HD] = k_sum
        sums_ref[:, v_at : v_at + HD] = v_sum


def in_vmem(count):
    return [pl.BlockSpec(memory_space=pltpu.VMEM)] * count


def attend(length, pre, bias, cosine, sine):
    seq_len, width = pre.shape
    heads = width // (3 * HD)
    return pl.pallas_call(
        functools.partial(attend_kernel, heads),
        out_shape=(
            jax.ShapeDtypeStruct((seq_len, width), BF),
            jax.ShapeDtypeStruct((seq_len, heads * HD), BF),
        ),
        in_specs=[pl.BlockSpec(memory_space=pltpu.SMEM)] + in_vmem(4),
        out_specs=tuple(in_vmem(2)),
        compiler_params=pltpu.CompilerParams(vmem_limit_bytes=32 << 20),
        cost_estimate=pl.CostEstimate(
            flops=3 * heads * HD * seq_len * seq_len,
            bytes_accessed=10 * seq_len * width,
            transcendentals=heads * seq_len * seq_len,
        ),
    )(length, pre, bias, cosine, sine)


def attend_back(length, qkv, grad, cosine, sine):
    seq_len, width = qkv.shape
    heads = width // (3 * HD)
    return pl.pallas_call(
        functools.partial(attend_back_kernel, heads),
        out_shape=(
            jax.ShapeDtypeStruct((seq_len, width), BF),
            jax.ShapeDtypeStruct((1, width), F32),
        ),
        in_specs=[pl.BlockSpec(memory_space=pltpu.SMEM)] + in_vmem(4),
        out_specs=tuple(in_vmem(2)),
        scratch_shapes=[pltpu.VMEM((seq_len, HD), F32), pltpu.VMEM((seq_len, HD), F32)],
        compiler_params=pltpu.CompilerParams(vmem_limit_bytes=32 << 20),
        cost_estimate=pl.CostEstimate(
            flops=8 * heads * HD * seq_len * seq_len,
            bytes_accessed=8 * seq_len * width,
            transcendentals=heads * seq_len * seq_len,
        ),
    )(length, qkv, grad, cosine, sine)


def padded(values, axis):
    size = values.shape[axis]
    more = -size % LANES
    if not more:
        return values
    return jnp.pad(values, [(0, more if i == axis else 0) for i in range(values.ndim)])


def packed(values, kind):
    tile = LANES * (16 if kind == BF else 8)
    values = values.astype(kind)
    return padded_to(values, -(-values.shape[-1] // tile) * tile)


def padded_to(values, size):
    more = size - values.shape[-1]
    return jnp.pad(values, [(0, 0)] * (values.ndim - 1) + [(0, more)])


def local(
    tokens,
    lengths,
    routes,
    norm1_gain,
    w_query,
    w_key,
    w_value,
    b_query,
    b_key,
    b_value,
    w_out,
    norm2_gain,
    router,
    shared_gate_vec,
    shared_gate,
    shared_up,
    shared_down,
    expert_gate,
    expert_up,
    expert_down,
    cotangent,
):
    ranks = lax.axis_size("tensor")
    groups = lax.axis_size("fsdp")
    rank = lax.axis_index("tensor")
    micros, _, rows, width = tokens.shape
    seq_len = rows * ranks
    heads = w_query.shape[1] // HD
    span = heads * HD
    experts = ranks * expert_gate.shape[0]
    shared_units = shared_gate.shape[1]
    expert_units = expert_gate.shape[2]
    cut = expert_units // (2 * LANES) * LANES
    own_first = rank * rows
    local_pos = own_first + jnp.arange(rows, dtype=jnp.int32)

    per_device = norm1_gain.shape[0]
    small = jnp.concatenate(
        [
            norm1_gain,
            norm2_gain,
            shared_gate_vec,
            router.reshape(-1),
            b_query.reshape(-1),
            b_key.reshape(-1),
            b_value.reshape(-1),
        ]
    )
    small_all = spread(groups, ranks, 1, packed(small, BF).reshape(1, -1, LANES), False)
    small_all = small_all.reshape(groups * ranks, -1)
    gain_one = small_all[:, :per_device].reshape(-1).astype(F32)
    gain_two = small_all[:, per_device : 2 * per_device].reshape(-1).astype(F32)
    gate_vec = small_all[:, 2 * per_device : 3 * per_device].reshape(-1)
    bias_at = per_device * (3 + experts)
    router_full = small_all[:, 3 * per_device : bias_at].reshape(width, experts)
    router_wide = jnp.concatenate([router_full, gate_vec[:, None]], axis=1)
    own_bias = lax.dynamic_index_in_dim(
        small_all.reshape(groups, ranks, -1), rank, 1, False
    )[:, bias_at : small.shape[0]].reshape(groups, 3, heads, HD // groups)
    bias = own_bias.transpose(1, 2, 0, 3).reshape(1, 3 * span).astype(F32)

    attn_w = lax.all_gather(
        jnp.concatenate([w_query, w_key, w_value, w_out.T], axis=1), "fsdp", axis=0, tiled=True
    )
    qkv_w, out_w = attn_w[:, : 3 * span], attn_w[:, 3 * span :]
    ranges = [
        (shared_gate, shared_up, shared_down),
        (expert_gate[0, :, :cut], expert_up[0, :, :cut], expert_down[0, :cut]),
        (expert_gate[0, :, cut:], expert_up[0, :, cut:], expert_down[0, cut:]),
    ]
    weights = [
        lax.all_gather(
            jnp.stack([padded(gate, 1), padded(up, 1), padded(down.T, 1)]), "fsdp", axis=0
        )
        for gate, up, down in ranges
    ]

    cosine, sine = rope_tables(seq_len)
    idle = Transfers(ranks, 0)
    token_own = [tokens[m, 0] for m in range(micros)]
    grads_own = []
    for m in range(micros):
        inside = (local_pos < lengths[m, 0])[:, None]
        grads_own.append(jnp.where(inside, cotangent[m, 0], jnp.zeros((), BF)))

    def attention(m, token_rows):
        normed = (normalize(token_rows.astype(F32))[0] * gain_one).astype(BF)
        pre = dot(normed, qkv_w, (1,), (0,))
        qkv, mixed = attend(lengths[m], pre, bias, cosine, sine)
        return normed, qkv, mixed, dot(mixed, out_w, (1,), (1,)).astype(BF)

    def second_norm(m, attended):
        hidden = token_own[m].astype(F32) + attended
        unit, inverse = normalize(hidden)
        return hidden, unit, inverse, (unit * gain_two).astype(BF)

    def routing(m, rows_two):
        logits = dot(rows_two, router_wide, (1,), (0,))
        probs = jax.nn.softmax(logits[:, :experts], axis=-1)
        shared_scale = jax.nn.sigmoid(logits[:, experts:])
        chosen = jnp.any(routes[m, 0] == rank, axis=1, keepdims=True)
        own_expert = (jnp.arange(experts, dtype=jnp.int32) == rank)[None, :]
        prob = jnp.sum(jnp.where(own_expert, probs, 0.0), axis=1, keepdims=True)
        return probs, shared_scale, chosen, own_expert, prob, jnp.where(chosen, prob, 0.0)

    def routing_back(route, dots):
        probs, shared_scale, chosen, own_expert, prob, _ = route
        expert_grad = jnp.where(chosen, dots[1] + dots[2], 0.0)
        grad_logits = probs * (jnp.where(own_expert, expert_grad, 0.0) - expert_grad * prob)
        grad_gate_logit = dots[0] * shared_scale * (1.0 - shared_scale)
        return jnp.concatenate([grad_logits, grad_gate_logit], axis=1).astype(BF)

    def second_norm_back(m, state, summed):
        grad_hidden, gain_part = norm_back(summed, state[1], state[2], gain_two)
        grad_hidden = grad_hidden + grads_own[m].astype(F32)
        return grad_hidden, grad_hidden.astype(BF), gain_part

    def attention_back(m, state, rows_grad):
        grad_mixed = dot(rows_grad, out_w, (1,), (0,)).astype(BF)
        grad_qkv, sums = attend_back(lengths[m], state[1], grad_mixed, cosine, sine)
        return grad_qkv, sums, dot(grad_qkv, qkv_w, (1,), (1,)).astype(BF)

    def first_norm_back(m, grad_hidden, summed):
        unit, inverse = normalize(token_own[m].astype(F32))
        grad_inputs, gain_part = norm_back(summed, unit, inverse, gain_one)
        return (grad_inputs + grad_hidden).astype(BF), gain_part

    def finished(m, hidden, moved):
        inside = (local_pos < lengths[m, 0]).astype(F32)[:, None]
        return (inside * (hidden + moved)).astype(BF)

    start = after(token_own[0], small_all)
    rows_a, grad_a = exchange(ranks, 2, [start, grads_own[0]])
    att_a = attention(0, rows_a)
    rows_b, sum_a = exchange(ranks, 3, [token_own[1]], [att_a[3]])
    att_b = attention(1, rows_b)
    norm_a = second_norm(0, sum_a)
    two_a, sum_b = exchange(ranks, 4, [norm_a[3]], [att_b[3]])
    norm_b = second_norm(1, sum_b)
    route_a = routing(0, two_a)

    def scale_of(route, which):
        return route[1] if which == 0 else route[5]

    act = {}
    dots_a, dots_b = [], []
    act[0, 0], acc_a, dots, (two_b,) = ffn(
        two_a, grad_a, scale_of(route_a, 0), weights[0], None, Transfers(ranks, 5, [norm_b[3]]), (0, 2, 3)
    )
    dots_a.append(dots)
    act[1, 0], acc_a, dots, (grad_b,) = ffn(
        two_a, grad_a, scale_of(route_a, 1), weights[1], acc_a, Transfers(ranks, 6, [grads_own[1]]), (0, 2, 3)
    )
    dots_a.append(dots)
    route_b = routing(1, two_b)
    acc_b = None
    for which in range(2):
        act[which, 1], acc_b, dots, _ = ffn(
            two_b, grad_b, scale_of(route_b, which), weights[which], acc_b, idle
        )
        dots_b.append(dots)

    def grads_of(which, transfers, at=()):
        per_micro = []
        for rows_two, grads, key in ((two_a, grad_a, 0), (two_b, grad_b, 1)):
            scaled, gate, up = act[which, key]
            per_micro.append((rows_two, grads, gate, up, scaled))
        return ffn_grads(groups, per_micro, transfers, at)

    def over_groups(grads):
        flat = grads.reshape(-1, grads.shape[-1])
        summed = lax.psum_scatter(flat, "fsdp", scatter_dimension=0, tiled=True)
        return with_layout_constraint(summed, Layout((0, 1))).reshape(grads.shape[1:])

    grads_0, _ = grads_of(0, idle)
    range_0 = over_groups(grads_0)
    scale_a = after(scale_of(route_a, 2), grads_0)
    act[2, 0], acc_a, dots, _ = ffn(two_a, grad_a, scale_a, weights[2], acc_a, idle)
    dots_a.append(dots)
    wide_a = routing_back(route_a, dots_a)
    back_a = (acc_a[1].astype(F32) + dot(wide_a, router_wide, (1,), (1,))).astype(BF)
    grads_1, (down_a,) = grads_of(1, Transfers(ranks, 7, [], [back_a]), (0, 2))
    range_1 = over_groups(grads_1)
    hid_a, send_a, gain_part_a = second_norm_back(0, norm_a, down_a)
    act[2, 1], acc_b, dots, (datt_a,) = ffn(
        two_b, grad_b, scale_of(route_b, 2), weights[2], acc_b, Transfers(ranks, 8, [send_a]), (0, 2, 3)
    )
    dots_b.append(dots)
    wide_b = routing_back(route_b, dots_b)
    back_b = (acc_b[1].astype(F32) + dot(wide_b, router_wide, (1,), (1,))).astype(BF)
    grad_qkv_a, sums_a, first_a = attention_back(0, att_a, datt_a)
    grads_2, (down_b, one_a) = grads_of(
        2, Transfers(ranks, 9, [], [back_b, first_a], [range_0]), (0, 2)
    )
    range_2 = over_groups(grads_2)
    hid_b, send_b, gain_part_b = second_norm_back(1, norm_b, down_b)
    datt_b, moved_a = exchange(ranks, 10, [send_b], [acc_a[0]], [range_1])
    grad_qkv_b, sums_b, first_b = attention_back(1, att_b, datt_b)
    one_b, moved_b = exchange(ranks, 11, [], [first_b, acc_b[0]], [range_2])

    def over_micros(left_a, right_a, left_b, right_b):
        return (dot(left_a, right_a, (0,), (0,)) + dot(left_b, right_b, (0,), (0,))).astype(BF)

    attn_g = jnp.concatenate(
        [
            over_micros(att_a[0], grad_qkv_a, att_b[0], grad_qkv_b),
            over_micros(datt_a, att_a[2], datt_b, att_b[2]),
        ],
        axis=1,
    )
    attn_g = lax.psum_scatter(attn_g, "fsdp", scatter_dimension=0, tiled=True).astype(F32)

    grad_in_a, one_part_a = first_norm_back(0, hid_a, one_a)
    grad_in_b, one_part_b = first_norm_back(1, hid_b, one_b)

    devices = groups * ranks
    total_wide = dot(two_a, wide_a, (0,), (0,)) + dot(two_b, wide_b, (0,), (0,))
    bias_part = (sums_a + sums_b).reshape(3, heads, groups, HD // groups).transpose(2, 0, 1, 3)
    bias_part = bias_part.reshape(groups, 1, -1)
    own_rank = (jnp.arange(ranks, dtype=jnp.int32) == rank).astype(F32)[None, :, None]
    parts = jnp.concatenate(
        [
            (one_part_a + one_part_b).reshape(devices, -1),
            (gain_part_a + gain_part_b).reshape(devices, -1),
            total_wide.reshape(devices, -1),
            (bias_part * own_rank).reshape(devices, -1),
        ],
        axis=1,
    )
    shares = spread(groups, ranks, 12, packed(parts, F32).reshape(devices, -1, LANES), True)
    shares = shares.reshape(-1)
    wide_g = shares[2 * per_device : (3 + experts) * per_device].reshape(per_device, experts + 1)
    bias_g = shares[bias_at : parts.shape[1]].reshape(3, heads, HD // groups)

    def plain(which):
        return [which[i].astype(F32) for i in range(3)]

    shared_g, low_g, high_g = plain(range_0), plain(range_1), plain(range_2)
    return (
        jnp.stack([finished(0, norm_a[0], moved_a), finished(1, norm_b[0], moved_b)])[:, None],
        jnp.stack([grad_in_a, grad_in_b])[:, None],
        shares[:per_device],
        attn_g[:, :span],
        attn_g[:, span : 2 * span],
        attn_g[:, 2 * span : 3 * span],
        bias_g[0],
        bias_g[1],
        bias_g[2],
        attn_g[:, 3 * span :].T,
        shares[per_device : 2 * per_device],
        wide_g[:, :experts],
        wide_g[:, experts],
        shared_g[0][:, :shared_units],
        shared_g[1][:, :shared_units],
        shared_g[2][:, :shared_units].T,
        jnp.concatenate([low_g[0], high_g[0]], axis=1)[None],
        jnp.concatenate([low_g[1], high_g[1]], axis=1)[None],
        jnp.concatenate([low_g[2].T, high_g[2].T], axis=0)[None],
    )


def solution(mesh):
    in_specs = (
        P(None, "fsdp", "tensor", None),
        P(None, "fsdp"),
        P(None, "fsdp", None, None),
        P(("fsdp", "tensor")),
        P("fsdp", "tensor"),
        P("fsdp", "tensor"),
        P("fsdp", "tensor"),
        P("tensor", "fsdp"),
        P("tensor", "fsdp"),
        P("tensor", "fsdp"),
        P("tensor", "fsdp"),
        P(("fsdp", "tensor")),
        P(("fsdp", "tensor"), None),
        P(("fsdp", "tensor")),
        P("fsdp", "tensor"),
        P("fsdp", "tensor"),
        P("tensor", "fsdp"),
        P("tensor", "fsdp", None),
        P("tensor", "fsdp", None),
        P("tensor", None, "fsdp"),
        P(None, "fsdp", "tensor", None),
    )
    out_specs = (
        P(None, "fsdp", "tensor", None),
        P(None, "fsdp", "tensor", None),
        P(("fsdp", "tensor")),
        P("fsdp", "tensor"),
        P("fsdp", "tensor"),
        P("fsdp", "tensor"),
        P("tensor", "fsdp"),
        P("tensor", "fsdp"),
        P("tensor", "fsdp"),
        P("tensor", "fsdp"),
        P(("fsdp", "tensor")),
        P(("fsdp", "tensor"), None),
        P(("fsdp", "tensor")),
        P("fsdp", "tensor"),
        P("fsdp", "tensor"),
        P("tensor", "fsdp"),
        P("tensor", "fsdp", None),
        P("tensor", "fsdp", None),
        P("tensor", None, "fsdp"),
    )
    return jax.shard_map(local, mesh=mesh, in_specs=in_specs, out_specs=out_specs, check_vma=False)
```

time: 1260 us -> 1090 us (0.87)
  Pallas kernels: 27.3 us -> 747 us
  waiting for transfers between devices: 396 us -> 118 us
  matrix products: 311 us -> 76.6 us
  starting transfers between devices: 218 us -> 0.58 us
  blocking collectives: 85.5 us -> 0 us
  other arithmetic: 131 us -> 66.9 us
  local copies, waits for them, and re-layouts: 71 us -> 55.8 us
    pallas_call x0 -> x16, Pallas kernels: none -> 721 us  [the longest x5 301 us: exchange(): pl.pallas_call(functools.partial(exchange_kernel, transfers), out_shape=t...]
    ppermute x144 -> x0, waiting for transfers between devices: 346 us -> none  [the longest x24 200 us: gather_rows(): lax.ppermute(downward, 'tensor', line_pairs(-1, range(1, chips - step + 1)))]
    dot_general x30 -> x18, matrix products: 311 us -> 76.6 us  [dot(): lax.dot_general(left, right, ((left_dims, right_dims), ((), ())), preferr...]
    ppermute x144 -> x0, starting transfers between devices: 217 us -> none  [the longest x24 95.6 us: scatter_rows(): upward = lax.ppermute(upward, 'tensor', line_pairs(1, range(0, step)))]
    convert_element_type x36 -> x7, other arithmetic: 88.1 us -> 9.82 us  [the longest x2 5.83 us: second_norm_back(): return (grad_hidden, grad_hidden.astype(BF), gain_part)]
    reduce_scatter x5 -> x4, waiting for transfers between devices: 49.1 us -> 117 us  [the longest x3 92.9 us: over_groups(): summed = lax.psum_scatter(flat, 'fsdp', scatter_dimension=0, tiled=True)]
    all_gather x1 -> x0, blocking collectives: 44.1 us -> none  [local(): small_all = lax.all_gather(small, ('fsdp', 'tensor'), axis=0, tiled=False)]
    psum x1 -> x0, blocking collectives: 41.4 us -> none  [local(): late = lax.psum(late, ('fsdp', 'tensor'))]
  transfers between devices with their start and end apart: 155 -> 8, of which waited for: 51 -> 2; matrix products, arithmetic and copies ran while one was open for 30% -> 14% of each run, Pallas kernels for 2% -> 56%
where the time goes in v2:
time: 1090 us; the launch traced here: 1080 us
  Pallas kernels  747 us (69%)
  waiting for transfers between devices  118 us (11%)
  matrix products  76.6 us (7%)
  other arithmetic  66.9 us (6%)
  local copies, waits for them, and re-layouts  55.8 us (5%)
  between operations  15.8 us (1%)
    pallas_call x5, Pallas kernels, exchange(): pl.pallas_call(functools.partial(exchange_kernel, transfers), out_shape=t...  301 us
    pallas_call x6, Pallas kernels, ffn(): pl.pallas_call(functools.partial(ffn_kernel, transfers, at, steps, first)...  227 us
    pallas_call x3, Pallas kernels, ffn_grads(): pl.pallas_call(functools.partial(ffn_grads_kernel, transfers, at, groups,...  167 us
    reduce_scatter x3, waiting for transfers between devices, over_groups(): summed = lax.psum_scatter(flat, 'fsdp', scatter_dimension=0, tiled=True)  92.9 us
    dot_general x18, matrix products, dot(): lax.dot_general(left, right, ((left_dims, right_dims), ((), ())), preferr...  76.6 us
    unnamed x164, local copies, waits for them, and re-layouts  27.9 us
    pallas_call x2, Pallas kernels, spread(): pl.pallas_call(functools.partial(spread_kernel, groups, ranks, reduces),...  25.9 us
    reduce_scatter x1, waiting for transfers between devices, local(): lax.psum_scatter(attn_g, 'fsdp', scatter_dimension=0, tiled=True)  24.1 us
  transfers between devices with their start and end apart: 8, of which 2 were waited for; matrix products, arithmetic and copies ran while one was open for 14% of the time, Pallas kernels for 56%

profile of v2, /device:TPU:0, one launch (start us, length us, event | category | flops | bytes accessed | tf_op | source)
XLA Modules:
  0.0 1080.4 jit_solution(456797293878809070)
XLA Ops:
  23.1 13.1 %shard_map.348 = bf16[32,16,128]{2,1,0:T(8,128)(2,1)} custom-call(bf16[1,16,128]{2,1,0:T(8,128)(2,1)} %pad_bitcast_fusion.3.value_ref), custom_call_target="tpu_custom_call" | custom-call | tf_op jit(solution)/shard_map/pallas_call | solution.py:467
  47.5 73.3 %shard_map.349 = (bf16[1024,2048]{1,0:T(8,128)(2,1)}, bf16[1024,2048]{1,0:T(8,128)(2,1)}) custom-call(bf16[128,2048]{1,0:T(8,128)(2,1)} %get-tuple-element.83.refs_0_, bf16[128,2048]{1,0:T(8,128)(2,1)} %get-tuple-element.289.refs_1_), custom_call_target="tpu_custom_call" | custom-call | tf_op jit(solution)/shard_map/pallas_call | solution.py:384
  120.8 3.1 fusion
  124.3 6.4 fusion.11.pre_ref
  130.7 5.1 shard_map.350
  136.7 4.4 convolution_convert_fusion.1.refs_1_
  141.1 50.6 %shard_map.351 = (bf16[1024,2048]{1,0:T(8,128)(2,1)}, f32[128,2048]{1,0:T(8,128)}) custom-call(bf16[128,2048]{1,0:T(8,128)(2,1)} %get-tuple-element.291.refs_0_, bf16[1024,2048]{1,0:T(8,128)(2,1)} %convolution_convert_fusion.1.refs_1_), custom_call_target="tpu_custom_call" | custom-call | tf_op jit(solution)/shard_map/pallas_call | solution.py:384
  191.7 3.2 fusion.3
  195.1 5.4 fusion.9.pre_ref
  200.5 5.3 shard_map.352
  206.7 5.2 convolution_convert_fusion.refs_1_
  212.8 51.3 %shard_map.353 = (bf16[1024,2048]{1,0:T(8,128)(2,1)}, f32[128,2048]{1,0:T(8,128)}) custom-call(bf16[128,2048]{1,0:T(8,128)(2,1)} %multiply_convert_fusion.3.refs_0_, bf16[1024,2048]{1,0:T(8,128)(2,1)} %convolution_convert_fusion.refs_1_), custom_call_target="tpu_custom_call" | custom-call | tf_op jit(solution)/shard_map/pallas_call | solution.py:384
  264.2 4.0 fusion.56
  272.3 46.7 %shard_map.354 = (bf16[1024,768]{1,0:T(8,128)(2,1)}, bf16[1024,768]{1,0:T(8,128)(2,1)}, bf16[1024,768]{1,0:T(8,128)(2,1)}, bf16[1024,2048]{1,0:T(8,128)(2,1)}, b...) custom-call(bf16[1024,2048]{1,0:T(8,128)(2,1)} %get-tuple-element.90.refs_0_, ...), custom_call_target="tpu_custom_call" | custom-call | flops 19327352832 | bytes 30932992 | tf_op jit(solution)/shard_map/pallas_call | solution.py:540
  319.0 3.4 fusion.55
  326.8 46.3 %shard_map.355 = (bf16[1024,640]{1,0:T(8,128)(2,1)}, bf16[1024,640]{1,0:T(8,128)(2,1)}, bf16[1024,640]{1,0:T(8,128)(2,1)}, bf16[1024,2048]{1,0:T(8,128)(2,1)}, b...) custom-call(bf16[1024,2048]{1,0:T(8,128)(2,1)} %get-tuple-element.90.refs_0_, ...), custom_call_target="tpu_custom_call" | custom-call | flops 16106127360 | bytes 28573696 | tf_op jit(solution)/shard_map/pallas_call | solution.py:540
  373.1 27.1 %shard_map.356 = (bf16[1024,768]{1,0:T(8,128)(2,1)}, bf16[1024,768]{1,0:T(8,128)(2,1)}, bf16[1024,768]{1,0:T(8,128)(2,1)}, bf16[1024,2048]{1,0:T(8,128)(2,1)}, b...) custom-call(bf16[1024,2048]{1,0:T(8,128)(2,1)} %get-tuple-element.95.refs_0_.refs_5_, ...), custom_call_target="tpu_custom_call" | custom-call | flops 19327352832 | bytes 30932992 | tf_op jit(solution)/shard_map/pallas_call | solution.py:540
  400.2 27.1 %shard_map.357 = bf16[4,3,512,768]{3,2,1,0:T(8,128)(2,1)} custom-call(bf16[1024,2048]{1,0:T(8,128)(2,1)} %get-tuple-element.90.refs_0_, bf16[1024,2048]{1,0:T(8,128)(2,1)} %get-tuple-element.91.refs_1_, bf16[1024,768]{1,0:T(8,128)(2,1)} %get-tuple-element.92.refs_2_, bf16[1024,768]{1,0:T(8,128)(2,1)} %get-tuple-element.93.refs_3_, ...), custom_call_target="tpu_custom_call" | custom-call | flops 19327352832 | bytes 35651584 | tf_op jit(solution)/shard_map/pallas_call | solution.py:592
  432.6 29.9 %shard_map.358 = (bf16[1024,768]{1,0:T(8,128)(2,1)}, bf16[1024,768]{1,0:T(8,128)(2,1)}, bf16[1024,768]{1,0:T(8,128)(2,1)}, bf16[1024,2048]{1,0:T(8,128)(2,1)}, b...) custom-call(bf16[1024,2048]{1,0:T(8,128)(2,1)} %get-tuple-element.90.refs_0_, bf16[1024,2048]{1,0:T(8,128)(2,1)} %get-tuple-element.91.refs_1_, ...), custom_call_target="tpu_custom_call" | custom-call | flops 19327352832 | bytes 30932992 | tf_op jit(solution)/shard_map/pallas_call | solution.py:540
  465.5 5.7 add_convert_fusion.1.refs_10_
  471.2 28.1 %shard_map.359 = (bf16[1024,640]{1,0:T(8,128)(2,1)}, bf16[1024,640]{1,0:T(8,128)(2,1)}, bf16[1024,640]{1,0:T(8,128)(2,1)}, bf16[1024,2048]{1,0:T(8,128)(2,1)}, b...) custom-call(bf16[1024,2048]{1,0:T(8,128)(2,1)} %get-tuple-element.95.refs_0_.refs_5_, ...), custom_call_target="tpu_custom_call" | custom-call | flops 16106127360 | bytes 28573696 | tf_op jit(solution)/shard_map/pallas_call | solution.py:540
  499.3 52.8 %shard_map.360 = (bf16[4,3,512,640]{3,2,1,0:T(8,128)(2,1)}, f32[128,2048]{1,0:T(8,128)}) custom-call(bf16[1024,2048]{1,0:T(8,128)(2,1)} %get-tuple-element.90.refs_0_, bf16[1024,2048]{1,0:T(8,128)(2,1)} %get-tuple-element.91.refs_1_, bf16[1024,640]{1,0:T(8,128)(2,1)} %get-tuple-element.112.refs_2_, bf16[1024,640]{1,0:T(8,128)(2,1)} %get-tuple-element.113.refs_3_, ...), custom_call_target="tpu_custom_call" | custom-call | flops 16106127360 | bytes 32505856 | tf_op jit(solution)/shard_map/pallas_call | solution.py:592
  558.9 3.1 fusion.73.refs_6_
  562.0 48.6 %shard_map.361 = (bf16[1024,768]{1,0:T(8,128)(2,1)}, bf16[1024,768]{1,0:T(8,128)(2,1)}, bf16[1024,768]{1,0:T(8,128)(2,1)}, bf16[1024,2048]{1,0:T(8,128)(2,1)}, b...) custom-call(bf16[1024,2048]{1,0:T(8,128)(2,1)} %get-tuple-element.95.refs_0_.refs_5_, ...), custom_call_target="tpu_custom_call" | custom-call | flops 19327352832 | bytes 30932992 | tf_op jit(solution)/shard_map/pallas_call | solution.py:540
  612.2 4.0 convolution_convert_fusion.5.grad_ref
  616.3 7.9 shard_map.362
  626.9 3.3 add_convert_fusion.refs_10_
  630.2 5.0 convolution_convert_fusion.3.refs_11_
  635.2 5.8 fusion.24
  641.0 87.1 %shard_map.363 = (bf16[4,3,512,768]{3,2,1,0:T(8,128)(2,1)}, f32[128,2048]{1,0:T(8,128)}, f32[128,2048]{1,0:T(8,128)}) custom-call(bf16[1024,2048]{1,0:T(8,128)(2,1)} %get-tuple-element.90.refs_0_, bf16[1024,2048]{1,0:T(8,128)(2,1)} %get-tuple-element.91.refs_1_, bf16[1024,768]{1,0:T(8,128)(2,1)} %get-tuple-element.105.refs_2_, ...), custom_call_target="tpu_custom_call" | custom-call | flops 19327352832 | bytes 35651584 | tf_op jit(solution)/shard_map/pallas_call | solution.py:592
  730.0 2.7 fusion.74.refs_0_
  732.7 52.9 %shard_map.364 = (bf16[1024,2048]{1,0:T(8,128)(2,1)}, f32[128,2048]{1,0:T(8,128)}) custom-call(bf16[128,2048]{1,0:T(8,128)(2,1)} %fusion.74.refs_0_, bf16[1024,2048]{1,0:T(8,128)(2,1)} %get-tuple-element.134.refs_1_, bf16[3,512,640]{2,1,0:T(8,128)(2,1)} %bitcast.142), custom_call_target="tpu_custom_call" | custom-call | tf_op jit(solution)/shard_map/pallas_call | solution.py:384
  785.6 4.3 fusion.6
  789.9 2.7 convolution_convert_fusion.4.grad_ref
  792.6 7.9 shard_map.365
  801.7 4.1 add_convert_fusion.2
  809.4 3.0 fusion.57
  821.2 3.2 copy.225
  824.4 3.2 copy.224
  827.6 3.1 copy.223
  831.1 6.8 convolution_convert_fusion.2.refs_0_
  837.9 24.1 %reduce-scatter.11.cloned.1.call-done = bf16[512,1024]{0,1:T(8,128)(2,1)} async-done(((bf16[2048,1024]{0,1:T(8,128)(2,1)}), bf16[512,1024]{0,1:T(8,128)(2,1)}) %reduce-scatter.11.cloned.1.call-update) | async-done | bytes 1048592 | tf_op jit(solution)/shard_map/reduce_scatter | solution.py:984
  867.5 92.9 %reduce-scatter.9.cloned.1.call-done = bf16[1536,768]{1,0:T(8,128)(2,1)} async-done(((bf16[6144,768]{1,0:T(8,128)(2,1)}), bf16[1536,768]{1,0:T(8,128)(2,1)}) %reduce-scatter.9.cloned.1.call-update) | async-done | bytes 2359312 | tf_op jit(solution)/shard_map/reduce_scatter | solution.py:945
  960.4 73.4 %shard_map.366 = (f32[128,2048]{1,0:T(8,128)}, f32[128,2048]{1,0:T(8,128)}) custom-call(bf16[1024,2048]{1,0:T(8,128)(2,1)} %convolution_convert_fusion.2.refs_0_, bf16[1024,2048]{1,0:T(8,128)(2,1)} %get-tuple-element.140.refs_1_, bf16[3,512,768]{2,1,0:T(8,128)(2,1)} %bitcast.140), custom_call_target="tpu_custom_call" | custom-call | tf_op jit(solution)/shard_map/pallas_call | solution.py:384
  1036.6 12.8 %shard_map.367 = f32[8,128]{1,0:T(8,128)} custom-call(f32[32,8,128]{2,1,0:T(8,128)} %bitcast.148), custom_call_target="tpu_custom_call" | custom-call | tf_op jit(solution)/shard_map/pallas_call | solution.py:467
  1054.2 2.9 slice_bitcast_fusion
  1057.1 3.0 fusion.21
  1060.1 3.4 copy.226
  (306 shorter events, 96.2 us)
Async XLA Ops:
  7.2 5.6 copy-start.42
  7.2 5.9 copy-start.43
  7.2 6.1 copy-start.44
  7.2 117.1 %all-gather.8.cloned.1.call-start = ((), (), s32[]{:S(2)}) async-start(), calls=%async_computation.4 | async-start | bytes 5242880 | tf_op jit(solution)/shard_map/all_gather | solution.py:835
  12.7 259.6 %all-gather.10.cloned.1.call-start = ((), (), s32[]{:S(2)}) async-start(), calls=%async_computation.9 | async-start | bytes 11796480 | tf_op jit(solution)/shard_map/all_gather | solution.py:845
  15.6 311.3 %all-gather.12.cloned.1.call-start = ((), (), s32[]{:S(2)}) async-start(), calls=%async_computation.10 | async-start | bytes 9830400 | tf_op jit(solution)/shard_map/all_gather | solution.py:845
  18.6 414.0 %all-gather.14.cloned.1.call-start = ((), (), s32[]{:S(2)}) async-start(), calls=%async_computation.11 | async-start | bytes 11796480 | tf_op jit(solution)/shard_map/all_gather | solution.py:845
  20.0 18.3 %copy-start.58 = (s32[2,1]{0,1:T(1,128)S(1)}, s32[2,1]{0,1:T(1,128)}, u32[]{:S(2)}) copy-start(s32[2,1]{0,1:T(1,128)} %param.22) | copy-start | bytes 28
  20.0 18.9 %copy-start.48 = (s32[2,1,1024,4]{2,3,1,0:T(4,128)S(1)}, s32[2,1,1024,4]{2,3,1,0:T(4,128)}, u32[]{:S(2)}) copy-start(s32[2,1,1024,4]{2,3,1,0:T(4,128)} %param.23) | copy-start | bytes 98308
  20.2 20.2 %copy-start.13 = (bf16[2,1,128,2048]{3,2,1,0:T(8,128)(2,1)S(1)}, bf16[2,1,128,2048]{3,2,1,0:T(8,128)(2,1)}, u32[]{:S(2)}) copy-start(bf16[2,1,128,2048]{3,2,1,0:T(8,128)(2,1)} %param.21) | copy-start | bytes 3145732
  21.8 619.1 %reduce-scatter.5.cloned.1.call-start = ((), (), s32[]{:S(2)}) async-start(), calls=%async_computation.5 | async-start | bytes 11796480 | tf_op jit(solution)/shard_map/reduce_scatter | solution.py:945
  39.2 155.7 %copy-start.46 = (f32[2048]{0:T(1024)}, f32[2048]{0:T(1024)S(1)}, u32[]{:S(2)}) copy-start(f32[2048]{0:T(1024)S(1)} %reshape.317) | copy-start | bytes 24580
  123.9 6.8 copy-start.53
  135.9 5.2 copy-start.4
  195.1 5.4 copy-start.51
  200.5 5.3 copy-start.14
  200.5 5.3 copy-start.39
  205.8 6.1 copy-start
  206.7 5.2 copy-start.9
  268.4 50.6 %copy-start.26 = (f32[1024,1]{1,0:T(8,128)}, f32[1024,1]{1,0:T(8,128)S(1)}, u32[]{:S(2)}) copy-start(f32[1024,1]{1,0:T(8,128)S(1)} %copy.228) | copy-start | bytes 12292
  270.2 48.8 %copy-start.49 = (f32[128]{0:T(128)}, f32[128]{0:T(128)S(1)}, u32[]{:S(2)}) copy-start(f32[128]{0:T(128)S(1)} %add_rsqrt_fusion.4) | copy-start | bytes 1540
  323.8 49.3 %copy-start.23 = (f32[1024,1]{1,0:T(8,128)}, f32[1024,1]{1,0:T(8,128)S(1)}, u32[]{:S(2)}) copy-start(f32[1024,1]{1,0:T(8,128)S(1)} %copy.230) | copy-start | bytes 12292
  427.4 305.3 %reduce-scatter.7.cloned.1.call-start = ((), (), s32[]{:S(2)}) async-start(), calls=%async_computation.6 | async-start | bytes 9830400 | tf_op jit(solution)/shard_map/reduce_scatter | solution.py:945
  427.6 36.8 %copy-start.24 = (f32[1024,1]{1,0:T(8,128)}, f32[1024,1]{1,0:T(8,128)S(1)}, u32[]{:S(2)}) copy-start(f32[1024,1]{1,0:T(8,128)S(1)} %copy.204) | copy-start | bytes 12292
  432.6 29.9 %copy-start.27 = (f32[1024,1]{1,0:T(8,128)S(1)}, f32[1024,1]{1,0:T(8,128)}, u32[]{:S(2)}) copy-start(f32[1024,1]{1,0:T(8,128)} %copy.191) | copy-start | bytes 12292
  552.1 6.8 copy-start.18
  552.1 309.9 %reduce-scatter.11.cloned.1.call-start = ((), (), s32[]{:S(2)}) async-start(), calls=%async_computation.8 | async-start | bytes 5242880 | tf_op jit(solution)/shard_map/reduce_scatter | solution.py:984
  562.0 48.6 %copy-start.25 = (f32[1024,1]{1,0:T(8,128)S(1)}, f32[1024,1]{1,0:T(8,128)}, u32[]{:S(2)}) copy-start(f32[1024,1]{1,0:T(8,128)} %copy-done.24) | copy-start | bytes 12292
  562.0 48.6 %copy-start.45 = (f32[1024,1]{1,0:T(8,128)S(1)}, f32[1024,1]{1,0:T(8,128)}, u32[]{:S(2)}) copy-start(f32[1024,1]{1,0:T(8,128)} %get-tuple-element.127) | copy-start | bytes 12292
  616.2 8.0 copy-start.3
  616.2 8.0 copy-start.68
  630.2 5.0 copy-start.30
  630.2 5.0 copy-start.47
  630.2 5.0 copy-start.54
  640.9 87.1 %copy-start.50 = (f32[128]{0:T(128)S(1)}, f32[128]{0:T(128)}, u32[]{:S(2)}) copy-start(f32[128]{0:T(128)} %copy-done.49) | copy-start | bytes 1540
  641.0 89.0 %copy-start.21 = (bf16[128,2048]{1,0:T(8,128)(2,1)S(1)}, bf16[128,2048]{1,0:T(8,128)(2,1)}, u32[]{:S(2)}) copy-start(bf16[128,2048]{1,0:T(8,128)(2,1)} %get-tuple-element.288.refs_6_) | copy-start | bytes 1572868
  730.0 55.6 %copy-start.1 = (bf16[1024,256]{1,0:T(8,128)(2,1)S(1)}, bf16[1024,256]{1,0:T(8,128)(2,1)}, u32[]{:S(2)}) copy-start(bf16[1024,256]{1,0:T(8,128)(2,1)} %copy-done) | copy-start | bytes 1572868
  785.6 16.1 %slice-start.6 = ((s8[6291456]{0:T(1024)(128)(4,1)}), s8[4194304]{0:T(1024)(128)(4,1)S(1)}, s32[]{:S(2)}) async-start(s8[6291456]{0:T(1024)(128)(4,1)} %bitcast.166), calls=%async_computation.18 | async-start | bytes 8388608
  789.9 11.8 %slice-start.7 = ((s8[6291456]{0:T(1024)(128)(4,1)}), s8[2097152]{0:T(1024)(128)(4,1)S(1)}, s32[]{:S(2)}) async-start(s8[6291456]{0:T(1024)(128)(4,1)} %bitcast.166), calls=%async_computation.19 | async-start | bytes 4194304
  792.6 9.1 copy-start.29
  792.6 9.1 copy-start.52
  808.4 152.0 %reduce-scatter.9.cloned.1.call-start = ((), (), s32[]{:S(2)}) async-start(), calls=%async_computation.7 | async-start | bytes 11796480 | tf_op jit(solution)/shard_map/reduce_scatter | solution.py:945
  821.2 9.8 copy-start.7
  960.4 73.4 %copy-start.15 = (bf16[2,1,128,2048]{3,2,1,0:T(8,128)(2,1)S(1)}, bf16[2,1,128,2048]{3,2,1,0:T(8,128)(2,1)}, u32[]{:S(2)}) copy-start(bf16[2,1,128,2048]{3,2,1,0:T(8,128)(2,1)} %param.21) | copy-start | bytes 3145732
  960.4 73.4 %copy-start.32 = (f32[128,2048]{1,0:T(8,128)S(1)}, f32[128,2048]{1,0:T(8,128)}, u32[]{:S(2)}) copy-start(f32[128,2048]{1,0:T(8,128)} %get-tuple-element.143) | copy-start | bytes 3145732
  1057.1 6.4 copy-start.10
  1057.1 6.4 copy-start.16
  1057.1 6.4 copy-start.56
  (37 other events, 92.4 us)
Sparse Core Ops, SparseCore 0:
  12.8 56.6 all-gather.7
  71.9 96.3 all-gather.9
  170.8 83.2 all-gather.11
  256.3 96.3 all-gather.13
  427.5 95.1 reduce-scatter.4
  552.2 84.6 reduce-scatter.6
  808.5 53.4 reduce-scatter.10
  865.4 94.9 reduce-scatter.8

commit v3 on v2

--- a/solution.py
+++ b/solution.py
@@ -54,29 +54,6 @@
     )
 
 
-class Place:
-    def __init__(self, ranks):
-        rank = lax.axis_index("tensor")
-        self.chips = ranks // 2
-        self.chip, self.core = rank // 2, rank % 2
-        self.partner = rank + 1 - 2 * self.core
-        self.above, self.below = rank + 2, rank - 2
-        self.not_top = self.chip < self.chips - 1
-        self.not_bottom = self.chip > 0
-
-    def meet(self):
-        barrier = pltpu.get_barrier_semaphore()
-
-        def greet(target):
-            pl.semaphore_signal(barrier, 1, device_id={"tensor": target}, device_id_type=MESH)
-
-        greet(self.partner)
-        pl.when(self.not_top)(lambda: greet(self.above))
-        pl.when(self.not_bottom)(lambda: greet(self.below))
-        peers = 1 + self.not_top.astype(jnp.int32) + self.not_bottom.astype(jnp.int32)
-        pl.semaphore_wait(barrier, peers)
-
-
 def gather_scratch(ranks):
     chips = ranks // 2
     pair = [pltpu.SemaphoreType.DMA((chips, CHUNKS))] * 2
@@ -310,29 +287,301 @@
                 downward(step, chip - (chips - step), chunk).wait_send()
 
 
-GATHER_REFS, SCATTER_REFS = 7, 12
+class Place:
+    def __init__(self, ranks, groups):
+        rank, group = lax.axis_index("tensor"), lax.axis_index("fsdp")
+        self.ranks, self.groups = ranks, groups
+        self.chips = ranks // 2
+        self.chip, self.core = rank // 2, rank % 2
+        self.partner = rank + 1 - 2 * self.core
+        self.above, self.below = rank + 2, rank - 2
+        self.not_top = self.chip < self.chips - 1
+        self.not_bottom = self.chip > 0
+        self.rank, self.group = rank, group
+        self.device = group * ranks + rank
+        near, far = group % 2, group // 2
+        self.beside = 2 * far + 1 - near
+        self.across = 2 * (1 - far) + near
+        self.opposite = 2 * (1 - far) + 1 - near
+        self.square = groups == 4
+
+    def name(self, device):
+        return {"fsdp": device // self.ranks, "tensor": device % self.ranks}
+
+    def meet(self, line, cross, everyone):
+        barrier = pltpu.get_barrier_semaphore()
+
+        def greet(name):
+            pl.semaphore_signal(barrier, 1, device_id=name, device_id_type=MESH)
+
+        if everyone:
+            devices = self.groups * self.ranks
+
+            def one(i, carry):
+                greet(self.name(lax.rem(self.device + i, devices)))
+                return carry
+
+            lax.fori_loop(1, devices, one, 0)
+            pl.semaphore_wait(barrier, devices - 1)
+            return
+        peers = 0
+        if line:
+            greet({"tensor": self.partner})
+            pl.when(self.not_top)(lambda: greet({"tensor": self.above}))
+            pl.when(self.not_bottom)(lambda: greet({"tensor": self.below}))
+            peers = 1 + self.not_top.astype(jnp.int32) + self.not_bottom.astype(jnp.int32)
+        if cross and self.square:
+            greet({"fsdp": self.beside})
+            greet({"fsdp": self.across})
+            peers = peers + 2
+        elif cross:
+            for i in range(1, self.groups):
+                greet({"fsdp": lax.rem(self.group + i, self.groups)})
+            peers = peers + self.groups - 1
+        pl.semaphore_wait(barrier, peers)
+
+
+def to_group(src, dst, send, recv, at, target):
+    return pltpu.make_async_remote_copy(
+        src_ref=src,
+        dst_ref=dst,
+        send_sem=send.at[at],
+        recv_sem=recv.at[at],
+        device_id={"fsdp": target},
+        device_id_type=MESH,
+    )
+
+
+def cross_gather_steps(place, block, whole, own_sem, send, recv):
+    group = place.group
+    half = block.shape[0] // 2
+
+    def own():
+        return pltpu.make_async_copy(block, whole.at[group], own_sem)
+
+    if not place.square:
+
+        def direct(i):
+            target = lax.rem(group + i, place.groups)
+            return to_group(block, whole.at[group], send, recv, i - 1, target)
+
+        own().start()
+        for i in range(1, place.groups):
+            direct(i).start()
+        yield
+        own().wait()
+        for i in range(1, place.groups):
+            source = lax.rem(group - i + place.groups, place.groups)
+            to_group(block, whole.at[source], send, recv, i - 1, source).wait_recv()
+            direct(i).wait_send()
+        return
+
+    def near(at):
+        return to_group(block, whole.at[group], send, recv, at, (place.beside, place.across)[at])
+
+    def came(at):
+        source = (place.beside, place.across)[at]
+        return to_group(whole.at[source], whole.at[source], send, recv, at, source)
+
+    def forward(at):
+        source, target = ((place.beside, place.across), (place.across, place.beside))[at]
+        piece = whole.at[source, pl.ds(at * half, half)]
+        return to_group(piece, piece, send, recv, 2 + at, target)
+
+    def far(at):
+        piece = whole.at[place.opposite, pl.ds(at * half, half)]
+        return to_group(piece, piece, send, recv, 2 + at, place.opposite)
+
+    for at in range(2):
+        near(at).start()
+    own().start()
+    yield
+    for at in range(2):
+        came(at).wait_recv()
+        forward(at).start()
+    yield
+    yield
+    own().wait()
+    for at in range(2):
+        far(at).wait_recv()
+        near(at).wait_send()
+        forward(at).wait_send()
+
+
+def cross_scatter_steps(place, partial, total, mine, near_in, far_in, own_sem, send, recv):
+    group = place.group
+    rows = total.shape[0]
+    half = rows // 2
+
+    def own():
+        return pltpu.make_async_copy(partial, mine, own_sem)
+
+    def loop(count, body):
+        def strip(i, carry):
+            body(pl.ds(i * STRIP, STRIP))
+            return carry
+
+        lax.fori_loop(0, count // STRIP, strip, 0)
+
+    if not place.square:
+
+        def direct(i):
+            target = lax.rem(group + i, place.groups)
+            return to_group(partial.at[target], near_in.at[group], send, recv, i - 1, target)
+
+        own().start()
+        for i in range(1, place.groups):
+            direct(i).start()
+        yield
+        own().wait()
+        for i in range(1, place.groups):
+            source = lax.rem(group - i + place.groups, place.groups)
+            to_group(partial.at[source], near_in.at[source], send, recv, i - 1, source).wait_recv()
+
+        def everything(cut):
+            value = mine[group, cut].astype(F32)
+            for i in range(1, place.groups):
+                value = value + near_in[lax.rem(group + i, place.groups), cut].astype(F32)
+            total[cut] = value
+
+        loop(rows, everything)
+        for i in range(1, place.groups):
+            direct(i).wait_send()
+        return
+
+    def first(at):
+        target = (place.beside, place.across)[at]
+        piece = partial.at[place.opposite, pl.ds(at * half, half)]
+        return to_group(piece, far_in.at[at], send, recv, at, target)
+
+    def second(at):
+        target = (place.beside, place.across)[at]
+        return to_group(mine.at[target], near_in.at[at], send, recv, 2 + at, target)
+
+    own().start()
+    for at in range(2):
+        first(at).start()
+    yield
+    own().wait()
+    for at in range(2):
+        target = (place.across, place.beside)[at]
+        first(at).wait_recv()
+
+        def join(cut, at=at, target=target):
+            place_in = pl.ds(at * half + cut.start, STRIP)
+            value = mine[target, place_in].astype(F32) + far_in[at, cut].astype(F32)
+            mine[target, place_in] = value.astype(BF)
+
+        loop(half, join)
+        second(1 - at).start()
+    yield
+    yield
+    for at in range(2):
+        second(at).wait_recv()
+
+    def everything(cut):
+        value = mine[group, cut].astype(F32) + near_in[0, cut].astype(F32)
+        total[cut] = value + near_in[1, cut].astype(F32)
+
+    loop(rows, everything)
+    for at in range(2):
+        first(at).wait_send()
+        second(at).wait_send()
+
+
+def spread_steps(place, value, everyone, own_sem, send, recv):
+    devices = place.groups * place.ranks
+    me = place.device
+
+    def copy(i):
+        target = lax.rem(me + i, devices)
+        return pltpu.make_async_remote_copy(
+            src_ref=value,
+            dst_ref=everyone.at[me],
+            send_sem=send.at[i],
+            recv_sem=recv.at[i],
+            device_id=place.name(target),
+            device_id_type=MESH,
+        )
+
+    def arrival(i):
+        source = lax.rem(me - i + devices, devices)
+        return pltpu.make_async_remote_copy(
+            src_ref=everyone.at[source],
+            dst_ref=everyone.at[source],
+            send_sem=send.at[i],
+            recv_sem=recv.at[i],
+            device_id=place.name(source),
+            device_id_type=MESH,
+        )
+
+    def start(i, carry):
+        copy(i).start()
+        return carry
+
+    def finish_one(i, carry):
+        arrival(i).wait_recv()
+        copy(i).wait_send()
+        return carry
+
+    def own():
+        return pltpu.make_async_copy(value, everyone.at[me], own_sem)
+
+    own().start()
+    lax.fori_loop(1, devices, start, 0)
+    yield
+    yield
+    yield
+    own().wait()
+    lax.fori_loop(1, devices, finish_one, 0)
+
+
+DMA = pltpu.SemaphoreType.DMA
 
 
 class Transfers:
-    def __init__(self, ranks, ident, blocks=(), partials=(), needed=()):
-        self.ranks, self.ident = ranks, ident
-        self.blocks, self.partials = list(blocks), list(partials)
-        self.inputs = self.blocks + self.partials + list(needed)
-        self.moves = len(self.blocks) + len(self.partials)
-        self.shapes, self.out_specs, self.scratch = [], [], []
+    def __init__(self, mesh_size, ident=0, moves=(), needed=()):
+        self.ranks, self.groups = mesh_size
+        self.ident = ident
+        self.kinds = [kind for kind, _ in moves]
+        self.inputs = [array for _, array in moves] + list(needed)
+        self.moves = len(self.kinds)
         anywhere = pl.BlockSpec(memory_space=pl.ANY)
+        vmem = pl.BlockSpec(memory_space=pltpu.VMEM)
         self.in_specs = [anywhere] * len(self.inputs)
-        for block in self.blocks:
-            self.shapes.append(
-                jax.ShapeDtypeStruct((ranks * block.shape[0], block.shape[1]), BF)
-            )
-            self.out_specs.append(anywhere)
-            self.scratch += gather_scratch(ranks)
-        for partial in self.partials:
-            rows, width = partial.shape[0] // ranks, partial.shape[1]
-            self.shapes.append(jax.ShapeDtypeStruct((rows, width), F32))
-            self.out_specs.append(pl.BlockSpec(memory_space=pltpu.VMEM))
-            self.scratch += scatter_scratch(ranks, rows, width)
+        self.shapes, self.out_specs, self.scratch, self.counts = [], [], [], []
+        for kind, array in moves:
+            shape, spec = array.shape, anywhere
+            if kind == "gather":
+                shape, dtype = (self.ranks * shape[0], shape[1]), BF
+                scratch = gather_scratch(self.ranks)
+            elif kind == "scatter":
+                shape, dtype, spec = (shape[0] // self.ranks, shape[1]), F32, vmem
+                scratch = scatter_scratch(self.ranks, *shape)
+            elif kind == "cross_gather":
+                shape, dtype = (self.groups,) + shape, BF
+                scratch = [DMA, DMA((max(4, self.groups),)), DMA((max(4, self.groups),))]
+            elif kind == "cross_scatter":
+                rest = shape[1:]
+                square = self.groups == 4
+                near = (2 if square else self.groups,) + rest
+                scratch = [
+                    pltpu.VMEM(shape, BF),
+                    pltpu.VMEM(near, BF),
+                    pltpu.VMEM((2, rest[0] // 2) + rest[1:], BF),
+                    DMA,
+                    DMA((max(4, self.groups),)),
+                    DMA((max(4, self.groups),)),
+                ]
+                shape, dtype, spec = rest, F32, vmem
+            else:
+                devices = self.ranks * self.groups
+                shape, dtype = (devices,) + shape, array.dtype
+                scratch = [DMA, DMA((devices,)), DMA((devices,))]
+            self.shapes.append(jax.ShapeDtypeStruct(shape, dtype))
+            self.out_specs.append(spec)
+            self.scratch += scratch
+            self.counts.append(len(scratch))
 
     def params(self):
         if not self.moves:
@@ -344,25 +593,39 @@
     def begin(self, inputs, outputs, scratch):
         if not self.moves:
             return lambda: False
-        place = Place(self.ranks)
+        steps_of = {
+            "gather": gather_steps,
+            "scatter": scatter_steps,
+            "cross_gather": cross_gather_steps,
+            "cross_scatter": cross_scatter_steps,
+            "spread": spread_steps,
+        }
+        place = Place(self.ranks, self.groups)
         scratch = list(scratch)
         running = []
-        for i in range(self.moves):
-            gathers = i < len(self.blocks)
-            count = GATHER_REFS if gathers else SCATTER_REFS
-            taken, scratch = scratch[:count], scratch[count:]
-            steps = gather_steps if gathers else scatter_steps
-            running.append(steps(place, inputs[i], outputs[i], *taken))
+        for i, kind in enumerate(self.kinds):
+            taken, scratch = scratch[: self.counts[i]], scratch[self.counts[i] :]
+            running.append((kind, steps_of[kind](place, inputs[i], outputs[i], *taken)))
         state = {"met": False, "running": running}
 
         def phase():
-            if not state["met"]:
-                place.meet()
+            first = not state["met"]
+            if first:
+                kinds = set(self.kinds)
+                place.meet(
+                    bool(kinds & {"gather", "scatter"}),
+                    bool(kinds & {"cross_gather", "cross_scatter"}),
+                    "spread" in kinds,
+                )
                 state["met"] = True
             still = []
-            for steps in state["running"]:
+            for kind, steps in state["running"]:
                 if next(steps, True) is None:
-                    still.append(steps)
+                    still.append((kind, steps))
+            if first:
+                for kind, steps in still:
+                    if kind == "scatter":
+                        next(steps)
             state["running"] = still
             return bool(still)
 
@@ -379,8 +642,8 @@
     finish(transfers.begin(refs[:moves], refs[count : count + moves], refs[count + moves :]))
 
 
-def exchange(ranks, ident, blocks=(), partials=(), needed=()):
-    transfers = Transfers(ranks, ident, blocks, partials, needed)
+def exchange(mesh_size, ident, moves, needed=()):
+    transfers = Transfers(mesh_size, ident, moves, needed)
     return pl.pallas_call(
         functools.partial(exchange_kernel, transfers),
         out_shape=tuple(transfers.shapes),
@@ -399,31 +662,20 @@
     pl.when(step == grid_steps - 1)(lambda: finish(phase))
 
 
-def spread_kernel(groups, ranks, reduces, value_ref, *refs):
-    out_ref, landing, send_sem, recv_sem, own_sem = refs[-5:]
-    devices = groups * ranks
-    me = lax.axis_index("fsdp") * ranks + lax.axis_index("tensor")
-    barrier = pltpu.get_barrier_semaphore()
-
-    def name(device):
-        return {"fsdp": device // ranks, "tensor": device % ranks}
-
-    def greet(i, carry):
-        target = lax.rem(me + i, devices)
-        pl.semaphore_signal(barrier, 1, device_id=name(target), device_id_type=MESH)
-        return carry
-
-    lax.fori_loop(1, devices, greet, 0)
-    pl.semaphore_wait(barrier, devices - 1)
+def share_kernel(mesh_size, value_ref, out_ref, landing, send, recv, own_sem):
+    ranks, groups = mesh_size
+    place = Place(ranks, groups)
+    place.meet(False, False, True)
+    devices, me = groups * ranks, place.device
 
     def copy(i):
         target = lax.rem(me + i, devices)
         return pltpu.make_async_remote_copy(
-            src_ref=value_ref.at[target] if reduces else value_ref.at[0],
+            src_ref=value_ref.at[target],
             dst_ref=landing.at[me],
-            send_sem=send_sem.at[i],
-            recv_sem=recv_sem.at[i],
-            device_id=name(target),
+            send_sem=send.at[i],
+            recv_sem=recv.at[i],
+            device_id=place.name(target),
             device_id_type=MESH,
         )
 
@@ -432,54 +684,94 @@
         return pltpu.make_async_remote_copy(
             src_ref=landing.at[source],
             dst_ref=landing.at[source],
-            send_sem=send_sem.at[i],
-            recv_sem=recv_sem.at[i],
-            device_id=name(source),
+            send_sem=send.at[i],
+            recv_sem=recv.at[i],
+            device_id=place.name(source),
             device_id_type=MESH,
         )
 
-    def send(i, carry):
+    def start(i, carry):
         copy(i).start()
         return carry
 
-    def receive(i, carry):
+    def finish_one(i, carry):
         arrival(i).wait_recv()
         copy(i).wait_send()
         return carry
 
-    own = pltpu.make_async_copy(
-        value_ref.at[me] if reduces else value_ref.at[0], landing.at[me], own_sem
-    )
+    own = pltpu.make_async_copy(value_ref.at[me], landing.at[me], own_sem)
     own.start()
-    lax.fori_loop(1, devices, send, 0)
-    lax.fori_loop(1, devices, receive, 0)
+    lax.fori_loop(1, devices, start, 0)
+    lax.fori_loop(1, devices, finish_one, 0)
     own.wait()
-    if reduces:
-        out_ref[...] = jnp.sum(landing[...], axis=0)
-    else:
-        out_ref[...] = landing[...]
-
-
-def spread(groups, ranks, ident, values, reduces, needed=()):
-    devices = groups * ranks
-    tail = values.shape[1:]
+    out_ref[...] = jnp.sum(landing[...], axis=0)
+
+
+def share(mesh_size, ident, values):
     vmem = pl.BlockSpec(memory_space=pltpu.VMEM)
+    devices = values.shape[0]
     return pl.pallas_call(
-        functools.partial(spread_kernel, groups, ranks, reduces),
-        out_shape=jax.ShapeDtypeStruct(tail if reduces else (devices,) + tail, values.dtype),
-        in_specs=[vmem] + [pl.BlockSpec(memory_space=pl.ANY)] * len(needed),
+        functools.partial(share_kernel, mesh_size),
+        out_shape=jax.ShapeDtypeStruct(values.shape[1:], values.dtype),
+        in_specs=[vmem],
         out_specs=vmem,
-        scratch_shapes=[
-            pltpu.VMEM((devices,) + tail, values.dtype),
-            pltpu.SemaphoreType.DMA((devices,)),
-            pltpu.SemaphoreType.DMA((devices,)),
-            pltpu.SemaphoreType.DMA,
+        scratch_shapes=[pltpu.VMEM(values.shape, values.dtype), DMA((devices,)), DMA((devices,)), DMA],
+        compiler_params=pltpu.CompilerParams(collective_id=ident, has_side_effects=True),
+    )(values)
+
+
+def column(values, at):
+    lanes = lax.broadcasted_iota(jnp.int32, values.shape, 1)
+    return jnp.sum(jnp.where(lanes == at, values, 0.0), axis=1, keepdims=True)
+
+
+def route_kernel(experts, rows_ref, router_ref, routes_ref, out_ref):
+    rank = lax.axis_index("tensor")
+    logits = dot(rows_ref[...], router_ref[...], (1,), (0,))
+    lanes = lax.broadcasted_iota(jnp.int32, logits.shape, 1)
+    inside = lanes < experts
+    top = jnp.max(jnp.where(inside, logits, -1e30), axis=1, keepdims=True)
+    exps = jnp.where(inside, jnp.exp(jnp.where(inside, logits, top) - top), 0.0)
+    probs = exps / jnp.sum(exps, axis=1, keepdims=True)
+    gate = jax.nn.sigmoid(column(logits, experts))
+    named = jnp.where(routes_ref[...] == rank, 1.0, 0.0)
+    chosen = jnp.max(named, axis=1, keepdims=True)
+    prob = column(probs, rank)
+    out = jnp.where(lanes == experts, gate, probs)
+    out = jnp.where(lanes == experts + 1, chosen * prob, out)
+    out = jnp.where(lanes == experts + 2, chosen, out)
+    out_ref[...] = jnp.where(lanes == experts + 3, prob, out)
+
+
+def routing(experts, rows, router, routes):
+    count, width = rows.shape
+    return pl.pallas_call(
+        functools.partial(route_kernel, experts),
+        grid=(count // ROW_BLOCK,),
+        in_specs=[
+            pl.BlockSpec((ROW_BLOCK, width), lambda i: (i, 0)),
+            pl.BlockSpec(router.shape, lambda i: (0, 0)),
+            pl.BlockSpec((ROW_BLOCK, routes.shape[1]), lambda i: (i, 0)),
         ],
-        compiler_params=pltpu.CompilerParams(collective_id=ident, has_side_effects=True),
-    )(values, *needed)
-
-
-def ffn_kernel(transfers, at, grid_steps, first, *refs):
+        out_specs=pl.BlockSpec((ROW_BLOCK, LANES), lambda i: (i, 0)),
+        out_shape=jax.ShapeDtypeStruct((count, LANES), F32),
+        cost_estimate=pl.CostEstimate(
+            flops=2 * count * width * LANES, bytes_accessed=2 * count * width, transcendentals=0
+        ),
+    )(rows, router, routes)
+
+
+def routing_back(experts, route, shared_dot, expert_dot):
+    rank = lax.axis_index("tensor")
+    lanes = lax.broadcasted_iota(jnp.int32, route.shape, 1)
+    gate, chosen, prob = [column(route, experts + i) for i in (0, 2, 3)]
+    expert_grad = chosen * expert_dot
+    logits = route * (jnp.where(lanes == rank, expert_grad, 0.0) - expert_grad * prob)
+    gate_logit = shared_dot * gate * (1.0 - gate)
+    return jnp.where(lanes < experts, logits, jnp.where(lanes == experts, gate_logit, 0.0))
+
+
+def ffn_kernel(transfers, at, grid_steps, experts, kind, *refs):
     refs = list(refs)
 
     def take(count):
@@ -487,24 +779,35 @@
         del refs[:count]
         return taken
 
-    rows_ref, grad_ref, scale_ref, w_ref = take(4)
-    before = () if first else take(2)
+    first, last = kind == "first", kind == "last"
+    rows_ref, grad_ref, route_ref, w_ref = take(4)
+    before = () if first else take(3)
+    router_ref = take(1)[0] if last else None
     sent = take(len(transfers.inputs))
     hidden_ref, gate_ref, up_ref, out_ref, back_ref, dots_ref = take(6)
     landed = take(transfers.moves)
+    w_vmem, w_sem = take(2)
     phase = transfers.begin(sent, landed, refs)
+    step = pl.program_id(0)
+
+    def weights():
+        return pltpu.make_async_copy(w_ref, w_vmem, w_sem)
+
+    pl.when(step == 0)(lambda: weights().start())
 
     def work():
-        groups, _, depth, units = w_ref.shape
-        gate_w, up_w, down_w = [w_ref[:, i].reshape(groups * depth, units) for i in range(3)]
-        rows, grad, scale = rows_ref[...], grad_ref[...], scale_ref[...]
+        pl.when(step == 0)(lambda: weights().wait())
+        groups, _, depth, units = w_vmem.shape
+        gate_w, up_w, down_w = [w_vmem[:, i].reshape(groups * depth, units) for i in range(3)]
+        rows, grad, route = rows_ref[...], grad_ref[...], route_ref[...]
+        scale = column(route, experts if first else experts + 1)
         gate_act = dot(rows, gate_w, (1,), (0,))
         up_act = dot(rows, up_w, (1,), (0,))
         back = dot(grad, down_w, (1,), (0,))
         sigmoid = 1.0 / (1.0 + jnp.exp(-gate_act))
         silu = gate_act * sigmoid
         hidden = (silu * up_act).astype(BF).astype(F32)
-        dots_ref[...] = jnp.sum(hidden * back, axis=1, keepdims=True)
+        dots = jnp.sum(hidden * back, axis=1, keepdims=True)
         scaled = (scale * hidden).astype(BF)
         hidden_ref[...] = scaled
         grad_hidden = scale * back
@@ -514,51 +817,67 @@
         up_ref[...] = grad_up
         moved = dot(scaled, down_w, (1,), (1,))
         turned = dot(grad_gate, gate_w, (1,), (1,)) + dot(grad_up, up_w, (1,), (1,))
-        if not first:
+        lanes = lax.broadcasted_iota(jnp.int32, route.shape, 1)
+        if first:
+            dots_ref[...] = jnp.where(lanes == 0, dots, 0.0)
+        else:
             moved = moved + before[0][...].astype(F32)
             turned = turned + before[1][...].astype(F32)
+            earlier = before[2][...]
+            if last:
+                wide = routing_back(experts, route, column(earlier, 0), column(earlier, 1) + dots)
+                wide = wide.astype(BF)
+                dots_ref[...] = wide
+                turned = turned + dot(wide, router_ref[...], (1,), (1,))
+            else:
+                dots_ref[...] = earlier + jnp.where(lanes == 1, dots, 0.0)
         out_ref[...] = moved.astype(BF)
         back_ref[...] = turned.astype(BF)
 
     beside(phase, at, grid_steps, work)
 
 
-def ffn(rows, grads, scale, weights, before, transfers, at=()):
+def ffn(experts, kind, rows, grads, route, weights, before, router, transfers, at=()):
     count, width = rows.shape
     units = weights.shape[3]
-    first = before is None
+    first, last = kind == "first", kind == "last"
     steps = count // ROW_BLOCK
 
     def block(size):
         return pl.BlockSpec((ROW_BLOCK, size), lambda i: (i, 0))
 
-    whole = pl.BlockSpec(weights.shape, lambda i: (0, 0, 0, 0), pipeline_mode=pl.Buffered(1))
     given = [] if first else list(before)
+    given_specs = [] if first else [block(width), block(width), block(LANES)]
+    if last:
+        given.append(router)
+        given_specs.append(
+            pl.BlockSpec(router.shape, lambda i: (0, 0), pipeline_mode=pl.Buffered(1))
+        )
     narrow = [jax.ShapeDtypeStruct((count, units), BF)] * 3
     wide = [jax.ShapeDtypeStruct((count, width), BF)] * 2
-    dots = [jax.ShapeDtypeStruct((count, 1), F32)]
+    dots = [jax.ShapeDtypeStruct((count, LANES), BF if last else F32)]
     results = pl.pallas_call(
-        functools.partial(ffn_kernel, transfers, at, steps, first),
+        functools.partial(ffn_kernel, transfers, at, steps, experts, kind),
         grid=(steps,),
-        in_specs=[block(width), block(width), block(1), whole]
-        + [block(width)] * len(given)
+        in_specs=[block(width), block(width), block(LANES), pl.BlockSpec(memory_space=pl.ANY)]
+        + given_specs
         + transfers.in_specs,
         out_specs=tuple(
-            [block(units)] * 3 + [block(width)] * 2 + [block(1)] + transfers.out_specs
+            [block(units)] * 3 + [block(width)] * 2 + [block(LANES)] + transfers.out_specs
         ),
         out_shape=tuple(narrow + wide + dots + transfers.shapes),
-        scratch_shapes=transfers.scratch,
+        scratch_shapes=[pltpu.VMEM(weights.shape, BF), DMA] + transfers.scratch,
         compiler_params=transfers.params(),
         cost_estimate=pl.CostEstimate(
             flops=12 * count * width * units,
             bytes_accessed=2 * (3 * width * units + 4 * count * width + 3 * count * units),
             transcendentals=count * units,
         ),
-    )(rows, grads, scale, weights, *given, *transfers.inputs)
-    return results[:3], results[3:5], results[5], results[6:]
-
-
-def ffn_grads_kernel(transfers, at, grid_steps, micros, *refs):
+    )(rows, grads, route, weights, *given, *transfers.inputs)
+    return results[:3], results[3:6], results[6:]
+
+
+def ffn_grads_kernel(transfers, at, grid_steps, micros, last, *refs):
     refs = list(refs)
 
     def take(count):
@@ -566,19 +885,25 @@
         del refs[:count]
         return taken
 
-    per_micro = [take(5) for _ in range(micros)]
+    per_micro = [take(6 if last else 5) for _ in range(micros)]
     sent = take(len(transfers.inputs))
-    (out_ref,) = take(1)
+    out_ref = take(1)[0]
+    wide_ref = take(1)[0] if last else None
     landed = take(transfers.moves)
     phase = transfers.begin(sent, landed, refs)
 
+    def summed(left, right):
+        total = None
+        for one in per_micro:
+            product = dot(one[left][...], one[right][...], (0,), (0,))
+            total = product if total is None else total + product
+        return total
+
     def work():
         for which, left in ((0, 0), (1, 0), (2, 1)):
-            total = None
-            for one in per_micro:
-                product = dot(one[left][...], one[2 + which][...], (0,), (0,))
-                total = product if total is None else total + product
-            out_ref[0, which] = total.astype(BF)
+            out_ref[0, which] = summed(left, 2 + which).astype(BF)
+        if last:
+            wide_ref[...] = summed(0, 5)
 
     beside(phase, at, grid_steps, work)
 
@@ -586,19 +911,26 @@
 def ffn_grads(groups, per_micro, transfers, at=()):
     count, width = per_micro[0][0].shape
     units = per_micro[0][2].shape[1]
+    last = len(per_micro[0]) == 6
     depth = width // groups
     columns = pl.BlockSpec((count, depth), lambda i: (0, i))
-    whole = pl.BlockSpec((count, units), lambda i: (0, 0), pipeline_mode=pl.Buffered(1))
+
+    def whole(size):
+        return pl.BlockSpec((count, size), lambda i: (0, 0), pipeline_mode=pl.Buffered(1))
+
+    shapes = [jax.ShapeDtypeStruct((groups, 3, depth, units), BF)]
+    specs = [pl.BlockSpec((1, 3, depth, units), lambda i: (i, 0, 0, 0))]
+    taken = [columns, columns] + [whole(units)] * 3
+    if last:
+        taken.append(whole(LANES))
+        shapes.append(jax.ShapeDtypeStruct((width, LANES), F32))
+        specs.append(pl.BlockSpec((depth, LANES), lambda i: (i, 0)))
     results = pl.pallas_call(
-        functools.partial(ffn_grads_kernel, transfers, at, groups, len(per_micro)),
+        functools.partial(ffn_grads_kernel, transfers, at, groups, len(per_micro), last),
         grid=(groups,),
-        in_specs=[columns, columns, whole, whole, whole] * len(per_micro) + transfers.in_specs,
-        out_specs=tuple(
-            [pl.BlockSpec((1, 3, depth, units), lambda i: (i, 0, 0, 0))] + transfers.out_specs
-        ),
-        out_shape=tuple(
-            [jax.ShapeDtypeStruct((groups, 3, depth, units), BF)] + transfers.shapes
-        ),
+        in_specs=taken * len(per_micro) + transfers.in_specs,
+        out_specs=tuple(specs + transfers.out_specs),
+        out_shape=tuple(shapes + transfers.shapes),
         scratch_shapes=transfers.scratch,
         compiler_params=transfers.params(),
         cost_estimate=pl.CostEstimate(
@@ -608,7 +940,45 @@
             transcendentals=0,
         ),
     )(*[array for one in per_micro for array in one], *transfers.inputs)
-    return results[0], results[1:]
+    return results[: len(shapes)], results[len(shapes) :]
+
+
+def attention_grads_kernel(micros, *refs):
+    out_ref = refs[-1]
+    span = refs[2].shape[1]
+    totals = [None, None]
+    for m in range(micros):
+        one = refs[4 * m : 4 * m + 4]
+        for which in range(2):
+            product = dot(one[which][...], one[2 + which][...], (0,), (0,))
+            totals[which] = product if totals[which] is None else totals[which] + product
+    out_ref[0, :, :span] = totals[0].astype(BF)
+    out_ref[0, :, span:] = totals[1].astype(BF)
+
+
+def attention_grads(groups, per_micro, needed):
+    count, width = per_micro[0][0].shape
+    depth = width // groups
+    spans = [per_micro[0][i].shape[1] for i in (2, 3)]
+    columns = pl.BlockSpec((count, depth), lambda i: (0, i))
+    whole = [
+        pl.BlockSpec((count, size), lambda i: (0, 0), pipeline_mode=pl.Buffered(1)) for size in spans
+    ]
+    kernel = functools.partial(attention_grads_kernel, len(per_micro))
+    return pl.pallas_call(
+        kernel,
+        grid=(groups,),
+        in_specs=([columns, columns] + whole) * len(per_micro)
+        + [pl.BlockSpec(memory_space=pl.ANY)] * len(needed),
+        out_specs=pl.BlockSpec((1, depth, sum(spans)), lambda i: (i, 0, 0)),
+        out_shape=jax.ShapeDtypeStruct((groups, depth, sum(spans)), BF),
+        compiler_params=pltpu.CompilerParams(vmem_limit_bytes=VMEM_BYTES),
+        cost_estimate=pl.CostEstimate(
+            flops=2 * len(per_micro) * count * width * sum(spans),
+            bytes_accessed=8 * len(per_micro) * count * width,
+            transcendentals=0,
+        ),
+    )(*[array for one in per_micro for array in one], *needed)
 
 
 def rope_tables(seq_len):
@@ -819,23 +1189,37 @@
             b_value.reshape(-1),
         ]
     )
-    small_all = spread(groups, ranks, 1, packed(small, BF).reshape(1, -1, LANES), False)
+    attn_own = jnp.concatenate([w_query, w_key, w_value, w_out.T], axis=1)
+    mesh_size = (ranks, groups)
+    grads_own = []
+    for m in range(micros):
+        inside = (local_pos < lengths[m, 0])[:, None]
+        grads_own.append(jnp.where(inside, cotangent[m, 0], jnp.zeros((), BF)))
+    token_own = [tokens[m, 0] for m in range(micros)]
+    rows_a, grad_a, attn_w, small_all = exchange(
+        mesh_size,
+        2,
+        [
+            ("gather", token_own[0]),
+            ("gather", grads_own[0]),
+            ("cross_gather", attn_own),
+            ("spread", packed(small, BF).reshape(-1, LANES)),
+        ],
+    )
+    attn_w = attn_w.reshape(width, -1)
+    qkv_w, out_w = attn_w[:, : 3 * span], attn_w[:, 3 * span :]
     small_all = small_all.reshape(groups * ranks, -1)
     gain_one = small_all[:, :per_device].reshape(-1).astype(F32)
     gain_two = small_all[:, per_device : 2 * per_device].reshape(-1).astype(F32)
     gate_vec = small_all[:, 2 * per_device : 3 * per_device].reshape(-1)
     bias_at = per_device * (3 + experts)
     router_full = small_all[:, 3 * per_device : bias_at].reshape(width, experts)
-    router_wide = jnp.concatenate([router_full, gate_vec[:, None]], axis=1)
+    router_wide = padded_to(jnp.concatenate([router_full, gate_vec[:, None]], axis=1), LANES)
     own_bias = lax.dynamic_index_in_dim(
         small_all.reshape(groups, ranks, -1), rank, 1, False
     )[:, bias_at : small.shape[0]].reshape(groups, 3, heads, HD // groups)
     bias = own_bias.transpose(1, 2, 0, 3).reshape(1, 3 * span).astype(F32)
 
-    attn_w = lax.all_gather(
-        jnp.concatenate([w_query, w_key, w_value, w_out.T], axis=1), "fsdp", axis=0, tiled=True
-    )
-    qkv_w, out_w = attn_w[:, : 3 * span], attn_w[:, 3 * span :]
     ranges = [
         (shared_gate, shared_up, shared_down),
         (expert_gate[0, :, :cut], expert_up[0, :, :cut], expert_down[0, :cut]),
@@ -849,12 +1233,7 @@
     ]
 
     cosine, sine = rope_tables(seq_len)
-    idle = Transfers(ranks, 0)
-    token_own = [tokens[m, 0] for m in range(micros)]
-    grads_own = []
-    for m in range(micros):
-        inside = (local_pos < lengths[m, 0])[:, None]
-        grads_own.append(jnp.where(inside, cotangent[m, 0], jnp.zeros((), BF)))
+    idle = Transfers(mesh_size)
 
     def attention(m, token_rows):
         normed = (normalize(token_rows.astype(F32))[0] * gain_one).astype(BF)
@@ -867,22 +1246,6 @@
         unit, inverse = normalize(hidden)
         return hidden, unit, inverse, (unit * gain_two).astype(BF)
 
-    def routing(m, rows_two):
-        logits = dot(rows_two, router_wide, (1,), (0,))
-        probs = jax.nn.softmax(logits[:, :experts], axis=-1)
-        shared_scale = jax.nn.sigmoid(logits[:, experts:])
-        chosen = jnp.any(routes[m, 0] == rank, axis=1, keepdims=True)
-        own_expert = (jnp.arange(experts, dtype=jnp.int32) == rank)[None, :]
-        prob = jnp.sum(jnp.where(own_expert, probs, 0.0), axis=1, keepdims=True)
-        return probs, shared_scale, chosen, own_expert, prob, jnp.where(chosen, prob, 0.0)
-
-    def routing_back(route, dots):
-        probs, shared_scale, chosen, own_expert, prob, _ = route
-        expert_grad = jnp.where(chosen, dots[1] + dots[2], 0.0)
-        grad_logits = probs * (jnp.where(own_expert, expert_grad, 0.0) - expert_grad * prob)
-        grad_gate_logit = dots[0] * shared_scale * (1.0 - shared_scale)
-        return jnp.concatenate([grad_logits, grad_gate_logit], axis=1).astype(BF)
-
     def second_norm_back(m, state, summed):
         grad_hidden, gain_part = norm_back(summed, state[1], state[2], gain_two)
         grad_hidden = grad_hidden + grads_own[m].astype(F32)
@@ -902,92 +1265,88 @@
         inside = (local_pos < lengths[m, 0]).astype(F32)[:, None]
         return (inside * (hidden + moved)).astype(BF)
 
-    start = after(token_own[0], small_all)
-    rows_a, grad_a = exchange(ranks, 2, [start, grads_own[0]])
     att_a = attention(0, rows_a)
-    rows_b, sum_a = exchange(ranks, 3, [token_own[1]], [att_a[3]])
+    rows_b, sum_a = exchange(
+        mesh_size, 3, [("gather", token_own[1]), ("scatter", att_a[3])]
+    )
     att_b = attention(1, rows_b)
     norm_a = second_norm(0, sum_a)
-    two_a, sum_b = exchange(ranks, 4, [norm_a[3]], [att_b[3]])
+    two_a, sum_b = exchange(mesh_size, 4, [("gather", norm_a[3]), ("scatter", att_b[3])])
     norm_b = second_norm(1, sum_b)
-    route_a = routing(0, two_a)
-
-    def scale_of(route, which):
-        return route[1] if which == 0 else route[5]
-
-    act = {}
-    dots_a, dots_b = [], []
-    act[0, 0], acc_a, dots, (two_b,) = ffn(
-        two_a, grad_a, scale_of(route_a, 0), weights[0], None, Transfers(ranks, 5, [norm_b[3]]), (0, 2, 3)
-    )
-    dots_a.append(dots)
-    act[1, 0], acc_a, dots, (grad_b,) = ffn(
-        two_a, grad_a, scale_of(route_a, 1), weights[1], acc_a, Transfers(ranks, 6, [grads_own[1]]), (0, 2, 3)
-    )
-    dots_a.append(dots)
-    route_b = routing(1, two_b)
-    acc_b = None
-    for which in range(2):
-        act[which, 1], acc_b, dots, _ = ffn(
-            two_b, grad_b, scale_of(route_b, which), weights[which], acc_b, idle
-        )
-        dots_b.append(dots)
-
-    def grads_of(which, transfers, at=()):
-        per_micro = []
-        for rows_two, grads, key in ((two_a, grad_a, 0), (two_b, grad_b, 1)):
-            scaled, gate, up = act[which, key]
-            per_micro.append((rows_two, grads, gate, up, scaled))
-        return ffn_grads(groups, per_micro, transfers, at)
+
+    def moving(ident, *moves, needed=()):
+        return Transfers(mesh_size, ident, moves, needed)
 
     def over_groups(grads):
         flat = grads.reshape(-1, grads.shape[-1])
         summed = lax.psum_scatter(flat, "fsdp", scatter_dimension=0, tiled=True)
         return with_layout_constraint(summed, Layout((0, 1))).reshape(grads.shape[1:])
 
-    grads_0, _ = grads_of(0, idle)
+    def grads_of(which, transfers, at=()):
+        per_micro = []
+        for key in range(micros):
+            rows_two, grads = ((two_a, grad_a), (two_b, grad_b))[key]
+            scaled, gate, up = act[which, key]
+            more = [(acc_a, acc_b)[key][2]] if which == 2 else []
+            per_micro.append([rows_two, grads, gate, up, scaled] + more)
+        return ffn_grads(groups, per_micro, transfers, at)
+
+    act = {}
+    part = functools.partial(ffn, experts)
+    route_a = routing(experts, two_a, router_wide, routes[0, 0])
+    act[0, 0], acc_a, (two_b,) = part(
+        "first", two_a, grad_a, route_a, weights[0], None, None,
+        moving(5, ("gather", norm_b[3])), (0, 2),
+    )
+    act[1, 0], acc_a, (grad_b,) = part(
+        "next", two_a, grad_a, route_a, weights[1], acc_a, None,
+        moving(6, ("gather", grads_own[1])), (0, 2),
+    )
+    route_b = routing(experts, two_b, router_wide, routes[1, 0])
+    act[0, 1], acc_b, _ = part("first", two_b, grad_b, route_b, weights[0], None, None, idle)
+    (grads_0,), _ = grads_of(0, idle)
     range_0 = over_groups(grads_0)
-    scale_a = after(scale_of(route_a, 2), grads_0)
-    act[2, 0], acc_a, dots, _ = ffn(two_a, grad_a, scale_a, weights[2], acc_a, idle)
-    dots_a.append(dots)
-    wide_a = routing_back(route_a, dots_a)
-    back_a = (acc_a[1].astype(F32) + dot(wide_a, router_wide, (1,), (1,))).astype(BF)
-    grads_1, (down_a,) = grads_of(1, Transfers(ranks, 7, [], [back_a]), (0, 2))
+    act[2, 0], acc_a, _ = part(
+        "last", two_a, grad_a, route_a, weights[2], acc_a, router_wide, moving(0, needed=[grads_0])
+    )
+    act[1, 1], acc_b, (down_a,) = part(
+        "next", two_b, grad_b, route_b, weights[1], acc_b, None,
+        moving(7, ("scatter", acc_a[1])), (0, 2),
+    )
+    hid_a, send_a, gain_part_a = second_norm_back(0, norm_a, down_a)
+    act[2, 1], acc_b, (datt_a, moved_a) = part(
+        "last", two_b, grad_b, route_b, weights[2], acc_b, router_wide,
+        moving(8, ("gather", send_a), ("scatter", acc_a[0])), (0, 2),
+    )
+    (grads_1,), (down_b,) = grads_of(
+        1, moving(9, ("scatter", acc_b[1]), needed=[range_0]), (0, 2)
+    )
     range_1 = over_groups(grads_1)
-    hid_a, send_a, gain_part_a = second_norm_back(0, norm_a, down_a)
-    act[2, 1], acc_b, dots, (datt_a,) = ffn(
-        two_b, grad_b, scale_of(route_b, 2), weights[2], acc_b, Transfers(ranks, 8, [send_a]), (0, 2, 3)
-    )
-    dots_b.append(dots)
-    wide_b = routing_back(route_b, dots_b)
-    back_b = (acc_b[1].astype(F32) + dot(wide_b, router_wide, (1,), (1,))).astype(BF)
+    hid_b, send_b, gain_part_b = second_norm_back(1, norm_b, down_b)
     grad_qkv_a, sums_a, first_a = attention_back(0, att_a, datt_a)
-    grads_2, (down_b, one_a) = grads_of(
-        2, Transfers(ranks, 9, [], [back_b, first_a], [range_0]), (0, 2)
+    (grads_2, total_wide), (datt_b, one_a, moved_b) = grads_of(
+        2,
+        moving(10, ("gather", send_b), ("scatter", first_a), ("scatter", acc_b[0])),
+        (0, 2),
     )
     range_2 = over_groups(grads_2)
-    hid_b, send_b, gain_part_b = second_norm_back(1, norm_b, down_b)
-    datt_b, moved_a = exchange(ranks, 10, [send_b], [acc_a[0]], [range_1])
     grad_qkv_b, sums_b, first_b = attention_back(1, att_b, datt_b)
-    one_b, moved_b = exchange(ranks, 11, [], [first_b, acc_b[0]], [range_2])
-
-    def over_micros(left_a, right_a, left_b, right_b):
-        return (dot(left_a, right_a, (0,), (0,)) + dot(left_b, right_b, (0,), (0,))).astype(BF)
-
-    attn_g = jnp.concatenate(
+    attn_parts = attention_grads(
+        groups,
         [
-            over_micros(att_a[0], grad_qkv_a, att_b[0], grad_qkv_b),
-            over_micros(datt_a, att_a[2], datt_b, att_b[2]),
+            (att_a[0], datt_a, grad_qkv_a, att_a[2]),
+            (att_b[0], datt_b, grad_qkv_b, att_b[2]),
         ],
-        axis=1,
-    )
-    attn_g = lax.psum_scatter(attn_g, "fsdp", scatter_dimension=0, tiled=True).astype(F32)
+        [range_1],
+    )
+    one_b, attn_g = exchange(
+        mesh_size, 11, [("scatter", first_b), ("cross_scatter", attn_parts)]
+    )
 
     grad_in_a, one_part_a = first_norm_back(0, hid_a, one_a)
     grad_in_b, one_part_b = first_norm_back(1, hid_b, one_b)
 
     devices = groups * ranks
-    total_wide = dot(two_a, wide_a, (0,), (0,)) + dot(two_b, wide_b, (0,), (0,))
     bias_part = (sums_a + sums_b).reshape(3, heads, groups, HD // groups).transpose(2, 0, 1, 3)
     bias_part = bias_part.reshape(groups, 1, -1)
     own_rank = (jnp.arange(ranks, dtype=jnp.int32) == rank).astype(F32)[None, :, None]
@@ -995,12 +1354,12 @@
         [
             (one_part_a + one_part_b).reshape(devices, -1),
             (gain_part_a + gain_part_b).reshape(devices, -1),
-            total_wide.reshape(devices, -1),
+            total_wide[:, : experts + 1].reshape(devices, -1),
             (bias_part * own_rank).reshape(devices, -1),
         ],
         axis=1,
     )
-    shares = spread(groups, ranks, 12, packed(parts, F32).reshape(devices, -1, LANES), True)
+    shares = share(mesh_size, 12, packed(parts, F32).reshape(devices, -1, LANES))
     shares = shares.reshape(-1)
     wide_g = shares[2 * per_device : (3 + experts) * per_device].reshape(per_device, experts + 1)
     bias_g = shares[bias_at : parts.shape[1]].reshape(3, heads, HD // groups)

time: 1090 us -> 895 us (0.82)
  waiting for transfers between devices: 118 us -> 0.15 us
  matrix products: 76.6 us -> 33.4 us
  other arithmetic: 66.9 us -> 50 us
    reduce_scatter x3, waiting for transfers between devices: 92.9 us -> 0.02 us  [over_groups(): summed = lax.psum_scatter(flat, 'fsdp', scatter_dimension=0, tiled=True)]
    pallas_call x5 -> x4, Pallas kernels: 301 us -> 253 us  [exchange(): pl.pallas_call(functools.partial(exchange_kernel, transfers), out_shape=t...]
    pallas_call x8 -> x10, Pallas kernels: 252 us -> 300 us  [the longest x6 262 us: ffn(): pl.pallas_call(functools.partial(ffn_kernel, transfers, at, steps, expert...]
    dot_general x18 -> x8, matrix products: 76.6 us -> 33.4 us  [dot(): lax.dot_general(left, right, ((left_dims, right_dims), ((), ())), preferr...]
    reduce_scatter x1 -> x0, waiting for transfers between devices: 24.1 us -> none  [local(): lax.psum_scatter(attn_g, 'fsdp', scatter_dimension=0, tiled=True)]
    unnamed x164 -> x140, local copies, waits for them, and re-layouts: 27.9 us -> 23.8 us
  transfers between devices with their start and end apart: 8 -> 6, of which waited for: 2 -> 0; matrix products, arithmetic and copies ran while one was open for 14% -> 12% of each run, Pallas kernels for 56% -> 79%
where the time goes in v3:
time: 895 us; the launch traced here: 891 us
  Pallas kernels  745 us (83%)
  other arithmetic  50 us (6%)
  local copies, waits for them, and re-layouts  46.4 us (5%)
  matrix products  33.4 us (4%)
  between operations  15.4 us (2%)
    pallas_call x6, Pallas kernels, ffn(): pl.pallas_call(functools.partial(ffn_kernel, transfers, at, steps, expert...  262 us
    pallas_call x4, Pallas kernels, exchange(): pl.pallas_call(functools.partial(exchange_kernel, transfers), out_shape=t...  253 us
    pallas_call x3, Pallas kernels, ffn_grads(): pl.pallas_call(functools.partial(ffn_grads_kernel, transfers, at, groups,...  165 us
    dot_general x8, matrix products, dot(): lax.dot_general(left, right, ((left_dims, right_dims), ((), ())), preferr...  33.4 us
    unnamed x140, local copies, waits for them, and re-layouts  23.8 us
  transfers between devices with their start and end apart: 6, of which 0 were waited for; matrix products, arithmetic and copies ran while one was open for 12% of the time, Pallas kernels for 79%

profile of v3, /device:TPU:0, one launch (start us, length us, event | category | flops | bytes accessed | tf_op | source)
XLA Modules:
  0.0 890.6 jit_solution(17318798491943884411)
XLA Ops:
  9.6 1.7 pad_maximum_fusion
  26.4 81.7 %shard_map.348 = (bf16[1024,2048]{1,0:T(8,128)(2,1)}, bf16[1024,2048]{1,0:T(8,128)(2,1)}, bf16[4,512,1024]{2,1,0:T(8,128)(2,1)}, bf16[32,16,128]{2,1,0:T(8,128)(2,1)}) custom-call(bf16[128,2048]{1,0:T(8,128)(2,1)} %get-tuple-element.287.refs_0_, bf16[128,2048]{1,0:T(8,128)(2,1)} %get-tuple-element.286.refs_1_, bf16[512,1024]{1,0:T(8,128)(2,1)} %pad_maximum_fusion.3.refs_2_, ...), custom_call_target="tpu_custom_call" | custom-call | tf_op jit(solution)/shard_map/pallas_call | solution.py:647
  112.2 2.0 fusion.48
  114.2 3.1 fusion
  118.4 1.9 broadcast_in_dim_reshape.4
  120.7 3.6 fusion.2.refs_0_
  124.5 3.4 fusion.10.pre_ref
  127.9 5.5 shard_map.349
  133.5 3.3 convolution_convert_fusion.1.refs_1_
  136.8 51.7 %shard_map.350 = (bf16[1024,2048]{1,0:T(8,128)(2,1)}, f32[128,2048]{1,0:T(8,128)}) custom-call(bf16[128,2048]{1,0:T(8,128)(2,1)} %get-tuple-element.288.refs_0_, bf16[1024,2048]{1,0:T(8,128)(2,1)} %convolution_convert_fusion.1.refs_1_), custom_call_target="tpu_custom_call" | custom-call | tf_op jit(solution)/shard_map/pallas_call | solution.py:647
  188.6 3.2 fusion.3
  194.2 3.4 fusion.8.pre_ref
  197.7 5.3 shard_map.351
  203.9 3.3 convolution_convert_fusion.refs_1_
  208.1 52.0 %shard_map.352 = (bf16[1024,2048]{1,0:T(8,128)(2,1)}, f32[128,2048]{1,0:T(8,128)}) custom-call(bf16[128,2048]{1,0:T(8,128)(2,1)} %multiply_convert_fusion.3.refs_0_, bf16[1024,2048]{1,0:T(8,128)(2,1)} %convolution_convert_fusion.refs_1_), custom_call_target="tpu_custom_call" | custom-call | tf_op jit(solution)/shard_map/pallas_call | solution.py:647
  261.3 5.5 shard_map.353.refs_2_
  270.3 43.6 %shard_map.354 = (bf16[1024,768]{1,0:T(8,128)(2,1)}, bf16[1024,768]{1,0:T(8,128)(2,1)}, bf16[1024,768]{1,0:T(8,128)(2,1)}, bf16[1024,2048]{1,0:T(8,128)(2,1)}, b...) custom-call(bf16[1024,2048]{1,0:T(8,128)(2,1)} %get-tuple-element.92.rows_ref.refs_0_, ...), custom_call_target="tpu_custom_call" | custom-call | flops 19327352832 | bytes 30932992 | tf_op jit(solution)/shard_map/pallas_call | solution.py:859
  313.8 5.5 shard_map.356.refs_2_
  319.3 43.5 %shard_map.355 = (bf16[1024,640]{1,0:T(8,128)(2,1)}, bf16[1024,640]{1,0:T(8,128)(2,1)}, bf16[1024,640]{1,0:T(8,128)(2,1)}, bf16[1024,2048]{1,0:T(8,128)(2,1)}, b...) custom-call(bf16[1024,2048]{1,0:T(8,128)(2,1)} %get-tuple-element.92.rows_ref.refs_0_, ...), custom_call_target="tpu_custom_call" | custom-call | flops 16106127360 | bytes 28573696 | tf_op jit(solution)/shard_map/pallas_call | solution.py:859
  362.8 27.3 %shard_map.357 = (bf16[1024,768]{1,0:T(8,128)(2,1)}, bf16[1024,768]{1,0:T(8,128)(2,1)}, bf16[1024,768]{1,0:T(8,128)(2,1)}, bf16[1024,2048]{1,0:T(8,128)(2,1)}, b...) custom-call(bf16[1024,2048]{1,0:T(8,128)(2,1)} %get-tuple-element.95.rows_ref.refs_0_.refs_5_.refs_6_, ...), custom_call_target="tpu_custom_call" | custom-call | flops 19327352832 | bytes 30932992 | tf_op jit(solution)/shard_map/pallas_call | solution.py:859
  390.0 27.3 %shard_map.358.refs_8_ = bf16[4,3,512,768]{3,2,1,0:T(8,128)(2,1)} custom-call(bf16[1024,2048]{1,0:T(8,128)(2,1)} %get-tuple-element.92.rows_ref.refs_0_, bf16[1024,2048]{1,0:T(8,128)(2,1)} %get-tuple-element.93.refs_1_, bf16[1024,768]{1,0:T(8,128)(2,1)} %get-tuple-element.106.refs_2_, bf16[1024,768]{1,0:T(8,128)(2,1)} %get-tuple-element.107.refs_3_, ...), custom_call_target="tpu_custom_call" | custom-call | flops 19327352832 | bytes 35651584 | tf_op jit(solution)/shard_map/pallas_call | solution.py:928
  417.5 33.5 %shard_map.359 = (bf16[1024,768]{1,0:T(8,128)(2,1)}, bf16[1024,768]{1,0:T(8,128)(2,1)}, bf16[1024,768]{1,0:T(8,128)(2,1)}, bf16[1024,2048]{1,0:T(8,128)(2,1)}, b...) custom-call(bf16[1024,2048]{1,0:T(8,128)(2,1)} %get-tuple-element.92.rows_ref.refs_0_, ...), custom_call_target="tpu_custom_call" | custom-call | flops 19327352832 | bytes 30932992 | tf_op jit(solution)/shard_map/pallas_call | solution.py:859
  451.0 46.8 %shard_map.360 = (bf16[1024,640]{1,0:T(8,128)(2,1)}, bf16[1024,640]{1,0:T(8,128)(2,1)}, bf16[1024,640]{1,0:T(8,128)(2,1)}, bf16[1024,2048]{1,0:T(8,128)(2,1)}, b...) custom-call(bf16[1024,2048]{1,0:T(8,128)(2,1)} %get-tuple-element.95.rows_ref.refs_0_.refs_5_.refs_6_, ...), custom_call_target="tpu_custom_call" | custom-call | flops 16106127360 | bytes 28573696 | tf_op jit(solution)/shard_map/pallas_call | solution.py:859
  497.8 1.7 multiply_reduce_fusion.1
  499.6 2.3 fusion.52.refs_8_
  501.9 67.0 %shard_map.361 = (bf16[1024,768]{1,0:T(8,128)(2,1)}, bf16[1024,768]{1,0:T(8,128)(2,1)}, bf16[1024,768]{1,0:T(8,128)(2,1)}, bf16[1024,2048]{1,0:T(8,128)(2,1)}, b...) custom-call(bf16[1024,2048]{1,0:T(8,128)(2,1)} %get-tuple-element.95.ro, ...), custom_call_target="tpu_custom_call" | custom-call | flops 19327352832 | bytes 30932992 | tf_op jit(solution)/shard_map/pallas_call | solution.py:859
  569.0 45.3 %shard_map.362 = (bf16[4,3,512,640]{3,2,1,0:T(8,128)(2,1)}, f32[128,2048]{1,0:T(8,128)}) custom-call(bf16[1024,2048]{1,0:T(8,128)(2,1)} %get-tuple-element.92.rows_ref.refs_0_, bf16[1024,2048]{1,0:T(8,128)(2,1)} %get-tuple-element.93.refs_1_, bf16[1024,640]{1,0:T(8,128)(2,1)} %get-tuple-element.127.refs_2_, bf16[1024,640]{1,0:T(8,128)(2,1)} %get-tuple-element.128.refs_3_, ...), custom_call_target="tpu_custom_call" | custom-call | flops 16106127360 | bytes 32505856 | tf_op jit(solution)/shard_map/pallas_call | solution.py:928
  614.5 3.9 convolution_convert_fusion.5.grad_ref
  618.5 8.0 shard_map.363
  626.6 5.4 convolution_convert_fusion.3.refs_13_
  633.6 92.3 %shard_map.364 = (bf16[4,3,512,768]{3,2,1,0:T(8,128)(2,1)}, f32[2048,128]{1,0:T(8,128)}, bf16[1024,2048]{1,0:T(8,128)(2,1)}, f32[128,2048]{1,0:T(8,128)}, f32[128,2048]{1,0:T(8,128)}) custom-call(bf16[1024,2048]{1,0:T(8,128)(2,1)} %get-tuple-element.92.rows_ref.refs_0_, bf16[1024,2048]{1,0:T(8,128)(2,1)} %get-tuple-element.93.refs_1_, ...), custom_call_target="tpu_custom_call" | custom-call | flops 19327352832 | bytes 35651584 | tf_op jit(solution)/shard_map/pallas_call | solution.py:928
  726.7 1.7 reshape.276
  728.4 3.7 convolution_convert_fusion.4.grad_ref
  732.1 7.9 shard_map.365
  741.3 3.1 convert_bitcast_fusion
  746.0 3.2 copy.143
  750.9 6.9 convolution_convert_fusion.2.refs_0_
  757.7 15.4 %shard_map.366.refs_1_ = bf16[4,512,1024]{2,1,0:T(8,128)(2,1)} custom-call(bf16[1024,2048]{1,0:T(8,128)(2,1)} %copy-done.26, bf16[1024,2048]{1,0:T(8,128)(2,1)} %get-tuple-element.136.refs_1_, bf16[1024,768]{1,0:T(8,128)(2,1)} %copy-done.8, bf16[1024,256]{1,0:T(8,128)(2,1)} %copy-done.4, bf16[1024,2048]{1,0:T(8,128)(2,1)} %copy-done.27, ...), custom_call_target="tpu_custom_call" | custom-call | flops 8589934592 | bytes 33554432 | tf_op jit(solution)/shard_map/pallas_call | solution.py:968
  773.2 67.9 %shard_map.367 = (f32[128,2048]{1,0:T(8,128)}, f32[512,1024]{1,0:T(8,128)}) custom-call(bf16[1024,2048]{1,0:T(8,128)(2,1)} %convolution_convert_fusion.2.refs_0_, bf16[4,512,1024]{2,1,0:T(8,128)(2,1)} %shard_map.366.refs_1_), custom_call_target="tpu_custom_call" | custom-call | tf_op jit(solution)/shard_map/pallas_call | solution.py:647
  841.1 3.0 slice_bitcast_fusion.2
  844.1 2.2 copy.140
  846.3 2.2 fusion.32
  849.4 11.7 %shard_map.368 = f32[8,128]{1,0:T(8,128)} custom-call(f32[32,8,128]{2,1,0:T(8,128)} %bitcast.152), custom_call_target="tpu_custom_call" | custom-call | tf_op jit(solution)/shard_map/pallas_call | solution.py:713
  866.0 2.5 fusion.44
  873.1 3.0 slice_bitcast_fusion
  876.3 2.2 copy.145
  878.6 3.2 fusion.19
  881.7 1.8 fusion.18
  (239 shorter events, 49.5 us)
Async XLA Ops:
  7.2 263.1 %all-gather.7.cloned.1.call-start = ((), (), s32[]{:S(2)}) async-start(), calls=%async_computation.6 | async-start | bytes 11796480 | tf_op jit(solution)/shard_map/all_gather | solution.py:1229
  11.3 308.0 %all-gather.9.cloned.1.call-start = ((), (), s32[]{:S(2)}) async-start(), calls=%async_computation.7 | async-start | bytes 9830400 | tf_op jit(solution)/shard_map/all_gather | solution.py:1229
  14.3 403.2 %all-gather.11.cloned.1.call-start = ((), (), s32[]{:S(2)}) async-start(), calls=%async_computation.8 | async-start | bytes 11796480 | tf_op jit(solution)/shard_map/all_gather | solution.py:1229
  15.9 5.1 copy-start.51
  15.9 5.3 copy-start.55
  15.9 5.3 copy-start.56
  15.9 5.3 copy-start.57
  15.9 7.1 copy-start.16
  17.6 6.5 copy-start.37
  17.6 7.7 copy-start.43
  17.6 7.7 copy-start.44
  17.6 7.7 copy-start.45
  17.6 551.3 %reduce-scatter.4.cloned.1.call-start = ((), (), s32[]{:S(2)}) async-start(), calls=%async_computation.3 | async-start | bytes 11796480 | tf_op jit(solution)/shard_map/reduce_scatter | solution.py:1282
  24.1 86.1 %copy-start.46 = (s32[2,1,1024,4]{2,3,1,0:T(4,128)S(1)}, s32[2,1,1024,4]{2,3,1,0:T(4,128)}, u32[]{:S(2)}) copy-start(s32[2,1,1024,4]{2,3,1,0:T(4,128)} %param.23) | copy-start | bytes 98308
  117.4 74.4 %copy-start.41 = (f32[2048]{0:T(1024)}, f32[2048]{0:T(1024)S(1)}, u32[]{:S(2)}) copy-start(f32[2048]{0:T(1024)S(1)} %reshape.282) | copy-start | bytes 24580
  120.6 77.1 %copy-start = (f32[1024,128]{1,0:T(8,128)}, f32[1024,128]{1,0:T(8,128)S(1)}, u32[]{:S(2)}) copy-start(f32[1024,128]{1,0:T(8,128)S(1)} %get-tuple-element.304.cos_ref) | copy-start | bytes 1572868
  120.6 77.1 %copy-start.2 = (f32[1024,128]{1,0:T(8,128)}, f32[1024,128]{1,0:T(8,128)S(1)}, u32[]{:S(2)}) copy-start(f32[1024,128]{1,0:T(8,128)S(1)} %get-tuple-element.305.sin_ref) | copy-start | bytes 1572868
  120.6 3.8 copy-start.33
  124.3 3.6 copy-start.26
  133.5 3.4 copy-start.4
  133.5 3.4 copy-start.6
  188.6 3.5 copy-start.19
  194.2 3.4 copy-start.27
  197.7 5.3 copy-start.17
  197.7 5.3 copy-start.36
  203.0 4.2 copy-start.5
  203.9 295.7 %copy-start.11 = (f32[128,2048]{1,0:T(8,128)}, f32[128,2048]{1,0:T(8,128)S(1)}, u32[]{:S(2)}) copy-start(f32[128,2048]{1,0:T(8,128)S(1)} %get-tuple-element.284) | copy-start | bytes 3145732
  207.2 53.0 %copy-start.31 = (bf16[2048,1]{1,0:T(8,128)(2,1)S(1)}, bf16[2048,1]{1,0:T(8,128)(2,1)}, u32[]{:S(2)}) copy-start(bf16[2048,1]{1,0:T(8,128)(2,1)} %broadcast_in_dim_reshape.4) | copy-start | bytes 12292
  268.4 45.5 %copy-start.47 = (f32[128]{0:T(128)}, f32[128]{0:T(128)S(1)}, u32[]{:S(2)}) copy-start(f32[128]{0:T(128)S(1)} %add_rsqrt_fusion.4) | copy-start | bytes 1540
  417.4 340.3 %reduce-scatter.6.cloned.1.call-start = ((), (), s32[]{:S(2)}) async-start(), calls=%async_computation.4 | async-start | bytes 9830400 | tf_op jit(solution)/shard_map/reduce_scatter | solution.py:1282
  451.0 48.5 %copy-start.23 = (bf16[128,2048]{1,0:T(8,128)(2,1)S(1)}, bf16[128,2048]{1,0:T(8,128)(2,1)}, u32[]{:S(2)}) copy-start(bf16[128,2048]{1,0:T(8,128)(2,1)} %get-tuple-element.286.refs_1_) | copy-start | bytes 1572868
  614.2 258.9 %reduce-scatter.8.cloned.1.call-start = ((), (), s32[]{:S(2)}) async-start(), calls=%async_computation.5 | async-start | bytes 11796480 | tf_op jit(solution)/shard_map/reduce_scatter | solution.py:1282
  614.5 3.9 copy-start.1
  614.5 3.9 copy-start.3
  614.5 3.9 copy-start.7
  618.5 8.1 copy-start.35
  626.5 5.5 copy-start.8
  626.5 5.5 copy-start.14
  626.5 5.5 copy-start.21
  626.6 5.5 copy-start.48
  626.6 5.9 copy-start.24
  746.0 4.8 copy-start.10
  841.1 5.2 copy-start.18
  841.1 5.2 copy-start.42
  844.1 21.8 %copy-start.12 = (f32[128,2048]{1,0:T(8,128)S(1)}, f32[128,2048]{1,0:T(8,128)}, u32[]{:S(2)}) copy-start(f32[128,2048]{1,0:T(8,128)} %copy-done.11) | copy-start | bytes 3145732
  844.1 21.8 %copy-start.20 = (f32[128,2048]{1,0:T(8,128)S(1)}, f32[128,2048]{1,0:T(8,128)}, u32[]{:S(2)}) copy-start(f32[128,2048]{1,0:T(8,128)} %get-tuple-element.116) | copy-start | bytes 3145732
  844.1 21.8 %copy-start.50 = (f32[128]{0:T(128)S(1)}, f32[128]{0:T(128)}, u32[]{:S(2)}) copy-start(f32[128]{0:T(128)} %get-tuple-element.258) | copy-start | bytes 1540
  878.5 3.2 copy-start.29
  (25 other events, 47.0 us)
Sparse Core Ops, SparseCore 0:
  11.4 128.8 all-gather.6
  142.7 82.5 all-gather.8
  227.7 96.3 all-gather.10
  417.5 93.2 reduce-scatter.3
  614.4 83.1 reduce-scatter.5
  726.1 121.6 reduce-scatter.7

commit v4 on v3

v4 whole, which is shorter than its diff:
```python
import functools

import jax
import jax.numpy as jnp
import numpy as np
from jax import lax
from jax.experimental import pallas as pl
from jax.experimental.layout import Layout, with_layout_constraint
from jax.experimental.pallas import tpu as pltpu
from jax.sharding import PartitionSpec as P

HD = 128
EPSILON = 1e-06
ROPE_BASE = 1000000.0
BF = jnp.bfloat16
F32 = jnp.float32
MESH = pl.DeviceIdType.MESH
QB = 256
LANES = 128
CHUNKS = 2
STRIP = 16
ROW_BLOCK = 256
VMEM_BYTES = 60 << 20


def dot(left, right, left_dims, right_dims):
    return lax.dot_general(
        left, right, ((left_dims, right_dims), ((), ())), preferred_element_type=F32
    )


def normalize(values):
    inverse = lax.rsqrt(jnp.mean(values * values, axis=-1, keepdims=True) + EPSILON)
    return (values * inverse, inverse)


def norm_back(grad_normed, unit, inverse, gain):
    grad_unit = grad_normed * gain
    grad_values = inverse * (grad_unit - unit * jnp.mean(grad_unit * unit, axis=-1, keepdims=True))
    return (grad_values, jnp.sum(grad_normed * unit, axis=0))


def remote(src, dst, sems, at, target):
    return pltpu.make_async_remote_copy(
        src_ref=src,
        dst_ref=dst,
        send_sem=sems[0].at[at],
        recv_sem=sems[1].at[at],
        device_id={"tensor": target},
        device_id_type=MESH,
    )


def gather_scratch(ranks):
    chips = ranks // 2
    pair = [pltpu.SemaphoreType.DMA((chips, CHUNKS))] * 2
    cross = [pltpu.SemaphoreType.DMA((2 * chips, CHUNKS))] * 2
    return [pltpu.SemaphoreType.DMA] + pair + pair + cross


def gather_steps(place, block, whole, local_sem, up_s, up_r, down_s, down_r, cross_s, cross_r):
    chips, chip, core = place.chips, place.chip, place.core
    rows = block.shape[0]
    part = rows // CHUNKS
    up, down, cross = (up_s, up_r), (down_s, down_r), (cross_s, cross_r)

    def at(owner, chunk):
        first = pl.multiple_of((2 * owner + core) * rows + chunk * part, part)
        return whole.at[pl.ds(first, part)]

    def theirs(owner, chunk):
        first = pl.multiple_of((2 * owner + 1 - core) * rows + chunk * part, part)
        return whole.at[pl.ds(first, part)]

    def own(chunk):
        return block.at[pl.ds(chunk * part, part)]

    def upward(step, chunk):
        source = own(chunk) if step == 0 else at(chip - step, chunk)
        return remote(source, at(chip - step, chunk), up, (step, chunk), place.above)

    def downward(step, chunk):
        source = own(chunk) if step == 0 else at(chip + step, chunk)
        return remote(source, at(chip + step, chunk), down, (step, chunk), place.below)

    def across(slot, owner, chunk):
        source = own(chunk) if slot == 0 else at(owner, chunk)
        return remote(source, at(owner, chunk), cross, (slot, chunk), place.partner)

    def arrived(slot, owner, chunk):
        return remote(theirs(owner, chunk), theirs(owner, chunk), cross, (slot, chunk), place.partner)

    def arrived_up(step, chunk):
        return remote(at(chip - step, chunk), at(chip - step, chunk), up, (step - 1, chunk), place.above)

    def arrived_down(step, chunk):
        return remote(at(chip + step, chunk), at(chip + step, chunk), down, (step - 1, chunk), place.below)

    both = range(CHUNKS)

    def mine():
        first = pl.multiple_of((2 * chip + core) * rows, rows)
        return pltpu.make_async_copy(block, whole.at[pl.ds(first, rows)], local_sem)

    def begin():
        for chunk in both:
            pl.when(place.not_top)(lambda: upward(0, chunk).start())
            pl.when(place.not_bottom)(lambda: downward(0, chunk).start())
        for chunk in both:
            across(0, chip, chunk).start()
        mine().start()

    def hop(step, chunk):
        @pl.when(chip >= step)
        def _():
            arrived_up(step, chunk).wait_recv()
            pl.when(place.not_top)(lambda: upward(step, chunk).start())
            across(2 * step - 1, chip - step, chunk).start()

        @pl.when(chip < chips - step)
        def _():
            arrived_down(step, chunk).wait_recv()
            pl.when(place.not_bottom)(lambda: downward(step, chunk).start())
            across(2 * step, chip + step, chunk).start()

    def end():
        mine().wait()
        for step in range(chips):
            for chunk in both:
                if step == 0:
                    arrived(0, chip, chunk).wait_recv()
                    across(0, chip, chunk).wait_send()
                else:

                    @pl.when(chip >= step)
                    def _():
                        arrived(2 * step - 1, chip - step, chunk).wait_recv()
                        across(2 * step - 1, chip - step, chunk).wait_send()

                    @pl.when(chip < chips - step)
                    def _():
                        arrived(2 * step, chip + step, chunk).wait_recv()
                        across(2 * step, chip + step, chunk).wait_send()

                @pl.when(place.not_top & (chip >= step))
                def _():
                    upward(step, chunk).wait_send()

                @pl.when(place.not_bottom & (chip < chips - step))
                def _():
                    downward(step, chunk).wait_send()

    hops = [functools.partial(hop, step, chunk) for step in range(1, chips) for chunk in both]
    return [begin] + hops + [end]


def scatter_scratch(ranks, rows, width):
    chips = ranks // 2
    line = [pltpu.SemaphoreType.DMA((chips, CHUNKS))] * 2
    buffers = [pltpu.VMEM((chips, rows, width), BF)] * 5
    return buffers + [pltpu.SemaphoreType.DMA((chips,))] + line * 3


def scatter_steps(
    place, partial, total, kept, pair, held, up_in, down_in, keep_sem,
    up_s, up_r, down_s, down_r, cross_s, cross_r,
):
    chips, chip, core = place.chips, place.chip, place.core
    rows = total.shape[0]
    part = rows // CHUNKS
    up, down, cross = (up_s, up_r), (down_s, down_r), (cross_s, cross_r)
    both = range(CHUNKS)

    def keep(k):
        first = pl.multiple_of((2 * k + core) * rows, rows)
        return pltpu.make_async_copy(partial.at[pl.ds(first, rows)], kept.at[k], keep_sem.at[k])

    def across(k, chunk):
        first = pl.multiple_of((2 * k + 1 - core) * rows + chunk * part, part)
        return remote(
            partial.at[pl.ds(first, part)],
            pair.at[k, pl.ds(chunk * part, part)],
            cross,
            (k, chunk),
            place.partner,
        )

    def upward(step, k, chunk):
        cut = pl.ds(chunk * part, part)
        return remote(held.at[k, cut], up_in.at[step, cut], up, (step, chunk), place.above)

    def downward(step, k, chunk):
        cut = pl.ds(chunk * part, part)
        return remote(held.at[k, cut], down_in.at[step, cut], down, (step, chunk), place.below)

    def add(k, chunk, target, others):
        def strip(i, carry):
            cut = pl.ds(chunk * part + i * STRIP, STRIP)
            value = kept[k, cut].astype(F32) + pair[k, cut].astype(F32)
            for ref, slot in others:
                value = value + ref[slot, cut].astype(F32)
            if target is None:
                total[cut] = value
            else:
                target[k, cut] = value.astype(BF)
            return carry

        lax.fori_loop(0, part // STRIP, strip, 0)

    order = []
    for i in range(chips):
        for k in (chips - 1 - i, i):
            if k not in order:
                order.append(k)
    def begin():
        for k in order:
            keep(k).start()
            for chunk in both:
                across(k, chunk).start()

    def hop(step, chunk):
        @pl.when(place.not_top & (chip <= step - 1))
        def _():
            k = chip + chips - step
            if chunk == 0:
                keep(k).wait()
            across(k, chunk).wait_recv()

            @pl.when(place.not_bottom)
            def _():
                upward(step - 1, k, chunk).wait_recv()
                add(k, chunk, held, [(up_in, step - 1)])

            pl.when(jnp.logical_not(place.not_bottom))(lambda: add(k, chunk, held, []))
            upward(step, k, chunk).start()

        @pl.when(place.not_bottom & (chip >= chips - step))
        def _():
            k = chip - (chips - step)
            if chunk == 0:
                keep(k).wait()
            across(k, chunk).wait_recv()

            @pl.when(place.not_top)
            def _():
                downward(step - 1, k, chunk).wait_recv()
                add(k, chunk, held, [(down_in, step - 1)])

            pl.when(jnp.logical_not(place.not_top))(lambda: add(k, chunk, held, []))
            downward(step, k, chunk).start()

    last = chips - 1

    def add_last(chunk):
        if chunk == 0:
            keep(chip).wait()
        across(chip, chunk).wait_recv()

        @pl.when(place.not_top & place.not_bottom)
        def _():
            upward(last, chip, chunk).wait_recv()
            downward(last, chip, chunk).wait_recv()
            add(chip, chunk, None, [(up_in, last), (down_in, last)])

        @pl.when(jnp.logical_not(place.not_top))
        def _():
            upward(last, chip, chunk).wait_recv()
            add(chip, chunk, None, [(up_in, last)])

        @pl.when(jnp.logical_not(place.not_bottom))
        def _():
            downward(last, chip, chunk).wait_recv()
            add(chip, chunk, None, [(down_in, last)])

    def end():
        for chunk in both:
            for k in range(chips):
                across(k, chunk).wait_send()
            for step in range(1, chips):

                @pl.when(place.not_top & (chip <= step - 1))
                def _():
                    upward(step, chip + chips - step, chunk).wait_send()

                @pl.when(place.not_bottom & (chip >= chips - step))
                def _():
                    downward(step, chip - (chips - step), chunk).wait_send()

    def first():
        begin()
        for chunk in both:
            hop(1, chunk)

    hops = [functools.partial(hop, step, chunk) for step in range(2, chips) for chunk in both]
    return [first] + hops + [functools.partial(add_last, chunk) for chunk in both] + [end]


class Place:
    def __init__(self, ranks, groups):
        rank, group = lax.axis_index("tensor"), lax.axis_index("fsdp")
        self.ranks, self.groups = ranks, groups
        self.chips = ranks // 2
        self.chip, self.core = rank // 2, rank % 2
        self.partner = rank + 1 - 2 * self.core
        self.above, self.below = rank + 2, rank - 2
        self.not_top = self.chip < self.chips - 1
        self.not_bottom = self.chip > 0
        self.rank, self.group = rank, group
        self.device = group * ranks + rank
        near, far = group % 2, group // 2
        self.beside = 2 * far + 1 - near
        self.across = 2 * (1 - far) + near
        self.opposite = 2 * (1 - far) + 1 - near
        self.square = groups == 4

    def name(self, device):
        return {"fsdp": device // self.ranks, "tensor": device % self.ranks}

    def meet(self, line, cross, everyone):
        barrier = pltpu.get_barrier_semaphore()

        def greet(name):
            pl.semaphore_signal(barrier, 1, device_id=name, device_id_type=MESH)

        if everyone:
            devices = self.groups * self.ranks

            def one(i, carry):
                greet(self.name(lax.rem(self.device + i, devices)))
                return carry

            lax.fori_loop(1, devices, one, 0)
            pl.semaphore_wait(barrier, devices - 1)
            return
        peers = 0
        if line:
            greet({"tensor": self.partner})
            pl.when(self.not_top)(lambda: greet({"tensor": self.above}))
            pl.when(self.not_bottom)(lambda: greet({"tensor": self.below}))
            peers = 1 + self.not_top.astype(jnp.int32) + self.not_bottom.astype(jnp.int32)
        if cross and self.square:
            greet({"fsdp": self.beside})
            greet({"fsdp": self.across})
            peers = peers + 2
        elif cross:
            for i in range(1, self.groups):
                greet({"fsdp": lax.rem(self.group + i, self.groups)})
            peers = peers + self.groups - 1
        pl.semaphore_wait(barrier, peers)


def to_group(src, dst, send, recv, at, target):
    return pltpu.make_async_remote_copy(
        src_ref=src,
        dst_ref=dst,
        send_sem=send.at[at],
        recv_sem=recv.at[at],
        device_id={"fsdp": target},
        device_id_type=MESH,
    )


def cross_gather_steps(place, block, whole, own_sem, send, recv):
    group = place.group
    half = block.shape[0] // 2

    def own():
        return pltpu.make_async_copy(block, whole.at[group], own_sem)

    if not place.square:

        def direct(i):
            target = lax.rem(group + i, place.groups)
            return to_group(block, whole.at[group], send, recv, i - 1, target)

        def begin_direct():
            own().start()
            for i in range(1, place.groups):
                direct(i).start()

        def end_direct():
            own().wait()
            for i in range(1, place.groups):
                source = lax.rem(group - i + place.groups, place.groups)
                to_group(block, whole.at[source], send, recv, i - 1, source).wait_recv()
                direct(i).wait_send()

        return [begin_direct, end_direct]

    def near(at):
        return to_group(block, whole.at[group], send, recv, at, (place.beside, place.across)[at])

    def came(at):
        source = (place.beside, place.across)[at]
        return to_group(whole.at[source], whole.at[source], send, recv, at, source)

    def forward(at):
        source, target = ((place.beside, place.across), (place.across, place.beside))[at]
        piece = whole.at[source, pl.ds(at * half, half)]
        return to_group(piece, piece, send, recv, 2 + at, target)

    def far(at):
        piece = whole.at[place.opposite, pl.ds(at * half, half)]
        return to_group(piece, piece, send, recv, 2 + at, place.opposite)

    def begin():
        for at in range(2):
            near(at).start()
        own().start()

    def pass_on():
        for at in range(2):
            came(at).wait_recv()
            forward(at).start()

    def end():
        own().wait()
        for at in range(2):
            far(at).wait_recv()
            near(at).wait_send()
            forward(at).wait_send()

    return [begin] + [nothing] * 5 + [pass_on, end]


def cross_scatter_steps(place, partial, total, mine, near_in, far_in, own_sem, send, recv):
    group = place.group
    rows = total.shape[0]
    half = rows // 2

    def own():
        return pltpu.make_async_copy(partial, mine, own_sem)

    def loop(count, body):
        def strip(i, carry):
            body(pl.ds(i * STRIP, STRIP))
            return carry

        lax.fori_loop(0, count // STRIP, strip, 0)

    if not place.square:

        def direct(i):
            target = lax.rem(group + i, place.groups)
            return to_group(partial.at[target], near_in.at[group], send, recv, i - 1, target)

        def begin_direct():
            own().start()
            for i in range(1, place.groups):
                direct(i).start()

        def sum_direct(cut):
            value = mine[group, cut].astype(F32)
            for i in range(1, place.groups):
                value = value + near_in[lax.rem(group + i, place.groups), cut].astype(F32)
            total[cut] = value

        def end_direct():
            own().wait()
            for i in range(1, place.groups):
                source = lax.rem(group - i + place.groups, place.groups)
                piece = partial.at[source]
                to_group(piece, near_in.at[source], send, recv, i - 1, source).wait_recv()
            loop(rows, sum_direct)
            for i in range(1, place.groups):
                direct(i).wait_send()

        return [begin_direct, end_direct]

    def first(at):
        target = (place.beside, place.across)[at]
        piece = partial.at[place.opposite, pl.ds(at * half, half)]
        return to_group(piece, far_in.at[at], send, recv, at, target)

    def second(at):
        target = (place.beside, place.across)[at]
        return to_group(mine.at[target], near_in.at[at], send, recv, 2 + at, target)

    def begin():
        own().start()
        for at in range(2):
            first(at).start()

    def join():
        own().wait()
        for at in range(2):
            target = (place.across, place.beside)[at]
            first(at).wait_recv()

            def one(cut, at=at, target=target):
                place_in = pl.ds(at * half + cut.start, STRIP)
                value = mine[target, place_in].astype(F32) + far_in[at, cut].astype(F32)
                mine[target, place_in] = value.astype(BF)

            loop(half, one)
            second(1 - at).start()

    def everything(cut):
        value = mine[group, cut].astype(F32) + near_in[0, cut].astype(F32)
        total[cut] = value + near_in[1, cut].astype(F32)

    def end():
        for at in range(2):
            second(at).wait_recv()
        loop(rows, everything)
        for at in range(2):
            first(at).wait_send()
            second(at).wait_send()

    return [begin, nothing, join, nothing, nothing, end]


def everyone_steps(place, piece_for, landing, own_sem, send, recv):
    devices = place.groups * place.ranks
    me = place.device

    def copy(i):
        target = lax.rem(me + i, devices)
        return pltpu.make_async_remote_copy(
            src_ref=piece_for(target),
            dst_ref=landing.at[me],
            send_sem=send.at[i],
            recv_sem=recv.at[i],
            device_id=place.name(target),
            device_id_type=MESH,
        )

    def arrival(i):
        source = lax.rem(me - i + devices, devices)
        return pltpu.make_async_remote_copy(
            src_ref=landing.at[source],
            dst_ref=landing.at[source],
            send_sem=send.at[i],
            recv_sem=recv.at[i],
            device_id=place.name(source),
            device_id_type=MESH,
        )

    def start(i, carry):
        copy(i).start()
        return carry

    def finish_one(i, carry):
        arrival(i).wait_recv()
        copy(i).wait_send()
        return carry

    def own():
        return pltpu.make_async_copy(piece_for(me), landing.at[me], own_sem)

    def begin():
        own().start()
        lax.fori_loop(1, devices, start, 0)

    def end():
        own().wait()
        lax.fori_loop(1, devices, finish_one, 0)

    return [begin, nothing, end]


def spread_steps(place, value, everyone, own_sem, send, recv):
    return everyone_steps(place, lambda target: value, everyone, own_sem, send, recv)


def share_steps(place, values, total, landing, own_sem, send, recv):
    phases = everyone_steps(place, lambda target: values.at[target], landing, own_sem, send, recv)

    def add_up():
        total[...] = jnp.sum(landing[...], axis=0)

    return phases + [add_up]


DMA = pltpu.SemaphoreType.DMA


class Transfers:
    def __init__(self, mesh_size, ident=0, moves=(), needed=()):
        self.ranks, self.groups = mesh_size
        self.ident = ident
        self.kinds = [move[0] for move in moves]
        self.parts = [move[2] if len(move) > 2 else None for move in moves]
        self.inputs = [move[1] for move in moves] + list(needed)
        self.moves = len(self.kinds)
        anywhere = pl.BlockSpec(memory_space=pl.ANY)
        vmem = pl.BlockSpec(memory_space=pltpu.VMEM)
        self.in_specs = [anywhere] * len(self.inputs)
        self.shapes, self.out_specs, self.scratch, self.counts = [], [], [], []
        for kind, array, *part in moves:
            shape, spec = array.shape[len(part[0]) :] if part else array.shape, anywhere
            if kind == "gather":
                shape, dtype = (self.ranks * shape[0], shape[1]), BF
                scratch = gather_scratch(self.ranks)
            elif kind == "scatter":
                shape, dtype, spec = (shape[0] // self.ranks, shape[1]), F32, vmem
                scratch = scatter_scratch(self.ranks, *shape)
            elif kind == "cross_gather":
                shape, dtype = (self.groups,) + shape, BF
                scratch = [DMA, DMA((max(4, self.groups),)), DMA((max(4, self.groups),))]
            elif kind == "cross_scatter":
                rest = shape[1:]
                square = self.groups == 4
                near = (2 if square else self.groups,) + rest
                scratch = [
                    pltpu.VMEM(shape, BF),
                    pltpu.VMEM(near, BF),
                    pltpu.VMEM((2, rest[0] // 2) + rest[1:], BF),
                    DMA,
                    DMA((max(4, self.groups),)),
                    DMA((max(4, self.groups),)),
                ]
                shape, dtype, spec = rest, F32, vmem
            elif kind == "share":
                devices = self.ranks * self.groups
                scratch = [pltpu.VMEM(shape, F32), DMA, DMA((devices,)), DMA((devices,))]
                shape, dtype, spec = shape[1:], F32, vmem
            else:
                devices = self.ranks * self.groups
                shape, dtype = (devices,) + shape, array.dtype
                scratch = [DMA, DMA((devices,)), DMA((devices,))]
            self.shapes.append(jax.ShapeDtypeStruct(shape, dtype))
            self.out_specs.append(spec)
            self.scratch += scratch
            self.counts.append(len(scratch))

    def params(self):
        if not self.moves:
            return pltpu.CompilerParams(vmem_limit_bytes=VMEM_BYTES)
        return pltpu.CompilerParams(
            collective_id=self.ident, has_side_effects=True, vmem_limit_bytes=VMEM_BYTES
        )

    def begin(self, inputs, outputs, scratch):
        if not self.moves:
            return []
        steps_of = {
            "gather": gather_steps,
            "scatter": scatter_steps,
            "cross_gather": cross_gather_steps,
            "cross_scatter": cross_scatter_steps,
            "spread": spread_steps,
            "share": share_steps,
        }
        place = Place(self.ranks, self.groups)
        scratch = list(scratch)
        lines = []
        for i, kind in enumerate(self.kinds):
            taken, scratch = scratch[: self.counts[i]], scratch[self.counts[i] :]
            given = inputs[i] if self.parts[i] is None else inputs[i].at[self.parts[i]]
            lines.append(steps_of[kind](place, given, outputs[i], *taken))

        def phase(number):
            if number == 0:
                kinds = set(self.kinds)
                place.meet(
                    bool(kinds & {"gather", "scatter"}),
                    bool(kinds & {"cross_gather", "cross_scatter"}),
                    bool(kinds & {"spread", "share"}),
                )
            for steps in lines:
                if number < len(steps):
                    steps[number]()

        return [functools.partial(phase, i) for i in range(max(map(len, lines)))]


def nothing():
    pass


def run_all(phases):
    for phase in phases:
        phase()


def exchange_kernel(transfers, *refs):
    count, moves = len(transfers.inputs), transfers.moves
    run_all(transfers.begin(refs[:moves], refs[count : count + moves], refs[count + moves :]))


def exchange(mesh_size, ident, moves, needed=()):
    transfers = Transfers(mesh_size, ident, moves, needed)
    return pl.pallas_call(
        functools.partial(exchange_kernel, transfers),
        out_shape=tuple(transfers.shapes),
        in_specs=transfers.in_specs,
        out_specs=tuple(transfers.out_specs),
        scratch_shapes=transfers.scratch,
        compiler_params=transfers.params(),
    )(*transfers.inputs)


def beside(phases, at, grid_steps, parts):
    step = pl.program_id(0)
    state = None
    for number, part in enumerate(parts):
        for phase, (when, ahead_of) in zip(phases, at):
            if ahead_of == number:
                pl.when(step == when)(phase)
        state = part(state)
    if phases:
        pl.when(step == grid_steps - 1)(lambda: run_all(phases[len(at) :]))


def column(values, at):
    lanes = lax.broadcasted_iota(jnp.int32, values.shape, 1)
    return jnp.sum(jnp.where(lanes == at, values, 0.0), axis=1, keepdims=True)


def routing(experts, length, first_row, rows, router, routes):
    rank = lax.axis_index("tensor")
    logits = dot(rows, router, (1,), (0,))
    lanes = lax.broadcasted_iota(jnp.int32, logits.shape, 1)
    inside = lanes < experts
    top = jnp.max(jnp.where(inside, logits, -1e30), axis=1, keepdims=True)
    exps = jnp.where(inside, jnp.exp(jnp.where(inside, logits, top) - top), 0.0)
    probs = exps / jnp.sum(exps, axis=1, keepdims=True)
    position = first_row + lax.broadcasted_iota(jnp.int32, (rows.shape[0], 1), 0)
    valid = jnp.where(position < length, 1.0, 0.0)
    gate = valid * jax.nn.sigmoid(column(logits, experts))
    chosen = valid * jnp.max(jnp.where(routes == rank, 1.0, 0.0), axis=1, keepdims=True)
    prob = column(probs, rank)
    out = jnp.where(lanes == experts, gate, probs)
    out = jnp.where(lanes == experts + 1, chosen * prob, out)
    out = jnp.where(lanes == experts + 2, chosen, out)
    return jnp.where(lanes == experts + 3, prob, out)


def routing_back(experts, route, shared_dot, expert_dot):
    rank = lax.axis_index("tensor")
    lanes = lax.broadcasted_iota(jnp.int32, route.shape, 1)
    gate, chosen, prob = [column(route, experts + i) for i in (0, 2, 3)]
    expert_grad = chosen * expert_dot
    logits = route * (jnp.where(lanes == rank, expert_grad, 0.0) - expert_grad * prob)
    gate_logit = shared_dot * gate * (1.0 - gate)
    return jnp.where(lanes < experts, logits, jnp.where(lanes == experts, gate_logit, 0.0))


def ffn_kernel(transfers, at, grid_steps, experts, kind, *refs):
    refs = list(refs)

    def take(count):
        taken = refs[:count]
        del refs[:count]
        return taken

    first, last = kind == "first", kind == "last"
    rows_ref, grad_ref, route_ref, w_ref = take(4)
    before = take(1) if first else take(3)
    router_ref = take(1)[0] if first or last else None
    sent = take(len(transfers.inputs))
    hidden_ref, gate_ref, up_ref, out_ref, back_ref, dots_ref = take(6)
    if first:
        made_ref = take(1)[0]
    landed = take(transfers.moves)
    w_vmem, w_sem = take(2)
    phases = transfers.begin(sent, landed, refs)
    step = pl.program_id(0)

    def weights():
        return pltpu.make_async_copy(w_ref, w_vmem, w_sem)

    pl.when(step == 0)(lambda: weights().start())

    def hidden_part(_):
        pl.when(step == 0)(lambda: weights().wait())
        groups, _, depth, units = w_vmem.shape
        gate_w, up_w, down_w = [w_vmem[:, i].reshape(groups * depth, units) for i in range(3)]
        rows, grad = rows_ref[...], grad_ref[...]
        if first:
            length = before[0][0]
            route = routing(experts, length, step * ROW_BLOCK, rows, router_ref[...], route_ref[...])
            made_ref[...] = route
        else:
            route = route_ref[...]
        scale = column(route, experts if first else experts + 1)
        gate_act = dot(rows, gate_w, (1,), (0,))
        up_act = dot(rows, up_w, (1,), (0,))
        back = dot(grad, down_w, (1,), (0,))
        sigmoid = 1.0 / (1.0 + jnp.exp(-gate_act))
        silu = gate_act * sigmoid
        hidden = (silu * up_act).astype(BF).astype(F32)
        dots = jnp.sum(hidden * back, axis=1, keepdims=True)
        scaled = (scale * hidden).astype(BF)
        hidden_ref[...] = scaled
        grad_hidden = scale * back
        grad_gate = (grad_hidden * up_act * (sigmoid * (1.0 + gate_act * (1.0 - sigmoid)))).astype(BF)
        gate_ref[...] = grad_gate
        grad_up = (grad_hidden * silu).astype(BF)
        up_ref[...] = grad_up
        return gate_w, up_w, down_w, scaled, grad_gate, grad_up, route, dots

    def outer_part(state):
        gate_w, up_w, down_w, scaled, grad_gate, grad_up, route, dots = state
        moved = dot(scaled, down_w, (1,), (1,))
        turned = dot(grad_gate, gate_w, (1,), (1,)) + dot(grad_up, up_w, (1,), (1,))
        lanes = lax.broadcasted_iota(jnp.int32, route.shape, 1)
        if first:
            dots_ref[...] = jnp.where(lanes == 0, dots, 0.0)
        else:
            moved = moved + before[0][...].astype(F32)
            turned = turned + before[1][...].astype(F32)
            earlier = before[2][...]
            if last:
                wide = routing_back(experts, route, column(earlier, 0), column(earlier, 1) + dots)
                wide = wide.astype(BF)
                dots_ref[...] = wide
                turned = turned + dot(wide, router_ref[...], (1,), (1,))
            else:
                dots_ref[...] = earlier + jnp.where(lanes == 1, dots, 0.0)
        out_ref[...] = moved.astype(BF)
        back_ref[...] = turned.astype(BF)

    beside(phases, at, grid_steps, [hidden_part, outer_part])


def ffn(experts, kind, rows, grads, route, weights, before, router, transfers, at=()):
    count, width = rows.shape
    units = weights.shape[3]
    first, last = kind == "first", kind == "last"
    steps = count // ROW_BLOCK

    def block(size):
        return pl.BlockSpec((ROW_BLOCK, size), lambda i: (i, 0))

    given = list(before)
    given_specs = [block(width), block(width), block(LANES)]
    if first:
        given_specs = [pl.BlockSpec(memory_space=pltpu.SMEM)]
    if first or last:
        given.append(router)
        given_specs.append(
            pl.BlockSpec(router.shape, lambda i: (0, 0), pipeline_mode=pl.Buffered(1))
        )
    narrow = [jax.ShapeDtypeStruct((count, units), BF)] * 3
    wide = [jax.ShapeDtypeStruct((count, width), BF)] * 2
    dots = [jax.ShapeDtypeStruct((count, LANES), BF if last else F32)]
    dots += [jax.ShapeDtypeStruct((count, LANES), F32)] * first
    results = pl.pallas_call(
        functools.partial(ffn_kernel, transfers, at, steps, experts, kind),
        grid=(steps,),
        in_specs=[block(width), block(width), block(route.shape[1]), pl.BlockSpec(memory_space=pl.ANY)]
        + given_specs
        + transfers.in_specs,
        out_specs=tuple(
            [block(units)] * 3
            + [block(width)] * 2
            + [block(LANES)] * len(dots)
            + transfers.out_specs
        ),
        out_shape=tuple(narrow + wide + dots + transfers.shapes),
        scratch_shapes=[pltpu.VMEM(weights.shape, BF), DMA] + transfers.scratch,
        compiler_params=transfers.params(),
        cost_estimate=pl.CostEstimate(
            flops=12 * count * width * units,
            bytes_accessed=2 * (3 * width * units + 4 * count * width + 3 * count * units),
            transcendentals=count * units,
        ),
    )(rows, grads, route, weights, *given, *transfers.inputs)
    made = 5 + len(dots)
    return results[:3], results[3:made], results[made:]


def ffn_grads_kernel(transfers, at, grid_steps, micros, last, *refs):
    refs = list(refs)

    def take(count):
        taken = refs[:count]
        del refs[:count]
        return taken

    per_micro = [take(6 if last else 5) for _ in range(micros)]
    sent = take(len(transfers.inputs))
    out_ref = take(1)[0]
    wide_ref = take(1)[0] if last else None
    landed = take(transfers.moves)
    phases = transfers.begin(sent, landed, refs)

    def summed(left, right):
        total = None
        for one in per_micro:
            product = dot(one[left][...], one[right][...], (0,), (0,))
            total = product if total is None else total + product
        return total

    def one_product(which):
        def part(_):
            out_ref[0, which] = summed((0, 0, 1)[which], 2 + which).astype(BF)
            if last and which == 2:
                wide_ref[...] = summed(0, 5)

        return part

    beside(phases, at, grid_steps, [one_product(which) for which in range(3)])


def ffn_grads(groups, per_micro, transfers, at=()):
    count, width = per_micro[0][0].shape
    units = per_micro[0][2].shape[1]
    last = len(per_micro[0]) == 6
    depth = width // groups
    columns = pl.BlockSpec((count, depth), lambda i: (0, i))

    def whole(size):
        return pl.BlockSpec((count, size), lambda i: (0, 0), pipeline_mode=pl.Buffered(1))

    shapes = [jax.ShapeDtypeStruct((groups, 3, depth, units), BF)]
    specs = [pl.BlockSpec((1, 3, depth, units), lambda i: (i, 0, 0, 0))]
    taken = [columns, columns] + [whole(units)] * 3
    if last:
        taken.append(whole(LANES))
        shapes.append(jax.ShapeDtypeStruct((width, LANES), F32))
        specs.append(pl.BlockSpec((depth, LANES), lambda i: (i, 0)))
    results = pl.pallas_call(
        functools.partial(ffn_grads_kernel, transfers, at, groups, len(per_micro), last),
        grid=(groups,),
        in_specs=taken * len(per_micro) + transfers.in_specs,
        out_specs=tuple(specs + transfers.out_specs),
        out_shape=tuple(shapes + transfers.shapes),
        scratch_shapes=transfers.scratch,
        compiler_params=transfers.params(),
        cost_estimate=pl.CostEstimate(
            flops=6 * len(per_micro) * count * width * units,
            bytes_accessed=2 * len(per_micro) * (2 * count * width + 3 * count * units)
            + 6 * width * units,
            transcendentals=0,
        ),
    )(*[array for one in per_micro for array in one], *transfers.inputs)
    return results[: len(shapes)], results[len(shapes) :]


def attention_grads_kernel(transfers, grid_steps, micros, *refs):
    refs = list(refs)

    def take(count):
        taken = refs[:count]
        del refs[:count]
        return taken

    per_micro = [take(4) for _ in range(micros)]
    sent = take(len(transfers.inputs))
    out_ref = take(1)[0]
    landed = take(transfers.moves)
    phases = transfers.begin(sent, landed, refs)

    def work(_):
        span = per_micro[0][2].shape[1]
        totals = [None, None]
        for one in per_micro:
            for which in range(2):
                product = dot(one[which][...], one[2 + which][...], (0,), (0,))
                totals[which] = product if totals[which] is None else totals[which] + product
        out_ref[0, :, :span] = totals[0].astype(BF)
        out_ref[0, :, span:] = totals[1].astype(BF)

    beside(phases, [(0, 0)], grid_steps, [work])


def attention_grads(groups, per_micro, transfers):
    count, width = per_micro[0][0].shape
    depth = width // groups
    spans = [per_micro[0][i].shape[1] for i in (2, 3)]
    columns = pl.BlockSpec((count, depth), lambda i: (0, i))
    whole = [
        pl.BlockSpec((count, size), lambda i: (0, 0), pipeline_mode=pl.Buffered(1)) for size in spans
    ]
    results = pl.pallas_call(
        functools.partial(attention_grads_kernel, transfers, groups, len(per_micro)),
        grid=(groups,),
        in_specs=([columns, columns] + whole) * len(per_micro) + transfers.in_specs,
        out_specs=tuple(
            [pl.BlockSpec((1, depth, sum(spans)), lambda i: (i, 0, 0))] + transfers.out_specs
        ),
        out_shape=tuple(
            [jax.ShapeDtypeStruct((groups, depth, sum(spans)), BF)] + transfers.shapes
        ),
        scratch_shapes=transfers.scratch,
        compiler_params=transfers.params(),
        cost_estimate=pl.CostEstimate(
            flops=2 * len(per_micro) * count * width * sum(spans),
            bytes_accessed=8 * len(per_micro) * count * width,
            transcendentals=0,
        ),
    )(*[array for one in per_micro for array in one], *transfers.inputs)
    return results[0], results[1:]


def pack_kernel(cut, gate_ref, up_ref, down_ref, *refs):
    low_ref, high_ref = refs[-2:]
    for out_ref, part in ((low_ref, slice(0, cut)), (high_ref, slice(cut, None))):
        out_ref[0] = gate_ref[0, :, part]
        out_ref[1] = up_ref[0, :, part]
        out_ref[2] = down_ref[0, part, :].T


def pack(cut, gate, up, down, needed):
    _, depth, units = gate.shape
    vmem = pl.BlockSpec(memory_space=pltpu.VMEM)
    return pl.pallas_call(
        functools.partial(pack_kernel, cut),
        in_specs=[vmem] * 3 + [pl.BlockSpec(memory_space=pl.ANY)] * len(needed),
        out_specs=(vmem, vmem),
        out_shape=tuple(
            jax.ShapeDtypeStruct((3, depth, size), BF) for size in (cut, units - cut)
        ),
        compiler_params=pltpu.CompilerParams(vmem_limit_bytes=VMEM_BYTES),
        cost_estimate=pl.CostEstimate(flops=0, bytes_accessed=12 * depth * units, transcendentals=0),
    )(gate, up, down, *needed)


def unpack_kernel(turned, *refs):
    count = len(refs) - 3
    for which, out_ref in enumerate(refs[count:]):
        first = 0
        for ref in refs[:count]:
            values = ref[which].astype(F32)
            if turned[which]:
                values = values.T
                size = min(values.shape[0], out_ref.shape[0] - first)
                out_ref[first : first + size, :] = values[:size]
            else:
                size = min(values.shape[1], out_ref.shape[1] - first)
                out_ref[:, first : first + size] = values[:, :size]
            first += size


def unpack(ranges, units, turned):
    depth = ranges[0].shape[1]
    vmem = pl.BlockSpec(memory_space=pltpu.VMEM)
    return pl.pallas_call(
        functools.partial(unpack_kernel, turned),
        in_specs=[vmem] * len(ranges),
        out_specs=(vmem,) * 3,
        out_shape=tuple(
            jax.ShapeDtypeStruct((units, depth) if turn else (depth, units), F32) for turn in turned
        ),
        compiler_params=pltpu.CompilerParams(vmem_limit_bytes=VMEM_BYTES),
        cost_estimate=pl.CostEstimate(flops=0, bytes_accessed=18 * depth * units, transcendentals=0),
    )(*ranges)


def rope_tables(seq_len):
    half = HD // 2
    frequency = np.float32(ROPE_BASE) ** (-(2.0 * np.arange(half, dtype=np.float32)) / HD)
    angles = np.arange(seq_len, dtype=np.float32)[:, None] * frequency[None, :].astype(np.float32)
    cosine, sine = np.cos(angles.astype(np.float64)), np.sin(angles.astype(np.float64))
    return (
        jnp.asarray(np.concatenate([cosine, cosine], axis=1).astype(np.float32)),
        jnp.asarray(np.concatenate([-sine, sine], axis=1).astype(np.float32)),
    )


def swap_halves(values):
    half = HD // 2
    return jnp.concatenate([values[:, half:], values[:, :half]], axis=1)


def block_weights(query, keys, first_row, length):
    scores = dot(query, keys, (1,), (1,)) * (HD ** (-0.5))
    rows = first_row + lax.broadcasted_iota(jnp.int32, scores.shape, 0)
    cols = lax.broadcasted_iota(jnp.int32, scores.shape, 1)
    scores = jnp.where((cols <= rows) & (cols < length), scores, -1e30)
    exps = jnp.exp(scores - jnp.max(scores, axis=1, keepdims=True))
    return exps / jnp.sum(exps, axis=1, keepdims=True)


def attend_kernel(heads, transfers, *refs):
    refs = list(refs)

    def take(count):
        taken = refs[:count]
        del refs[:count]
        return taken

    length_ref, x_ref, gain_ref, w_ref, bias_ref, cos_ref, sin_ref = take(7)
    sent = take(len(transfers.inputs))
    normed_ref, qkv_ref, mixed_ref, out_ref = take(4)
    landed = take(transfers.moves)
    rows_vmem, out_vmem, in_sem, normed_sem, out_sem = take(5)
    phases = transfers.begin(sent, landed, refs)
    seq_len, width = x_ref.shape
    groups, depth, columns = w_ref.shape
    span = heads * HD
    length = length_ref[0]
    blocks = [pl.ds(row, QB) for row in range(0, seq_len, QB)]

    def fetch(i):
        return pltpu.make_async_copy(x_ref.at[blocks[i]], rows_vmem.at[blocks[i]], in_sem.at[i])

    def keep(i):
        return pltpu.make_async_copy(rows_vmem.at[blocks[i]], normed_ref.at[blocks[i]], normed_sem.at[i])

    def give(i):
        return pltpu.make_async_copy(out_vmem.at[blocks[i]], out_ref.at[blocks[i]], out_sem.at[i])

    for i in range(len(blocks)):
        fetch(i).start()
    run_all(phases[:1])
    weights = w_ref[...].reshape(groups * depth, columns)
    qkv_w, out_w = weights[:, : 3 * span], weights[:, 3 * span :]
    for i in range(len(blocks)):
        row, end = i * QB, (i + 1) * QB
        if i >= 2:
            run_all(phases[i - 1 : i])
        fetch(i).wait()
        values = rows_vmem[row:end, :].astype(F32)
        normed = (normalize(values)[0] * gain_ref[...]).astype(BF)
        rows_vmem[row:end, :] = normed
        keep(i).start()
        pre = dot(normed, qkv_w, (1,), (0,)) + bias_ref[...]
        cosine, sine = cos_ref[row:end, :], sin_ref[row:end, :]
        for at in range(0, 3 * span, HD):
            part = pre[:, at : at + HD]
            if at < 2 * span:
                part = part * cosine + swap_halves(part) * sine
            qkv_ref[row:end, at : at + HD] = part.astype(BF)
        for head in range(heads):
            q_at, k_at, v_at = (head * HD, span + head * HD, 2 * span + head * HD)
            shares = block_weights(
                qkv_ref[row:end, q_at : q_at + HD], qkv_ref[:end, k_at : k_at + HD], row, length
            )
            mixed = dot(shares.astype(BF), qkv_ref[:end, v_at : v_at + HD], (1,), (0,))
            mixed_ref[row:end, q_at : q_at + HD] = mixed.astype(BF)
        out_vmem[row:end, :] = dot(mixed_ref[row:end, :], out_w, (1,), (1,)).astype(BF)
        give(i).start()
    run_all(phases[max(1, len(blocks) - 1) :])
    for i in range(len(blocks)):
        keep(i).wait()
        give(i).wait()


def attend_back_kernel(heads, transfers, *refs):
    refs = list(refs)

    def take(count):
        taken = refs[:count]
        del refs[:count]
        return taken

    length_ref, datt_ref, w_ref, qkv_ref, cos_ref, sin_ref = take(6)
    sent = take(len(transfers.inputs))
    turned_ref, sums_ref, out_ref = take(3)
    landed = take(transfers.moves)
    rows_vmem, out_vmem, grad_vmem, key_acc, value_acc, in_sem, out_sem = take(7)
    phases = transfers.begin(sent, landed, refs)
    run_all(phases[:1])
    seq_len, width = datt_ref.shape
    groups, depth, columns = w_ref.shape
    span = heads * HD
    length = length_ref[0]
    scale = HD ** (-0.5)
    blocks = [pl.ds(row, QB) for row in range(0, seq_len, QB)]

    def fetch(i):
        return pltpu.make_async_copy(datt_ref.at[blocks[i]], rows_vmem.at[blocks[i]], in_sem.at[i])

    def give(i):
        return pltpu.make_async_copy(out_vmem.at[blocks[i]], out_ref.at[blocks[i]], out_sem.at[i])

    for i in range(len(blocks)):
        fetch(i).start()
    weights = w_ref[...].reshape(groups * depth, columns)
    qkv_w, out_w = weights[:, : 3 * span], weights[:, 3 * span :]
    key_acc[...] = jnp.zeros_like(key_acc)
    value_acc[...] = jnp.zeros_like(value_acc)
    query_sums = [jnp.zeros((1, HD), F32) for _ in range(heads)]
    for i in range(len(blocks)):
        row, end = i * QB, (i + 1) * QB
        fetch(i).wait()
        grad_vmem[row:end, :] = dot(rows_vmem[row:end, :], out_w, (1,), (0,)).astype(BF)
        for head in range(heads):
            q_at, k_at, v_at = (head * HD, span + head * HD, 2 * span + head * HD)
            query = qkv_ref[row:end, q_at : q_at + HD]
            keys = qkv_ref[:end, k_at : k_at + HD]
            grad = grad_vmem[row:end, q_at : q_at + HD]
            shares = block_weights(query, keys, row, length)
            grad_shares = dot(grad, qkv_ref[:end, v_at : v_at + HD], (1,), (1,))
            inner = jnp.sum(shares * grad_shares, axis=1, keepdims=True)
            grad_scores = (scale * shares * (grad_shares - inner)).astype(BF)
            turned = dot(grad_scores, keys, (1,), (0,))
            grad_query = (
                turned * cos_ref[row:end, :] - swap_halves(turned) * sin_ref[row:end, :]
            ).astype(BF)
            turned_ref[row:end, q_at : q_at + HD] = grad_query
            query_sums[head] += jnp.sum(grad_query.astype(F32), axis=0, keepdims=True)
            key_acc[:end, q_at : q_at + HD] += dot(grad_scores, query, (0,), (0,))
            value_acc[:end, q_at : q_at + HD] += dot(shares.astype(BF), grad, (0,), (0,))
    key_sums = [jnp.zeros((1, HD), F32) for _ in range(heads)]
    value_sums = [jnp.zeros((1, HD), F32) for _ in range(heads)]
    for i in range(len(blocks)):
        row, end = i * QB, (i + 1) * QB
        for head in range(heads):
            q_at, k_at, v_at = (head * HD, span + head * HD, 2 * span + head * HD)
            turned = key_acc[row:end, q_at : q_at + HD]
            grad_key = (
                turned * cos_ref[row:end, :] - swap_halves(turned) * sin_ref[row:end, :]
            ).astype(BF)
            grad_value = value_acc[row:end, q_at : q_at + HD].astype(BF)
            turned_ref[row:end, k_at : k_at + HD] = grad_key
            turned_ref[row:end, v_at : v_at + HD] = grad_value
            key_sums[head] += jnp.sum(grad_key.astype(F32), axis=0, keepdims=True)
            value_sums[head] += jnp.sum(grad_value.astype(F32), axis=0, keepdims=True)
        out_vmem[row:end, :] = dot(turned_ref[row:end, :], qkv_w, (1,), (1,)).astype(BF)
        give(i).start()
    for at, sums in enumerate(query_sums + key_sums + value_sums):
        sums_ref[:, at * HD : (at + 1) * HD] = sums
    for i in range(len(blocks)):
        give(i).wait()
    run_all(phases[1:])


def in_vmem(count):
    return [pl.BlockSpec(memory_space=pltpu.VMEM)] * count


def attend(length, rows, gain, weights, bias, cosine, sine, transfers):
    seq_len, width = rows.shape
    span = weights.shape[2] // 4
    heads, blocks = span // HD, seq_len // QB
    anywhere = pl.BlockSpec(memory_space=pl.ANY)
    results = pl.pallas_call(
        functools.partial(attend_kernel, heads, transfers),
        out_shape=tuple(
            [
                jax.ShapeDtypeStruct((seq_len, width), BF),
                jax.ShapeDtypeStruct((seq_len, 3 * span), BF),
                jax.ShapeDtypeStruct((seq_len, span), BF),
                jax.ShapeDtypeStruct((seq_len, width), BF),
            ]
            + transfers.shapes
        ),
        in_specs=[pl.BlockSpec(memory_space=pltpu.SMEM), anywhere] + in_vmem(5) + transfers.in_specs,
        out_specs=tuple([anywhere] + in_vmem(2) + [anywhere] + transfers.out_specs),
        scratch_shapes=[pltpu.VMEM((seq_len, width), BF)] * 2
        + [DMA((blocks,))] * 3
        + transfers.scratch,
        compiler_params=transfers.params(),
        cost_estimate=pl.CostEstimate(
            flops=8 * seq_len * width * span + 3 * span * seq_len * seq_len,
            bytes_accessed=8 * seq_len * width,
            transcendentals=heads * seq_len * seq_len,
        ),
    )(length, rows, gain, weights, bias, cosine, sine, *transfers.inputs)
    return results[:4], results[4:]


def attend_back(length, rows, weights, qkv, cosine, sine, transfers):
    seq_len, width = rows.shape
    span = weights.shape[2] // 4
    heads, blocks = span // HD, seq_len // QB
    anywhere = pl.BlockSpec(memory_space=pl.ANY)
    results = pl.pallas_call(
        functools.partial(attend_back_kernel, heads, transfers),
        out_shape=tuple(
            [
                jax.ShapeDtypeStruct((seq_len, 3 * span), BF),
                jax.ShapeDtypeStruct((1, 3 * span), F32),
                jax.ShapeDtypeStruct((seq_len, width), BF),
            ]
            + transfers.shapes
        ),
        in_specs=[pl.BlockSpec(memory_space=pltpu.SMEM), anywhere] + in_vmem(4) + transfers.in_specs,
        out_specs=tuple(in_vmem(2) + [anywhere] + transfers.out_specs),
        scratch_shapes=[pltpu.VMEM((seq_len, width), BF)] * 2
        + [pltpu.VMEM((seq_len, span), BF)]
        + [pltpu.VMEM((seq_len, span), F32)] * 2
        + [DMA((blocks,))] * 2
        + transfers.scratch,
        compiler_params=transfers.params(),
        cost_estimate=pl.CostEstimate(
            flops=8 * seq_len * width * span + 8 * span * seq_len * seq_len,
            bytes_accessed=8 * seq_len * width,
            transcendentals=heads * seq_len * seq_len,
        ),
    )(length, rows, weights, qkv, cosine, sine, *transfers.inputs)
    return results[:3], results[3:]


def padded(values, axis):
    size = values.shape[axis]
    more = -size % LANES
    if not more:
        return values
    return jnp.pad(values, [(0, more if i == axis else 0) for i in range(values.ndim)])


def packed(values, kind):
    tile = LANES * (16 if kind == BF else 8)
    values = values.astype(kind)
    return padded_to(values, -(-values.shape[-1] // tile) * tile)


def padded_to(values, size):
    more = size - values.shape[-1]
    return jnp.pad(values, [(0, 0)] * (values.ndim - 1) + [(0, more)])


def local(
    tokens,
    lengths,
    routes,
    norm1_gain,
    w_query,
    w_key,
    w_value,
    b_query,
    b_key,
    b_value,
    w_out,
    norm2_gain,
    router,
    shared_gate_vec,
    shared_gate,
    shared_up,
    shared_down,
    expert_gate,
    expert_up,
    expert_down,
    cotangent,
):
    ranks = lax.axis_size("tensor")
    groups = lax.axis_size("fsdp")
    rank = lax.axis_index("tensor")
    micros, _, rows, width = tokens.shape
    seq_len = rows * ranks
    heads = w_query.shape[1] // HD
    span = heads * HD
    experts = ranks * expert_gate.shape[0]
    shared_units = shared_gate.shape[1]
    expert_units = expert_gate.shape[2]
    cut = expert_units // (2 * LANES) * LANES
    own_first = rank * rows
    local_pos = own_first + jnp.arange(rows, dtype=jnp.int32)

    per_device = norm1_gain.shape[0]
    small = jnp.concatenate(
        [
            norm1_gain,
            norm2_gain,
            shared_gate_vec,
            router.reshape(-1),
            b_query.reshape(-1),
            b_key.reshape(-1),
            b_value.reshape(-1),
        ]
    )
    attn_own = jnp.concatenate([w_query, w_key, w_value, w_out.T], axis=1)
    mesh_size = (ranks, groups)
    rows_a, attn_w, small_all = exchange(
        mesh_size,
        2,
        [
            ("gather", tokens, (0, 0)),
            ("cross_gather", attn_own),
            ("spread", packed(small, BF).reshape(-1, LANES)),
        ],
    )
    small_all = small_all.reshape(groups * ranks, -1)
    gain_one = small_all[:, :per_device].reshape(-1).astype(F32)
    gain_two = small_all[:, per_device : 2 * per_device].reshape(-1).astype(F32)
    gate_vec = small_all[:, 2 * per_device : 3 * per_device].reshape(-1)
    bias_at = per_device * (3 + experts)
    router_full = small_all[:, 3 * per_device : bias_at].reshape(width, experts)
    router_wide = padded_to(jnp.concatenate([router_full, gate_vec[:, None]], axis=1), LANES)
    own_bias = lax.dynamic_index_in_dim(
        small_all.reshape(groups, ranks, -1), rank, 1, False
    )[:, bias_at : small.shape[0]].reshape(groups, 3, heads, HD // groups)
    bias = own_bias.transpose(1, 2, 0, 3).reshape(1, 3 * span).astype(F32)

    def over_fsdp(packed_range):
        return lax.all_gather(packed_range, "fsdp", axis=0)

    low, high = pack(cut, expert_gate, expert_up, expert_down, [small_all])
    weights = [
        over_fsdp(jnp.stack([padded(shared_gate, 1), padded(shared_up, 1), padded(shared_down.T, 1)])),
        over_fsdp(low),
        over_fsdp(high),
    ]

    cosine, sine = rope_tables(seq_len)
    idle = Transfers(mesh_size)
    token_own = [tokens[m, 0] for m in range(micros)]
    grads_own = []
    for m in range(micros):
        inside = (local_pos < lengths[m, 0])[:, None]
        grads_own.append(jnp.where(inside, cotangent[m, 0], jnp.zeros((), BF)))

    def moving(ident, *moves, needed=()):
        return Transfers(mesh_size, ident, moves, needed)

    def attention(m, token_rows, transfers):
        return attend(lengths[m], token_rows, gain_one[None], attn_w, bias, cosine, sine, transfers)

    def second_norm(m, attended):
        hidden = token_own[m].astype(F32) + attended
        unit, inverse = normalize(hidden)
        return hidden, unit, inverse, (unit * gain_two).astype(BF)

    def second_norm_back(m, state, summed):
        grad_hidden, gain_part = norm_back(summed, state[1], state[2], gain_two)
        grad_hidden = grad_hidden + grads_own[m].astype(F32)
        return grad_hidden, grad_hidden.astype(BF), gain_part

    def first_norm_back(m, grad_hidden, summed):
        unit, inverse = normalize(token_own[m].astype(F32))
        grad_inputs, gain_part = norm_back(summed, unit, inverse, gain_one)
        return (grad_inputs + grad_hidden).astype(BF), gain_part

    def finished(m, hidden, moved):
        inside = (local_pos < lengths[m, 0]).astype(F32)[:, None]
        return (inside * (hidden + moved)).astype(BF)

    att_a, (rows_b,) = attention(0, rows_a, moving(3, ("gather", tokens, (1, 0))))
    grad_a, sum_a = exchange(
        mesh_size, 4, [("gather", cotangent, (0, 0)), ("scatter", att_a[3])]
    )
    norm_a = second_norm(0, sum_a)
    att_b, (two_a,) = attention(1, rows_b, moving(5, ("gather", norm_a[3])))

    def over_groups(grads):
        flat = grads.reshape(-1, grads.shape[-1])
        summed = lax.psum_scatter(flat, "fsdp", scatter_dimension=0, tiled=True)
        return with_layout_constraint(summed, Layout((0, 1))).reshape(grads.shape[1:])

    def grads_of(which, transfers, at=()):
        per_micro = []
        for key in range(micros):
            rows_two, grads = ((two_a, grad_a), (two_b, grad_b))[key]
            scaled, gate, up = act[which, key]
            more = [(acc_a, acc_b)[key][2]] if which == 2 else []
            per_micro.append([rows_two, grads, gate, up, scaled] + more)
        return ffn_grads(groups, per_micro, transfers, at)

    act = {}
    part = functools.partial(ffn, experts)
    single = ((0, 0), (1, 0), (2, 0), (3, 0))
    act[0, 0], acc_a, (grad_b, sum_b) = part(
        "first", two_a, grad_a, routes[0, 0], weights[0], [lengths[0]], router_wide,
        moving(6, ("gather", cotangent, (1, 0)), ("scatter", att_b[3])), ((0, 0), (1, 1), (3, 0)),
    )
    acc_a, route_a = acc_a[:3], acc_a[3]
    norm_b = second_norm(1, sum_b)
    act[1, 0], acc_a, (two_b,) = part(
        "next", two_a, grad_a, route_a, weights[1], acc_a, None,
        moving(7, ("gather", norm_b[3])), single,
    )
    act[0, 1], acc_b, _ = part(
        "first", two_b, grad_b, routes[1, 0], weights[0], [lengths[1]], router_wide, idle
    )
    acc_b, route_b = acc_b[:3], acc_b[3]
    (grads_0,), _ = grads_of(0, idle)
    range_0 = over_groups(grads_0)
    act[2, 0], acc_a, _ = part(
        "last", two_a, grad_a, route_a, weights[2], acc_a, router_wide, moving(0, needed=[grads_0])
    )
    act[1, 1], acc_b, (down_a,) = part(
        "next", two_b, grad_b, route_b, weights[1], acc_b, None,
        moving(8, ("scatter", acc_a[1])), single,
    )
    hid_a, send_a, gain_part_a = second_norm_back(0, norm_a, down_a)
    (grads_1,), (datt_a,) = grads_of(
        1, moving(9, ("gather", send_a)), ((0, 0), (1, 0), (2, 0), (3, 0))
    )
    range_1 = over_groups(grads_1)
    (grad_qkv_a, sums_a, first_a), _ = attend_back(
        lengths[0], datt_a, attn_w, att_a[1], cosine, sine, moving(0, needed=[grads_1])
    )
    act[2, 1], acc_b, (one_a,) = part(
        "last", two_b, grad_b, route_b, weights[2], acc_b, router_wide,
        moving(10, ("scatter", first_a)), single,
    )
    (grads_2, total_wide), (down_b,) = grads_of(
        2, moving(11, ("scatter", acc_b[1]), needed=[range_0]), ((0, 0), (1, 1), (2, 1), (3, 1))
    )
    range_2 = over_groups(grads_2)
    hid_b, send_b, gain_part_b = second_norm_back(1, norm_b, down_b)
    datt_b, moved_a = exchange(mesh_size, 12, [("gather", send_b), ("scatter", acc_a[0])])
    (grad_qkv_b, sums_b, first_b), _ = attend_back(
        lengths[1], datt_b, attn_w, att_b[1], cosine, sine, idle
    )
    attn_parts, (one_b,) = attention_grads(
        groups,
        [
            (att_a[0], datt_a, grad_qkv_a, att_a[2]),
            (att_b[0], datt_b, grad_qkv_b, att_b[2]),
        ],
        moving(13, ("scatter", first_b), needed=[range_1]),
    )

    grad_in_a, one_part_a = first_norm_back(0, hid_a, one_a)
    grad_in_b, one_part_b = first_norm_back(1, hid_b, one_b)

    devices = groups * ranks
    bias_part = (sums_a + sums_b).reshape(3, heads, groups, HD // groups).transpose(2, 0, 1, 3)
    bias_part = bias_part.reshape(groups, 1, -1)
    own_rank = (jnp.arange(ranks, dtype=jnp.int32) == rank).astype(F32)[None, :, None]
    parts = jnp.concatenate(
        [
            (one_part_a + one_part_b).reshape(devices, -1),
            (gain_part_a + gain_part_b).reshape(devices, -1),
            total_wide[:, : experts + 1].reshape(devices, -1),
            (bias_part * own_rank).reshape(devices, -1),
        ],
        axis=1,
    )
    moved_b, attn_g, shares = exchange(
        mesh_size,
        14,
        [
            ("scatter", acc_b[0]),
            ("cross_scatter", attn_parts),
            ("share", packed(parts, F32).reshape(devices, -1, LANES)),
        ],
        [range_2],
    )
    shares = shares.reshape(-1)
    wide_g = shares[2 * per_device : (3 + experts) * per_device].reshape(per_device, experts + 1)
    bias_g = shares[bias_at : parts.shape[1]].reshape(3, heads, HD // groups)

    shared_g = unpack([range_0], shared_units, (True, True, True))
    expert_g = unpack([range_1, range_2], expert_units, (False, False, True))
    return (
        jnp.stack([finished(0, norm_a[0], moved_a), finished(1, norm_b[0], moved_b)])[:, None],
        jnp.stack([grad_in_a, grad_in_b])[:, None],
        shares[:per_device],
        attn_g[:, :span],
        attn_g[:, span : 2 * span],
        attn_g[:, 2 * span : 3 * span],
        bias_g[0],
        bias_g[1],
        bias_g[2],
        attn_g[:, 3 * span :].T,
        shares[per_device : 2 * per_device],
        wide_g[:, :experts],
        wide_g[:, experts],
        shared_g[0].T,
        shared_g[1].T,
        shared_g[2],
        expert_g[0][None],
        expert_g[1][None],
        expert_g[2][None],
    )


def solution(mesh):
    in_specs = (
        P(None, "fsdp", "tensor", None),
        P(None, "fsdp"),
        P(None, "fsdp", None, None),
        P(("fsdp", "tensor")),
        P("fsdp", "tensor"),
        P("fsdp", "tensor"),
        P("fsdp", "tensor"),
        P("tensor", "fsdp"),
        P("tensor", "fsdp"),
        P("tensor", "fsdp"),
        P("tensor", "fsdp"),
        P(("fsdp", "tensor")),
        P(("fsdp", "tensor"), None),
        P(("fsdp", "tensor")),
        P("fsdp", "tensor"),
        P("fsdp", "tensor"),
        P("tensor", "fsdp"),
        P("tensor", "fsdp", None),
        P("tensor", "fsdp", None),
        P("tensor", None, "fsdp"),
        P(None, "fsdp", "tensor", None),
    )
    out_specs = (
        P(None, "fsdp", "tensor", None),
        P(None, "fsdp", "tensor", None),
        P(("fsdp", "tensor")),
        P("fsdp", "tensor"),
        P("fsdp", "tensor"),
        P("fsdp", "tensor"),
        P("tensor", "fsdp"),
        P("tensor", "fsdp"),
        P("tensor", "fsdp"),
        P("tensor", "fsdp"),
        P(("fsdp", "tensor")),
        P(("fsdp", "tensor"), None),
        P(("fsdp", "tensor")),
        P("fsdp", "tensor"),
        P("fsdp", "tensor"),
        P("tensor", "fsdp"),
        P("tensor", "fsdp", None),
        P("tensor", "fsdp", None),
        P("tensor", None, "fsdp"),
    )
    return jax.shard_map(local, mesh=mesh, in_specs=in_specs, out_specs=out_specs, check_vma=False)
```

time: 895 us -> 891 us (level)
  Pallas kernels: 745 us -> 814 us
  matrix products: 33.4 us -> 0 us
  other arithmetic: 50 us -> 28.9 us
  local copies, waits for them, and re-layouts: 46.4 us -> 26.3 us
    pallas_call x8, Pallas kernels: 64.8 us -> 184 us  [the longest x2 84.9 us: attend(): pl.pallas_call(functools.partial(attend_kernel, heads, transfers), out_sh...]
    pallas_call x3, Pallas kernels: 165 us -> 123 us  [ffn_grads(): pl.pallas_call(functools.partial(ffn_grads_kernel, transfers, at, groups,...]
    dot_general x8 -> x0, matrix products: 33.4 us -> none  [dot(): lax.dot_general(left, right, ((left_dims, right_dims), ((), ())), preferr...]
    unnamed x140 -> x72, local copies, waits for them, and re-layouts: 23.8 us -> 11.2 us
  transfers between devices with their start and end apart: 6 -> 6, of which waited for: 0 -> 0; matrix products, arithmetic and copies ran while one was open for 12% -> 4% of each run, Pallas kernels for 79% -> 86%
where the time goes in v4:
time: 891 us; the launch traced here: 886 us
  Pallas kernels  814 us (91%)
  other arithmetic  28.9 us (3%)
  local copies, waits for them, and re-layouts  26.3 us (3%)
  between operations  15 us (2%)
    pallas_call x6, Pallas kernels, ffn(): pl.pallas_call(functools.partial(ffn_kernel, transfers, at, steps, expert...  259 us
    pallas_call x4, Pallas kernels, exchange(): pl.pallas_call(functools.partial(exchange_kernel, transfers), out_shape=t...  249 us
    pallas_call x3, Pallas kernels, ffn_grads(): pl.pallas_call(functools.partial(ffn_grads_kernel, transfers, at, groups,...  123 us
    pallas_call x2, Pallas kernels, attend(): pl.pallas_call(functools.partial(attend_kernel, heads, transfers), out_sh...  84.9 us
    pallas_call x1, Pallas kernels, attention_grads(): pl.pallas_call(functools.partial(attention_grads_kernel, transfers, group...  43.6 us
    pallas_call x2, Pallas kernels, attend_back(): pl.pallas_call(functools.partial(attend_back_kernel, heads, transfers), o...  39.9 us
  transfers between devices with their start and end apart: 6, of which 0 were waited for; matrix products, arithmetic and copies ran while one was open for 4% of the time, Pallas kernels for 86%

profile of v4, /device:TPU:0, one launch (start us, length us, event | category | flops | bytes accessed | tf_op | source)
XLA Modules:
  0.0 885.6 jit_solution(14608568865305632424)
XLA Ops:
  7.3 1.5 copy.96
  9.6 1.7 pad_maximum_fusion
  13.2 1.1 pad_maximum_fusion.1.refs_1_
  14.3 95.0 %shard_map.366 = (bf16[1024,2048]{1,0:T(8,128)(2,1)}, bf16[4,512,1024]{2,1,0:T(8,128)(2,1)}, bf16[32,16,128]{2,1,0:T(8,128)(2,1)}) custom-call(bf16[2,1,128,2048]{3,2,1,0:T(8,128)(2,1)} %refs_7_.1, bf16[512,1024]{1,0:T(8,128)(2,1)} %pad_maximum_fusion.1.refs_1_, bf16[16,128]{1,0:T(8,128)(2,1)} %pad_bitcast_fusion.3.refs_2_), custom_call_target="tpu_custom_call" | custom-call | tf_op jit(solution)/shard_map/pallas_call | solution.py:684
  109.4 1.6 copy.114
  111.0 4.8 shard_map.371
  116.5 0.9 slice.131
  117.5 1.0 copy.108
  118.5 1.0 copy.107
  122.7 1.1 broadcast_in_dim_reshape.4
  124.4 42.4 %shard_map.367 = (bf16[1024,2048]{1,0:T(8,128)(2,1)}, bf16[1024,768]{1,0:T(8,128)(2,1)}, bf16[1024,256]{1,0:T(8,128)(2,1)}, bf16[1024,2048]{1,0:T(8,128)(2,1)}, bf16[1024,2048]{1,0:T(8,128)(2,1)}) custom-call(s32[1]{0:T(128)} %bitcast.2.refs_0_.refs_4_, bf16[1024,2048]{1,0:T(8,128)(2,1)} %get-tuple-element.103.refs_1_, f32[1,2048]{1,0:T(1,128)} %reshape.253.refs_2_, ...), custom_call_target="tpu_custom_call" | custom-call | flops 5100273664 | bytes 16777216 | tf_op jit(solution)/shard_map/pallas_call | solution.py:1222
  166.8 52.2 %shard_map.368 = (bf16[1024,2048]{1,0:T(8,128)(2,1)}, f32[128,2048]{1,0:T(8,128)}) custom-call(bf16[2,1,128,2048]{3,2,1,0:T(8,128)(2,1)} %refs_6_.3, bf16[1024,2048]{1,0:T(8,128)(2,1)} %get-tuple-element.106.refs_1_), custom_call_target="tpu_custom_call" | custom-call | tf_op jit(solution)/shard_map/pallas_call | solution.py:684
  219.0 2.1 fusion.19
  221.2 1.2 fusion.24.refs_5_.refs_7_
  222.3 0.9 multiply_convert_fusion.3.refs_7_
  223.3 42.4 %shard_map.369 = (bf16[1024,2048]{1,0:T(8,128)(2,1)}, bf16[1024,768]{1,0:T(8,128)(2,1)}, bf16[1024,256]{1,0:T(8,128)(2,1)}, bf16[1024,2048]{1,0:T(8,128)(2,1)}, bf16[1024,2048]{1,0:T(8,128)(2,1)}) custom-call(s32[1]{0:T(128)} %bitcast.8.refs_0_.refs_4_, bf16[1024,2048]{1,0:T(8,128)(2,1)} %get-tuple-element.108.refs_1_, f32[1,2048]{1,0:T(1,128)} %reshape.253.refs_2_, ...), custom_call_target="tpu_custom_call" | custom-call | flops 5100273664 | bytes 16777216 | tf_op jit(solution)/shard_map/pallas_call | solution.py:1222
  265.7 65.9 %shard_map.370 = (bf16[1024,768]{1,0:T(8,128)(2,1)}, bf16[1024,768]{1,0:T(8,128)(2,1)}, bf16[1024,768]{1,0:T(8,128)(2,1)}, bf16[1024,2048]{1,0:T(8,128)(2,1)}, b...) custom-call(bf16[1024,2048]{1,0:T(8,128)(2,1)} %get-tuple-element.10, ...), custom_call_target="tpu_custom_call" | custom-call | flops 19327352832 | bytes 30932992 | tf_op jit(solution)/shard_map/pallas_call | solution.py:840
  331.6 1.4 multiply_reduce_fusion.4
  333.1 0.9 copy-done
  334.1 0.9 multiply_convert_fusion.2.refs_7_
  335.0 41.3 %shard_map.372 = (bf16[1024,640]{1,0:T(8,128)(2,1)}, bf16[1024,640]{1,0:T(8,128)(2,1)}, bf16[1024,640]{1,0:T(8,128)(2,1)}, bf16[1024,2048]{1,0:T(8,128)(2,1)}, b...) custom-call(bf16[1024,2048]{1,0:T(8,128)(2,1)} %get-tuple-element.109.refs_0_, ...), custom_call_target="tpu_custom_call" | custom-call | flops 16106127360 | bytes 28573696 | tf_op jit(solution)/shard_map/pallas_call | solution.py:840
  376.4 29.6 %shard_map.373 = (bf16[1024,768]{1,0:T(8,128)(2,1)}, bf16[1024,768]{1,0:T(8,128)(2,1)}, bf16[1024,768]{1,0:T(8,128)(2,1)}, bf16[1024,2048]{1,0:T(8,128)(2,1)}, b...) custom-call(bf16[1024,2048]{1,0:T(8,128)(2,1)} %get-tuple-element.125.refs_0_.refs_5_.refs_6_, ...), custom_call_target="tpu_custom_call" | custom-call | flops 19327352832 | bytes 30932992 | tf_op jit(solution)/shard_map/pallas_call | solution.py:840
  406.0 27.2 %shard_map.374.refs_8_ = bf16[4,3,512,768]{3,2,1,0:T(8,128)(2,1)} custom-call(bf16[1024,2048]{1,0:T(8,128)(2,1)} %get-tuple-element.109.refs_0_, bf16[1024,2048]{1,0:T(8,128)(2,1)} %get-tuple-element.110.refs_1_, bf16[1024,768]{1,0:T(8,128)(2,1)} %get-tuple-element.122.refs_2_, bf16[1024,768]{1,0:T(8,128)(2,1)} %get-tuple-element.123.refs_3_, ...), custom_call_target="tpu_custom_call" | custom-call | flops 19327352832 | bytes 35651584 | tf_op jit(solution)/shard_map/pallas_call | solution.py:915
  433.9 33.5 %shard_map.375 = (bf16[1024,768]{1,0:T(8,128)(2,1)}, bf16[1024,768]{1,0:T(8,128)(2,1)}, bf16[1024,768]{1,0:T(8,128)(2,1)}, bf16[1024,2048]{1,0:T(8,128)(2,1)}, b...) custom-call(bf16[1024,2048]{1,0:T(8,128)(2,1)} %get-tuple-element.109.refs_0_, ...), custom_call_target="tpu_custom_call" | custom-call | flops 19327352832 | bytes 30932992 | tf_op jit(solution)/shard_map/pallas_call | solution.py:840
  467.4 43.6 %shard_map.376 = (bf16[1024,640]{1,0:T(8,128)(2,1)}, bf16[1024,640]{1,0:T(8,128)(2,1)}, bf16[1024,640]{1,0:T(8,128)(2,1)}, bf16[1024,2048]{1,0:T(8,128)(2,1)}, b...) custom-call(bf16[1024,2048]{1,0:T(8,128)(2,1)} %get-tuple-element.125.refs_0_.refs_5_.refs_6_, ...), custom_call_target="tpu_custom_call" | custom-call | flops 16106127360 | bytes 28573696 | tf_op jit(solution)/shard_map/pallas_call | solution.py:840
  511.0 1.9 multiply_reduce_fusion.1
  513.1 1.5 fusion.35
  514.6 47.2 %shard_map.377 = (bf16[4,3,512,640]{3,2,1,0:T(8,128)(2,1)}, bf16[1024,2048]{1,0:T(8,128)(2,1)}) custom-call(bf16[1024,2048]{1,0:T(8,128)(2,1)} %get-tuple-element.109.refs_0_, bf16[1024,2048]{1,0:T(8,128)(2,1)} %get-tuple-element.110.refs_1_, bf16[1024,640]{1,0:T(8,128)(2,1)} %get-tuple-element.142.refs_2_, bf16[1024,640]{1,0:T(8,128)(2,1)} %get-tuple-element.143.refs_3_, ...), custom_call_target="tpu_custom_call" | custom-call | flops 16106127360 | bytes 32505856 | tf_op jit(solution)/shard_map/pallas_call | solution.py:915
  561.9 19.8 %shard_map.378 = (bf16[1024,768]{1,0:T(8,128)(2,1)}, f32[1,768]{1,0:T(1,128)}, bf16[1024,2048]{1,0:T(8,128)(2,1)}) custom-call(s32[1]{0:T(128)} %bitcast.2.refs_0_.refs_4_, bf16[1024,2048]{1,0:T(8,128)(2,1)} %get-tuple-element.149.refs_1_, bf16[4,512,1024]{2,1,0:T(8,128)(2,1)} %get-tuple-element.105.refs_3_.refs_2_, ...), custom_call_target="tpu_custom_call" | custom-call | flops 6442450944 | bytes 16777216 | tf_op jit(solution)/shard_map/pallas_call | solution.py:1253
  581.7 44.9 %shard_map.379 = (bf16[1024,768]{1,0:T(8,128)(2,1)}, bf16[1024,768]{1,0:T(8,128)(2,1)}, bf16[1024,768]{1,0:T(8,128)(2,1)}, bf16[1024,2048]{1,0:T(8,128)(2,1)}, b...) custom-call(bf16[1024,2048]{1,0:T(8,128)(2,1)} %get-tuple-element.125.refs_0_.refs_5_.refs_6_, ...), custom_call_target="tpu_custom_call" | custom-call | flops 19327352832 | bytes 30932992 | tf_op jit(solution)/shard_map/pallas_call | solution.py:840
  626.7 48.2 %shard_map.380 = (bf16[4,3,512,768]{3,2,1,0:T(8,128)(2,1)}, f32[2048,128]{1,0:T(8,128)}, f32[128,2048]{1,0:T(8,128)}) custom-call(bf16[1024,2048]{1,0:T(8,128)(2,1)} %get-tuple-element.109.refs_0_, bf16[1024,2048]{1,0:T(8,128)(2,1)} %get-tuple-element.110.refs_1_, bf16[1024,768]{1,0:T(8,128)(2,1)} %get-tuple-element.130.refs_2_, ...), custom_call_target="tpu_custom_call" | custom-call | flops 19327352832 | bytes 35651584 | tf_op jit(solution)/shard_map/pallas_call | solution.py:915
  676.6 4.0 shard_map.385
  680.6 1.7 reshape.245
  682.3 1.6 multiply_reduce_fusion
  684.0 2.7 fusion.34
  686.7 53.8 %shard_map.381 = (bf16[1024,2048]{1,0:T(8,128)(2,1)}, f32[128,2048]{1,0:T(8,128)}) custom-call(bf16[128,2048]{1,0:T(8,128)(2,1)} %get-tuple-element.298.refs_0_, bf16[1024,2048]{1,0:T(8,128)(2,1)} %get-tuple-element.159.refs_1_), custom_call_target="tpu_custom_call" | custom-call | tf_op jit(solution)/shard_map/pallas_call | solution.py:684
  740.5 20.1 %shard_map.382 = (bf16[1024,768]{1,0:T(8,128)(2,1)}, f32[1,768]{1,0:T(1,128)}, bf16[1024,2048]{1,0:T(8,128)(2,1)}) custom-call(s32[1]{0:T(128)} %bitcast.8.refs_0_.refs_4_, bf16[1024,2048]{1,0:T(8,128)(2,1)} %get-tuple-element.166.refs_1_.refs_5_, bf16[4,512,1024]{2,1,0:T(8,128)(2,1)} %get-tuple-element.105.refs_3_.refs_2_, ...), custom_call_target="tpu_custom_call" | custom-call | flops 6442450944 | bytes 16777216 | tf_op jit(solution)/shard_map/pallas_call | solution.py:1253
  761.5 43.6 %shard_map.383 = (bf16[4,512,1024]{2,1,0:T(8,128)(2,1)}, f32[128,2048]{1,0:T(8,128)}) custom-call(bf16[1024,2048]{1,0:T(8,128)(2,1)} %get-tuple-element.162.refs_0_, bf16[1024,2048]{1,0:T(8,128)(2,1)} %get-tuple-element.149.refs_1_, bf16[1024,768]{1,0:T(8,128)(2,1)} %get-tuple-element.163.refs_2_, bf16[1024,256]{1,0:T(8,128)(2,1)} %get-tuple-element.164.refs_3_, ...), custom_call_target="tpu_custom_call" | custom-call | flops 8589934592 | bytes 33554432 | tf_op jit(solution)/shard_map/pallas_call | solution.py:968
  805.2 2.2 fusion.13
  808.3 2.8 fusion.25
  811.1 1.1 maximum_bitcast_fusion.1
  812.9 48.3 %shard_map.384 = (f32[128,2048]{1,0:T(8,128)}, f32[512,1024]{1,0:T(8,128)}, f32[8,128]{1,0:T(8,128)}) custom-call(bf16[1024,2048]{1,0:T(8,128)(2,1)} %get-tuple-element.161.refs_0_, bf16[4,512,1024]{2,1,0:T(8,128)(2,1)} %get-tuple-element.171.refs_1_, f32[32,8,128]{2,1,0:T(8,128)} %bitcast.108, bf16[3,512,768]{2,1,0:T(8,128)(2,1)} %bitcast.95), custom_call_target="tpu_custom_call" | custom-call | tf_op jit(solution)/shard_map/pallas_call | solution.py:684
  861.2 1.3 fusion.39
  864.0 6.4 shard_map.386
  872.4 2.7 slice_bitcast_fusion
  875.1 1.0 copy.104
  876.1 1.4 fusion.23
  877.5 1.1 maximum_bitcast_fusion
  (133 shorter events, 16.0 us)
Async XLA Ops:
  7.2 1.6 copy-start.7
  7.2 1.9 copy-start.8
  7.2 258.5 %all-gather.7.cloned.1.call-start = ((), (), s32[]{:S(2)}) async-start(), calls=%async_computation.6 | async-start | bytes 11796480 | tf_op jit(solution)/shard_map/all_gather | solution.py:1372
  11.2 0.7 copy-start.27
  11.2 0.7 copy-start.28
  11.2 0.8 copy-start.29
  11.2 0.9 copy-start.22
  11.2 1.1 copy-start.10
  11.3 1.2 copy-start.24
  11.3 1.2 copy-start.25
  11.3 1.2 copy-start.26
  11.3 1.9 copy-start.11
  11.3 1.9 copy-start.12
  11.3 1.9 copy-start.13
  11.3 323.7 %all-gather.11.cloned.1.call-start = ((), (), s32[]{:S(2)}) async-start(), calls=%async_computation.8 | async-start | bytes 9830400 | tf_op jit(solution)/shard_map/all_gather | solution.py:1372
  115.7 1.7 copy-start.9
  115.7 1.8 copy-start.16
  115.8 318.1 %all-gather.9.cloned.1.call-start = ((), (), s32[]{:S(2)}) async-start(), calls=%async_computation.7 | async-start | bytes 11796480 | tf_op jit(solution)/shard_map/all_gather | solution.py:1372
  115.8 8.0 copy-start.23
  116.5 510.2 %reduce-scatter.4.cloned.1.call-start = ((), (), s32[]{:S(2)}) async-start(), calls=%async_computation.3 | async-start | bytes 11796480 | tf_op jit(solution)/shard_map/reduce_scatter | solution.py:1423
  120.4 46.4 %copy-start.14 = (f32[32,64]{1,0:T(8,128)}, f32[32,64]{1,0:T(8,128)S(1)}, u32[]{:S(2)}) copy-start(f32[32,64]{1,0:T(8,128)S(1)} %get-tuple-element.316) | copy-start | bytes 24580
  166.8 52.2 %copy-start.2 = (bf16[2,1,128,2048]{3,2,1,0:T(8,128)(2,1)S(1)}, bf16[2,1,128,2048]{3,2,1,0:T(8,128)(2,1)}, u32[]{:S(2)}) copy-start(bf16[2,1,128,2048]{3,2,1,0:T(8,128)(2,1)} %refs_7_.1) | copy-start | bytes 3145732
  333.1 1.0 copy-start
  333.1 1.0 copy-start.17
  433.2 328.4 %reduce-scatter.6.cloned.1.call-start = ((), (), s32[]{:S(2)}) async-start(), calls=%async_computation.4 | async-start | bytes 9830400 | tf_op jit(solution)/shard_map/reduce_scatter | solution.py:1423
  511.0 1.9 copy-start.4
  511.0 2.1 copy-start.5
  561.9 251.0 %reduce-scatter.8.cloned.1.call-start = ((), (), s32[]{:S(2)}) async-start(), calls=%async_computation.5 | async-start | bytes 11796480 | tf_op jit(solution)/shard_map/reduce_scatter | solution.py:1423
  674.9 0.7 copy-start.15
  674.9 1.6 copy-start.20
  674.9 1.6 copy-start.21
  675.6 6.7 copy-start.1
  675.6 6.7 copy-start.18
  740.5 20.2 %copy-start.19 = (f32[1,768]{1,0:T(1,128)S(1)}, f32[1,768]{1,0:T(1,128)}, u32[]{:S(2)}) copy-start(f32[1,768]{1,0:T(1,128)} %get-tuple-element.175) | copy-start | bytes 9220
  761.5 43.6 %copy-start.3 = (bf16[2,1,128,2048]{3,2,1,0:T(8,128)(2,1)S(1)}, bf16[2,1,128,2048]{3,2,1,0:T(8,128)(2,1)}, u32[]{:S(2)}) copy-start(bf16[2,1,128,2048]{3,2,1,0:T(8,128)(2,1)} %refs_7_.1) | copy-start | bytes 3145732
  811.1 1.6 copy-start.6
Sparse Core Ops, SparseCore 0:
  11.5 127.9 all-gather.6
  141.9 83.2 all-gather.10
  227.6 96.3 all-gather.8
  433.3 93.9 reduce-scatter.3
  562.0 81.6 reduce-scatter.5
  675.1 95.3 reduce-scatter.7

commit v5 on v4

--- a/solution.py
+++ b/solution.py
@@ -986,27 +986,66 @@
     return results[0], results[1:]
 
 
-def pack_kernel(cut, gate_ref, up_ref, down_ref, *refs):
-    low_ref, high_ref = refs[-2:]
-    for out_ref, part in ((low_ref, slice(0, cut)), (high_ref, slice(cut, None))):
-        out_ref[0] = gate_ref[0, :, part]
-        out_ref[1] = up_ref[0, :, part]
-        out_ref[2] = down_ref[0, part, :].T
-
-
-def pack(cut, gate, up, down, needed):
-    _, depth, units = gate.shape
-    vmem = pl.BlockSpec(memory_space=pltpu.VMEM)
-    return pl.pallas_call(
-        functools.partial(pack_kernel, cut),
-        in_specs=[vmem] * 3 + [pl.BlockSpec(memory_space=pl.ANY)] * len(needed),
-        out_specs=(vmem, vmem),
-        out_shape=tuple(
-            jax.ShapeDtypeStruct((3, depth, size), BF) for size in (cut, units - cut)
-        ),
-        compiler_params=pltpu.CompilerParams(vmem_limit_bytes=VMEM_BYTES),
-        cost_estimate=pl.CostEstimate(flops=0, bytes_accessed=12 * depth * units, transcendentals=0),
-    )(gate, up, down, *needed)
+def opening_kernel(transfers, cut, *refs):
+    refs = list(refs)
+
+    def take(count):
+        taken = refs[:count]
+        del refs[:count]
+        return taken
+
+    sent, given = take(len(transfers.inputs)), take(6)
+    landed, made = take(transfers.moves), take(3)
+    held, packed_refs, in_sem, out_sem = take(6), take(3), take(1)[0], take(1)[0]
+    phases = transfers.begin(sent, landed, refs)
+    fetches = [
+        pltpu.make_async_copy(source, target, in_sem.at[at])
+        for at, (source, target) in enumerate(zip(given, held))
+    ]
+    gives = [
+        pltpu.make_async_copy(source, target, out_sem.at[at])
+        for at, (source, target) in enumerate(zip(packed_refs, made))
+    ]
+    for fetch in fetches:
+        fetch.start()
+    run_all(phases[:1])
+    for fetch in fetches[:3]:
+        fetch.wait()
+    units = held[0].shape[0]
+    packed_refs[0][...] = jnp.zeros_like(packed_refs[0])
+    for which in range(3):
+        packed_refs[0][which, :, :units] = held[which][...].T
+    gives[0].start()
+    for fetch in fetches[3:]:
+        fetch.wait()
+    for at, part in ((1, slice(0, cut)), (2, slice(cut, None))):
+        packed_refs[at][0] = held[3][0, :, part]
+        packed_refs[at][1] = held[4][0, :, part]
+        packed_refs[at][2] = held[5][0, part, :].T
+        gives[at].start()
+    run_all(phases[1:])
+    for give in gives:
+        give.wait()
+
+
+def opening(mesh_size, ident, moves, cut, shared, expert):
+    transfers = Transfers(mesh_size, ident, moves)
+    anywhere = pl.BlockSpec(memory_space=pl.ANY)
+    units, depth = shared[0].shape
+    sizes = (-(-units // LANES) * LANES, cut, expert[0].shape[2] - cut)
+    shapes = [(3, depth, size) for size in sizes]
+    results = pl.pallas_call(
+        functools.partial(opening_kernel, transfers, cut),
+        in_specs=transfers.in_specs + [anywhere] * 6,
+        out_specs=tuple(transfers.out_specs + [anywhere] * 3),
+        out_shape=tuple(transfers.shapes + [jax.ShapeDtypeStruct(shape, BF) for shape in shapes]),
+        scratch_shapes=[pltpu.VMEM(array.shape, BF) for array in (*shared, *expert)]
+        + [pltpu.VMEM(shape, BF) for shape in shapes]
+        + [DMA((6,)), DMA((3,))]
+        + transfers.scratch,
+        compiler_params=transfers.params(),
+    )(*transfers.inputs, *shared, *expert)
+    return results[: transfers.moves], results[transfers.moves :]
 
 
 def unpack_kernel(turned, *refs):
@@ -1056,13 +1095,11 @@
     return jnp.concatenate([values[:, half:], values[:, :half]], axis=1)
 
 
-def block_weights(query, keys, first_row, length):
+def block_scores(query, keys, first_row, length):
     scores = dot(query, keys, (1,), (1,)) * (HD ** (-0.5))
     rows = first_row + lax.broadcasted_iota(jnp.int32, scores.shape, 0)
     cols = lax.broadcasted_iota(jnp.int32, scores.shape, 1)
-    scores = jnp.where((cols <= rows) & (cols < length), scores, -1e30)
-    exps = jnp.exp(scores - jnp.max(scores, axis=1, keepdims=True))
-    return exps / jnp.sum(exps, axis=1, keepdims=True)
+    return jnp.where((cols <= rows) & (cols < length), scores, -1e30)
 
 
 def attend_kernel(heads, transfers, *refs):
@@ -1075,7 +1112,7 @@
 
     length_ref, x_ref, gain_ref, w_ref, bias_ref, cos_ref, sin_ref = take(7)
     sent = take(len(transfers.inputs))
-    normed_ref, qkv_ref, mixed_ref, out_ref = take(4)
+    normed_ref, qkv_ref, mixed_ref, logs_ref, out_ref = take(5)
     landed = take(transfers.moves)
     rows_vmem, out_vmem, in_sem, normed_sem, out_sem = take(5)
     phases = transfers.begin(sent, landed, refs)
@@ -1117,9 +1154,14 @@
             qkv_ref[row:end, at : at + HD] = part.astype(BF)
         for head in range(heads):
             q_at, k_at, v_at = (head * HD, span + head * HD, 2 * span + head * HD)
-            shares = block_weights(
+            scores = block_scores(
                 qkv_ref[row:end, q_at : q_at + HD], qkv_ref[:end, k_at : k_at + HD], row, length
             )
+            top = jnp.max(scores, axis=1, keepdims=True)
+            exps = jnp.exp(scores - top)
+            totals = jnp.sum(exps, axis=1, keepdims=True)
+            shares = exps * (1.0 / totals)
+            logs_ref[row:end, head : head + 1] = top + jnp.log(totals)
             mixed = dot(shares.astype(BF), qkv_ref[:end, v_at : v_at + HD], (1,), (0,))
             mixed_ref[row:end, q_at : q_at + HD] = mixed.astype(BF)
         out_vmem[row:end, :] = dot(mixed_ref[row:end, :], out_w, (1,), (1,)).astype(BF)
@@ -1138,7 +1180,7 @@
         del refs[:count]
         return taken
 
-    length_ref, datt_ref, w_ref, qkv_ref, cos_ref, sin_ref = take(6)
+    length_ref, datt_ref, w_ref, qkv_ref, logs_ref, cos_ref, sin_ref = take(7)
     sent = take(len(transfers.inputs))
     turned_ref, sums_ref, out_ref = take(3)
     landed = take(transfers.moves)
@@ -1174,7 +1216,9 @@
             query = qkv_ref[row:end, q_at : q_at + HD]
             keys = qkv_ref[:end, k_at : k_at + HD]
             grad = grad_vmem[row:end, q_at : q_at + HD]
-            shares = block_weights(query, keys, row, length)
+            shares = jnp.exp(
+                block_scores(query, keys, row, length) - logs_ref[row:end, head : head + 1]
+            )
             grad_shares = dot(grad, qkv_ref[:end, v_at : v_at + HD], (1,), (1,))
             inner = jnp.sum(shares * grad_shares, axis=1, keepdims=True)
             grad_scores = (scale * shares * (grad_shares - inner)).astype(BF)
@@ -1226,12 +1270,13 @@
                 jax.ShapeDtypeStruct((seq_len, width), BF),
                 jax.ShapeDtypeStruct((seq_len, 3 * span), BF),
                 jax.ShapeDtypeStruct((seq_len, span), BF),
+                jax.ShapeDtypeStruct((seq_len, heads), F32),
                 jax.ShapeDtypeStruct((seq_len, width), BF),
             ]
             + transfers.shapes
         ),
         in_specs=[pl.BlockSpec(memory_space=pltpu.SMEM), anywhere] + in_vmem(5) + transfers.in_specs,
-        out_specs=tuple([anywhere] + in_vmem(2) + [anywhere] + transfers.out_specs),
+        out_specs=tuple([anywhere] + in_vmem(3) + [anywhere] + transfers.out_specs),
         scratch_shapes=[pltpu.VMEM((seq_len, width), BF)] * 2
         + [DMA((blocks,))] * 3
         + transfers.scratch,
@@ -1242,10 +1287,10 @@
             transcendentals=heads * seq_len * seq_len,
         ),
     )(length, rows, gain, weights, bias, cosine, sine, *transfers.inputs)
-    return results[:4], results[4:]
-
-
-def attend_back(length, rows, weights, qkv, cosine, sine, transfers):
+    return results[:5], results[5:]
+
+
+def attend_back(length, rows, weights, qkv, logs, cosine, sine, transfers):
     seq_len, width = rows.shape
     span = weights.shape[2] // 4
     heads, blocks = span // HD, seq_len // QB
@@ -1260,7 +1305,7 @@
             ]
             + transfers.shapes
         ),
-        in_specs=[pl.BlockSpec(memory_space=pltpu.SMEM), anywhere] + in_vmem(4) + transfers.in_specs,
+        in_specs=[pl.BlockSpec(memory_space=pltpu.SMEM), anywhere] + in_vmem(5) + transfers.in_specs,
         out_specs=tuple(in_vmem(2) + [anywhere] + transfers.out_specs),
         scratch_shapes=[pltpu.VMEM((seq_len, width), BF)] * 2
         + [pltpu.VMEM((seq_len, span), BF)]
@@ -1273,7 +1318,7 @@
             bytes_accessed=8 * seq_len * width,
             transcendentals=heads * seq_len * seq_len,
         ),
-    )(length, rows, weights, qkv, cosine, sine, *transfers.inputs)
+    )(length, rows, weights, qkv, logs, cosine, sine, *transfers.inputs)
     return results[:3], results[3:]
 
 
@@ -1347,7 +1392,7 @@
     )
     attn_own = jnp.concatenate([w_query, w_key, w_value, w_out.T], axis=1)
     mesh_size = (ranks, groups)
-    rows_a, attn_w, small_all = exchange(
+    (rows_a, attn_w, small_all), own_ranges = opening(
         mesh_size,
         2,
         [
@@ -1355,6 +1400,9 @@
             ("cross_gather", attn_own),
             ("spread", packed(small, BF).reshape(-1, LANES)),
         ],
+        cut,
+        (shared_gate.T, shared_up.T, shared_down),
+        (expert_gate, expert_up, expert_down),
     )
     small_all = small_all.reshape(groups * ranks, -1)
     gain_one = small_all[:, :per_device].reshape(-1).astype(F32)
@@ -1368,15 +1416,7 @@
     )[:, bias_at : small.shape[0]].reshape(groups, 3, heads, HD // groups)
     bias = own_bias.transpose(1, 2, 0, 3).reshape(1, 3 * span).astype(F32)
 
-    def over_fsdp(packed_range):
-        return lax.all_gather(packed_range, "fsdp", axis=0)
-
-    low, high = pack(cut, expert_gate, expert_up, expert_down, [small_all])
-    weights = [
-        over_fsdp(jnp.stack([padded(shared_gate, 1), padded(shared_up, 1), padded(shared_down.T, 1)])),
-        over_fsdp(low),
-        over_fsdp(high),
-    ]
+    weights = [lax.all_gather(own_range, "fsdp", axis=0) for own_range in own_ranges]
 
     cosine, sine = rope_tables(seq_len)
     idle = Transfers(mesh_size)
@@ -1413,7 +1453,7 @@
 
     att_a, (rows_b,) = attention(0, rows_a, moving(3, ("gather", tokens, (1, 0))))
     grad_a, sum_a = exchange(
-        mesh_size, 4, [("gather", cotangent, (0, 0)), ("scatter", att_a[3])]
+        mesh_size, 4, [("gather", cotangent, (0, 0)), ("scatter", att_a[4])]
     )
     norm_a = second_norm(0, sum_a)
     att_b, (two_a,) = attention(1, rows_b, moving(5, ("gather", norm_a[3])))
@@ -1437,7 +1477,7 @@
     single = ((0, 0), (1, 0), (2, 0), (3, 0))
     act[0, 0], acc_a, (grad_b, sum_b) = part(
         "first", two_a, grad_a, routes[0, 0], weights[0], [lengths[0]], router_wide,
-        moving(6, ("gather", cotangent, (1, 0)), ("scatter", att_b[3])), ((0, 0), (1, 1), (3, 0)),
+        moving(6, ("gather", cotangent, (1, 0)), ("scatter", att_b[4])), ((0, 0), (1, 1), (3, 0)),
     )
     acc_a, route_a = acc_a[:3], acc_a[3]
     norm_b = second_norm(1, sum_b)
@@ -1464,7 +1504,7 @@
     )
     range_1 = over_groups(grads_1)
     (grad_qkv_a, sums_a, first_a), _ = attend_back(
-        lengths[0], datt_a, attn_w, att_a[1], cosine, sine, moving(0, needed=[grads_1])
+        lengths[0], datt_a, attn_w, att_a[1], att_a[3], cosine, sine, moving(0, needed=[grads_1])
     )
     act[2, 1], acc_b, (one_a,) = part(
         "last", two_b, grad_b, route_b, weights[2], acc_b, router_wide,
@@ -1477,7 +1517,7 @@
     hid_b, send_b, gain_part_b = second_norm_back(1, norm_b, down_b)
     datt_b, moved_a = exchange(mesh_size, 12, [("gather", send_b), ("scatter", acc_a[0])])
     (grad_qkv_b, sums_b, first_b), _ = attend_back(
-        lengths[1], datt_b, attn_w, att_b[1], cosine, sine, idle
+        lengths[1], datt_b, attn_w, att_b[1], att_b[3], cosine, sine, idle
     )
     attn_parts, (one_b,) = attention_grads(
         groups,

time: 891 us -> 874 us (0.981)
  Pallas kernels: 814 us -> 799 us
    pallas_call x4 -> x3, Pallas kernels: 249 us -> 154 us  [exchange(): pl.pallas_call(functools.partial(exchange_kernel, transfers), out_shape=t...]
    pallas_call x1, Pallas kernels: 4.75 us -> 83.4 us  [opening(): pl.pallas_call(functools.partial(opening_kernel, transfers, cut), in_spec...]
  transfers between devices with their start and end apart: 6 -> 6, of which waited for: 0 -> 0; matrix products, arithmetic and copies ran while one was open for 4% -> 4% of each run, Pallas kernels for 86% -> 76%
where the time goes in v5:
time: 874 us; the launch traced here: 870 us
  Pallas kernels  799 us (91%)
  other arithmetic  27.8 us (3%)
  local copies, waits for them, and re-layouts  26.8 us (3%)
  between operations  15.1 us (2%)
    pallas_call x6, Pallas kernels, ffn(): pl.pallas_call(functools.partial(ffn_kernel, transfers, at, steps, expert...  259 us
    pallas_call x3, Pallas kernels, exchange(): pl.pallas_call(functools.partial(exchange_kernel, transfers), out_shape=t...  154 us
    pallas_call x3, Pallas kernels, ffn_grads(): pl.pallas_call(functools.partial(ffn_grads_kernel, transfers, at, groups,...  122 us
    pallas_call x2, Pallas kernels, attend(): pl.pallas_call(functools.partial(attend_kernel, heads, transfers), out_sh...  86.5 us
    pallas_call x1, Pallas kernels, opening(): pl.pallas_call(functools.partial(opening_kernel, transfers, cut), in_spec...  83.4 us
    pallas_call x1, Pallas kernels, attention_grads(): pl.pallas_call(functools.partial(attention_grads_kernel, transfers, group...  43.7 us
    pallas_call x2, Pallas kernels, attend_back(): pl.pallas_call(functools.partial(attend_back_kernel, heads, transfers), o...  39.4 us
  transfers between devices with their start and end apart: 6, of which 0 were waited for; matrix products, arithmetic and copies ran while one was open for 4% of the time, Pallas kernels for 76%

profile of v5, /device:TPU:0, one launch (start us, length us, event | category | flops | bytes accessed | tf_op | source)
XLA Modules:
  0.0 870.0 jit_solution(562711672952000655)
XLA Ops:
  7.2 0.7 reshape.235
  9.4 0.8 copy.86
  10.3 2.1 concatenate.13
  13.0 1.1 copy.85
  14.1 2.2 pad_maximum_fusion.refs_1_
  16.3 83.4 %shard_map.366 = (bf16[1024,2048]{1,0:T(8,128)(2,1)}, bf16[4,512,1024]{2,1,0:T(8,128)(2,1)}, bf16[32,16,128]{2,1,0:T(8,128)(2,1)}, bf16[3,512,768]{2,1,0:T(8,128...) custom-call(bf16[2,1,128,2048]{3,2,1,0:T(8,128)(2,1)} %refs_7_.3, ...), custom_call_target="tpu_custom_call" | custom-call | tf_op jit(solution)/shard_map/pallas_call | solution.py:1037
  101.3 1.0 copy.99
  102.4 1.0 copy.98
  105.9 1.1 broadcast_in_dim_reshape.4
  107.6 43.4 %shard_map.367 = (bf16[1024,2048]{1,0:T(8,128)(2,1)}, bf16[1024,768]{1,0:T(8,128)(2,1)}, bf16[1024,256]{1,0:T(8,128)(2,1)}, f32[1024,2]{1,0:T(8,128)}, bf16[1024...) custom-call(s32[1]{0:T(128)} %bitcast.2.refs_0_.refs_4_, bf16[1024,2048]{1,0:T(8,128)(2,1)} %get-tuple-element.106.refs_1_, ...), custom_call_target="tpu_custom_call" | custom-call | flops 5100273664 | bytes 16777216 | tf_op jit(solution)/shard_map/pallas_call | solution.py:1266
  151.0 52.0 %shard_map.368 = (bf16[1024,2048]{1,0:T(8,128)(2,1)}, f32[128,2048]{1,0:T(8,128)}) custom-call(bf16[2,1,128,2048]{3,2,1,0:T(8,128)(2,1)} %refs_6_.7, bf16[1024,2048]{1,0:T(8,128)(2,1)} %get-tuple-element.109.refs_1_), custom_call_target="tpu_custom_call" | custom-call | tf_op jit(solution)/shard_map/pallas_call | solution.py:684
  203.0 2.3 fusion.19
  205.3 1.2 fusion.24.refs_5_.refs_7_
  206.5 0.9 multiply_convert_fusion.3.refs_7_
  207.4 43.1 %shard_map.369 = (bf16[1024,2048]{1,0:T(8,128)(2,1)}, bf16[1024,768]{1,0:T(8,128)(2,1)}, bf16[1024,256]{1,0:T(8,128)(2,1)}, f32[1024,2]{1,0:T(8,128)}, bf16[1024...) custom-call(s32[1]{0:T(128)} %bitcast.10.refs_0_.refs_4_, bf16[1024,2048]{1,0:T(8,128)(2,1)} %get-tuple-element.111.refs_1_, ...), custom_call_target="tpu_custom_call" | custom-call | flops 5100273664 | bytes 16777216 | tf_op jit(solution)/shard_map/pallas_call | solution.py:1266
  250.6 66.1 %shard_map.370 = (bf16[1024,768]{1,0:T(8,128)(2,1)}, bf16[1024,768]{1,0:T(8,128)(2,1)}, bf16[1024,768]{1,0:T(8,128)(2,1)}, bf16[1024,2048]{1,0:T(8,128)(2,1)}, b...) custom-call(bf16[1024,2048]{1,0:T(8,128)(2,1)} %get-tuple-element.11, ...), custom_call_target="tpu_custom_call" | custom-call | flops 19327352832 | bytes 30932992 | tf_op jit(solution)/shard_map/pallas_call | solution.py:840
  316.7 1.4 multiply_reduce_fusion.4
  318.1 0.9 copy-done
  319.1 0.9 multiply_convert_fusion.2.refs_7_
  320.0 41.4 %shard_map.371 = (bf16[1024,640]{1,0:T(8,128)(2,1)}, bf16[1024,640]{1,0:T(8,128)(2,1)}, bf16[1024,640]{1,0:T(8,128)(2,1)}, bf16[1024,2048]{1,0:T(8,128)(2,1)}, b...) custom-call(bf16[1024,2048]{1,0:T(8,128)(2,1)} %get-tuple-element.112.refs_0_, ...), custom_call_target="tpu_custom_call" | custom-call | flops 16106127360 | bytes 28573696 | tf_op jit(solution)/shard_map/pallas_call | solution.py:840
  361.4 29.6 %shard_map.372 = (bf16[1024,768]{1,0:T(8,128)(2,1)}, bf16[1024,768]{1,0:T(8,128)(2,1)}, bf16[1024,768]{1,0:T(8,128)(2,1)}, bf16[1024,2048]{1,0:T(8,128)(2,1)}, b...) custom-call(bf16[1024,2048]{1,0:T(8,128)(2,1)} %get-tuple-element.129.refs_0_.refs_5_.refs_6_, ...), custom_call_target="tpu_custom_call" | custom-call | flops 19327352832 | bytes 30932992 | tf_op jit(solution)/shard_map/pallas_call | solution.py:840
  391.0 27.1 %shard_map.373.refs_8_ = bf16[4,3,512,768]{3,2,1,0:T(8,128)(2,1)} custom-call(bf16[1024,2048]{1,0:T(8,128)(2,1)} %get-tuple-element.112.refs_0_, bf16[1024,2048]{1,0:T(8,128)(2,1)} %get-tuple-element.113.refs_1_, bf16[1024,768]{1,0:T(8,128)(2,1)} %get-tuple-element.126.refs_2_, bf16[1024,768]{1,0:T(8,128)(2,1)} %get-tuple-element.127.refs_3_, ...), custom_call_target="tpu_custom_call" | custom-call | flops 19327352832 | bytes 35651584 | tf_op jit(solution)/shard_map/pallas_call | solution.py:915
  418.9 33.2 %shard_map.374 = (bf16[1024,768]{1,0:T(8,128)(2,1)}, bf16[1024,768]{1,0:T(8,128)(2,1)}, bf16[1024,768]{1,0:T(8,128)(2,1)}, bf16[1024,2048]{1,0:T(8,128)(2,1)}, b...) custom-call(bf16[1024,2048]{1,0:T(8,128)(2,1)} %get-tuple-element.112.refs_0_, ...), custom_call_target="tpu_custom_call" | custom-call | flops 19327352832 | bytes 30932992 | tf_op jit(solution)/shard_map/pallas_call | solution.py:840
  452.2 43.6 %shard_map.375 = (bf16[1024,640]{1,0:T(8,128)(2,1)}, bf16[1024,640]{1,0:T(8,128)(2,1)}, bf16[1024,640]{1,0:T(8,128)(2,1)}, bf16[1024,2048]{1,0:T(8,128)(2,1)}, b...) custom-call(bf16[1024,2048]{1,0:T(8,128)(2,1)} %get-tuple-element.129.refs_0_.refs_5_.refs_6_, ...), custom_call_target="tpu_custom_call" | custom-call | flops 16106127360 | bytes 28573696 | tf_op jit(solution)/shard_map/pallas_call | solution.py:840
  495.8 1.9 multiply_reduce_fusion.1
  497.9 1.5 fusion.35
  499.4 47.4 %shard_map.376 = (bf16[4,3,512,640]{3,2,1,0:T(8,128)(2,1)}, bf16[1024,2048]{1,0:T(8,128)(2,1)}) custom-call(bf16[1024,2048]{1,0:T(8,128)(2,1)} %get-tuple-element.112.refs_0_, bf16[1024,2048]{1,0:T(8,128)(2,1)} %get-tuple-element.113.refs_1_, bf16[1024,640]{1,0:T(8,128)(2,1)} %get-tuple-element.146.refs_2_, bf16[1024,640]{1,0:T(8,128)(2,1)} %get-tuple-element.147.refs_3_, ...), custom_call_target="tpu_custom_call" | custom-call | flops 16106127360 | bytes 32505856 | tf_op jit(solution)/shard_map/pallas_call | solution.py:915
  546.9 19.6 %shard_map.377 = (bf16[1024,768]{1,0:T(8,128)(2,1)}, f32[1,768]{1,0:T(1,128)}, bf16[1024,2048]{1,0:T(8,128)(2,1)}) custom-call(s32[1]{0:T(128)} %bitcast.2.refs_0_.refs_4_, bf16[1024,2048]{1,0:T(8,128)(2,1)} %get-tuple-element.153.refs_1_, bf16[4,512,1024]{2,1,0:T(8,128)(2,1)} %get-tuple-element.108.refs_3_.refs_2_, ...), custom_call_target="tpu_custom_call" | custom-call | flops 6442450944 | bytes 16777216 | tf_op jit(solution)/shard_map/pallas_call | solution.py:1298
  566.5 44.9 %shard_map.378 = (bf16[1024,768]{1,0:T(8,128)(2,1)}, bf16[1024,768]{1,0:T(8,128)(2,1)}, bf16[1024,768]{1,0:T(8,128)(2,1)}, bf16[1024,2048]{1,0:T(8,128)(2,1)}, b...) custom-call(bf16[1024,2048]{1,0:T(8,128)(2,1)} %get-tuple-element.129.refs_0_.refs_5_.refs_6_, ...), custom_call_target="tpu_custom_call" | custom-call | flops 19327352832 | bytes 30932992 | tf_op jit(solution)/shard_map/pallas_call | solution.py:840
  611.5 47.9 %shard_map.379 = (bf16[4,3,512,768]{3,2,1,0:T(8,128)(2,1)}, f32[2048,128]{1,0:T(8,128)}, f32[128,2048]{1,0:T(8,128)}) custom-call(bf16[1024,2048]{1,0:T(8,128)(2,1)} %get-tuple-element.112.refs_0_, bf16[1024,2048]{1,0:T(8,128)(2,1)} %get-tuple-element.113.refs_1_, bf16[1024,768]{1,0:T(8,128)(2,1)} %get-tuple-element.134.refs_2_, ...), custom_call_target="tpu_custom_call" | custom-call | flops 19327352832 | bytes 35651584 | tf_op jit(solution)/shard_map/pallas_call | solution.py:915
  661.0 4.0 shard_map.384
  665.0 1.7 reshape.245
  666.8 1.6 multiply_reduce_fusion
  668.4 2.7 fusion.34
  671.2 53.9 %shard_map.380 = (bf16[1024,2048]{1,0:T(8,128)(2,1)}, f32[128,2048]{1,0:T(8,128)}) custom-call(bf16[128,2048]{1,0:T(8,128)(2,1)} %get-tuple-element.304.refs_0_, bf16[1024,2048]{1,0:T(8,128)(2,1)} %get-tuple-element.164.refs_1_), custom_call_target="tpu_custom_call" | custom-call | tf_op jit(solution)/shard_map/pallas_call | solution.py:684
  725.0 19.7 %shard_map.381 = (bf16[1024,768]{1,0:T(8,128)(2,1)}, f32[1,768]{1,0:T(1,128)}, bf16[1024,2048]{1,0:T(8,128)(2,1)}) custom-call(s32[1]{0:T(128)} %bitcast.10.refs_0_.refs_4_, bf16[1024,2048]{1,0:T(8,128)(2,1)} %get-tuple-element.171.refs_1_.refs_5_, bf16[4,512,1024]{2,1,0:T(8,128)(2,1)} %get-tuple-element.108.refs_3_.refs_2_, ...), custom_call_target="tpu_custom_call" | custom-call | flops 6442450944 | bytes 16777216 | tf_op jit(solution)/shard_map/pallas_call | solution.py:1298
  745.7 43.7 %shard_map.382 = (bf16[4,512,1024]{2,1,0:T(8,128)(2,1)}, f32[128,2048]{1,0:T(8,128)}) custom-call(bf16[1024,2048]{1,0:T(8,128)(2,1)} %get-tuple-element.167.refs_0_, bf16[1024,2048]{1,0:T(8,128)(2,1)} %get-tuple-element.153.refs_1_, bf16[1024,768]{1,0:T(8,128)(2,1)} %get-tuple-element.168.refs_2_, bf16[1024,256]{1,0:T(8,128)(2,1)} %get-tuple-element.169.refs_3_, ...), custom_call_target="tpu_custom_call" | custom-call | flops 8589934592 | bytes 33554432 | tf_op jit(solution)/shard_map/pallas_call | solution.py:968
  789.4 2.2 fusion.13
  792.5 2.8 fusion.25
  795.3 1.1 maximum_bitcast_fusion.1
  797.1 48.3 %shard_map.383 = (f32[128,2048]{1,0:T(8,128)}, f32[512,1024]{1,0:T(8,128)}, f32[8,128]{1,0:T(8,128)}) custom-call(bf16[1024,2048]{1,0:T(8,128)(2,1)} %get-tuple-element.166.refs_0_, bf16[4,512,1024]{2,1,0:T(8,128)(2,1)} %get-tuple-element.177.refs_1_, f32[32,8,128]{2,1,0:T(8,128)} %bitcast.101, bf16[3,512,768]{2,1,0:T(8,128)(2,1)} %bitcast.90), custom_call_target="tpu_custom_call" | custom-call | tf_op jit(solution)/shard_map/pallas_call | solution.py:684
  845.4 1.3 fusion.39
  847.4 0.7 slice.119
  848.1 6.4 shard_map.385
  856.6 2.7 slice_bitcast_fusion
  859.3 1.0 copy.95
  860.3 1.4 fusion.23
  861.6 1.1 maximum_bitcast_fusion
  (100 shorter events, 14.9 us)
Async XLA Ops:
  7.2 243.4 %all-gather.7.cloned.1.call-start = ((), (), s32[]{:S(2)}) async-start(), calls=%async_computation.6 | async-start | bytes 11796480 | tf_op jit(solution)/shard_map/all_gather | solution.py:1419
  99.8 1.6 copy-start.10
  99.8 220.3 %all-gather.11.cloned.1.call-start = ((), (), s32[]{:S(2)}) async-start(), calls=%async_computation.8 | async-start | bytes 9830400 | tf_op jit(solution)/shard_map/all_gather | solution.py:1419
  99.8 3.6 copy-start.7
  100.5 318.4 %all-gather.9.cloned.1.call-start = ((), (), s32[]{:S(2)}) async-start(), calls=%async_computation.7 | async-start | bytes 11796480 | tf_op jit(solution)/shard_map/all_gather | solution.py:1419
  100.6 6.5 copy-start.16
  101.3 510.2 %reduce-scatter.4.cloned.1.call-start = ((), (), s32[]{:S(2)}) async-start(), calls=%async_computation.3 | async-start | bytes 11796480 | tf_op jit(solution)/shard_map/reduce_scatter | solution.py:1463
  103.6 47.4 %copy-start.8 = (f32[32,64]{1,0:T(8,128)}, f32[32,64]{1,0:T(8,128)S(1)}, u32[]{:S(2)}) copy-start(f32[32,64]{1,0:T(8,128)S(1)} %get-tuple-element.322) | copy-start | bytes 24580
  151.0 52.0 %copy-start.2 = (bf16[2,1,128,2048]{3,2,1,0:T(8,128)(2,1)S(1)}, bf16[2,1,128,2048]{3,2,1,0:T(8,128)(2,1)}, u32[]{:S(2)}) copy-start(bf16[2,1,128,2048]{3,2,1,0:T(8,128)(2,1)} %refs_7_.3) | copy-start | bytes 3145732
  318.1 1.0 copy-start
  318.1 1.0 copy-start.11
  418.2 327.5 %reduce-scatter.6.cloned.1.call-start = ((), (), s32[]{:S(2)}) async-start(), calls=%async_computation.4 | async-start | bytes 9830400 | tf_op jit(solution)/shard_map/reduce_scatter | solution.py:1463
  495.7 1.9 copy-start.4
  495.8 2.1 copy-start.5
  546.8 250.3 %reduce-scatter.8.cloned.1.call-start = ((), (), s32[]{:S(2)}) async-start(), calls=%async_computation.5 | async-start | bytes 11796480 | tf_op jit(solution)/shard_map/reduce_scatter | solution.py:1463
  659.4 0.7 copy-start.9
  659.4 1.6 copy-start.14
  659.4 1.6 copy-start.15
  660.1 6.7 copy-start.1
  660.1 6.7 copy-start.12
  725.0 19.8 %copy-start.13 = (f32[1,768]{1,0:T(1,128)S(1)}, f32[1,768]{1,0:T(1,128)}, u32[]{:S(2)}) copy-start(f32[1,768]{1,0:T(1,128)} %get-tuple-element.181) | copy-start | bytes 9220
  745.7 43.7 %copy-start.3 = (bf16[2,1,128,2048]{3,2,1,0:T(8,128)(2,1)S(1)}, bf16[2,1,128,2048]{3,2,1,0:T(8,128)(2,1)}, u32[]{:S(2)}) copy-start(bf16[2,1,128,2048]{3,2,1,0:T(8,128)(2,1)} %refs_7_.3) | copy-start | bytes 3145732
  795.3 1.6 copy-start.6
Sparse Core Ops, SparseCore 0:
  99.9 94.4 all-gather.6
  196.3 83.2 all-gather.10
  281.4 96.3 all-gather.8
  418.3 93.9 reduce-scatter.3
  547.0 81.4 reduce-scatter.5
  659.5 95.4 reduce-scatter.7

commit v6 on v5

--- a/solution.py
+++ b/solution.py
@@ -420,7 +420,7 @@
             near(at).wait_send()
             forward(at).wait_send()
 
-    return [begin] + [nothing] * 5 + [pass_on, end]
+    return [begin] + [nothing] * 4 + [pass_on, nothing, end]
 
 
 def cross_scatter_steps(place, partial, total, mine, near_in, far_in, own_sem, send, recv):
@@ -758,15 +758,20 @@
     phases = transfers.begin(sent, landed, refs)
     step = pl.program_id(0)
 
-    def weights():
-        return pltpu.make_async_copy(w_ref, w_vmem, w_sem)
-
-    pl.when(step == 0)(lambda: weights().start())
+    def fetch(which):
+        return pltpu.make_async_copy(w_ref.at[:, which], w_vmem.at[which], w_sem.at[which])
+
+    @pl.when(step == 0)
+    def _():
+        for which in range(3):
+            fetch(which).start()
+
+    def weight(which):
+        pl.when(step == 0)(lambda: fetch(which).wait())
+        _, groups, depth, units = w_vmem.shape
+        return w_vmem[which].reshape(groups * depth, units)
 
     def hidden_part(_):
-        pl.when(step == 0)(lambda: weights().wait())
-        groups, _, depth, units = w_vmem.shape
-        gate_w, up_w, down_w = [w_vmem[:, i].reshape(groups * depth, units) for i in range(3)]
         rows, grad = rows_ref[...], grad_ref[...]
         if first:
             length = before[0][0]
@@ -775,8 +780,11 @@
         else:
             route = route_ref[...]
         scale = column(route, experts if first else experts + 1)
+        gate_w = weight(0)
         gate_act = dot(rows, gate_w, (1,), (0,))
+        up_w = weight(1)
         up_act = dot(rows, up_w, (1,), (0,))
+        down_w = weight(2)
         back = dot(grad, down_w, (1,), (0,))
         sigmoid = 1.0 / (1.0 + jnp.exp(-gate_act))
         silu = gate_act * sigmoid
@@ -850,7 +858,11 @@
             + transfers.out_specs
         ),
         out_shape=tuple(narrow + wide + dots + transfers.shapes),
-        scratch_shapes=[pltpu.VMEM(weights.shape, BF), DMA] + transfers.scratch,
+        scratch_shapes=[
+            pltpu.VMEM((3, weights.shape[0]) + weights.shape[2:], BF),
+            DMA((3,)),
+        ]
+        + transfers.scratch,
         compiler_params=transfers.params(),
         cost_estimate=pl.CostEstimate(
             flops=12 * count * width * units,
@@ -1392,13 +1404,13 @@
     )
     attn_own = jnp.concatenate([w_query, w_key, w_value, w_out.T], axis=1)
     mesh_size = (ranks, groups)
-    (rows_a, attn_w, small_all), own_ranges = opening(
+    (small_all, attn_w, rows_a), own_ranges = opening(
         mesh_size,
         2,
         [
+            ("spread", packed(small, BF).reshape(-1, LANES)),
+            ("cross_gather", attn_own),
             ("gather", tokens, (0, 0)),
-            ("cross_gather", attn_own),
-            ("spread", packed(small, BF).reshape(-1, LANES)),
         ],
         cut,
         (shared_gate.T, shared_up.T, shared_down),
@@ -1452,11 +1464,12 @@
         return (inside * (hidden + moved)).astype(BF)
 
     att_a, (rows_b,) = attention(0, rows_a, moving(3, ("gather", tokens, (1, 0))))
-    grad_a, sum_a = exchange(
-        mesh_size, 4, [("gather", cotangent, (0, 0)), ("scatter", att_a[4])]
+    att_b, (grad_a, sum_a) = attention(
+        1, rows_b, moving(4, ("gather", cotangent, (0, 0)), ("scatter", att_a[4]))
     )
     norm_a = second_norm(0, sum_a)
-    att_b, (two_a,) = attention(1, rows_b, moving(5, ("gather", norm_a[3])))
+    two_a, sum_b = exchange(mesh_size, 5, [("gather", norm_a[3]), ("scatter", att_b[4])])
+    norm_b = second_norm(1, sum_b)
 
     def over_groups(grads):
         flat = grads.reshape(-1, grads.shape[-1])
@@ -1475,12 +1488,11 @@
     act = {}
     part = functools.partial(ffn, experts)
     single = ((0, 0), (1, 0), (2, 0), (3, 0))
-    act[0, 0], acc_a, (grad_b, sum_b) = part(
+    act[0, 0], acc_a, (grad_b,) = part(
         "first", two_a, grad_a, routes[0, 0], weights[0], [lengths[0]], router_wide,
-        moving(6, ("gather", cotangent, (1, 0)), ("scatter", att_b[4])), ((0, 0), (1, 1), (3, 0)),
+        moving(6, ("gather", cotangent, (1, 0))), single,
     )
     acc_a, route_a = acc_a[:3], acc_a[3]
-    norm_b = second_norm(1, sum_b)
     act[1, 0], acc_a, (two_b,) = part(
         "next", two_a, grad_a, route_a, weights[1], acc_a, None,
         moving(7, ("gather", norm_b[3])), single,
@@ -1503,21 +1515,23 @@
         1, moving(9, ("gather", send_a)), ((0, 0), (1, 0), (2, 0), (3, 0))
     )
     range_1 = over_groups(grads_1)
-    (grad_qkv_a, sums_a, first_a), _ = attend_back(
-        lengths[0], datt_a, attn_w, att_a[1], att_a[3], cosine, sine, moving(0, needed=[grads_1])
-    )
-    act[2, 1], acc_b, (one_a,) = part(
+    act[2, 1], acc_b, (moved_a,) = part(
         "last", two_b, grad_b, route_b, weights[2], acc_b, router_wide,
-        moving(10, ("scatter", first_a)), single,
+        moving(10, ("scatter", acc_a[0]), needed=[grads_1]), single,
     )
     (grads_2, total_wide), (down_b,) = grads_of(
         2, moving(11, ("scatter", acc_b[1]), needed=[range_0]), ((0, 0), (1, 1), (2, 1), (3, 1))
     )
     range_2 = over_groups(grads_2)
     hid_b, send_b, gain_part_b = second_norm_back(1, norm_b, down_b)
-    datt_b, moved_a = exchange(mesh_size, 12, [("gather", send_b), ("scatter", acc_a[0])])
-    (grad_qkv_b, sums_b, first_b), _ = attend_back(
-        lengths[1], datt_b, attn_w, att_b[1], att_b[3], cosine, sine, idle
+
+    (grad_qkv_a, sums_a, first_a), (datt_b,) = attend_back(
+        lengths[0], datt_a, attn_w, att_a[1], att_a[3], cosine, sine,
+        moving(12, ("gather", send_b)),
+    )
+    (grad_qkv_b, sums_b, first_b), (one_a,) = attend_back(
+        lengths[1], datt_b, attn_w, att_b[1], att_b[3], cosine, sine,
+        moving(15, ("scatter", first_a), needed=[range_1]),
     )
     attn_parts, (one_b,) = attention_grads(
         groups,
@@ -1525,7 +1539,7 @@
             (att_a[0], datt_a, grad_qkv_a, att_a[2]),
             (att_b[0], datt_b, grad_qkv_b, att_b[2]),
         ],
-        moving(13, ("scatter", first_b), needed=[range_1]),
+        moving(13, ("scatter", first_b)),
     )
 
     grad_in_a, one_part_a = first_norm_back(0, hid_a, one_a)

time: 874 us -> 853 us (0.976)
  Pallas kernels: 799 us -> 781 us
    pallas_call x2, Pallas kernels: 39.4 us -> 95.7 us  [attend_back(): pl.pallas_call(functools.partial(attend_back_kernel, heads, transfers), o...]
    pallas_call x3 -> x2, Pallas kernels: 154 us -> 101 us  [exchange(): pl.pallas_call(functools.partial(exchange_kernel, transfers), out_shape=t...]
    pallas_call x1, Pallas kernels: 83.4 us -> 57.3 us  [opening(): pl.pallas_call(functools.partial(opening_kernel, transfers, cut), in_spec...]
    pallas_call x2, Pallas kernels: 86.5 us -> 103 us  [attend(): pl.pallas_call(functools.partial(attend_kernel, heads, transfers), out_sh...]
    pallas_call x6, Pallas kernels: 259 us -> 249 us  [ffn(): pl.pallas_call(functools.partial(ffn_kernel, transfers, at, steps, expert...]
  transfers between devices with their start and end apart: 6 -> 6, of which waited for: 0 -> 0; matrix products, arithmetic and copies ran while one was open for 4% -> 4% of each run, Pallas kernels for 76% -> 79%
where the time goes in v6:
time: 853 us; the launch traced here: 849 us
  Pallas kernels  781 us (92%)
  other arithmetic  26.1 us (3%)
  local copies, waits for them, and re-layouts  25.1 us (3%)
  between operations  14.9 us (2%)
    pallas_call x6, Pallas kernels, ffn(): pl.pallas_call(functools.partial(ffn_kernel, transfers, at, steps, expert...  249 us
    pallas_call x3, Pallas kernels, ffn_grads(): pl.pallas_call(functools.partial(ffn_grads_kernel, transfers, at, groups,...  120 us
    pallas_call x2, Pallas kernels, attend(): pl.pallas_call(functools.partial(attend_kernel, heads, transfers), out_sh...  103 us
    pallas_call x2, Pallas kernels, exchange(): pl.pallas_call(functools.partial(exchange_kernel, transfers), out_shape=t...  101 us
    pallas_call x2, Pallas kernels, attend_back(): pl.pallas_call(functools.partial(attend_back_kernel, heads, transfers), o...  95.7 us
    pallas_call x1, Pallas kernels, opening(): pl.pallas_call(functools.partial(opening_kernel, transfers, cut), in_spec...  57.3 us
    pallas_call x1, Pallas kernels, attention_grads(): pl.pallas_call(functools.partial(attention_grads_kernel, transfers, group...  44.4 us
  transfers between devices with their start and end apart: 6, of which 0 were waited for; matrix products, arithmetic and copies ran while one was open for 4% of the time, Pallas kernels for 79%

profile of v6, /device:TPU:0, one launch (start us, length us, event | category | flops | bytes accessed | tf_op | source)
XLA Modules:
  0.0 848.6 jit_solution(4728394321264412349)
XLA Ops:
  7.2 0.7 reshape.235
  8.0 0.7 reshape.236
  8.7 0.7 reshape.237
  9.4 0.8 copy.85
  10.3 2.1 concatenate.12
  13.0 1.1 copy.86
  14.1 2.2 pad_maximum_fusion.refs_1_
  16.3 57.3 %shard_map.366 = (bf16[32,16,128]{2,1,0:T(8,128)(2,1)}, bf16[4,512,1024]{2,1,0:T(8,128)(2,1)}, bf16[1024,2048]{1,0:T(8,128)(2,1)}, bf16[3,512,768]{2,1,0:T(8,128...) custom-call(bf16[16,128]{1,0:T(8,128)(2,1)} %pad_bitcast_fusion.refs_0_, ...), custom_call_target="tpu_custom_call" | custom-call | tf_op jit(solution)/shard_map/pallas_call | solution.py:1049
  75.3 1.0 copy.99
  76.3 1.0 copy.98
  79.9 1.1 broadcast_in_dim_reshape.4
  81.6 44.0 %shard_map.367 = (bf16[1024,2048]{1,0:T(8,128)(2,1)}, bf16[1024,768]{1,0:T(8,128)(2,1)}, bf16[1024,256]{1,0:T(8,128)(2,1)}, f32[1024,2]{1,0:T(8,128)}, bf16[1024...) custom-call(s32[1]{0:T(128)} %bitcast.3.refs_0_.refs_4_, bf16[1024,2048]{1,0:T(8,128)(2,1)} %get-tuple-element.106.refs_1_, ...), custom_call_target="tpu_custom_call" | custom-call | flops 5100273664 | bytes 16777216 | tf_op jit(solution)/shard_map/pallas_call | solution.py:1278
  125.6 58.9 %shard_map.368 = (bf16[1024,2048]{1,0:T(8,128)(2,1)}, bf16[1024,768]{1,0:T(8,128)(2,1)}, bf16[1024,256]{1,0:T(8,128)(2,1)}, f32[1024,2]{1,0:T(8,128)}, bf16[1024...) custom-call(s32[1]{0:T(128)} %bitcast.2.refs_0_.refs_4_, ...), custom_call_target="tpu_custom_call" | custom-call | flops 5100273664 | bytes 16777216 | tf_op jit(solution)/shard_map/pallas_call | solution.py:1278
  184.5 2.1 fusion.19
  186.7 1.0 multiply_convert_fusion.3.refs_0_
  187.6 52.0 %shard_map.369 = (bf16[1024,2048]{1,0:T(8,128)(2,1)}, f32[128,2048]{1,0:T(8,128)}) custom-call(bf16[128,2048]{1,0:T(8,128)(2,1)} %multiply_convert_fusion.3.refs_0_, bf16[1024,2048]{1,0:T(8,128)(2,1)} %get-tuple-element.112.refs_1_), custom_call_target="tpu_custom_call" | custom-call | tf_op jit(solution)/shard_map/pallas_call | solution.py:684
  239.6 1.4 multiply_reduce_fusion.4
  241.1 1.2 fusion.24.refs_5_.refs_7_
  242.2 0.9 multiply_convert_fusion.2.refs_7_
  243.2 43.9 %shard_map.370 = (bf16[1024,768]{1,0:T(8,128)(2,1)}, bf16[1024,768]{1,0:T(8,128)(2,1)}, bf16[1024,768]{1,0:T(8,128)(2,1)}, bf16[1024,2048]{1,0:T(8,128)(2,1)}, b...) custom-call(bf16[1024,2048]{1,0:T(8,128)(2,1)} %get-tuple-element.113.refs_0_, ...), custom_call_target="tpu_custom_call" | custom-call | flops 19327352832 | bytes 30932992 | tf_op jit(solution)/shard_map/pallas_call | solution.py:848
  287.1 43.1 %shard_map.371 = (bf16[1024,640]{1,0:T(8,128)(2,1)}, bf16[1024,640]{1,0:T(8,128)(2,1)}, bf16[1024,640]{1,0:T(8,128)(2,1)}, bf16[1024,2048]{1,0:T(8,128)(2,1)}, b...) custom-call(bf16[1024,2048]{1,0:T(8,128)(2,1)} %get-tuple-element.113.refs_0_, ...), custom_call_target="tpu_custom_call" | custom-call | flops 16106127360 | bytes 28573696 | tf_op jit(solution)/shard_map/pallas_call | solution.py:848
  330.2 34.2 %shard_map.372 = (bf16[1024,768]{1,0:T(8,128)(2,1)}, bf16[1024,768]{1,0:T(8,128)(2,1)}, bf16[1024,768]{1,0:T(8,128)(2,1)}, bf16[1024,2048]{1,0:T(8,128)(2,1)}, b...) custom-call(bf16[1024,2048]{1,0:T(8,128)(2,1)} %get-tuple-element.122.refs_0_.refs_5_.refs_6_, ...), custom_call_target="tpu_custom_call" | custom-call | flops 19327352832 | bytes 30932992 | tf_op jit(solution)/shard_map/pallas_call | solution.py:848
  364.4 27.1 %shard_map.373.refs_8_ = bf16[4,3,512,768]{3,2,1,0:T(8,128)(2,1)} custom-call(bf16[1024,2048]{1,0:T(8,128)(2,1)} %get-tuple-element.113.refs_0_, bf16[1024,2048]{1,0:T(8,128)(2,1)} %get-tuple-element.114.refs_1_, bf16[1024,768]{1,0:T(8,128)(2,1)} %get-tuple-element.132.refs_2_, bf16[1024,768]{1,0:T(8,128)(2,1)} %get-tuple-element.133.refs_3_, ...), custom_call_target="tpu_custom_call" | custom-call | flops 19327352832 | bytes 35651584 | tf_op jit(solution)/shard_map/pallas_call | solution.py:927
  392.3 36.2 %shard_map.374 = (bf16[1024,768]{1,0:T(8,128)(2,1)}, bf16[1024,768]{1,0:T(8,128)(2,1)}, bf16[1024,768]{1,0:T(8,128)(2,1)}, bf16[1024,2048]{1,0:T(8,128)(2,1)}, b...) custom-call(bf16[1024,2048]{1,0:T(8,128)(2,1)} %get-tuple-element.113.refs_0_, ...), custom_call_target="tpu_custom_call" | custom-call | flops 19327352832 | bytes 30932992 | tf_op jit(solution)/shard_map/pallas_call | solution.py:848
  428.5 43.8 %shard_map.375 = (bf16[1024,640]{1,0:T(8,128)(2,1)}, bf16[1024,640]{1,0:T(8,128)(2,1)}, bf16[1024,640]{1,0:T(8,128)(2,1)}, bf16[1024,2048]{1,0:T(8,128)(2,1)}, b...) custom-call(bf16[1024,2048]{1,0:T(8,128)(2,1)} %get-tuple-element.122.refs_0_.refs_5_.refs_6_, ...), custom_call_target="tpu_custom_call" | custom-call | flops 16106127360 | bytes 28573696 | tf_op jit(solution)/shard_map/pallas_call | solution.py:848
  472.3 1.8 multiply_reduce_fusion.1
  474.3 1.2 fusion.35
  475.5 46.3 %shard_map.376 = (bf16[4,3,512,640]{3,2,1,0:T(8,128)(2,1)}, bf16[1024,2048]{1,0:T(8,128)(2,1)}) custom-call(bf16[1024,2048]{1,0:T(8,128)(2,1)} %get-tuple-element.113.refs_0_, bf16[1024,2048]{1,0:T(8,128)(2,1)} %get-tuple-element.114.refs_1_, bf16[1024,640]{1,0:T(8,128)(2,1)} %get-tuple-element.143.refs_2_, bf16[1024,640]{1,0:T(8,128)(2,1)} %get-tuple-element.144.refs_3_, ...), custom_call_target="tpu_custom_call" | custom-call | flops 16106127360 | bytes 32505856 | tf_op jit(solution)/shard_map/pallas_call | solution.py:927
  521.8 47.9 %shard_map.377 = (bf16[1024,768]{1,0:T(8,128)(2,1)}, bf16[1024,768]{1,0:T(8,128)(2,1)}, bf16[1024,768]{1,0:T(8,128)(2,1)}, bf16[1024,2048]{1,0:T(8,128)(2,1)}, b...) custom-call(bf16[1024,2048]{1,0:T(8,128)(2,1)} %get-tuple-element.122.refs_0_.refs_5_.refs_6_, ...), custom_call_target="tpu_custom_call" | custom-call | flops 19327352832 | bytes 30932992 | tf_op jit(solution)/shard_map/pallas_call | solution.py:848
  569.8 46.2 %shard_map.378 = (bf16[4,3,512,768]{3,2,1,0:T(8,128)(2,1)}, f32[2048,128]{1,0:T(8,128)}, f32[128,2048]{1,0:T(8,128)}) custom-call(bf16[1024,2048]{1,0:T(8,128)(2,1)} %get-tuple-element.113.refs_0_, bf16[1024,2048]{1,0:T(8,128)(2,1)} %get-tuple-element.114.refs_1_, bf16[1024,768]{1,0:T(8,128)(2,1)} %get-tuple-element.157.refs_2_, ...), custom_call_target="tpu_custom_call" | custom-call | flops 19327352832 | bytes 35651584 | tf_op jit(solution)/shard_map/pallas_call | solution.py:927
  617.6 0.9 fusion.22
  618.5 4.2 shard_map.383
  622.7 1.7 reshape.245
  624.8 2.5 fusion.34
  627.4 49.3 %shard_map.379 = (bf16[1024,768]{1,0:T(8,128)(2,1)}, f32[1,768]{1,0:T(1,128)}, bf16[1024,2048]{1,0:T(8,128)(2,1)}, bf16[1024,2048]{1,0:T(8,128)(2,1)}) custom-call(s32[1]{0:T(128)} %bitcast.3.refs_0_.refs_4_, bf16[1024,2048]{1,0:T(8,128)(2,1)} %get-tuple-element.154.refs_1_, bf16[4,512,1024]{2,1,0:T(8,128)(2,1)} %get-tuple-element.108.refs_3_.refs_2_, ...), custom_call_target="tpu_custom_call" | custom-call | flops 6442450944 | bytes 16777216 | tf_op jit(solution)/shard_map/pallas_call | solution.py:1310
  676.7 46.4 %shard_map.380 = (bf16[1024,768]{1,0:T(8,128)(2,1)}, f32[1,768]{1,0:T(1,128)}, bf16[1024,2048]{1,0:T(8,128)(2,1)}, f32[128,2048]{1,0:T(8,128)}) custom-call(s32[1]{0:T(128)} %bitcast.2.refs_0_.refs_4_, bf16[1024,2048]{1,0:T(8,128)(2,1)} %get-tuple-element.170.refs_1_.refs_5_, bf16[4,512,1024]{2,1,0:T(8,128)(2,1)} %get-tuple-element.108.refs_3_.refs_2_, ...), custom_call_target="tpu_custom_call" | custom-call | flops 6442450944 | bytes 16777216 | tf_op jit(solution)/shard_map/pallas_call | solution.py:1310
  724.0 44.4 %shard_map.381 = (bf16[4,512,1024]{2,1,0:T(8,128)(2,1)}, f32[128,2048]{1,0:T(8,128)}) custom-call(bf16[1024,2048]{1,0:T(8,128)(2,1)} %get-tuple-element.153.refs_0_, bf16[1024,2048]{1,0:T(8,128)(2,1)} %get-tuple-element.154.refs_1_, bf16[1024,768]{1,0:T(8,128)(2,1)} %get-tuple-element.167.refs_2_, bf16[1024,256]{1,0:T(8,128)(2,1)} %get-tuple-element.168.refs_3_, ...), custom_call_target="tpu_custom_call" | custom-call | flops 8589934592 | bytes 33554432 | tf_op jit(solution)/shard_map/pallas_call | solution.py:980
  768.4 2.2 fusion.13
  771.5 2.5 fusion.25
  774.0 1.1 maximum_bitcast_fusion.1
  775.0 49.3 %shard_map.382 = (f32[128,2048]{1,0:T(8,128)}, f32[512,1024]{1,0:T(8,128)}, f32[8,128]{1,0:T(8,128)}) custom-call(bf16[1024,2048]{1,0:T(8,128)(2,1)} %get-tuple-element.152.refs_0_, bf16[4,512,1024]{2,1,0:T(8,128)(2,1)} %get-tuple-element.177.refs_1_, f32[32,8,128]{2,1,0:T(8,128)} %bitcast.101, bf16[3,512,768]{2,1,0:T(8,128)(2,1)} %bitcast.90), custom_call_target="tpu_custom_call" | custom-call | tf_op jit(solution)/shard_map/pallas_call | solution.py:684
  824.4 1.4 fusion.39
  826.5 0.7 slice.119
  827.2 6.4 shard_map.384
  835.6 1.4 slice_bitcast_fusion
  837.0 2.1 copy.95
  839.1 1.4 fusion.23
  840.5 1.1 maximum_bitcast_fusion
  (105 shorter events, 12.9 us)
Async XLA Ops:
  7.2 236.0 %all-gather.7.cloned.1.call-start = ((), (), s32[]{:S(2)}) async-start(), calls=%async_computation.6 | async-start | bytes 11796480 | tf_op jit(solution)/shard_map/all_gather | solution.py:1431
  73.7 1.6 copy-start.13
  73.7 213.4 %all-gather.9.cloned.1.call-start = ((), (), s32[]{:S(2)}) async-start(), calls=%async_computation.7 | async-start | bytes 9830400 | tf_op jit(solution)/shard_map/all_gather | solution.py:1431
  73.8 3.6 copy-start.10
  74.5 317.9 %all-gather.11.cloned.1.call-start = ((), (), s32[]{:S(2)}) async-start(), calls=%async_computation.8 | async-start | bytes 11796480 | tf_op jit(solution)/shard_map/all_gather | solution.py:1431
  74.5 6.5 copy-start.19
  75.2 494.6 %reduce-scatter.4.cloned.1.call-start = ((), (), s32[]{:S(2)}) async-start(), calls=%async_computation.3 | async-start | bytes 11796480 | tf_op jit(solution)/shard_map/reduce_scatter | solution.py:1476
  77.6 48.0 %copy-start.11 = (f32[32,64]{1,0:T(8,128)}, f32[32,64]{1,0:T(8,128)S(1)}, u32[]{:S(2)}) copy-start(f32[32,64]{1,0:T(8,128)S(1)} %get-tuple-element.322) | copy-start | bytes 24580
  125.6 59.0 %copy-start.2 = (bf16[2,1,128,2048]{3,2,1,0:T(8,128)(2,1)S(1)}, bf16[2,1,128,2048]{3,2,1,0:T(8,128)(2,1)}, u32[]{:S(2)}) copy-start(bf16[2,1,128,2048]{3,2,1,0:T(8,128)(2,1)} %refs_7_.4) | copy-start | bytes 3145732
  241.1 1.2 copy-start
  241.1 46.0 %copy-start.14 = (f32[128]{0:T(128)}, f32[128]{0:T(128)S(1)}, u32[]{:S(2)}) copy-start(f32[128]{0:T(128)S(1)} %add_rsqrt_fusion.2) | copy-start | bytes 1540
  391.6 285.1 %reduce-scatter.6.cloned.1.call-start = ((), (), s32[]{:S(2)}) async-start(), calls=%async_computation.4 | async-start | bytes 9830400 | tf_op jit(solution)/shard_map/reduce_scatter | solution.py:1476
  472.3 1.8 copy-start.5
  472.3 2.0 copy-start.8
  521.8 253.2 %reduce-scatter.8.cloned.1.call-start = ((), (), s32[]{:S(2)}) async-start(), calls=%async_computation.5 | async-start | bytes 11796480 | tf_op jit(solution)/shard_map/reduce_scatter | solution.py:1476
  616.0 0.7 copy-start.12
  616.0 1.5 copy-start.17
  616.0 1.5 copy-start.18
  616.0 1.5 copy-start.9
  618.5 5.9 copy-start.1
  618.5 5.9 copy-start.4
  618.5 5.9 copy-start.15
  676.7 46.4 %copy-start.16 = (f32[1,768]{1,0:T(1,128)S(1)}, f32[1,768]{1,0:T(1,128)}, u32[]{:S(2)}) copy-start(f32[1,768]{1,0:T(1,128)} %get-tuple-element.181) | copy-start | bytes 9220
  724.0 44.4 %copy-start.3 = (bf16[2,1,128,2048]{3,2,1,0:T(8,128)(2,1)S(1)}, bf16[2,1,128,2048]{3,2,1,0:T(8,128)(2,1)}, u32[]{:S(2)}) copy-start(bf16[2,1,128,2048]{3,2,1,0:T(8,128)(2,1)} %refs_7_.4) | copy-start | bytes 3145732
  824.3 11.3 %copy-start.6 = (f32[512,1024]{1,0:T(8,128)S(1)}, f32[512,1024]{1,0:T(8,128)}, u32[]{:S(2)}) copy-start(f32[512,1024]{1,0:T(8,128)} %get-tuple-element.186) | copy-start | bytes 6291460
  837.0 3.5 copy-start.7
Sparse Core Ops, SparseCore 0:
  73.8 93.1 all-gather.6
  168.9 83.2 all-gather.8
  254.0 96.3 all-gather.10
  391.7 93.4 reduce-scatter.3
  521.9 83.5 reduce-scatter.5
  616.2 96.3 reduce-scatter.7

commit v7 on v6

--- a/solution.py
+++ b/solution.py
@@ -719,7 +719,8 @@
     position = first_row + lax.broadcasted_iota(jnp.int32, (rows.shape[0], 1), 0)
     valid = jnp.where(position < length, 1.0, 0.0)
     gate = valid * jax.nn.sigmoid(column(logits, experts))
-    chosen = valid * jnp.max(jnp.where(routes == rank, 1.0, 0.0), axis=1, keepdims=True)
+    named = jnp.max(jnp.where(routes == rank, 1.0, 0.0), axis=0, keepdims=True)
+    chosen = valid * jnp.broadcast_to(named, (8, rows.shape[0])).T[:, :1]
     prob = column(probs, rank)
     out = jnp.where(lanes == experts, gate, probs)
     out = jnp.where(lanes == experts + 1, chosen * prob, out)
@@ -758,20 +759,15 @@
     phases = transfers.begin(sent, landed, refs)
     step = pl.program_id(0)
 
-    def fetch(which):
-        return pltpu.make_async_copy(w_ref.at[:, which], w_vmem.at[which], w_sem.at[which])
-
-    @pl.when(step == 0)
-    def _():
-        for which in range(3):
-            fetch(which).start()
-
-    def weight(which):
-        pl.when(step == 0)(lambda: fetch(which).wait())
-        _, groups, depth, units = w_vmem.shape
-        return w_vmem[which].reshape(groups * depth, units)
+    def weights():
+        return pltpu.make_async_copy(w_ref, w_vmem, w_sem)
+
+    pl.when(step == 0)(lambda: weights().start())
 
     def hidden_part(_):
+        pl.when(step == 0)(lambda: weights().wait())
+        groups, _, depth, units = w_vmem.shape
+        gate_w, up_w, down_w = [w_vmem[:, i].reshape(groups * depth, units) for i in range(3)]
         rows, grad = rows_ref[...], grad_ref[...]
         if first:
             length = before[0][0]
@@ -780,11 +776,8 @@
         else:
             route = route_ref[...]
         scale = column(route, experts if first else experts + 1)
-        gate_w = weight(0)
         gate_act = dot(rows, gate_w, (1,), (0,))
-        up_w = weight(1)
         up_act = dot(rows, up_w, (1,), (0,))
-        down_w = weight(2)
         back = dot(grad, down_w, (1,), (0,))
         sigmoid = 1.0 / (1.0 + jnp.exp(-gate_act))
         silu = gate_act * sigmoid
@@ -848,7 +841,12 @@
     results = pl.pallas_call(
         functools.partial(ffn_kernel, transfers, at, steps, experts, kind),
         grid=(steps,),
-        in_specs=[block(width), block(width), block(route.shape[1]), pl.BlockSpec(memory_space=pl.ANY)]
+        in_specs=[
+            block(width),
+            block(width),
+            pl.BlockSpec((route.shape[0], ROW_BLOCK), lambda i: (0, i)) if first else block(LANES),
+            pl.BlockSpec(memory_space=pl.ANY),
+        ]
         + given_specs
         + transfers.in_specs,
         out_specs=tuple(
@@ -858,11 +856,7 @@
             + transfers.out_specs
         ),
         out_shape=tuple(narrow + wide + dots + transfers.shapes),
-        scratch_shapes=[
-            pltpu.VMEM((3, weights.shape[0]) + weights.shape[2:], BF),
-            DMA((3,)),
-        ]
-        + transfers.scratch,
+        scratch_shapes=[pltpu.VMEM(weights.shape, BF), DMA] + transfers.scratch,
         compiler_params=transfers.params(),
         cost_estimate=pl.CostEstimate(
             flops=12 * count * width * units,
@@ -966,7 +960,7 @@
         out_ref[0, :, :span] = totals[0].astype(BF)
         out_ref[0, :, span:] = totals[1].astype(BF)
 
-    beside(phases, [(0, 0)], grid_steps, [work])
+    beside(phases, [(0, 0), (grid_steps - 1, 0)], grid_steps, [work])
 
 
 def attention_grads(groups, per_micro, transfers):
@@ -1078,14 +1072,19 @@
 
 def unpack(ranges, units, turned):
     depth = ranges[0].shape[1]
-    vmem = pl.BlockSpec(memory_space=pltpu.VMEM)
+    rows = min(LANES, depth)
+    shapes = [(units, depth) if turn else (depth, units) for turn in turned]
     return pl.pallas_call(
         functools.partial(unpack_kernel, turned),
-        in_specs=[vmem] * len(ranges),
-        out_specs=(vmem,) * 3,
-        out_shape=tuple(
-            jax.ShapeDtypeStruct((units, depth) if turn else (depth, units), F32) for turn in turned
+        grid=(depth // rows,),
+        in_specs=[pl.BlockSpec((3, rows, array.shape[2]), lambda i: (0, i, 0)) for array in ranges],
+        out_specs=tuple(
+            pl.BlockSpec((units, rows), lambda i: (0, i))
+            if turn
+            else pl.BlockSpec((rows, units), lambda i: (i, 0))
+            for turn in turned
         ),
+        out_shape=tuple(jax.ShapeDtypeStruct(shape, F32) for shape in shapes),
         compiler_params=pltpu.CompilerParams(vmem_limit_bytes=VMEM_BYTES),
         cost_estimate=pl.CostEstimate(flops=0, bytes_accessed=18 * depth * units, transcendentals=0),
     )(*ranges)
@@ -1221,6 +1220,8 @@
     query_sums = [jnp.zeros((1, HD), F32) for _ in range(heads)]
     for i in range(len(blocks)):
         row, end = i * QB, (i + 1) * QB
+        if i >= 2:
+            run_all(phases[i - 1 : i])
         fetch(i).wait()
         grad_vmem[row:end, :] = dot(rows_vmem[row:end, :], out_w, (1,), (0,)).astype(BF)
         for head in range(heads):
@@ -1242,6 +1243,8 @@
             query_sums[head] += jnp.sum(grad_query.astype(F32), axis=0, keepdims=True)
             key_acc[:end, q_at : q_at + HD] += dot(grad_scores, query, (0,), (0,))
             value_acc[:end, q_at : q_at + HD] += dot(shares.astype(BF), grad, (0,), (0,))
+    done = max(1, len(blocks) - 1)
+    run_all(phases[done : done + 1])
     key_sums = [jnp.zeros((1, HD), F32) for _ in range(heads)]
     value_sums = [jnp.zeros((1, HD), F32) for _ in range(heads)]
     for i in range(len(blocks)):
@@ -1263,7 +1266,7 @@
         sums_ref[:, at * HD : (at + 1) * HD] = sums
     for i in range(len(blocks)):
         give(i).wait()
-    run_all(phases[1:])
+    run_all(phases[done + 1 :])
 
 
 def in_vmem(count):
@@ -1489,7 +1492,7 @@
     part = functools.partial(ffn, experts)
     single = ((0, 0), (1, 0), (2, 0), (3, 0))
     act[0, 0], acc_a, (grad_b,) = part(
-        "first", two_a, grad_a, routes[0, 0], weights[0], [lengths[0]], router_wide,
+        "first", two_a, grad_a, routes[0, 0].T, weights[0], [lengths[0]], router_wide,
         moving(6, ("gather", cotangent, (1, 0))), single,
     )
     acc_a, route_a = acc_a[:3], acc_a[3]
@@ -1498,7 +1501,7 @@
         moving(7, ("gather", norm_b[3])), single,
     )
     act[0, 1], acc_b, _ = part(
-        "first", two_b, grad_b, routes[1, 0], weights[0], [lengths[1]], router_wide, idle
+        "first", two_b, grad_b, routes[1, 0].T, weights[0], [lengths[1]], router_wide, idle
     )
     acc_b, route_b = acc_b[:3], acc_b[3]
     (grads_0,), _ = grads_of(0, idle)

time: 853 us -> 836 us (0.980)
  Pallas kernels: 781 us -> 765 us
    pallas_call x6, Pallas kernels: 249 us -> 238 us  [ffn(): pl.pallas_call(functools.partial(ffn_kernel, transfers, at, steps, expert...]
  transfers between devices with their start and end apart: 6 -> 6, of which waited for: 0 -> 0; matrix products, arithmetic and copies ran while one was open for 4% -> 3% of each run, Pallas kernels for 79% -> 79%
where the time goes in v7:
time: 836 us; the launch traced here: 832 us
  Pallas kernels  765 us (92%)
  other arithmetic  26.1 us (3%)
  local copies, waits for them, and re-layouts  23.7 us (3%)
  between operations  14.9 us (2%)
    pallas_call x6, Pallas kernels, ffn(): pl.pallas_call(functools.partial(ffn_kernel, transfers, at, steps, expert...  238 us
    pallas_call x3, Pallas kernels, ffn_grads(): pl.pallas_call(functools.partial(ffn_grads_kernel, transfers, at, groups,...  123 us
    pallas_call x2, Pallas kernels, attend(): pl.pallas_call(functools.partial(attend_kernel, heads, transfers), out_sh...  103 us
    pallas_call x2, Pallas kernels, exchange(): pl.pallas_call(functools.partial(exchange_kernel, transfers), out_shape=t...  100 us
    pallas_call x2, Pallas kernels, attend_back(): pl.pallas_call(functools.partial(attend_back_kernel, heads, transfers), o...  88.9 us
    pallas_call x1, Pallas kernels, opening(): pl.pallas_call(functools.partial(opening_kernel, transfers, cut), in_spec...  57.3 us
    pallas_call x1, Pallas kernels, attention_grads(): pl.pallas_call(functools.partial(attention_grads_kernel, transfers, group...  44.3 us
  transfers between devices with their start and end apart: 6, of which 0 were waited for; matrix products, arithmetic and copies ran while one was open for 3% of the time, Pallas kernels for 79%

profile of v7, /device:TPU:0, one launch (start us, length us, event | category | flops | bytes accessed | tf_op | source)
XLA Modules:
  0.0 831.6 jit_solution(15026267681054585411)
XLA Ops:
  7.2 0.7 reshape.235
  8.0 0.7 reshape.236
  8.7 0.7 reshape.237
  9.4 0.8 copy.77
  10.3 2.1 concatenate.12
  13.0 1.1 copy.78
  14.1 2.2 pad_maximum_fusion.refs_1_
  16.3 57.3 %shard_map.366 = (bf16[32,16,128]{2,1,0:T(8,128)(2,1)}, bf16[4,512,1024]{2,1,0:T(8,128)(2,1)}, bf16[1024,2048]{1,0:T(8,128)(2,1)}, bf16[3,512,768]{2,1,0:T(8,128...) custom-call(bf16[16,128]{1,0:T(8,128)(2,1)} %pad_bitcast_fusion.refs_0_, ...), custom_call_target="tpu_custom_call" | custom-call | tf_op jit(solution)/shard_map/pallas_call | solution.py:1043
  73.8 0.7 all-gather.9.cloned.1.call-update
  77.8 1.1 broadcast_in_dim_reshape.4
  79.5 44.5 %shard_map.367 = (bf16[1024,2048]{1,0:T(8,128)(2,1)}, bf16[1024,768]{1,0:T(8,128)(2,1)}, bf16[1024,256]{1,0:T(8,128)(2,1)}, f32[1024,2]{1,0:T(8,128)}, bf16[1024...) custom-call(s32[1]{0:T(128)} %bitcast.3.refs_0_.refs_4_, bf16[1024,2048]{1,0:T(8,128)(2,1)} %get-tuple-element.106.refs_1_, ...), custom_call_target="tpu_custom_call" | custom-call | flops 5100273664 | bytes 16777216 | tf_op jit(solution)/shard_map/pallas_call | solution.py:1281
  124.0 58.9 %shard_map.368 = (bf16[1024,2048]{1,0:T(8,128)(2,1)}, bf16[1024,768]{1,0:T(8,128)(2,1)}, bf16[1024,256]{1,0:T(8,128)(2,1)}, f32[1024,2]{1,0:T(8,128)}, bf16[1024...) custom-call(s32[1]{0:T(128)} %bitcast.2.refs_0_.refs_4_, ...), custom_call_target="tpu_custom_call" | custom-call | flops 5100273664 | bytes 16777216 | tf_op jit(solution)/shard_map/pallas_call | solution.py:1281
  183.0 2.1 fusion.19
  185.1 1.0 multiply_convert_fusion.3.refs_0_
  186.1 52.0 %shard_map.369 = (bf16[1024,2048]{1,0:T(8,128)(2,1)}, f32[128,2048]{1,0:T(8,128)}) custom-call(bf16[128,2048]{1,0:T(8,128)(2,1)} %multiply_convert_fusion.3.refs_0_, bf16[1024,2048]{1,0:T(8,128)(2,1)} %get-tuple-element.112.refs_1_), custom_call_target="tpu_custom_call" | custom-call | tf_op jit(solution)/shard_map/pallas_call | solution.py:684
  238.1 1.5 multiply_reduce_fusion.4
  240.3 1.1 fusion.24.refs_5_.refs_7_
  241.4 0.9 multiply_convert_fusion.2.refs_7_
  242.4 43.1 %shard_map.370 = (bf16[1024,768]{1,0:T(8,128)(2,1)}, bf16[1024,768]{1,0:T(8,128)(2,1)}, bf16[1024,768]{1,0:T(8,128)(2,1)}, bf16[1024,2048]{1,0:T(8,128)(2,1)}, b...) custom-call(bf16[1024,2048]{1,0:T(8,128)(2,1)} %get-tuple-element.113.refs_0_, ...), custom_call_target="tpu_custom_call" | custom-call | flops 19327352832 | bytes 30932992 | tf_op jit(solution)/shard_map/pallas_call | solution.py:841
  285.5 43.1 %shard_map.371 = (bf16[1024,640]{1,0:T(8,128)(2,1)}, bf16[1024,640]{1,0:T(8,128)(2,1)}, bf16[1024,640]{1,0:T(8,128)(2,1)}, bf16[1024,2048]{1,0:T(8,128)(2,1)}, b...) custom-call(bf16[1024,2048]{1,0:T(8,128)(2,1)} %get-tuple-element.113.refs_0_, ...), custom_call_target="tpu_custom_call" | custom-call | flops 16106127360 | bytes 28573696 | tf_op jit(solution)/shard_map/pallas_call | solution.py:841
  328.6 29.6 %shard_map.372 = (bf16[1024,768]{1,0:T(8,128)(2,1)}, bf16[1024,768]{1,0:T(8,128)(2,1)}, bf16[1024,768]{1,0:T(8,128)(2,1)}, bf16[1024,2048]{1,0:T(8,128)(2,1)}, b...) custom-call(bf16[1024,2048]{1,0:T(8,128)(2,1)} %get-tuple-element.122.refs_0_.refs_5_.refs_6_, ...), custom_call_target="tpu_custom_call" | custom-call | flops 19327352832 | bytes 30932992 | tf_op jit(solution)/shard_map/pallas_call | solution.py:841
  358.2 27.1 %shard_map.373.refs_8_ = bf16[4,3,512,768]{3,2,1,0:T(8,128)(2,1)} custom-call(bf16[1024,2048]{1,0:T(8,128)(2,1)} %get-tuple-element.113.refs_0_, bf16[1024,2048]{1,0:T(8,128)(2,1)} %get-tuple-element.114.refs_1_, bf16[1024,768]{1,0:T(8,128)(2,1)} %get-tuple-element.132.refs_2_, bf16[1024,768]{1,0:T(8,128)(2,1)} %get-tuple-element.133.refs_3_, ...), custom_call_target="tpu_custom_call" | custom-call | flops 19327352832 | bytes 35651584 | tf_op jit(solution)/shard_map/pallas_call | solution.py:921
  386.1 32.9 %shard_map.374 = (bf16[1024,768]{1,0:T(8,128)(2,1)}, bf16[1024,768]{1,0:T(8,128)(2,1)}, bf16[1024,768]{1,0:T(8,128)(2,1)}, bf16[1024,2048]{1,0:T(8,128)(2,1)}, b...) custom-call(bf16[1024,2048]{1,0:T(8,128)(2,1)} %get-tuple-element.113.refs_0_, ...), custom_call_target="tpu_custom_call" | custom-call | flops 19327352832 | bytes 30932992 | tf_op jit(solution)/shard_map/pallas_call | solution.py:841
  419.0 43.7 %shard_map.375 = (bf16[1024,640]{1,0:T(8,128)(2,1)}, bf16[1024,640]{1,0:T(8,128)(2,1)}, bf16[1024,640]{1,0:T(8,128)(2,1)}, bf16[1024,2048]{1,0:T(8,128)(2,1)}, b...) custom-call(bf16[1024,2048]{1,0:T(8,128)(2,1)} %get-tuple-element.122.refs_0_.refs_5_.refs_6_, ...), custom_call_target="tpu_custom_call" | custom-call | flops 16106127360 | bytes 28573696 | tf_op jit(solution)/shard_map/pallas_call | solution.py:841
  462.7 1.7 multiply_reduce_fusion.1
  464.7 1.2 fusion.35
  465.8 47.3 %shard_map.376 = (bf16[4,3,512,640]{3,2,1,0:T(8,128)(2,1)}, bf16[1024,2048]{1,0:T(8,128)(2,1)}) custom-call(bf16[1024,2048]{1,0:T(8,128)(2,1)} %get-tuple-element.113.refs_0_, bf16[1024,2048]{1,0:T(8,128)(2,1)} %get-tuple-element.114.refs_1_, bf16[1024,640]{1,0:T(8,128)(2,1)} %get-tuple-element.143.refs_2_, bf16[1024,640]{1,0:T(8,128)(2,1)} %get-tuple-element.144.refs_3_, ...), custom_call_target="tpu_custom_call" | custom-call | flops 16106127360 | bytes 32505856 | tf_op jit(solution)/shard_map/pallas_call | solution.py:921
  513.2 45.5 %shard_map.377 = (bf16[1024,768]{1,0:T(8,128)(2,1)}, bf16[1024,768]{1,0:T(8,128)(2,1)}, bf16[1024,768]{1,0:T(8,128)(2,1)}, bf16[1024,2048]{1,0:T(8,128)(2,1)}, b...) custom-call(bf16[1024,2048]{1,0:T(8,128)(2,1)} %get-tuple-element.122.refs_0_.refs_5_.refs_6_, ...), custom_call_target="tpu_custom_call" | custom-call | flops 19327352832 | bytes 30932992 | tf_op jit(solution)/shard_map/pallas_call | solution.py:841
  558.8 48.1 %shard_map.378 = (bf16[4,3,512,768]{3,2,1,0:T(8,128)(2,1)}, f32[2048,128]{1,0:T(8,128)}, f32[128,2048]{1,0:T(8,128)}) custom-call(bf16[1024,2048]{1,0:T(8,128)(2,1)} %get-tuple-element.113.refs_0_, bf16[1024,2048]{1,0:T(8,128)(2,1)} %get-tuple-element.114.refs_1_, bf16[1024,768]{1,0:T(8,128)(2,1)} %get-tuple-element.157.refs_2_, ...), custom_call_target="tpu_custom_call" | custom-call | flops 19327352832 | bytes 35651584 | tf_op jit(solution)/shard_map/pallas_call | solution.py:921
  608.5 0.9 fusion.22
  609.4 4.6 shard_map.383
  614.0 1.7 reshape.245
  616.1 2.5 fusion.34
  618.7 46.7 %shard_map.379 = (bf16[1024,768]{1,0:T(8,128)(2,1)}, f32[1,768]{1,0:T(1,128)}, bf16[1024,2048]{1,0:T(8,128)(2,1)}, bf16[1024,2048]{1,0:T(8,128)(2,1)}) custom-call(s32[1]{0:T(128)} %bitcast.3.refs_0_.refs_4_, bf16[1024,2048]{1,0:T(8,128)(2,1)} %get-tuple-element.154.refs_1_, bf16[4,512,1024]{2,1,0:T(8,128)(2,1)} %get-tuple-element.108.refs_3_.refs_2_, ...), custom_call_target="tpu_custom_call" | custom-call | flops 6442450944 | bytes 16777216 | tf_op jit(solution)/shard_map/pallas_call | solution.py:1313
  665.4 42.2 %shard_map.380 = (bf16[1024,768]{1,0:T(8,128)(2,1)}, f32[1,768]{1,0:T(1,128)}, bf16[1024,2048]{1,0:T(8,128)(2,1)}, f32[128,2048]{1,0:T(8,128)}) custom-call(s32[1]{0:T(128)} %bitcast.2.refs_0_.refs_4_, bf16[1024,2048]{1,0:T(8,128)(2,1)} %get-tuple-element.170.refs_1_.refs_5_, bf16[4,512,1024]{2,1,0:T(8,128)(2,1)} %get-tuple-element.108.refs_3_.refs_2_, ...), custom_call_target="tpu_custom_call" | custom-call | flops 6442450944 | bytes 16777216 | tf_op jit(solution)/shard_map/pallas_call | solution.py:1313
  708.5 44.3 %shard_map.381 = (bf16[4,512,1024]{2,1,0:T(8,128)(2,1)}, f32[128,2048]{1,0:T(8,128)}) custom-call(bf16[1024,2048]{1,0:T(8,128)(2,1)} %get-tuple-element.153.refs_0_, bf16[1024,2048]{1,0:T(8,128)(2,1)} %get-tuple-element.154.refs_1_, bf16[1024,768]{1,0:T(8,128)(2,1)} %get-tuple-element.167.refs_2_, bf16[1024,256]{1,0:T(8,128)(2,1)} %get-tuple-element.168.refs_3_, ...), custom_call_target="tpu_custom_call" | custom-call | flops 8589934592 | bytes 33554432 | tf_op jit(solution)/shard_map/pallas_call | solution.py:974
  752.8 2.2 fusion.13
  755.9 2.5 fusion.25
  758.4 1.1 maximum_bitcast_fusion.1
  759.5 48.2 %shard_map.382 = (f32[128,2048]{1,0:T(8,128)}, f32[512,1024]{1,0:T(8,128)}, f32[8,128]{1,0:T(8,128)}) custom-call(bf16[1024,2048]{1,0:T(8,128)(2,1)} %get-tuple-element.152.refs_0_, bf16[4,512,1024]{2,1,0:T(8,128)(2,1)} %get-tuple-element.177.refs_1_, f32[32,8,128]{2,1,0:T(8,128)} %bitcast.107, bf16[3,512,768]{2,1,0:T(8,128)(2,1)} %bitcast.96), custom_call_target="tpu_custom_call" | custom-call | tf_op jit(solution)/shard_map/pallas_call | solution.py:684
  807.7 1.4 fusion.38
  809.8 0.7 slice.119
  810.5 6.1 shard_map.384
  817.3 0.7 slice_reduce_fusion
  818.7 1.4 slice_bitcast_fusion
  820.0 2.1 copy.85
  822.1 1.4 fusion.23
  823.5 1.1 maximum_bitcast_fusion
  (103 shorter events, 12.2 us)
Async XLA Ops:
  7.2 235.2 %all-gather.7.cloned.1.call-start = ((), (), s32[]{:S(2)}) async-start(), calls=%async_computation.6 | async-start | bytes 11796480 | tf_op jit(solution)/shard_map/all_gather | solution.py:1434
  73.7 1.6 copy-start.10
  73.7 211.8 %all-gather.9.cloned.1.call-start = ((), (), s32[]{:S(2)}) async-start(), calls=%async_computation.7 | async-start | bytes 9830400 | tf_op jit(solution)/shard_map/all_gather | solution.py:1434
  74.5 4.5 copy-start.19
  74.5 311.6 %all-gather.11.cloned.1.call-start = ((), (), s32[]{:S(2)}) async-start(), calls=%async_computation.8 | async-start | bytes 11796480 | tf_op jit(solution)/shard_map/all_gather | solution.py:1434
  75.2 483.6 %reduce-scatter.4.cloned.1.call-start = ((), (), s32[]{:S(2)}) async-start(), calls=%async_computation.3 | async-start | bytes 11796480 | tf_op jit(solution)/shard_map/reduce_scatter | solution.py:1479
  75.5 48.5 %copy-start.11 = (f32[32,64]{1,0:T(8,128)}, f32[32,64]{1,0:T(8,128)S(1)}, u32[]{:S(2)}) copy-start(f32[32,64]{1,0:T(8,128)S(1)} %get-tuple-element.322) | copy-start | bytes 24580
  124.0 59.0 %copy-start.2 = (bf16[2,1,128,2048]{3,2,1,0:T(8,128)(2,1)S(1)}, bf16[2,1,128,2048]{3,2,1,0:T(8,128)(2,1)}, u32[]{:S(2)}) copy-start(bf16[2,1,128,2048]{3,2,1,0:T(8,128)(2,1)} %refs_7_.4) | copy-start | bytes 3145732
  238.1 1.5 copy-start.13
  239.5 1.9 copy-start
  239.6 45.9 %copy-start.14 = (f32[128]{0:T(128)}, f32[128]{0:T(128)S(1)}, u32[]{:S(2)}) copy-start(f32[128]{0:T(128)S(1)} %add_rsqrt_fusion.2) | copy-start | bytes 1540
  385.3 280.1 %reduce-scatter.6.cloned.1.call-start = ((), (), s32[]{:S(2)}) async-start(), calls=%async_computation.4 | async-start | bytes 9830400 | tf_op jit(solution)/shard_map/reduce_scatter | solution.py:1479
  462.7 1.8 copy-start.5
  462.7 1.9 copy-start.8
  513.2 246.3 %reduce-scatter.8.cloned.1.call-start = ((), (), s32[]{:S(2)}) async-start(), calls=%async_computation.5 | async-start | bytes 11796480 | tf_op jit(solution)/shard_map/reduce_scatter | solution.py:1479
  606.9 0.7 copy-start.12
  606.9 1.5 copy-start.17
  606.9 1.5 copy-start.18
  606.9 1.5 copy-start.9
  609.4 6.3 copy-start.1
  609.4 6.3 copy-start.4
  609.4 6.3 copy-start.15
  665.4 42.2 %copy-start.16 = (f32[1,768]{1,0:T(1,128)S(1)}, f32[1,768]{1,0:T(1,128)}, u32[]{:S(2)}) copy-start(f32[1,768]{1,0:T(1,128)} %get-tuple-element.181) | copy-start | bytes 9220
  708.5 44.3 %copy-start.3 = (bf16[2,1,128,2048]{3,2,1,0:T(8,128)(2,1)S(1)}, bf16[2,1,128,2048]{3,2,1,0:T(8,128)(2,1)}, u32[]{:S(2)}) copy-start(bf16[2,1,128,2048]{3,2,1,0:T(8,128)(2,1)} %refs_7_.4) | copy-start | bytes 3145732
  807.7 11.0 %copy-start.6 = (f32[512,1024]{1,0:T(8,128)S(1)}, f32[512,1024]{1,0:T(8,128)}, u32[]{:S(2)}) copy-start(f32[512,1024]{1,0:T(8,128)} %get-tuple-element.186) | copy-start | bytes 6291460
  820.0 3.5 copy-start.7
Sparse Core Ops, SparseCore 0:
  73.8 93.1 all-gather.6
  168.9 83.2 all-gather.8
  254.0 96.3 all-gather.10
  385.5 93.0 reduce-scatter.3
  513.3 81.2 reduce-scatter.5
  607.1 94.6 reduce-scatter.7

commit v8 on v7

--- a/solution.py
+++ b/solution.py
@@ -360,69 +360,6 @@
     )
 
 
-def cross_gather_steps(place, block, whole, own_sem, send, recv):
-    group = place.group
-    half = block.shape[0] // 2
-
-    def own():
-        return pltpu.make_async_copy(block, whole.at[group], own_sem)
-
-    if not place.square:
-
-        def direct(i):
-            target = lax.rem(group + i, place.groups)
-            return to_group(block, whole.at[group], send, recv, i - 1, target)
-
-        def begin_direct():
-            own().start()
-            for i in range(1, place.groups):
-                direct(i).start()
-
-        def end_direct():
-            own().wait()
-            for i in range(1, place.groups):
-                source = lax.rem(group - i + place.groups, place.groups)
-                to_group(block, whole.at[source], send, recv, i - 1, source).wait_recv()
-                direct(i).wait_send()
-
-        return [begin_direct, end_direct]
-
-    def near(at):
-        return to_group(block, whole.at[group], send, recv, at, (place.beside, place.across)[at])
-
-    def came(at):
-        source = (place.beside, place.across)[at]
-        return to_group(whole.at[source], whole.at[source], send, recv, at, source)
-
-    def forward(at):
-        source, target = ((place.beside, place.across), (place.across, place.beside))[at]
-        piece = whole.at[source, pl.ds(at * half, half)]
-        return to_group(piece, piece, send, recv, 2 + at, target)
-
-    def far(at):
-        piece = whole.at[place.opposite, pl.ds(at * half, half)]
-        return to_group(piece, piece, send, recv, 2 + at, place.opposite)
-
-    def begin():
-        for at in range(2):
-            near(at).start()
-        own().start()
-
-    def pass_on():
-        for at in range(2):
-            came(at).wait_recv()
-            forward(at).start()
-
-    def end():
-        own().wait()
-        for at in range(2):
-            far(at).wait_recv()
-            near(at).wait_send()
-            forward(at).wait_send()
-
-    return [begin] + [nothing] * 4 + [pass_on, nothing, end]
-
-
 def cross_scatter_steps(place, partial, total, mine, near_in, far_in, own_sem, send, recv):
     group = place.group
     rows = total.shape[0]
@@ -472,17 +409,24 @@
         piece = partial.at[place.opposite, pl.ds(at * half, half)]
         return to_group(piece, far_in.at[at], send, recv, at, target)
 
-    def second(at):
+    def second(at, part):
         target = (place.beside, place.across)[at]
-        return to_group(mine.at[target], near_in.at[at], send, recv, 2 + at, target)
+        cut = pl.ds(part * half, half)
+        return to_group(
+            mine.at[target, cut], near_in.at[at, cut], send, recv, 2 + 2 * at + part, target
+        )
 
     def begin():
         own().start()
         for at in range(2):
             first(at).start()
 
+    def plain():
+        own().wait()
+        for at in range(2):
+            second(at, at).start()
+
     def join():
-        own().wait()
         for at in range(2):
             target = (place.across, place.beside)[at]
             first(at).wait_recv()
@@ -493,7 +437,7 @@
                 mine[target, place_in] = value.astype(BF)
 
             loop(half, one)
-            second(1 - at).start()
+            second(1 - at, at).start()
 
     def everything(cut):
         value = mine[group, cut].astype(F32) + near_in[0, cut].astype(F32)
@@ -501,13 +445,15 @@
 
     def end():
         for at in range(2):
-            second(at).wait_recv()
+            for part in range(2):
+                second(at, part).wait_recv()
         loop(rows, everything)
         for at in range(2):
             first(at).wait_send()
-            second(at).wait_send()
-
-    return [begin, nothing, join, nothing, nothing, end]
+            for part in range(2):
+                second(at, part).wait_send()
+
+    return [begin, plain, join, nothing, nothing, nothing, end]
 
 
 def everyone_steps(place, piece_for, landing, own_sem, send, recv):
@@ -595,9 +541,6 @@
             elif kind == "scatter":
                 shape, dtype, spec = (shape[0] // self.ranks, shape[1]), F32, vmem
                 scratch = scatter_scratch(self.ranks, *shape)
-            elif kind == "cross_gather":
-                shape, dtype = (self.groups,) + shape, BF
-                scratch = [DMA, DMA((max(4, self.groups),)), DMA((max(4, self.groups),))]
             elif kind == "cross_scatter":
                 rest = shape[1:]
                 square = self.groups == 4
@@ -607,8 +550,8 @@
                     pltpu.VMEM(near, BF),
                     pltpu.VMEM((2, rest[0] // 2) + rest[1:], BF),
                     DMA,
-                    DMA((max(4, self.groups),)),
-                    DMA((max(4, self.groups),)),
+                    DMA((max(6, self.groups),)),
+                    DMA((max(6, self.groups),)),
                 ]
                 shape, dtype, spec = rest, F32, vmem
             elif kind == "share":
@@ -637,7 +580,6 @@
         steps_of = {
             "gather": gather_steps,
             "scatter": scatter_steps,
-            "cross_gather": cross_gather_steps,
             "cross_scatter": cross_scatter_steps,
             "spread": spread_steps,
             "share": share_steps,
@@ -655,7 +597,7 @@
                 kinds = set(self.kinds)
                 place.meet(
                     bool(kinds & {"gather", "scatter"}),
-                    bool(kinds & {"cross_gather", "cross_scatter"}),
+                    "cross_scatter" in kinds,
                     bool(kinds & {"spread", "share"}),
                 )
             for steps in lines:
@@ -1125,7 +1067,7 @@
     sent = take(len(transfers.inputs))
     normed_ref, qkv_ref, mixed_ref, logs_ref, out_ref = take(5)
     landed = take(transfers.moves)
-    rows_vmem, out_vmem, in_sem, normed_sem, out_sem = take(5)
+    rows_vmem, out_vmem, w_vmem, in_sem, normed_sem, out_sem, w_sem = take(7)
     phases = transfers.begin(sent, landed, refs)
     seq_len, width = x_ref.shape
     groups, depth, columns = w_ref.shape
@@ -1142,10 +1084,14 @@
     def give(i):
         return pltpu.make_async_copy(out_vmem.at[blocks[i]], out_ref.at[blocks[i]], out_sem.at[i])
 
-    for i in range(len(blocks)):
+    fetch_w = pltpu.make_async_copy(w_ref, w_vmem, w_sem)
+    fetch(0).start()
+    fetch_w.start()
+    run_all(phases[:1])
+    for i in range(1, len(blocks)):
         fetch(i).start()
-    run_all(phases[:1])
-    weights = w_ref[...].reshape(groups * depth, columns)
+    fetch_w.wait()
+    weights = w_vmem[...].reshape(groups * depth, columns)
     qkv_w, out_w = weights[:, : 3 * span], weights[:, 3 * span :]
     for i in range(len(blocks)):
         row, end = i * QB, (i + 1) * QB
@@ -1195,7 +1141,7 @@
     sent = take(len(transfers.inputs))
     turned_ref, sums_ref, out_ref = take(3)
     landed = take(transfers.moves)
-    rows_vmem, out_vmem, grad_vmem, key_acc, value_acc, in_sem, out_sem = take(7)
+    rows_vmem, out_vmem, w_vmem, grad_vmem, key_acc, value_acc, in_sem, out_sem, w_sem = take(9)
     phases = transfers.begin(sent, landed, refs)
     run_all(phases[:1])
     seq_len, width = datt_ref.shape
@@ -1211,9 +1157,12 @@
     def give(i):
         return pltpu.make_async_copy(out_vmem.at[blocks[i]], out_ref.at[blocks[i]], out_sem.at[i])
 
+    fetch_w = pltpu.make_async_copy(w_ref, w_vmem, w_sem)
+    fetch_w.start()
     for i in range(len(blocks)):
         fetch(i).start()
-    weights = w_ref[...].reshape(groups * depth, columns)
+    fetch_w.wait()
+    weights = w_vmem[...].reshape(groups * depth, columns)
     qkv_w, out_w = weights[:, : 3 * span], weights[:, 3 * span :]
     key_acc[...] = jnp.zeros_like(key_acc)
     value_acc[...] = jnp.zeros_like(value_acc)
@@ -1290,10 +1239,16 @@
             ]
             + transfers.shapes
         ),
-        in_specs=[pl.BlockSpec(memory_space=pltpu.SMEM), anywhere] + in_vmem(5) + transfers.in_specs,
+        in_specs=[pl.BlockSpec(memory_space=pltpu.SMEM), anywhere]
+        + in_vmem(1)
+        + [anywhere]
+        + in_vmem(3)
+        + transfers.in_specs,
         out_specs=tuple([anywhere] + in_vmem(3) + [anywhere] + transfers.out_specs),
         scratch_shapes=[pltpu.VMEM((seq_len, width), BF)] * 2
+        + [pltpu.VMEM(weights.shape, BF)]
         + [DMA((blocks,))] * 3
+        + [DMA]
         + transfers.scratch,
         compiler_params=transfers.params(),
         cost_estimate=pl.CostEstimate(
@@ -1320,12 +1275,15 @@
             ]
             + transfers.shapes
         ),
-        in_specs=[pl.BlockSpec(memory_space=pltpu.SMEM), anywhere] + in_vmem(5) + transfers.in_specs,
+        in_specs=[pl.BlockSpec(memory_space=pltpu.SMEM), anywhere, anywhere]
+        + in_vmem(4)
+        + transfers.in_specs,
         out_specs=tuple(in_vmem(2) + [anywhere] + transfers.out_specs),
         scratch_shapes=[pltpu.VMEM((seq_len, width), BF)] * 2
-        + [pltpu.VMEM((seq_len, span), BF)]
+        + [pltpu.VMEM(weights.shape, BF), pltpu.VMEM((seq_len, span), BF)]
         + [pltpu.VMEM((seq_len, span), F32)] * 2
         + [DMA((blocks,))] * 2
+        + [DMA]
         + transfers.scratch,
         compiler_params=transfers.params(),
         cost_estimate=pl.CostEstimate(
@@ -1407,12 +1365,14 @@
     )
     attn_own = jnp.concatenate([w_query, w_key, w_value, w_out.T], axis=1)
     mesh_size = (ranks, groups)
-    (small_all, attn_w, rows_a), own_ranges = opening(
+    attn_own = with_layout_constraint(attn_own, Layout((0, 1)))
+    attn_w = lax.all_gather(attn_own, "fsdp", axis=0, tiled=True)
+    attn_w = with_layout_constraint(attn_w, Layout((0, 1))).reshape((groups,) + attn_own.shape)
+    (small_all, rows_a), own_ranges = opening(
         mesh_size,
         2,
         [
             ("spread", packed(small, BF).reshape(-1, LANES)),
-            ("cross_gather", attn_own),
             ("gather", tokens, (0, 0)),
         ],
         cut,
@@ -1561,13 +1521,13 @@
         ],
         axis=1,
     )
-    moved_b, attn_g, shares = exchange(
+    shares, attn_g, moved_b = exchange(
         mesh_size,
         14,
         [
+            ("share", packed(parts, F32).reshape(devices, -1, LANES)),
+            ("cross_scatter", attn_parts),
             ("scatter", acc_b[0]),
-            ("cross_scatter", attn_parts),
-            ("share", packed(parts, F32).reshape(devices, -1, LANES)),
         ],
         [range_2],
     )

time: 836 us -> 815 us (0.975)
  Pallas kernels: 765 us -> 747 us
    pallas_call x1, Pallas kernels: 57.3 us -> 47.5 us  [opening(): pl.pallas_call(functools.partial(opening_kernel, transfers, cut), in_spec...]
  transfers between devices with their start and end apart: 6 -> 7, of which waited for: 0 -> 0; matrix products, arithmetic and copies ran while one was open for 3% -> 4% of each run, Pallas kernels for 79% -> 86%
where the time goes in v8:
time: 815 us; the launch traced here: 810 us
  Pallas kernels  747 us (92%)
  other arithmetic  26.1 us (3%)
  local copies, waits for them, and re-layouts  20.1 us (2%)
  between operations  14.9 us (2%)
    pallas_call x6, Pallas kernels, ffn(): pl.pallas_call(functools.partial(ffn_kernel, transfers, at, steps, expert...  238 us
    pallas_call x3, Pallas kernels, ffn_grads(): pl.pallas_call(functools.partial(ffn_grads_kernel, transfers, at, groups,...  122 us
    pallas_call x2, Pallas kernels, attend(): pl.pallas_call(functools.partial(attend_kernel, heads, transfers), out_sh...  100 us
    pallas_call x2, Pallas kernels, exchange(): pl.pallas_call(functools.partial(exchange_kernel, transfers), out_shape=t...  98.8 us
    pallas_call x2, Pallas kernels, attend_back(): pl.pallas_call(functools.partial(attend_back_kernel, heads, transfers), o...  85 us
    pallas_call x1, Pallas kernels, opening(): pl.pallas_call(functools.partial(opening_kernel, transfers, cut), in_spec...  47.5 us
    pallas_call x1, Pallas kernels, attention_grads(): pl.pallas_call(functools.partial(attention_grads_kernel, transfers, group...  44.3 us
  transfers between devices with their start and end apart: 7, of which 0 were waited for; matrix products, arithmetic and copies ran while one was open for 4% of the time, Pallas kernels for 86%

profile of v8, /device:TPU:0, one launch (start us, length us, event | category | flops | bytes accessed | tf_op | source)
XLA Modules:
  0.0 809.9 jit_solution(3366892189894692208)
XLA Ops:
  7.3 1.1 copy.78
  8.4 2.2 pad_maximum_fusion
  11.9 47.5 %shard_map.366 = (bf16[32,16,128]{2,1,0:T(8,128)(2,1)}, bf16[1024,2048]{1,0:T(8,128)(2,1)}, bf16[3,512,768]{2,1,0:T(8,128)(2,1)}, bf16[3,512,640]{2,1,0:T(8,128)(2,1)}, bf16[3,512,768]{2,1,0:T(8,128)(2,1)}) custom-call(bf16[16,128]{1,0:T(8,128)(2,1)} %pad_bitcast_fusion.refs_0_, bf16[2,1,128,2048]{3,2,1,0:T(8,128)(2,1)} %refs_7_.4, ...), custom_call_target="tpu_custom_call" | custom-call | tf_op jit(solution)/shard_map/pallas_call | solution.py:985
  59.5 0.7 all-gather.12.cloned.1.call-update
  61.2 0.7 reshape.257.refs_2_
  63.4 1.1 broadcast_in_dim_reshape.4
  65.7 1.1 fusion.24.refs_5_.refs_7_
  66.9 42.6 %shard_map.367 = (bf16[1024,2048]{1,0:T(8,128)(2,1)}, bf16[1024,768]{1,0:T(8,128)(2,1)}, bf16[1024,256]{1,0:T(8,128)(2,1)}, f32[1024,2]{1,0:T(8,128)}, bf16[1024...) custom-call(s32[1]{0:T(128)} %bitcast.3.refs_0_.refs_4_, bf16[1024,2048]{1,0:T(8,128)(2,1)} %get-tuple-element.105.refs_1_, ...), custom_call_target="tpu_custom_call" | custom-call | flops 5100273664 | bytes 16777216 | tf_op jit(solution)/shard_map/pallas_call | solution.py:1230
  109.5 57.7 %shard_map.368 = (bf16[1024,2048]{1,0:T(8,128)(2,1)}, bf16[1024,768]{1,0:T(8,128)(2,1)}, bf16[1024,256]{1,0:T(8,128)(2,1)}, f32[1024,2]{1,0:T(8,128)}, bf16[1024...) custom-call(s32[1]{0:T(128)} %bitcast.2.refs_0_.refs_4_, ...), custom_call_target="tpu_custom_call" | custom-call | flops 5100273664 | bytes 16777216 | tf_op jit(solution)/shard_map/pallas_call | solution.py:1230
  167.3 2.1 fusion.19
  169.4 1.0 multiply_convert_fusion.3.refs_0_
  170.3 52.0 %shard_map.369 = (bf16[1024,2048]{1,0:T(8,128)(2,1)}, f32[128,2048]{1,0:T(8,128)}) custom-call(bf16[128,2048]{1,0:T(8,128)(2,1)} %multiply_convert_fusion.3.refs_0_, bf16[1024,2048]{1,0:T(8,128)(2,1)} %get-tuple-element.110.refs_1_), custom_call_target="tpu_custom_call" | custom-call | tf_op jit(solution)/shard_map/pallas_call | solution.py:626
  222.4 1.4 multiply_reduce_fusion.4
  223.9 0.9 copy-done
  224.8 0.9 multiply_convert_fusion.2.refs_7_
  225.8 43.4 %shard_map.370 = (bf16[1024,768]{1,0:T(8,128)(2,1)}, bf16[1024,768]{1,0:T(8,128)(2,1)}, bf16[1024,768]{1,0:T(8,128)(2,1)}, bf16[1024,2048]{1,0:T(8,128)(2,1)}, b...) custom-call(bf16[1024,2048]{1,0:T(8,128)(2,1)} %get-tuple-element.111.refs_0_, ...), custom_call_target="tpu_custom_call" | custom-call | flops 19327352832 | bytes 30932992 | tf_op jit(solution)/shard_map/pallas_call | solution.py:783
  269.2 43.1 %shard_map.371 = (bf16[1024,640]{1,0:T(8,128)(2,1)}, bf16[1024,640]{1,0:T(8,128)(2,1)}, bf16[1024,640]{1,0:T(8,128)(2,1)}, bf16[1024,2048]{1,0:T(8,128)(2,1)}, b...) custom-call(bf16[1024,2048]{1,0:T(8,128)(2,1)} %get-tuple-element.111.refs_0_, ...), custom_call_target="tpu_custom_call" | custom-call | flops 16106127360 | bytes 28573696 | tf_op jit(solution)/shard_map/pallas_call | solution.py:783
  312.3 29.6 %shard_map.372 = (bf16[1024,768]{1,0:T(8,128)(2,1)}, bf16[1024,768]{1,0:T(8,128)(2,1)}, bf16[1024,768]{1,0:T(8,128)(2,1)}, bf16[1024,2048]{1,0:T(8,128)(2,1)}, b...) custom-call(bf16[1024,2048]{1,0:T(8,128)(2,1)} %get-tuple-element.120.refs_0_.refs_5_.refs_6_, ...), custom_call_target="tpu_custom_call" | custom-call | flops 19327352832 | bytes 30932992 | tf_op jit(solution)/shard_map/pallas_call | solution.py:783
  341.8 27.2 %shard_map.373.refs_8_ = bf16[4,3,512,768]{3,2,1,0:T(8,128)(2,1)} custom-call(bf16[1024,2048]{1,0:T(8,128)(2,1)} %get-tuple-element.111.refs_0_, bf16[1024,2048]{1,0:T(8,128)(2,1)} %get-tuple-element.112.refs_1_, bf16[1024,768]{1,0:T(8,128)(2,1)} %get-tuple-element.130.refs_2_, bf16[1024,768]{1,0:T(8,128)(2,1)} %get-tuple-element.131.refs_3_, ...), custom_call_target="tpu_custom_call" | custom-call | flops 19327352832 | bytes 35651584 | tf_op jit(solution)/shard_map/pallas_call | solution.py:863
  369.8 33.2 %shard_map.374 = (bf16[1024,768]{1,0:T(8,128)(2,1)}, bf16[1024,768]{1,0:T(8,128)(2,1)}, bf16[1024,768]{1,0:T(8,128)(2,1)}, bf16[1024,2048]{1,0:T(8,128)(2,1)}, b...) custom-call(bf16[1024,2048]{1,0:T(8,128)(2,1)} %get-tuple-element.111.refs_0_, ...), custom_call_target="tpu_custom_call" | custom-call | flops 19327352832 | bytes 30932992 | tf_op jit(solution)/shard_map/pallas_call | solution.py:783
  402.9 43.6 %shard_map.375 = (bf16[1024,640]{1,0:T(8,128)(2,1)}, bf16[1024,640]{1,0:T(8,128)(2,1)}, bf16[1024,640]{1,0:T(8,128)(2,1)}, bf16[1024,2048]{1,0:T(8,128)(2,1)}, b...) custom-call(bf16[1024,2048]{1,0:T(8,128)(2,1)} %get-tuple-element.120.refs_0_.refs_5_.refs_6_, ...), custom_call_target="tpu_custom_call" | custom-call | flops 16106127360 | bytes 28573696 | tf_op jit(solution)/shard_map/pallas_call | solution.py:783
  446.6 1.8 multiply_reduce_fusion.1
  448.6 1.2 fusion.35
  449.8 47.0 %shard_map.376 = (bf16[4,3,512,640]{3,2,1,0:T(8,128)(2,1)}, bf16[1024,2048]{1,0:T(8,128)(2,1)}) custom-call(bf16[1024,2048]{1,0:T(8,128)(2,1)} %get-tuple-element.111.refs_0_, bf16[1024,2048]{1,0:T(8,128)(2,1)} %get-tuple-element.112.refs_1_, bf16[1024,640]{1,0:T(8,128)(2,1)} %get-tuple-element.141.refs_2_, bf16[1024,640]{1,0:T(8,128)(2,1)} %get-tuple-element.142.refs_3_, ...), custom_call_target="tpu_custom_call" | custom-call | flops 16106127360 | bytes 32505856 | tf_op jit(solution)/shard_map/pallas_call | solution.py:863
  496.8 45.5 %shard_map.377 = (bf16[1024,768]{1,0:T(8,128)(2,1)}, bf16[1024,768]{1,0:T(8,128)(2,1)}, bf16[1024,768]{1,0:T(8,128)(2,1)}, bf16[1024,2048]{1,0:T(8,128)(2,1)}, b...) custom-call(bf16[1024,2048]{1,0:T(8,128)(2,1)} %get-tuple-element.120.refs_0_.refs_5_.refs_6_, ...), custom_call_target="tpu_custom_call" | custom-call | flops 19327352832 | bytes 30932992 | tf_op jit(solution)/shard_map/pallas_call | solution.py:783
  542.4 48.0 %shard_map.378 = (bf16[4,3,512,768]{3,2,1,0:T(8,128)(2,1)}, f32[2048,128]{1,0:T(8,128)}, f32[128,2048]{1,0:T(8,128)}) custom-call(bf16[1024,2048]{1,0:T(8,128)(2,1)} %get-tuple-element.111.refs_0_, bf16[1024,2048]{1,0:T(8,128)(2,1)} %get-tuple-element.112.refs_1_, bf16[1024,768]{1,0:T(8,128)(2,1)} %get-tuple-element.153.refs_2_, ...), custom_call_target="tpu_custom_call" | custom-call | flops 19327352832 | bytes 35651584 | tf_op jit(solution)/shard_map/pallas_call | solution.py:863
  592.0 0.9 fusion.22
  592.9 4.6 shard_map.383
  597.5 1.8 reshape.249
  599.8 2.5 fusion.34
  602.3 44.0 %shard_map.379 = (bf16[1024,768]{1,0:T(8,128)(2,1)}, f32[1,768]{1,0:T(1,128)}, bf16[1024,2048]{1,0:T(8,128)(2,1)}, bf16[1024,2048]{1,0:T(8,128)(2,1)}) custom-call(s32[1]{0:T(128)} %bitcast.3.refs_0_.refs_4_, bf16[1024,2048]{1,0:T(8,128)(2,1)} %get-tuple-element.150.refs_1_, bf16[4,512,1024]{2,1,0:T(8,128)(2,1)} %bitcast.126, ...), custom_call_target="tpu_custom_call" | custom-call | flops 6442450944 | bytes 16777216 | tf_op jit(solution)/shard_map/pallas_call | solution.py:1268
  646.4 41.0 %shard_map.380 = (bf16[1024,768]{1,0:T(8,128)(2,1)}, f32[1,768]{1,0:T(1,128)}, bf16[1024,2048]{1,0:T(8,128)(2,1)}, f32[128,2048]{1,0:T(8,128)}) custom-call(s32[1]{0:T(128)} %bitcast.2.refs_0_.refs_4_, bf16[1024,2048]{1,0:T(8,128)(2,1)} %get-tuple-element.163.refs_1_.refs_5_, bf16[4,512,1024]{2,1,0:T(8,128)(2,1)} %bitcast.127, ...), custom_call_target="tpu_custom_call" | custom-call | flops 6442450944 | bytes 16777216 | tf_op jit(solution)/shard_map/pallas_call | solution.py:1268
  687.4 0.7 add_reduce_fusion
  688.3 44.3 %shard_map.381 = (bf16[4,512,1024]{2,1,0:T(8,128)(2,1)}, f32[128,2048]{1,0:T(8,128)}) custom-call(bf16[1024,2048]{1,0:T(8,128)(2,1)} %get-tuple-element.168.refs_0_, bf16[1024,2048]{1,0:T(8,128)(2,1)} %get-tuple-element.150.refs_1_, bf16[1024,768]{1,0:T(8,128)(2,1)} %get-tuple-element.169.refs_2_, bf16[1024,256]{1,0:T(8,128)(2,1)} %get-tuple-element.170.refs_3_, ...), custom_call_target="tpu_custom_call" | custom-call | flops 8589934592 | bytes 33554432 | tf_op jit(solution)/shard_map/pallas_call | solution.py:916
  732.6 2.2 fusion.13
  735.1 0.7 copy.89
  735.8 2.5 fusion.25
  738.2 1.1 maximum_bitcast_fusion.1
  739.3 46.7 %shard_map.382 = (f32[8,128]{1,0:T(8,128)}, f32[512,1024]{1,0:T(8,128)}, f32[128,2048]{1,0:T(8,128)}) custom-call(f32[32,8,128]{2,1,0:T(8,128)} %bitcast.108, bf16[4,512,1024]{2,1,0:T(8,128)(2,1)} %get-tuple-element.179.refs_1_, bf16[1024,2048]{1,0:T(8,128)(2,1)} %get-tuple-element.180.refs_2_, bf16[3,512,768]{2,1,0:T(8,128)(2,1)} %bitcast.97), custom_call_target="tpu_custom_call" | custom-call | tf_op jit(solution)/shard_map/pallas_call | solution.py:626
  786.0 1.4 fusion.38
  787.4 0.7 slice.125
  788.1 0.7 slice.119
  788.9 6.1 shard_map.384
  795.6 0.7 slice_reduce_fusion
  797.0 1.4 slice_bitcast_fusion
  798.4 2.1 copy.85
  800.5 1.4 fusion.23
  801.8 1.1 maximum_bitcast_fusion
  (120 shorter events, 9.8 us)
Async XLA Ops:
  7.2 3.5 copy-start.24
  7.2 3.6 copy-start.25
  7.2 3.7 copy-start.26
  7.2 3.7 copy-start.19
  7.2 3.9 copy-start.23
  7.2 3.9 copy-start.22
  7.3 3.9 copy-start.21
  7.3 59.6 %all-gather.8.cloned.1.call-start = ((), (), s32[]{:S(2)}) async-start(), calls=%async_computation.3 | async-start | bytes 5242880 | tf_op jit(solution)/shard_map/all_gather | solution.py:1369
  10.6 215.1 %all-gather.10.cloned.1.call-start = ((), (), s32[]{:S(2)}) async-start(), calls=%async_computation.7 | async-start | bytes 11796480 | tf_op jit(solution)/shard_map/all_gather | solution.py:1394
  59.4 1.4 copy-start.10
  59.4 209.7 %all-gather.12.cloned.1.call-start = ((), (), s32[]{:S(2)}) async-start(), calls=%async_computation.8 | async-start | bytes 9830400 | tf_op jit(solution)/shard_map/all_gather | solution.py:1394
  60.2 4.3 copy-start.20
  60.2 4.9 copy-start.13
  60.2 309.6 %all-gather.14.cloned.1.call-start = ((), (), s32[]{:S(2)}) async-start(), calls=%async_computation.9 | async-start | bytes 11796480 | tf_op jit(solution)/shard_map/all_gather | solution.py:1394
  60.8 481.6 %reduce-scatter.4.cloned.1.call-start = ((), (), s32[]{:S(2)}) async-start(), calls=%async_computation.4 | async-start | bytes 11796480 | tf_op jit(solution)/shard_map/reduce_scatter | solution.py:1439
  61.1 1.0 copy-start.11
  109.5 57.7 %copy-start.2 = (bf16[2,1,128,2048]{3,2,1,0:T(8,128)(2,1)S(1)}, bf16[2,1,128,2048]{3,2,1,0:T(8,128)(2,1)}, u32[]{:S(2)}) copy-start(bf16[2,1,128,2048]{3,2,1,0:T(8,128)(2,1)} %refs_7_.4) | copy-start | bytes 3145732
  223.8 1.0 copy-start
  223.8 1.0 copy-start.14
  369.0 277.4 %reduce-scatter.6.cloned.1.call-start = ((), (), s32[]{:S(2)}) async-start(), calls=%async_computation.5 | async-start | bytes 9830400 | tf_op jit(solution)/shard_map/reduce_scatter | solution.py:1439
  446.6 1.8 copy-start.5
  446.6 2.0 copy-start.8
  496.8 242.5 %reduce-scatter.8.cloned.1.call-start = ((), (), s32[]{:S(2)}) async-start(), calls=%async_computation.6 | async-start | bytes 11796480 | tf_op jit(solution)/shard_map/reduce_scatter | solution.py:1439
  590.4 0.7 copy-start.12
  590.4 1.5 copy-start.17
  590.4 1.5 copy-start.18
  590.4 1.5 copy-start.9
  592.9 6.4 copy-start.1
  592.9 6.4 copy-start.4
  592.9 6.4 copy-start.15
  646.4 41.0 %copy-start.16 = (f32[1,768]{1,0:T(1,128)S(1)}, f32[1,768]{1,0:T(1,128)}, u32[]{:S(2)}) copy-start(f32[1,768]{1,0:T(1,128)} %get-tuple-element.177) | copy-start | bytes 9220
  688.3 44.3 %copy-start.3 = (bf16[2,1,128,2048]{3,2,1,0:T(8,128)(2,1)S(1)}, bf16[2,1,128,2048]{3,2,1,0:T(8,128)(2,1)}, u32[]{:S(2)}) copy-start(bf16[2,1,128,2048]{3,2,1,0:T(8,128)(2,1)} %refs_7_.4) | copy-start | bytes 3145732
  786.0 11.0 %copy-start.6 = (f32[512,1024]{1,0:T(8,128)S(1)}, f32[512,1024]{1,0:T(8,128)}, u32[]{:S(2)}) copy-start(f32[512,1024]{1,0:T(8,128)} %get-tuple-element.184) | copy-start | bytes 6291460
  798.4 3.5 copy-start.7
Sparse Core Ops, SparseCore 0:
  10.8 55.4 all-gather.7
  68.1 96.3 all-gather.9
  166.3 83.2 all-gather.11
  251.3 96.3 all-gather.13
  369.1 93.4 reduce-scatter.3
  496.9 82.4 reduce-scatter.5
  590.6 95.4 reduce-scatter.7

commit v9 on v8

--- a/solution.py
+++ b/solution.py
@@ -91,10 +91,10 @@
         return remote(theirs(owner, chunk), theirs(owner, chunk), cross, (slot, chunk), place.partner)
 
     def arrived_up(step, chunk):
-        return remote(at(chip - step, chunk), at(chip - step, chunk), up, (step - 1, chunk), place.above)
+        return remote(at(chip - step, chunk), at(chip - step, chunk), up, (step - 1, chunk), place.partner)
 
     def arrived_down(step, chunk):
-        return remote(at(chip + step, chunk), at(chip + step, chunk), down, (step - 1, chunk), place.below)
+        return remote(at(chip + step, chunk), at(chip + step, chunk), down, (step - 1, chunk), place.partner)
 
     both = range(CHUNKS)
 
@@ -192,6 +192,10 @@
     def downward(step, k, chunk):
         cut = pl.ds(chunk * part, part)
         return remote(held.at[k, cut], down_in.at[step, cut], down, (step, chunk), place.below)
+
+    def came(buffer, sems, step, chunk):
+        piece = buffer.at[step, pl.ds(chunk * part, part)]
+        return remote(piece, piece, sems, (step, chunk), place.partner)
 
     def add(k, chunk, target, others):
         def strip(i, carry):
@@ -228,7 +232,7 @@
 
             @pl.when(place.not_bottom)
             def _():
-                upward(step - 1, k, chunk).wait_recv()
+                came(up_in, up, step - 1, chunk).wait_recv()
                 add(k, chunk, held, [(up_in, step - 1)])
 
             pl.when(jnp.logical_not(place.not_bottom))(lambda: add(k, chunk, held, []))
@@ -243,7 +247,7 @@
 
             @pl.when(place.not_top)
             def _():
-                downward(step - 1, k, chunk).wait_recv()
+                came(down_in, down, step - 1, chunk).wait_recv()
                 add(k, chunk, held, [(down_in, step - 1)])
 
             pl.when(jnp.logical_not(place.not_top))(lambda: add(k, chunk, held, []))
@@ -258,18 +262,18 @@
 
         @pl.when(place.not_top & place.not_bottom)
         def _():
-            upward(last, chip, chunk).wait_recv()
-            downward(last, chip, chunk).wait_recv()
+            came(up_in, up, last, chunk).wait_recv()
+            came(down_in, down, last, chunk).wait_recv()
             add(chip, chunk, None, [(up_in, last), (down_in, last)])
 
         @pl.when(jnp.logical_not(place.not_top))
         def _():
-            upward(last, chip, chunk).wait_recv()
+            came(up_in, up, last, chunk).wait_recv()
             add(chip, chunk, None, [(up_in, last)])
 
         @pl.when(jnp.logical_not(place.not_bottom))
         def _():
-            downward(last, chip, chunk).wait_recv()
+            came(down_in, down, last, chunk).wait_recv()
             add(chip, chunk, None, [(down_in, last)])
 
     def end():

time: 815 us -> 815 us (level)
  no operation moved by 1% of the time
where the time goes in v9:
time: 815 us; the launch traced here: 810 us
  Pallas kernels  747 us (92%)
  other arithmetic  26.1 us (3%)
  local copies, waits for them, and re-layouts  20.1 us (2%)
  between operations  14.9 us (2%)
    pallas_call x6, Pallas kernels, ffn(): pl.pallas_call(functools.partial(ffn_kernel, transfers, at, steps, expert...  238 us
    pallas_call x3, Pallas kernels, ffn_grads(): pl.pallas_call(functools.partial(ffn_grads_kernel, transfers, at, groups,...  122 us
    pallas_call x2, Pallas kernels, attend(): pl.pallas_call(functools.partial(attend_kernel, heads, transfers), out_sh...  100 us
    pallas_call x2, Pallas kernels, exchange(): pl.pallas_call(functools.partial(exchange_kernel, transfers), out_shape=t...  98.8 us
    pallas_call x2, Pallas kernels, attend_back(): pl.pallas_call(functools.partial(attend_back_kernel, heads, transfers), o...  85 us
    pallas_call x1, Pallas kernels, opening(): pl.pallas_call(functools.partial(opening_kernel, transfers, cut), in_spec...  47.5 us
    pallas_call x1, Pallas kernels, attention_grads(): pl.pallas_call(functools.partial(attention_grads_kernel, transfers, group...  44.3 us
  transfers between devices with their start and end apart: 7, of which 0 were waited for; matrix products, arithmetic and copies ran while one was open for 4% of the time, Pallas kernels for 86%

profile of v9, /device:TPU:0, one launch (start us, length us, event | category | flops | bytes accessed | tf_op | source)
XLA Modules:
  0.0 809.9 jit_solution(8628944686859055272)
XLA Ops:
  7.3 1.1 copy.78
  8.4 2.2 pad_maximum_fusion
  11.9 47.5 %shard_map.366 = (bf16[32,16,128]{2,1,0:T(8,128)(2,1)}, bf16[1024,2048]{1,0:T(8,128)(2,1)}, bf16[3,512,768]{2,1,0:T(8,128)(2,1)}, bf16[3,512,640]{2,1,0:T(8,128)(2,1)}, bf16[3,512,768]{2,1,0:T(8,128)(2,1)}) custom-call(bf16[16,128]{1,0:T(8,128)(2,1)} %pad_bitcast_fusion.refs_0_, bf16[2,1,128,2048]{3,2,1,0:T(8,128)(2,1)} %refs_7_.4, ...), custom_call_target="tpu_custom_call" | custom-call | tf_op jit(solution)/shard_map/pallas_call | solution.py:989
  59.5 0.7 all-gather.12.cloned.1.call-update
  61.2 0.7 reshape.257.refs_2_
  63.4 1.1 broadcast_in_dim_reshape.4
  65.7 1.1 fusion.24.refs_5_.refs_7_
  66.9 42.6 %shard_map.367 = (bf16[1024,2048]{1,0:T(8,128)(2,1)}, bf16[1024,768]{1,0:T(8,128)(2,1)}, bf16[1024,256]{1,0:T(8,128)(2,1)}, f32[1024,2]{1,0:T(8,128)}, bf16[1024...) custom-call(s32[1]{0:T(128)} %bitcast.3.refs_0_.refs_4_, bf16[1024,2048]{1,0:T(8,128)(2,1)} %get-tuple-element.105.refs_1_, ...), custom_call_target="tpu_custom_call" | custom-call | flops 5100273664 | bytes 16777216 | tf_op jit(solution)/shard_map/pallas_call | solution.py:1234
  109.5 57.7 %shard_map.368 = (bf16[1024,2048]{1,0:T(8,128)(2,1)}, bf16[1024,768]{1,0:T(8,128)(2,1)}, bf16[1024,256]{1,0:T(8,128)(2,1)}, f32[1024,2]{1,0:T(8,128)}, bf16[1024...) custom-call(s32[1]{0:T(128)} %bitcast.2.refs_0_.refs_4_, ...), custom_call_target="tpu_custom_call" | custom-call | flops 5100273664 | bytes 16777216 | tf_op jit(solution)/shard_map/pallas_call | solution.py:1234
  167.3 2.1 fusion.19
  169.4 1.0 multiply_convert_fusion.3.refs_0_
  170.3 52.0 %shard_map.369 = (bf16[1024,2048]{1,0:T(8,128)(2,1)}, f32[128,2048]{1,0:T(8,128)}) custom-call(bf16[128,2048]{1,0:T(8,128)(2,1)} %multiply_convert_fusion.3.refs_0_, bf16[1024,2048]{1,0:T(8,128)(2,1)} %get-tuple-element.110.refs_1_), custom_call_target="tpu_custom_call" | custom-call | tf_op jit(solution)/shard_map/pallas_call | solution.py:630
  222.4 1.4 multiply_reduce_fusion.4
  223.9 0.9 copy-done
  224.8 0.9 multiply_convert_fusion.2.refs_7_
  225.8 43.4 %shard_map.370 = (bf16[1024,768]{1,0:T(8,128)(2,1)}, bf16[1024,768]{1,0:T(8,128)(2,1)}, bf16[1024,768]{1,0:T(8,128)(2,1)}, bf16[1024,2048]{1,0:T(8,128)(2,1)}, b...) custom-call(bf16[1024,2048]{1,0:T(8,128)(2,1)} %get-tuple-element.111.refs_0_, ...), custom_call_target="tpu_custom_call" | custom-call | flops 19327352832 | bytes 30932992 | tf_op jit(solution)/shard_map/pallas_call | solution.py:787
  269.2 43.1 %shard_map.371 = (bf16[1024,640]{1,0:T(8,128)(2,1)}, bf16[1024,640]{1,0:T(8,128)(2,1)}, bf16[1024,640]{1,0:T(8,128)(2,1)}, bf16[1024,2048]{1,0:T(8,128)(2,1)}, b...) custom-call(bf16[1024,2048]{1,0:T(8,128)(2,1)} %get-tuple-element.111.refs_0_, ...), custom_call_target="tpu_custom_call" | custom-call | flops 16106127360 | bytes 28573696 | tf_op jit(solution)/shard_map/pallas_call | solution.py:787
  312.3 29.6 %shard_map.372 = (bf16[1024,768]{1,0:T(8,128)(2,1)}, bf16[1024,768]{1,0:T(8,128)(2,1)}, bf16[1024,768]{1,0:T(8,128)(2,1)}, bf16[1024,2048]{1,0:T(8,128)(2,1)}, b...) custom-call(bf16[1024,2048]{1,0:T(8,128)(2,1)} %get-tuple-element.120.refs_0_.refs_5_.refs_6_, ...), custom_call_target="tpu_custom_call" | custom-call | flops 19327352832 | bytes 30932992 | tf_op jit(solution)/shard_map/pallas_call | solution.py:787
  341.8 27.2 %shard_map.373.refs_8_ = bf16[4,3,512,768]{3,2,1,0:T(8,128)(2,1)} custom-call(bf16[1024,2048]{1,0:T(8,128)(2,1)} %get-tuple-element.111.refs_0_, bf16[1024,2048]{1,0:T(8,128)(2,1)} %get-tuple-element.112.refs_1_, bf16[1024,768]{1,0:T(8,128)(2,1)} %get-tuple-element.130.refs_2_, bf16[1024,768]{1,0:T(8,128)(2,1)} %get-tuple-element.131.refs_3_, ...), custom_call_target="tpu_custom_call" | custom-call | flops 19327352832 | bytes 35651584 | tf_op jit(solution)/shard_map/pallas_call | solution.py:867
  369.8 33.2 %shard_map.374 = (bf16[1024,768]{1,0:T(8,128)(2,1)}, bf16[1024,768]{1,0:T(8,128)(2,1)}, bf16[1024,768]{1,0:T(8,128)(2,1)}, bf16[1024,2048]{1,0:T(8,128)(2,1)}, b...) custom-call(bf16[1024,2048]{1,0:T(8,128)(2,1)} %get-tuple-element.111.refs_0_, ...), custom_call_target="tpu_custom_call" | custom-call | flops 19327352832 | bytes 30932992 | tf_op jit(solution)/shard_map/pallas_call | solution.py:787
  402.9 43.6 %shard_map.375 = (bf16[1024,640]{1,0:T(8,128)(2,1)}, bf16[1024,640]{1,0:T(8,128)(2,1)}, bf16[1024,640]{1,0:T(8,128)(2,1)}, bf16[1024,2048]{1,0:T(8,128)(2,1)}, b...) custom-call(bf16[1024,2048]{1,0:T(8,128)(2,1)} %get-tuple-element.120.refs_0_.refs_5_.refs_6_, ...), custom_call_target="tpu_custom_call" | custom-call | flops 16106127360 | bytes 28573696 | tf_op jit(solution)/shard_map/pallas_call | solution.py:787
  446.6 1.8 multiply_reduce_fusion.1
  448.6 1.2 fusion.35
  449.8 47.0 %shard_map.376 = (bf16[4,3,512,640]{3,2,1,0:T(8,128)(2,1)}, bf16[1024,2048]{1,0:T(8,128)(2,1)}) custom-call(bf16[1024,2048]{1,0:T(8,128)(2,1)} %get-tuple-element.111.refs_0_, bf16[1024,2048]{1,0:T(8,128)(2,1)} %get-tuple-element.112.refs_1_, bf16[1024,640]{1,0:T(8,128)(2,1)} %get-tuple-element.141.refs_2_, bf16[1024,640]{1,0:T(8,128)(2,1)} %get-tuple-element.142.refs_3_, ...), custom_call_target="tpu_custom_call" | custom-call | flops 16106127360 | bytes 32505856 | tf_op jit(solution)/shard_map/pallas_call | solution.py:867
  496.8 45.5 %shard_map.377 = (bf16[1024,768]{1,0:T(8,128)(2,1)}, bf16[1024,768]{1,0:T(8,128)(2,1)}, bf16[1024,768]{1,0:T(8,128)(2,1)}, bf16[1024,2048]{1,0:T(8,128)(2,1)}, b...) custom-call(bf16[1024,2048]{1,0:T(8,128)(2,1)} %get-tuple-element.120.refs_0_.refs_5_.refs_6_, ...), custom_call_target="tpu_custom_call" | custom-call | flops 19327352832 | bytes 30932992 | tf_op jit(solution)/shard_map/pallas_call | solution.py:787
  542.4 48.0 %shard_map.378 = (bf16[4,3,512,768]{3,2,1,0:T(8,128)(2,1)}, f32[2048,128]{1,0:T(8,128)}, f32[128,2048]{1,0:T(8,128)}) custom-call(bf16[1024,2048]{1,0:T(8,128)(2,1)} %get-tuple-element.111.refs_0_, bf16[1024,2048]{1,0:T(8,128)(2,1)} %get-tuple-element.112.refs_1_, bf16[1024,768]{1,0:T(8,128)(2,1)} %get-tuple-element.153.refs_2_, ...), custom_call_target="tpu_custom_call" | custom-call | flops 19327352832 | bytes 35651584 | tf_op jit(solution)/shard_map/pallas_call | solution.py:867
  592.0 0.9 fusion.22
  592.9 4.6 shard_map.383
  597.5 1.8 reshape.249
  599.8 2.5 fusion.34
  602.3 44.0 %shard_map.379 = (bf16[1024,768]{1,0:T(8,128)(2,1)}, f32[1,768]{1,0:T(1,128)}, bf16[1024,2048]{1,0:T(8,128)(2,1)}, bf16[1024,2048]{1,0:T(8,128)(2,1)}) custom-call(s32[1]{0:T(128)} %bitcast.3.refs_0_.refs_4_, bf16[1024,2048]{1,0:T(8,128)(2,1)} %get-tuple-element.150.refs_1_, bf16[4,512,1024]{2,1,0:T(8,128)(2,1)} %bitcast.126, ...), custom_call_target="tpu_custom_call" | custom-call | flops 6442450944 | bytes 16777216 | tf_op jit(solution)/shard_map/pallas_call | solution.py:1272
  646.4 41.0 %shard_map.380 = (bf16[1024,768]{1,0:T(8,128)(2,1)}, f32[1,768]{1,0:T(1,128)}, bf16[1024,2048]{1,0:T(8,128)(2,1)}, f32[128,2048]{1,0:T(8,128)}) custom-call(s32[1]{0:T(128)} %bitcast.2.refs_0_.refs_4_, bf16[1024,2048]{1,0:T(8,128)(2,1)} %get-tuple-element.163.refs_1_.refs_5_, bf16[4,512,1024]{2,1,0:T(8,128)(2,1)} %bitcast.127, ...), custom_call_target="tpu_custom_call" | custom-call | flops 6442450944 | bytes 16777216 | tf_op jit(solution)/shard_map/pallas_call | solution.py:1272
  687.4 0.7 add_reduce_fusion
  688.3 44.3 %shard_map.381 = (bf16[4,512,1024]{2,1,0:T(8,128)(2,1)}, f32[128,2048]{1,0:T(8,128)}) custom-call(bf16[1024,2048]{1,0:T(8,128)(2,1)} %get-tuple-element.168.refs_0_, bf16[1024,2048]{1,0:T(8,128)(2,1)} %get-tuple-element.150.refs_1_, bf16[1024,768]{1,0:T(8,128)(2,1)} %get-tuple-element.169.refs_2_, bf16[1024,256]{1,0:T(8,128)(2,1)} %get-tuple-element.170.refs_3_, ...), custom_call_target="tpu_custom_call" | custom-call | flops 8589934592 | bytes 33554432 | tf_op jit(solution)/shard_map/pallas_call | solution.py:920
  732.6 2.2 fusion.13
  735.1 0.7 copy.89
  735.8 2.5 fusion.25
  738.2 1.1 maximum_bitcast_fusion.1
  739.3 46.7 %shard_map.382 = (f32[8,128]{1,0:T(8,128)}, f32[512,1024]{1,0:T(8,128)}, f32[128,2048]{1,0:T(8,128)}) custom-call(f32[32,8,128]{2,1,0:T(8,128)} %bitcast.108, bf16[4,512,1024]{2,1,0:T(8,128)(2,1)} %get-tuple-element.179.refs_1_, bf16[1024,2048]{1,0:T(8,128)(2,1)} %get-tuple-element.180.refs_2_, bf16[3,512,768]{2,1,0:T(8,128)(2,1)} %bitcast.97), custom_call_target="tpu_custom_call" | custom-call | tf_op jit(solution)/shard_map/pallas_call | solution.py:630
  786.0 1.4 fusion.38
  787.4 0.7 slice.125
  788.1 0.7 slice.119
  788.9 6.1 shard_map.384
  795.6 0.7 slice_reduce_fusion
  797.0 1.4 slice_bitcast_fusion
  798.4 2.1 copy.85
  800.5 1.4 fusion.23
  801.8 1.1 maximum_bitcast_fusion
  (120 shorter events, 9.8 us)
Async XLA Ops:
  7.2 3.5 copy-start.24
  7.2 3.6 copy-start.25
  7.2 3.7 copy-start.26
  7.2 3.7 copy-start.19
  7.2 3.9 copy-start.23
  7.2 3.9 copy-start.22
  7.3 3.9 copy-start.21
  7.3 59.6 %all-gather.8.cloned.1.call-start = ((), (), s32[]{:S(2)}) async-start(), calls=%async_computation.3 | async-start | bytes 5242880 | tf_op jit(solution)/shard_map/all_gather | solution.py:1373
  10.6 215.1 %all-gather.10.cloned.1.call-start = ((), (), s32[]{:S(2)}) async-start(), calls=%async_computation.7 | async-start | bytes 11796480 | tf_op jit(solution)/shard_map/all_gather | solution.py:1398
  59.4 1.4 copy-start.10
  59.4 209.7 %all-gather.12.cloned.1.call-start = ((), (), s32[]{:S(2)}) async-start(), calls=%async_computation.8 | async-start | bytes 9830400 | tf_op jit(solution)/shard_map/all_gather | solution.py:1398
  60.2 4.3 copy-start.20
  60.2 4.9 copy-start.13
  60.2 309.6 %all-gather.14.cloned.1.call-start = ((), (), s32[]{:S(2)}) async-start(), calls=%async_computation.9 | async-start | bytes 11796480 | tf_op jit(solution)/shard_map/all_gather | solution.py:1398
  60.8 481.6 %reduce-scatter.4.cloned.1.call-start = ((), (), s32[]{:S(2)}) async-start(), calls=%async_computation.4 | async-start | bytes 11796480 | tf_op jit(solution)/shard_map/reduce_scatter | solution.py:1443
  61.1 1.0 copy-start.11
  109.5 57.7 %copy-start.2 = (bf16[2,1,128,2048]{3,2,1,0:T(8,128)(2,1)S(1)}, bf16[2,1,128,2048]{3,2,1,0:T(8,128)(2,1)}, u32[]{:S(2)}) copy-start(bf16[2,1,128,2048]{3,2,1,0:T(8,128)(2,1)} %refs_7_.4) | copy-start | bytes 3145732
  223.8 1.0 copy-start
  223.8 1.0 copy-start.14
  369.0 277.4 %reduce-scatter.6.cloned.1.call-start = ((), (), s32[]{:S(2)}) async-start(), calls=%async_computation.5 | async-start | bytes 9830400 | tf_op jit(solution)/shard_map/reduce_scatter | solution.py:1443
  446.6 1.8 copy-start.5
  446.6 2.0 copy-start.8
  496.8 242.5 %reduce-scatter.8.cloned.1.call-start = ((), (), s32[]{:S(2)}) async-start(), calls=%async_computation.6 | async-start | bytes 11796480 | tf_op jit(solution)/shard_map/reduce_scatter | solution.py:1443
  590.4 0.7 copy-start.12
  590.4 1.5 copy-start.17
  590.4 1.5 copy-start.18
  590.4 1.5 copy-start.9
  592.9 6.4 copy-start.1
  592.9 6.4 copy-start.4
  592.9 6.4 copy-start.15
  646.4 41.0 %copy-start.16 = (f32[1,768]{1,0:T(1,128)S(1)}, f32[1,768]{1,0:T(1,128)}, u32[]{:S(2)}) copy-start(f32[1,768]{1,0:T(1,128)} %get-tuple-element.177) | copy-start | bytes 9220
  688.3 44.3 %copy-start.3 = (bf16[2,1,128,2048]{3,2,1,0:T(8,128)(2,1)S(1)}, bf16[2,1,128,2048]{3,2,1,0:T(8,128)(2,1)}, u32[]{:S(2)}) copy-start(bf16[2,1,128,2048]{3,2,1,0:T(8,128)(2,1)} %refs_7_.4) | copy-start | bytes 3145732
  786.0 11.0 %copy-start.6 = (f32[512,1024]{1,0:T(8,128)S(1)}, f32[512,1024]{1,0:T(8,128)}, u32[]{:S(2)}) copy-start(f32[512,1024]{1,0:T(8,128)} %get-tuple-element.184) | copy-start | bytes 6291460
  798.4 3.5 copy-start.7
Sparse Core Ops, SparseCore 0:
  10.8 55.4 all-gather.7
  68.1 96.3 all-gather.9
  166.3 83.2 all-gather.11
  251.3 96.3 all-gather.13
  369.1 93.4 reduce-scatter.3
  496.9 82.4 reduce-scatter.5
  590.6 95.4 reduce-scatter.7
